TPU v7x, 32 devices: a whole 2x2x4 slice. The times are simulated.
32 devices in a mesh: dp: 4 (over y, core), seq: 8 (over z, x).
Axes of the slice: x: 2, y: 2, z: 4, core: 2. Of those that a mesh axis runs over, the one named last changes fastest.
Arguments:
- tokens: bfloat16 [2, 4, 4096, 2048], P(None, 'dp', 'seq'), may hold values from -6 to 6
- segment_ids: int32 [2, 4, 4096], P(None, 'dp'), may hold values from 0 to 3, as said below
- w_qkv: bfloat16 [2048, 6144], P(('dp', 'seq')), may hold values from -0.125 to 0.125
- w_out: bfloat16 [2048, 2048], P(('dp', 'seq')), may hold values from -0.5 to 0.5
- w_gate_up: bfloat16 [2048, 11008], P(('dp', 'seq')), may hold values from -0.125 to 0.125
- w_down: bfloat16 [5504, 2048], P(('dp', 'seq')), may hold values from -0.078125 to 0.078125
- gain_attn: bfloat16 [2048], P(('dp', 'seq')), may hold values from 0.5 to 1.5
- gain_mlp: bfloat16 [2048], P(('dp', 'seq')), may hold values from 0.5 to 1.5
- cotangent: bfloat16 [2, 4, 4096, 2048], P(None, 'dp', 'seq'), may hold values from -6 to 6
Outputs:
- layer_out: bfloat16 [2, 4, 4096, 2048], P(None, 'dp', 'seq')
- grad_tokens: float32 [2, 4, 4096, 2048], P(None, 'dp', 'seq')
- grad_w_qkv: float32 [2048, 6144], P(('dp', 'seq'))
- grad_w_out: float32 [2048, 2048], P(('dp', 'seq'))
- grad_w_gate_up: float32 [2048, 11008], P(('dp', 'seq'))
- grad_w_down: float32 [5504, 2048], P(('dp', 'seq'))
- grad_gain_attn: float32 [2048], P(('dp', 'seq'))
- grad_gain_mlp: float32 [2048], P(('dp', 'seq'))
Inputs may be any that keep to these rules, and one draw needn't show every extreme that they name: `segment_ids`: along each sequence the ids start at 0 and never fall; every document but the last of a sequence has 16 tokens or more; for each of the 4 sequence slots, one of the 2 micro-batches, drawn from the seed, holds a single document over all 4096 tokens.
All inputs are finite; a program needn't handle non-finite values.
Results may differ from a plain program's by a relative error of at most 0.013.
Values may be sent and summed in bfloat16 or wider, within the bound.
No kernel may reach another device: no remote copies, remote signals or barrier semaphores. Data moves between devices by JAX's collectives and lax.ppermute only.
A program may use at most 832 MiB of HBM per device.

v0:
```python
import math

import jax
import jax.numpy as jnp
from jax import lax
from jax.sharding import PartitionSpec as P

D = 2048
H = 16
HD = 128
FF = 5504
WINDOW = 2048
MB = 2


epsilon = 1e-05
masked_score = -1e30


def from_behind(block, axis, distance):
    devices = range(lax.axis_size(axis))
    route = [(i - distance, i) for i in devices if i - distance in devices]
    return lax.ppermute(block, axis, route)


def fetch_weights(w_qkv, w_out, w_gate_up, w_down, gain_attn, gain_mlp):
    return (
        lax.all_gather(w_qkv, ("dp", "seq"), axis=0, tiled=True),
        lax.all_gather(w_out, ("dp", "seq"), axis=0, tiled=True),
        lax.all_gather(w_gate_up, ("dp", "seq"), axis=0, tiled=True),
        lax.all_gather(w_down, ("dp", "seq"), axis=0, tiled=True),
        lax.all_gather(gain_attn, ("dp", "seq"), axis=0, tiled=True),
        lax.all_gather(gain_mlp, ("dp", "seq"), axis=0, tiled=True),
    )


def norm_forward(values, gain_vector):
    row_scale = lax.rsqrt(jnp.mean(values * values, axis=-1, keepdims=True) + epsilon)
    normed = values * row_scale
    rounded = (normed * gain_vector.astype(jnp.float32)).astype(jnp.bfloat16)
    return (normed, row_scale, rounded)


def norm_backward(grad_in, normed, row_scale, gain_vector):
    gain_grad = jnp.sum(grad_in * normed, axis=0)
    scaled = grad_in * gain_vector.astype(jnp.float32)
    inner_mean = jnp.mean(scaled * normed, axis=-1, keepdims=True)
    return (row_scale * (scaled - normed * inner_mean), gain_grad)


def collect_keys(keys_values, reach_blocks):
    arrived = [from_behind(keys_values, "seq", offset) for offset in range(reach_blocks, 0, -1)]
    return jnp.concatenate(arrived + [keys_values], axis=0)


def return_grads(grad_window, reach_blocks, row_count):
    summed = grad_window[reach_blocks * row_count :]
    for offset in range(1, reach_blocks + 1):
        start_row = (reach_blocks - offset) * row_count
        block_grad = grad_window[start_row : start_row + row_count]
        summed = summed + from_behind(block_grad.astype(jnp.bfloat16), "seq", -offset).astype(
            block_grad.dtype
        )
    return summed


def window_mask(segment_row, seq_index, row_count, reach_blocks):
    key_span = (reach_blocks + 1) * row_count
    query_pos = seq_index * row_count + jnp.arange(row_count, dtype=jnp.int32)
    key_pos = (seq_index - reach_blocks) * row_count + jnp.arange(key_span, dtype=jnp.int32)
    padded = jnp.concatenate(
        [jnp.full((reach_blocks * row_count,), -1, jnp.int32), segment_row], axis=0
    )
    query_seg = lax.dynamic_slice_in_dim(segment_row, seq_index * row_count, row_count)
    key_seg = lax.dynamic_slice_in_dim(padded, seq_index * row_count, key_span)
    live_pairs = (query_seg[:, None] == key_seg[None, :]) & (key_pos[None, :] <= query_pos[:, None])
    return live_pairs & (query_pos[:, None] - key_pos[None, :] < WINDOW) & (key_pos[None, :] >= 0)


def window_scores(queries, key_rows, live_pairs):
    scores = jnp.einsum("qhd,khd->hqk", queries, key_rows, preferred_element_type=jnp.float32) * (
        1.0 / math.sqrt(HD)
    )
    return jnp.where(live_pairs[None], scores, masked_score)


def forward_micro(tokens_f32, segment_row, weights, seq_index, reach_blocks):
    w_qkv, w_out, w_gate_up, w_down, gain_attn, gain_mlp = weights
    row_count = tokens_f32.shape[0]
    normed_attn, scale_attn, h_attn = norm_forward(tokens_f32, gain_attn)
    qkv_rows = jnp.dot(h_attn, w_qkv, preferred_element_type=jnp.float32).astype(jnp.bfloat16)
    queries = qkv_rows[:, :D].reshape(row_count, H, HD)
    window_rows = collect_keys(qkv_rows[:, D:], reach_blocks)
    key_span = window_rows.shape[0]
    key_rows = window_rows[:, :D].reshape(key_span, H, HD)
    value_rows = window_rows[:, D:].reshape(key_span, H, HD)
    live_pairs = window_mask(segment_row, seq_index, row_count, reach_blocks)
    scores = window_scores(queries, key_rows, live_pairs)
    row_max = jnp.max(scores, axis=-1, keepdims=True)
    exp_scores = jnp.exp(scores - row_max)
    totals = jnp.sum(exp_scores, axis=-1, keepdims=True)
    attn_probs = exp_scores / totals
    log_total = row_max + jnp.log(totals)
    attended = (
        jnp.einsum(
            "hqk,khd->qhd",
            attn_probs.astype(jnp.bfloat16),
            value_rows,
            preferred_element_type=jnp.float32,
        )
        .reshape(row_count, D)
        .astype(jnp.bfloat16)
    )
    mid_stream = tokens_f32 + jnp.dot(attended, w_out, preferred_element_type=jnp.float32)
    normed_mlp, scale_mlp, h_mlp = norm_forward(mid_stream, gain_mlp)
    gate_up = jnp.dot(h_mlp, w_gate_up, preferred_element_type=jnp.float32)
    gate_pre = gate_up[:, :FF]
    up_pre = gate_up[:, FF:]
    activated = (jax.nn.silu(gate_pre) * up_pre).astype(jnp.bfloat16)
    layer_out = (
        mid_stream + jnp.dot(activated, w_down, preferred_element_type=jnp.float32)
    ).astype(jnp.bfloat16)
    saved_state = (
        normed_attn,
        scale_attn,
        h_attn,
        queries,
        key_rows,
        value_rows,
        live_pairs,
        log_total,
        attended,
        normed_mlp,
        scale_mlp,
        h_mlp,
        gate_pre,
        up_pre,
        activated,
    )
    return (layer_out, saved_state)


def backward_micro(cotangent_row, saved_state, weights, reach_blocks):
    (
        normed_attn,
        scale_attn,
        h_attn,
        queries,
        key_rows,
        value_rows,
        live_pairs,
        log_total,
        attended,
        normed_mlp,
        scale_mlp,
        h_mlp,
        gate_pre,
        up_pre,
        activated,
    ) = saved_state
    w_qkv, w_out, w_gate_up, w_down, gain_attn, gain_mlp = weights
    row_count = cotangent_row.shape[0]
    grad_act = jnp.einsum("re,fe->rf", cotangent_row, w_down, preferred_element_type=jnp.float32)
    sigmoid_gate = jax.nn.sigmoid(gate_pre)
    grad_gate = grad_act * up_pre * sigmoid_gate * (1.0 + gate_pre * (1.0 - sigmoid_gate))
    grad_up = grad_act * (gate_pre * sigmoid_gate)
    grad_gate_up = jnp.concatenate([grad_gate, grad_up], axis=-1).astype(jnp.bfloat16)
    grad_h_mlp = jnp.einsum(
        "rf,df->rd", grad_gate_up, w_gate_up, preferred_element_type=jnp.float32
    )
    grad_mid_norm, grad_gain_mlp = norm_backward(grad_h_mlp, normed_mlp, scale_mlp, gain_mlp)
    grad_mid = cotangent_row.astype(jnp.float32) + grad_mid_norm
    grad_branch = grad_mid.astype(jnp.bfloat16)
    grad_attended = (
        jnp.einsum("re,de->rd", grad_branch, w_out, preferred_element_type=jnp.float32)
        .astype(jnp.bfloat16)
        .reshape(row_count, H, HD)
    )
    scores = window_scores(queries, key_rows, live_pairs)
    attn_probs = jnp.exp(scores - log_total)
    grad_probs = jnp.einsum(
        "qhd,khd->hqk", grad_attended, value_rows, preferred_element_type=jnp.float32
    )
    row_inner = jnp.sum(attn_probs * grad_probs, axis=-1, keepdims=True)
    grad_scores = (attn_probs * (grad_probs - row_inner)).astype(jnp.bfloat16)
    factor = 1.0 / math.sqrt(HD)
    grad_queries = (
        jnp.einsum("hqk,khd->qhd", grad_scores, key_rows, preferred_element_type=jnp.float32)
        * factor
    )
    grad_keys = (
        jnp.einsum("hqk,qhd->khd", grad_scores, queries, preferred_element_type=jnp.float32)
        * factor
    )
    grad_values = jnp.einsum(
        "hqk,qhd->khd",
        attn_probs.astype(jnp.bfloat16),
        grad_attended,
        preferred_element_type=jnp.float32,
    )
    key_span = key_rows.shape[0]
    grad_window = jnp.concatenate(
        [grad_keys.reshape(key_span, D), grad_values.reshape(key_span, D)], axis=-1
    )
    grad_own = return_grads(grad_window, reach_blocks, row_count)
    grad_qkv = jnp.concatenate([grad_queries.reshape(row_count, D), grad_own], axis=-1).astype(
        jnp.bfloat16
    )
    grad_h_attn = jnp.einsum("re,de->rd", grad_qkv, w_qkv, preferred_element_type=jnp.float32)
    grad_tok_norm, grad_gain_attn = norm_backward(grad_h_attn, normed_attn, scale_attn, gain_attn)
    grad_tokens = grad_mid + grad_tok_norm
    return (grad_tokens, grad_qkv, grad_branch, grad_gate_up, grad_gain_attn, grad_gain_mlp)


def shards(tokens, segment_ids, w_qkv, w_out, w_gate_up, w_down, gain_attn, gain_mlp, cotangent):
    row_count = tokens.shape[2]
    seq_index = lax.axis_index("seq")
    reach_blocks = min(WINDOW // row_count, lax.axis_size("seq") - 1)
    shared = fetch_weights(w_qkv, w_out, w_gate_up, w_down, gain_attn, gain_mlp)
    outputs = []
    input_grads = []
    h_attn_list = []
    qkv_grad_list = []
    attended_list = []
    branch_grad_list = []
    h_mlp_list = []
    gate_grad_list = []
    act_list = []
    gain_attn_sum = jnp.zeros((D,), jnp.float32)
    gain_mlp_sum = jnp.zeros((D,), jnp.float32)
    for micro in range(MB):
        tokens_f32 = tokens[micro, 0].astype(jnp.float32)
        segment_row = segment_ids[micro, 0]
        layer_out, saved_state = forward_micro(
            tokens_f32, segment_row, shared, seq_index, reach_blocks
        )
        grad_tokens, grad_qkv, grad_branch, grad_gate_up, grad_gain_attn, grad_gain_mlp = (
            backward_micro(cotangent[micro, 0], saved_state, shared, reach_blocks)
        )
        outputs.append(layer_out)
        input_grads.append(grad_tokens)
        h_attn_list.append(saved_state[2])
        attended_list.append(saved_state[8])
        h_mlp_list.append(saved_state[11])
        act_list.append(saved_state[14])
        qkv_grad_list.append(grad_qkv)
        branch_grad_list.append(grad_branch)
        gate_grad_list.append(grad_gate_up)
        gain_attn_sum = gain_attn_sum + grad_gain_attn
        gain_mlp_sum = gain_mlp_sum + grad_gain_mlp
    cotangent_rows = cotangent.reshape(MB * row_count, D)
    term_qkv = jnp.einsum(
        "rd,re->de",
        jnp.concatenate(h_attn_list, axis=0),
        jnp.concatenate(qkv_grad_list, axis=0),
        preferred_element_type=jnp.float32,
    )
    term_out = jnp.einsum(
        "rd,re->de",
        jnp.concatenate(attended_list, axis=0),
        jnp.concatenate(branch_grad_list, axis=0),
        preferred_element_type=jnp.float32,
    )
    term_gate_up = jnp.einsum(
        "rd,re->de",
        jnp.concatenate(h_mlp_list, axis=0),
        jnp.concatenate(gate_grad_list, axis=0),
        preferred_element_type=jnp.float32,
    )
    term_down = jnp.einsum(
        "rf,re->fe",
        jnp.concatenate(act_list, axis=0),
        cotangent_rows,
        preferred_element_type=jnp.float32,
    )
    reduced = (
        lax.psum_scatter(term_qkv, ("dp", "seq"), scatter_dimension=0, tiled=True),
        lax.psum_scatter(term_out, ("dp", "seq"), scatter_dimension=0, tiled=True),
        lax.psum_scatter(term_gate_up, ("dp", "seq"), scatter_dimension=0, tiled=True),
        lax.psum_scatter(term_down, ("dp", "seq"), scatter_dimension=0, tiled=True),
        lax.psum_scatter(gain_attn_sum, ("dp", "seq"), scatter_dimension=0, tiled=True),
        lax.psum_scatter(gain_mlp_sum, ("dp", "seq"), scatter_dimension=0, tiled=True),
    )
    layer_outs = jnp.stack(outputs, axis=0)[:, None]
    token_grads = jnp.stack(input_grads, axis=0)[:, None]
    return (
        layer_outs,
        token_grads,
        reduced[0],
        reduced[1],
        reduced[2],
        reduced[3],
        reduced[4],
        reduced[5],
    )


def solution(mesh):
    placed = (
        P(None, "dp", "seq", None),
        P(None, "dp", None),
        P(("dp", "seq"), None),
        P(("dp", "seq"), None),
        P(("dp", "seq"), None),
        P(("dp", "seq"), None),
        P(("dp", "seq")),
        P(("dp", "seq")),
        P(None, "dp", "seq", None),
    )
    return jax.shard_map(
        shards,
        mesh=mesh,
        in_specs=placed,
        out_specs=(
            P(None, "dp", "seq", None),
            P(None, "dp", "seq", None),
            P(("dp", "seq"), None),
            P(("dp", "seq"), None),
            P(("dp", "seq"), None),
            P(("dp", "seq"), None),
            P(("dp", "seq")),
            P(("dp", "seq")),
        ),
        check_vma=False,
    )
```

profile of v0, /device:TPU:0, one launch (start us, length us, event | category | flops | bytes accessed | tf_op | source)
XLA Modules:
  0.0 6674.7 jit_solution(9004203214569769984)
XLA Ops:
  11.7 43.6 all-reduce.9
  63.0 106.9 %all-gather.6.cloned.1.call-done = bf16[2048,6144]{1,0:T(8,128)(2,1)} async-done(((bf16[64,6144]{1,0:T(8,128)(2,1)}), bf16[2048,6144]{1,0:T(8,128)(2,1)}) %all-gather.6.cloned.1.call-update) | async-done | bytes 25165840 | tf_op jit(solution)/shard_map/all_gather | solution.py:28
  169.9 18.6 convolution_convert_fusion
  206.3 463.3 %all-gather.12.cloned.1.call-done = bf16[32,172,2048]{2,1,0:T(8,128)(2,1)} async-done(((bf16[1,172,2048]{2,1,0:T(8,128)(2,1)}), bf16[32,172,2048]{2,1,0:T(8,128)(2,1)}) %all-gather.12.cloned.1.call-update) | async-done | bytes 22544400 | tf_op jit(solution)/shard_map/all_gather | solution.py:31
  669.5 22.1 reshape.382
  700.3 18.0 convolution_convert_fusion.1
  749.4 101.9 %collective-permute-done.6 = bf16[512,4096]{1,0:T(8,128)(2,1)} collective-permute-done((bf16[512,4096]{1,0:T(8,128)(2,1)}, bf16[512,4096]{1,0:T(8,128)(2,1)}, u32[]{:S(2)}, u32[]{:S(2)}) %collective-permute-start.6) | collective-permute-done | bytes 4194336 | tf_op jit(solution)/shard_map/ppermute | solution.py:23
  851.2 6.8 collective-permute-start.2
  864.5 7.7 slice_bitcast_fusion
  872.1 13.8 copy.74
  886.0 115.6 %collective-permute-done = bf16[512,4096]{1,0:T(8,128)(2,1)} collective-permute-done((bf16[512,4096]{1,0:T(8,128)(2,1)}, bf16[512,4096]{1,0:T(8,128)(2,1)}, u32[]{:S(2)}, u32[]{:S(2)}) %collective-permute-start) | collective-permute-done | bytes 4194336 | tf_op jit(solution)/shard_map/ppermute | solution.py:23
  1004.1 128.2 %collective-permute-done.1 = bf16[512,4096]{1,0:T(8,128)(2,1)} collective-permute-done((bf16[512,4096]{1,0:T(8,128)(2,1)}, bf16[512,4096]{1,0:T(8,128)(2,1)}, u32[]{:S(2)}, u32[]{:S(2)}) %collective-permute-start.1) | collective-permute-done | bytes 4194336 | tf_op jit(solution)/shard_map/ppermute | solution.py:23
  1134.8 167.2 %collective-permute-done.2 = bf16[512,4096]{1,0:T(8,128)(2,1)} collective-permute-done((bf16[512,4096]{1,0:T(8,128)(2,1)}, bf16[512,4096]{1,0:T(8,128)(2,1)}, u32[]{:S(2)}, u32[]{:S(2)}) %collective-permute-start.2) | collective-permute-done | bytes 4194336 | tf_op jit(solution)/shard_map/ppermute | solution.py:23
  1308.2 7.5 slice_bitcast_fusion.1
  1315.7 13.8 copy.72
  1329.5 34.4 fusion.144
  1363.9 26.5 fusion.1
  1390.4 35.4 fusion.125
  1425.9 11.5 multiply_reduce_fusion.7
  1438.0 34.5 fusion.143
  1472.5 26.5 fusion.2
  1499.0 34.4 fusion.122
  1533.4 10.7 multiply_reduce_fusion.6
  1547.2 34.0 fusion.145
  1581.2 27.0 multiply_convert_fusion.5
  1608.2 38.3 multiply_reduce_fusion.3
  1646.4 34.1 fusion.146
  1680.5 26.6 multiply_convert_fusion.3
  1707.1 34.8 multiply_reduce_fusion.2
  1741.9 9.6 fusion.138
  1761.6 37.0 fusion.7
  1798.6 59.4 multiply_reduce_fusion
  1858.0 15.1 fusion.106
  1873.1 8.5 convolution_convert_fusion.3
  1884.3 66.4 multiply_convert_fusion
  1950.6 23.6 broadcast_multiply_fusion
  1974.3 21.1 fusion.5
  1995.4 12.5 fusion.141
  2013.1 59.1 multiply_reduce_fusion.1
  2072.2 66.5 multiply_convert_fusion.1
  2138.7 23.4 broadcast_multiply_fusion.1
  2162.1 36.9 fusion.9
  2199.0 21.1 fusion.6
  2220.1 21.6 multiply_convert_fusion.8
  2241.7 13.0 fusion.140
  2256.1 53.5 collective-permute-done.12
  2310.8 489.3 %collective-permute-done.15 = bf16[512,4096]{0,1:T(8,128)(2,1)} collective-permute-done((bf16[512,4096]{0,1:T(8,128)(2,1)}, bf16[512,4096]{0,1:T(8,128)(2,1)}, u32[]{:S(2)}, u32[]{:S(2)}) %collective-permute-start.15) | collective-permute-done | bytes 4194336 | tf_op jit(solution)/shard_map/ppermute | solution.py:23
  2802.7 22.9 multiply_convert_fusion.9
  2825.6 11.6 fusion.60
  2837.2 556.6 %collective-permute-done.11 = bf16[512,4096]{0,1:T(8,128)(2,1)} collective-permute-done((bf16[512,4096]{0,1:T(8,128)(2,1)}, bf16[512,4096]{0,1:T(8,128)(2,1)}, u32[]{:S(2)}, u32[]{:S(2)}) %collective-permute-start.11) | collective-permute-done | bytes 4194336 | tf_op jit(solution)/shard_map/ppermute | solution.py:23
  3393.8 11.6 fusion.66
  3405.4 38.1 fusion.23
  3445.1 64.1 fusion.15
  3509.3 32.0 fusion.39
  3541.3 1629.6 %fusion = f32[176,2048]{1,0:T(8,128)S(1)} fusion(f32[5504,2048]{1,0:T(8,128)} %fusion.39), kind=kCustom, calls=%all-reduce-scatter | all-reduce-scatter fusion | flops 11534337 | bytes 46530560
  5175.7 18.9 fusion.116
  5194.6 18.1 fusion.117
  5215.1 28.5 collective-permute-done.16
  5243.7 6.0 concatenate.72
  5252.4 18.7 fusion.71
  5271.1 25.9 fusion.93
  5297.0 167.0 %all-reduce.8 = (f32[2048]{0:T(1024)S(1)}, f32[2048]{0:T(1024)S(1)}) all-reduce(f32[2048]{0:T(1024)S(1)} %add.201, f32[2048]{0:T(1024)S(1)} %add.202), channel_id=6, replica_groups=mesh['dp'=4,'seq'=8] {'dp','seq'}, use_global_device_ids=true, to_apply=%region_20.21.clone | all-reduce | flops 4096 | bytes 32768
  5465.3 7.3 fusion.100
  5484.1 1183.3 %reduce-scatter.10.cloned.1.call-done = f32[64,11008]{1,0:T(8,128)} async-done(((f32[2048,11008]{1,0:T(8,128)}), f32[64,11008]{1,0:T(8,128)}) %reduce-scatter.10.cloned.1.call-update) | async-done | bytes 2818064 | tf_op jit(solution)/shard_map/reduce_scatter | solution.py:279
  (206 shorter events, 137.6 us)
Async XLA Ops:
  7.2 162.7 %all-gather.6.cloned.1.call-start = ((), (), s32[]{:S(2)}) async-start(), calls=%async_computation.3 | async-start | bytes 25952256 | tf_op jit(solution)/shard_map/all_gather | solution.py:28
  7.9 661.6 %all-gather.12.cloned.1.call-start = ((), (), s32[]{:S(2)}) async-start(), calls=%async_computation.9 | async-start | bytes 23789568 | tf_op jit(solution)/shard_map/all_gather | solution.py:31
  8.7 1417.2 %all-gather.8.cloned.1.call-start = ((), (), s32[]{:S(2)}) async-start(), calls=%async_computation.4 | async-start | bytes 8650752 | tf_op jit(solution)/shard_map/all_gather | solution.py:29
  9.4 1537.8 %all-gather.10.cloned.1.call-start = ((), (), s32[]{:S(2)}) async-start(), calls=%async_computation.5 | async-start | bytes 46497792 | tf_op jit(solution)/shard_map/all_gather | solution.py:30
  10.0 5474.1 %reduce-scatter.8.cloned.1.call-start = ((), (), s32[]{:S(2)}) async-start(), calls=%async_computation.7 | async-start | bytes 17301504 | tf_op jit(solution)/shard_map/reduce_scatter | solution.py:278
  63.0 637.3 %copy-start.23 = (bf16[512,2048]{1,0:T(8,128)(2,1)}, bf16[512,2048]{1,0:T(8,128)(2,1)S(1)}, u32[]{:S(2)}) copy-start(bf16[512,2048]{1,0:T(8,128)(2,1)S(1)} %get-tuple-element.68) | copy-start | bytes 6291460
  188.5 13.4 copy-start.11
  191.3 546.4 %collective-permute-start.4 = (bf16[512,4096]{1,0:T(8,128)(2,1)}, bf16[512,4096]{1,0:T(8,128)(2,1)}, u32[]{:S(2)}, u32[]{:S(2)}) collective-permute-start(bf16[512,4096]{1,0:T(8,128)(2,1)} %slice.126), channel_id=1, source_target_pairs={{0,4},{1,5},{2,6},{3,7},{8,12},{9,13},{10,14},{11,15},{16,20},{17,... | collective-permute-start | bytes 12582920 | tf_op jit(solution)/shard_map/ppermute | solution.py:23
  196.8 546.8 %collective-permute-start.5 = (bf16[512,4096]{1,0:T(8,128)(2,1)}, bf16[512,4096]{1,0:T(8,128)(2,1)}, u32[]{:S(2)}, u32[]{:S(2)}) collective-permute-start(bf16[512,4096]{1,0:T(8,128)(2,1)} %slice.126), channel_id=1, source_target_pairs={{0,3},{1,4},{2,5},{3,6},{4,7},{8,11},{9,12},{10,13},{11,14},{12,15... | collective-permute-start | bytes 12582920 | tf_op jit(solution)/shard_map/ppermute | solution.py:23
  691.7 169.3 %collective-permute-start.7 = (bf16[512,4096]{1,0:T(8,128)(2,1)}, bf16[512,4096]{1,0:T(8,128)(2,1)}, u32[]{:S(2)}, u32[]{:S(2)}) collective-permute-start(bf16[512,4096]{1,0:T(8,128)(2,1)} %slice.126), channel_id=1, source_target_pairs={{0,1},{1,2},{2,3},{3,4},{4,5},{5,6},{6,7},{8,9},{9,10},{10,11},{11... | collective-permute-start | bytes 12582920 | tf_op jit(solution)/shard_map/ppermute | solution.py:23
  696.8 154.4 %collective-permute-start.6 = (bf16[512,4096]{1,0:T(8,128)(2,1)}, bf16[512,4096]{1,0:T(8,128)(2,1)}, u32[]{:S(2)}, u32[]{:S(2)}) collective-permute-start(bf16[512,4096]{1,0:T(8,128)(2,1)} %slice.126), channel_id=1, source_target_pairs={{0,2},{1,3},{2,4},{3,5},{4,6},{5,7},{8,10},{9,11},{10,12},{11,13},... | collective-permute-start | bytes 12582920 | tf_op jit(solution)/shard_map/ppermute | solution.py:23
  729.0 600.5 %copy-start.6 = (bf16[512,2048]{0,1:T(8,128)(2,1)}, bf16[512,2048]{0,1:T(8,128)(2,1)S(1)}, u32[]{:S(2)}) copy-start(bf16[512,2048]{0,1:T(8,128)(2,1)S(1)} %copy.71) | copy-start | bytes 6291460
  729.0 575.6 %collective-permute-start.3 = (bf16[512,4096]{1,0:T(8,128)(2,1)}, bf16[512,4096]{1,0:T(8,128)(2,1)}, u32[]{:S(2)}, u32[]{:S(2)}) collective-permute-start(bf16[512,4096]{1,0:T(8,128)(2,1)} %slice.120), channel_id=1, source_target_pairs={{0,1},{1,2},{2,3},{3,4},{4,5},{5,6},{6,7},{8,9},{9,10},{10,11},{11... | collective-permute-start | bytes 12582920 | tf_op jit(solution)/shard_map/ppermute | solution.py:23
  737.8 263.9 %collective-permute-start = (bf16[512,4096]{1,0:T(8,128)(2,1)}, bf16[512,4096]{1,0:T(8,128)(2,1)}, u32[]{:S(2)}, u32[]{:S(2)}) collective-permute-start(bf16[512,4096]{1,0:T(8,128)(2,1)} %slice.120), channel_id=1, source_target_pairs={{0,4},{1,5},{2,6},{3,7},{8,12},{9,13},{10,14},{11,15},{16,20},{17,... | collective-permute-start | bytes 12582920 | tf_op jit(solution)/shard_map/ppermute | solution.py:23
  743.5 388.8 %collective-permute-start.1 = (bf16[512,4096]{1,0:T(8,128)(2,1)}, bf16[512,4096]{1,0:T(8,128)(2,1)}, u32[]{:S(2)}, u32[]{:S(2)}) collective-permute-start(bf16[512,4096]{1,0:T(8,128)(2,1)} %slice.120), channel_id=1, source_target_pairs={{0,3},{1,4},{2,5},{3,6},{4,7},{8,11},{9,12},{10,13},{11,14},{12,15... | collective-permute-start | bytes 12582920 | tf_op jit(solution)/shard_map/ppermute | solution.py:23
  851.2 450.7 %collective-permute-start.2 = (bf16[512,4096]{1,0:T(8,128)(2,1)}, bf16[512,4096]{1,0:T(8,128)(2,1)}, u32[]{:S(2)}, u32[]{:S(2)}) collective-permute-start(bf16[512,4096]{1,0:T(8,128)(2,1)} %slice.120), channel_id=1, source_target_pairs={{0,2},{1,3},{2,4},{3,5},{4,6},{5,7},{8,10},{9,11},{10,12},{11,13},... | collective-permute-start | bytes 12582920 | tf_op jit(solution)/shard_map/ppermute | solution.py:23
  1363.9 26.5 copy-start.26
  1390.4 35.4 copy-start.32
  1425.9 12.1 copy-start.5
  1425.9 12.1 copy-start.8
  1533.4 10.7 copy-start.49
  1533.4 10.7 copy-start.27
  1533.4 10.7 copy-start.33
  1533.4 12.0 copy-start
  1533.4 12.0 copy-start.28
  1533.4 12.0 copy-start.34
  1544.1 197.8 %copy-start.40 = (f32[512]{0:T(512)}, f32[512]{0:T(512)S(1)}, u32[]{:S(2)}) copy-start(f32[512]{0:T(512)S(1)} %add_rsqrt_fusion) | copy-start | bytes 6148
  1547.2 34.0 copy-start.15
  1646.4 95.5 %copy-start.42 = (f32[512]{0:T(512)}, f32[512]{0:T(512)S(1)}, u32[]{:S(2)}) copy-start(f32[512]{0:T(512)S(1)} %broadcast_multiply_fusion.5) | copy-start | bytes 6148
  1646.4 34.1 copy-start.16
  1741.9 9.7 copy-start.44
  1741.9 11.0 copy-start.48
  1884.2 3599.9 %reduce-scatter.6.cloned.1.call-start = ((), (), s32[]{:S(2)}) async-start(), calls=%async_computation.6 | async-start | bytes 51904512 | tf_op jit(solution)/shard_map/reduce_scatter | solution.py:277
  1884.3 66.4 copy-start.9
  1995.4 17.7 copy-start.10
  1995.4 17.7 copy-start.21
  2007.9 301.7 %collective-permute-start.12 = (bf16[512,4096]{0,1:T(8,128)(2,1)}, bf16[512,4096]{0,1:T(8,128)(2,1)}, u32[]{:S(2)}, u32[]{:S(2)}) collective-permute-start(bf16[512,4096]{0,1:T(8,128)(2,1)} %get-tuple-element.58), channel_id=1, source_target_pairs={{1,0},{2,1},{3,2},{4,3},{5,4},{6,5},{7,6},{9,8},{10,9},{11,10},{12... | collective-permute-start | bytes 12582920 | tf_op jit(solution)/shard_map/ppermute | solution.py:23
  2009.2 790.9 %collective-permute-start.15 = (bf16[512,4096]{0,1:T(8,128)(2,1)}, bf16[512,4096]{0,1:T(8,128)(2,1)}, u32[]{:S(2)}, u32[]{:S(2)}) collective-permute-start(bf16[512,4096]{0,1:T(8,128)(2,1)} %get-tuple-element.59), channel_id=1, source_target_pairs={{4,0},{5,1},{6,2},{7,3},{12,8},{13,9},{14,10},{15,11},{20,16},{21,... | collective-permute-start | bytes 12582920 | tf_op jit(solution)/shard_map/ppermute | solution.py:23
  2010.5 790.9 %collective-permute-start.14 = (bf16[512,4096]{0,1:T(8,128)(2,1)}, bf16[512,4096]{0,1:T(8,128)(2,1)}, u32[]{:S(2)}, u32[]{:S(2)}) collective-permute-start(bf16[512,4096]{0,1:T(8,128)(2,1)} %get-tuple-element.60), channel_id=1, source_target_pairs={{3,0},{4,1},{5,2},{6,3},{7,4},{11,8},{12,9},{13,10},{14,11},{15,12... | collective-permute-start | bytes 12582920 | tf_op jit(solution)/shard_map/ppermute | solution.py:23
  2011.8 813.9 %collective-permute-start.13 = (bf16[512,4096]{0,1:T(8,128)(2,1)}, bf16[512,4096]{0,1:T(8,128)(2,1)}, u32[]{:S(2)}, u32[]{:S(2)}) collective-permute-start(bf16[512,4096]{0,1:T(8,128)(2,1)} %get-tuple-element.61), channel_id=1, source_target_pairs={{2,0},{3,1},{4,2},{5,3},{6,4},{7,5},{10,8},{11,9},{12,10},{13,11},... | collective-permute-start | bytes 12582920 | tf_op jit(solution)/shard_map/ppermute | solution.py:23
  2072.2 66.5 copy-start.7
  2241.7 1163.7 %copy-start.20 = (bf16[16,128,512]{2,1,0:T(8,128)(2,1)}, bf16[16,128,512]{2,1,0:T(8,128)(2,1)S(1)}, u32[]{:S(2)}) copy-start(bf16[16,128,512]{2,1,0:T(8,128)(2,1)S(1)} %multiply_convert_fusion.8) | copy-start | bytes 6291460
  2254.8 582.4 %collective-permute-start.8 = (bf16[512,4096]{0,1:T(8,128)(2,1)}, bf16[512,4096]{0,1:T(8,128)(2,1)}, u32[]{:S(2)}, u32[]{:S(2)}) collective-permute-start(bf16[512,4096]{0,1:T(8,128)(2,1)} %get-tuple-element.54), channel_id=1, source_target_pairs={{1,0},{2,1},{3,2},{4,3},{5,4},{6,5},{7,6},{9,8},{10,9},{11,10},{12... | collective-permute-start | bytes 12582920 | tf_op jit(solution)/shard_map/ppermute | solution.py:23
  2309.5 1084.2 %collective-permute-start.11 = (bf16[512,4096]{0,1:T(8,128)(2,1)}, bf16[512,4096]{0,1:T(8,128)(2,1)}, u32[]{:S(2)}, u32[]{:S(2)}) collective-permute-start(bf16[512,4096]{0,1:T(8,128)(2,1)} %get-tuple-element.55), channel_id=1, source_target_pairs={{4,0},{5,1},{6,2},{7,3},{12,8},{13,9},{14,10},{15,11},{20,16},{21,... | collective-permute-start | bytes 12582920 | tf_op jit(solution)/shard_map/ppermute | solution.py:23
  2800.1 593.7 %collective-permute-start.10 = (bf16[512,4096]{0,1:T(8,128)(2,1)}, bf16[512,4096]{0,1:T(8,128)(2,1)}, u32[]{:S(2)}, u32[]{:S(2)}) collective-permute-start(bf16[512,4096]{0,1:T(8,128)(2,1)} %get-tuple-element.56), channel_id=1, source_target_pairs={{3,0},{4,1},{5,2},{6,3},{7,4},{11,8},{12,9},{13,10},{14,11},{15,12... | collective-permute-start | bytes 12582920 | tf_op jit(solution)/shard_map/ppermute | solution.py:23
  2801.4 592.4 %collective-permute-start.9 = (bf16[512,4096]{0,1:T(8,128)(2,1)}, bf16[512,4096]{0,1:T(8,128)(2,1)}, u32[]{:S(2)}, u32[]{:S(2)}) collective-permute-start(bf16[512,4096]{0,1:T(8,128)(2,1)} %get-tuple-element.57), channel_id=1, source_target_pairs={{2,0},{3,1},{4,2},{5,3},{6,4},{7,5},{10,8},{11,9},{12,10},{13,11},... | collective-permute-start | bytes 12582920 | tf_op jit(solution)/shard_map/ppermute | solution.py:23
  3443.6 3223.8 %reduce-scatter.10.cloned.1.call-start = ((), (), s32[]{:S(2)}) async-start(), calls=%async_computation.8 | async-start | bytes 92995584 | tf_op jit(solution)/shard_map/reduce_scatter | solution.py:279
  5171.0 23.6 copy-start.13
  5171.0 72.7 %collective-permute-start.16 = (f32[124,2048]{1,0:T(8,128)S(1)}, f32[124,2048]{1,0:T(8,128)S(1)}, u32[]{:S(2)}, u32[]{:S(2)}) collective-permute-start(f32[124,2048]{1,0:T(8,128)S(1)} %slice.144), channel_id=1, source_target_pairs={{0,1},{1,2},{2,3},{3,4},{4,5},{5,6},{6,7},{7,8},{8,9},{9,10},{10,1... | collective-permute-start | bytes 3047432
  5194.6 18.1 copy-start.46
  5194.6 18.1 copy-start.47
  5252.4 18.7 copy-start.3
  5252.4 18.7 copy-start.31
  5252.4 18.7 copy-start.37
  5252.4 18.7 copy-start.39
  5271.1 25.9 copy-start.19
  5271.1 194.1 %copy-start.29 = (f32[2048]{0:T(1024)S(1)}, f32[2048]{0:T(1024)}, u32[]{:S(2)}) copy-start(f32[2048]{0:T(1024)} %convert_element_type.153) | copy-start | bytes 24580
  5271.1 194.1 %copy-start.41 = (f32[512]{0:T(512)S(1)}, f32[512]{0:T(512)}, u32[]{:S(2)}) copy-start(f32[512]{0:T(512)} %copy-done.40) | copy-start | bytes 6148
  5271.1 194.1 %copy-start.45 = (f32[512]{0:T(512)S(1)}, f32[512]{0:T(512)}, u32[]{:S(2)}) copy-start(f32[512]{0:T(512)} %copy-done.44) | copy-start | bytes 6148
  5465.3 9.6 copy-start.14
  5465.3 10.8 copy-start.17
  5465.3 12.0 copy-start.18
  5465.3 12.0 copy-start.35
  5465.3 12.0 copy-start.43
  (14 other events, 60.4 us)
Sparse Core Ops, SparseCore 0:
  11.0 158.8 all-gather.5
  172.8 496.7 all-gather.11
  672.5 100.7 all-gather.7
  776.1 516.3 all-gather.9
  1884.3 1280.9 reduce-scatter.7
  3443.7 917.9 reduce-scatter.5
  4364.7 2302.6 reduce-scatter.9
where the time goes:
time: 6710 us; the launch traced here: 6670 us
  waiting for transfers between devices  3400 us (51%)
  blocking collectives  1840 us (27%)
  matrix products  921 us (14%)
  other arithmetic  291 us (4%)
  local copies, waits for them, and re-layouts  157 us (2%)
    unnamed x3, blocking collectives  1840 us
    ppermute x16, waiting for transfers between devices, from_behind(): return lax.ppermute(block, axis, route)  1610 us
    reduce_scatter x1, waiting for transfers between devices, shards(): lax.psum_scatter(term_gate_up, ('dp', 'seq'), scatter_dimension=0, tiled=...  1180 us
    all_gather x1, waiting for transfers between devices, fetch_weights(): lax.all_gather(w_down, ('dp', 'seq'), axis=0, tiled=True)  463 us
  transfers between devices with their start and end apart: 24, of which 11 were waited for; matrix products, arithmetic and copies ran while one was open for 40% of the time, Pallas kernels for 0%

commit v1 on v0

v1 whole, which is shorter than its diff:
```python
import functools
import math

import jax
import jax.numpy as jnp
from jax import lax
from jax.experimental import pallas as pl
from jax.experimental.pallas import tpu as pltpu
from jax.sharding import PartitionSpec as P

D = 2048
H = 16
HD = 128
FF = 5504
WINDOW = 2048
MB = 2
TILE = 512

EPSILON = 1e-05
MASKED = -1e30
LOG2E = 1.4426950408889634
SCALE = 1.0 / math.sqrt(HD)

bf16 = jnp.bfloat16
f32 = jnp.float32


def digits_of(size):
    if size == 8:
        return [(1, 2), (2, 4)]
    if size == 32:
        return [(1, 4), (4, 2), (8, 4)]
    return [(1, size)] if size > 1 else []


def digit_index(axis, digit):
    stride, size = digit
    return lax.rem(lax.axis_index(axis) // stride, size)


def shift(block, axis, digit, distance):
    stride, size = digit
    total = lax.axis_size(axis)
    route = []
    for i in range(total):
        own = (i // stride) % size
        route.append((i, i + ((own + distance) % size - own) * stride))
    return lax.ppermute(block, axis, route)


def pick(array, index, dim):
    return lax.dynamic_index_in_dim(array, index, dim, keepdims=False)


def scatter_digit(parts, axis, digit, dim, out_type):
    own = digit_index(axis, digit)
    size = digit[1]
    got = []
    for distance in range(1, size):
        piece = pick(parts, lax.rem(own + distance, size), dim)
        got.append(shift(piece, axis, digit, distance))
    total = pick(parts, own, dim).astype(f32)
    for piece in got:
        total = total + piece.astype(f32)
    return total.astype(out_type)


def gather_small(block):
    for axis in ("seq", "dp"):
        for digit in digits_of(lax.axis_size(axis)) if axis == "seq" else [(1, 2), (2, lax.axis_size("dp") // 2)]:
            size = digit[1]
            if size == 1:
                continue
            own = digit_index(axis, digit)
            pieces = [block] + [shift(block, axis, digit, d) for d in range(1, size)]
            stacked = jnp.stack(pieces, axis=0)
            order = lax.rem(own - jnp.arange(size) + size, size)
            block = jnp.concatenate(
                [jnp.sum(jnp.where((order == t).reshape((size,) + (1,) * block.ndim), stacked, 0), axis=0) for t in range(size)],
                axis=-1,
            ).astype(block.dtype)
    return block


def scatter_small(terms):
    k = terms.shape[0]
    dp, seq = lax.axis_size("dp"), lax.axis_size("seq")
    terms = scatter_digit(terms.reshape(k, dp // 2, 2, -1), "dp", (1, 2), 2, f32)
    if dp > 2:
        terms = scatter_digit(terms, "dp", (2, dp // 2), 1, f32)
    else:
        terms = terms[:, 0]
    for digit in reversed(digits_of(seq)):
        terms = scatter_digit(terms.reshape(k, digit[1], -1), "seq", digit, 1, f32)
    return terms


def weight_grad(rows_side, cols_side, seq_first):
    tokens, row_total = rows_side.shape
    dp, seq = lax.axis_size("dp"), lax.axis_size("seq")
    ys = dp // 2
    own = row_total // (dp * seq)
    cols = cols_side.shape[1]
    slow = digits_of(seq)[::-1]
    core, height = (1, 2), (2, ys)
    c = digit_index("dp", core)
    if seq_first:
        fast = digits_of(seq)[0]
        first, first_axis, first_own = fast, "seq", digit_index("seq", fast)
        lhs = rows_side.reshape(tokens, ys, 2, seq // fast[1], fast[1], own)
        lhs = lhs.transpose(2, 4, 1, 3, 5, 0)
    else:
        first, first_axis, first_own = height, "dp", digit_index("dp", height)
        lhs = rows_side.reshape(tokens, ys, 2, seq, own)
        lhs = lhs.transpose(2, 1, 3, 4, 0)
    size = first[1]
    lhs = lhs.reshape(2, size, -1, tokens)

    def term(core_index, first_index):
        side = pick(pick(lhs, core_index, 0), first_index, 0)
        return jnp.dot(side, cols_side, preferred_element_type=f32)

    order = [lax.rem(first_own + d, size) for d in range(1, size)] + [first_own]
    from_core = [shift(term(1 - c, index).astype(bf16), "dp", core, 1) for index in order]
    sums = [term(c, index) + got.astype(f32) for index, got in zip(order, from_core)]
    total = sums[-1]
    for distance in range(1, size):
        total = total + shift(sums[distance - 1].astype(bf16), first_axis, first, distance).astype(f32)
    total = total.astype(bf16)
    if seq_first:
        rest = [(axis, digit) for axis, digit in [("dp", height)] + [("seq", d) for d in slow[:-1]]]
    else:
        rest = [("seq", d) for d in slow[-1:]] + [("seq", d) for d in slow[:-1]]
    if not seq_first:
        fast = slow[-1]
        total = total.reshape(seq // fast[1], fast[1], own, cols)
        total = scatter_digit(total, "seq", fast, 1, bf16 if len(slow) > 1 else f32)
        rest = [("seq", d) for d in slow[:-1]]
    for n, (axis, digit) in enumerate(rest):
        total = total.reshape(digit[1], -1, cols)
        total = scatter_digit(total, axis, digit, 0, f32 if n == len(rest) - 1 else bf16)
    return total.reshape(own, cols).astype(f32)


def dot_nt(a, b):
    return lax.dot_general(a, b, (((1,), (1,)), ((), ())), preferred_element_type=f32)


def dot_tn(a, b):
    return lax.dot_general(a, b, (((0,), (0,)), ((), ())), preferred_element_type=f32)


def dot_nn(a, b):
    return lax.dot_general(a, b, (((1,), (0,)), ((), ())), preferred_element_type=f32)


def forward_kernel(bounds, q_ref, k_ref, v_ref, lo_ref, o_ref, lse_ref, acc):
    i = pl.program_id(1)
    q = q_ref[...]
    lo = lo_ref[...]
    factor = SCALE * LOG2E

    def step(j, carry, masked, first=False):
        m, l = carry
        rows = pl.ds(pl.multiple_of(j * TILE, TILE), TILE)
        s = dot_nt(k_ref[rows, :], q) * factor
        if masked:
            key = j * TILE + lax.broadcasted_iota(jnp.int32, (TILE, TILE), 0)
            query = i * TILE + lax.broadcasted_iota(jnp.int32, (TILE, TILE), 1)
            s = jnp.where((key >= lo) & (key <= query), s, MASKED)
        new = jnp.maximum(m, jnp.max(s, axis=0, keepdims=True))
        p = jnp.exp2(s - new)
        old = jnp.exp2(m - new)
        acc[...] = acc[...] * old + dot_tn(v_ref[rows, :], p.astype(bf16))
        return new, l * old + jnp.sum(p, axis=0, keepdims=True)

    acc[...] = jnp.zeros_like(acc)
    carry = (jnp.full((1, TILE), MASKED, f32), jnp.zeros((1, TILE), f32))
    start = bounds[0, i]
    middle = bounds[1, i]
    carry = lax.fori_loop(start, middle, lambda j, c: step(j, c, True), carry)
    carry = lax.fori_loop(middle, i, lambda j, c: step(j, c, False), carry)
    m, l = step(i, carry, True)
    o_ref[...] = (acc[...] / l).T.astype(bf16)
    lse_ref[0] = m + jnp.log2(l)


def attend(qkv, bounds, low, heads):
    length = qkv.shape[0]
    blocks = length // TILE
    whole = lambda part: pl.BlockSpec((length, HD), lambda h, i, b: (0, part * heads + h))
    return pl.pallas_call(
        forward_kernel,
        grid_spec=pltpu.PrefetchScalarGridSpec(
            num_scalar_prefetch=1,
            grid=(heads, blocks),
            in_specs=[
                pl.BlockSpec((TILE, HD), lambda h, i, b: (i, h)),
                whole(1),
                whole(2),
                pl.BlockSpec((1, TILE), lambda h, i, b: (0, i)),
            ],
            out_specs=[
                pl.BlockSpec((TILE, HD), lambda h, i, b: (i, h)),
                pl.BlockSpec((1, 1, TILE), lambda h, i, b: (h, 0, i)),
            ],
            scratch_shapes=[pltpu.VMEM((HD, TILE), f32)],
        ),
        out_shape=[
            jax.ShapeDtypeStruct((length, heads * HD), bf16),
            jax.ShapeDtypeStruct((heads, 1, length), f32),
        ],
        compiler_params=pltpu.CompilerParams(vmem_limit_bytes=32 * 1024 * 1024),
        cost_estimate=pl.CostEstimate(
            flops=4 * heads * length * 1792 * HD,
            bytes_accessed=8 * heads * length * HD,
            transcendentals=heads * length * 1792,
        ),
        name="attend",
    )(bounds, qkv, qkv, qkv, low)


def backward_kernel(bounds, q_ref, k_ref, v_ref, do_ref, lse_ref, delta_ref, lo_ref, dq_ref, dk_ref, dv_ref, dq, dk, dv):
    j = pl.program_id(1)
    k = k_ref[...]
    v = v_ref[...]
    factor = SCALE * LOG2E

    def step(i, masked):
        rows = pl.ds(pl.multiple_of(i * TILE, TILE), TILE)
        q = q_ref[rows, :]
        do = do_ref[rows, :]
        s = dot_nt(k, q) * factor
        p = jnp.exp2(s - lse_ref[0, :, rows])
        if masked:
            key = j * TILE + lax.broadcasted_iota(jnp.int32, (TILE, TILE), 0)
            query = i * TILE + lax.broadcasted_iota(jnp.int32, (TILE, TILE), 1)
            p = jnp.where((key >= lo_ref[:, rows]) & (key <= query), p, 0.0)
        dp = dot_nt(v, do)
        ds = (p * (dp - delta_ref[0, :, rows])).astype(bf16)
        dv[...] += dot_nn(p.astype(bf16), do)
        dk[...] += dot_nn(ds, q)
        dq[rows, :] += dot_tn(ds, k)

    @pl.when(j == 0)
    def _():
        dq[...] = jnp.zeros_like(dq)

    dk[...] = jnp.zeros_like(dk)
    dv[...] = jnp.zeros_like(dv)
    step(j, True)
    middle = bounds[2, j]
    end = bounds[3, j]

    @pl.loop(j + 1, middle)
    def _(i):
        step(i, False)

    @pl.loop(middle, end)
    def _(i):
        step(i, True)

    own = pl.ds(pl.multiple_of(j * TILE, TILE), TILE)
    dq_ref[...] = (dq[own, :] * SCALE).astype(bf16)
    dk_ref[...] = (dk[...] * SCALE).astype(bf16)
    dv_ref[...] = dv[...].astype(bf16)


def attend_back(qkv, grad, lse, delta, bounds, low, heads):
    length = qkv.shape[0]
    blocks = length // TILE
    whole = pl.BlockSpec((length, HD), lambda h, j, b: (0, h))
    line = pl.BlockSpec((1, 1, length), lambda h, j, b: (h, 0, 0))
    block = lambda part: pl.BlockSpec((TILE, HD), lambda h, j, b: (j, part * heads + h))
    piece = jax.ShapeDtypeStruct((length, heads * HD), bf16)
    return pl.pallas_call(
        backward_kernel,
        grid_spec=pltpu.PrefetchScalarGridSpec(
            num_scalar_prefetch=1,
            grid=(heads, blocks),
            in_specs=[
                whole,
                block(1),
                block(2),
                whole,
                line,
                line,
                pl.BlockSpec((1, length), lambda h, j, b: (0, 0)),
            ],
            out_specs=[block(0)] * 3,
            scratch_shapes=[
                pltpu.VMEM((length, HD), f32),
                pltpu.VMEM((TILE, HD), f32),
                pltpu.VMEM((TILE, HD), f32),
            ],
        ),
        out_shape=[piece] * 3,
        compiler_params=pltpu.CompilerParams(vmem_limit_bytes=40 * 1024 * 1024),
        cost_estimate=pl.CostEstimate(
            flops=10 * heads * length * 1792 * HD,
            bytes_accessed=16 * heads * length * HD,
            transcendentals=heads * length * 1792,
        ),
        name="attend_back",
    )(bounds, qkv, qkv, qkv, grad, lse, delta, low)


def key_bounds(segments):
    length = segments.shape[0]
    blocks = length // TILE
    place = jnp.arange(length, dtype=jnp.int32)
    start = jnp.zeros_like(place)
    for value in range(1, 4):
        earlier = jnp.sum(segments < value, dtype=jnp.int32)
        start = jnp.where(segments == value, earlier, start)
    low = jnp.maximum(start, place - (WINDOW - 1))
    index = jnp.arange(blocks, dtype=jnp.int32)
    first = low[::TILE]
    last = low[TILE - 1 :: TILE]
    begin = first // TILE
    middle = jnp.clip((last + TILE - 1) // TILE, begin, index)
    full = (last[None, :] <= index[:, None] * TILE) & (index[None, :] > index[:, None])
    some = (first[None, :] < (index[:, None] + 1) * TILE) & (index[None, :] > index[:, None])
    back_middle = index + 1 + jnp.sum(full, axis=1, dtype=jnp.int32)
    back_end = index + 1 + jnp.sum(some, axis=1, dtype=jnp.int32)
    return low[None], jnp.stack([begin, middle, back_middle, back_end])


def to_heads(rows, micros, heads):
    parts = rows.shape[1] // D
    count = rows.shape[0] // micros
    split = rows.reshape(micros, count, parts, H // heads, heads * HD).transpose(0, 3, 1, 2, 4)
    split = split.reshape(micros * H // heads, count, parts * heads * HD)
    got = lax.all_to_all(split, "seq", 0, 0, tiled=True)
    return got.reshape(-1, parts * heads * HD)


def to_rows(whole, micros, heads):
    seq = lax.axis_size("seq")
    parts = whole.shape[1] // (heads * HD)
    got = lax.all_to_all(whole.reshape(seq, -1, parts * heads * HD), "seq", 0, 0, tiled=True)
    count = got.shape[1]
    got = got.reshape(micros, H // heads, count, parts, heads * HD).transpose(0, 2, 3, 1, 4)
    return got.reshape(micros * count, parts * D)


def norm_scale(values):
    return lax.rsqrt(jnp.mean(values * values, axis=-1, keepdims=True) + EPSILON)


def norm_backward(grad_in, values, row_scale, gain):
    normed = values * row_scale
    gain_grad = jnp.sum(grad_in * normed, axis=0)
    scaled = grad_in * gain
    inner = jnp.mean(scaled * normed, axis=-1, keepdims=True)
    return row_scale * (scaled - normed * inner), gain_grad


def nt(a, b):
    return jnp.einsum("re,de->rd", a, b, preferred_element_type=f32)


def shards(tokens, segment_ids, w_qkv, w_out, w_gate_up, w_down, gain_attn, gain_mlp, cotangent):
    rows = tokens.shape[2]
    seq = lax.axis_size("seq")
    gather = lambda w: lax.all_gather(w, ("dp", "seq"), axis=0, tiled=True)
    gains = gather_small(jnp.stack([gain_attn, gain_mlp])).astype(f32)
    gain_a, gain_m = gains[0], gains[1]
    full_qkv, full_out, full_gate_up, full_down = (gather(w) for w in (w_qkv, w_out, w_gate_up, w_down))

    micros = 1 if H % seq == 0 else MB
    groups = MB // micros
    heads = micros * H // seq
    x = tokens.reshape(MB * rows, D).astype(f32)
    cot = cotangent.reshape(MB * rows, D)
    scale_a = norm_scale(x)
    h_attn = (x * scale_a * gain_a).astype(bf16)

    saved = []
    attended_parts = []
    for g in range(groups):
        if micros == 1:
            segments = segment_ids[g, 0]
        else:
            segments = pick(segment_ids[:, 0], lax.axis_index("seq") * micros // seq, 0)
        low, bounds = key_bounds(segments)
        part = h_attn[g * micros * rows : (g + 1) * micros * rows]
        qkv_rows = jnp.dot(part, full_qkv, preferred_element_type=f32).astype(bf16)
        qkv = to_heads(qkv_rows, micros, heads)
        mixed, lse = attend(qkv, bounds, low, heads)
        saved.append((qkv, low, bounds, mixed, lse))
        attended_parts.append(to_rows(mixed, micros, heads))
    attended = jnp.concatenate(attended_parts, axis=0)

    mid = x + jnp.dot(attended, full_out, preferred_element_type=f32)
    scale_m = norm_scale(mid)
    h_mlp = (mid * scale_m * gain_m).astype(bf16)
    gate_up = jnp.dot(h_mlp, full_gate_up, preferred_element_type=f32)
    gate, up = gate_up[:, :FF], gate_up[:, FF:]
    sig = jax.nn.sigmoid(gate)
    act = (gate * sig * up).astype(bf16)
    layer_out = (mid + jnp.dot(act, full_down, preferred_element_type=f32)).astype(bf16)

    grad_act = nt(cot, full_down)
    half_d = D // 2
    down_terms = [weight_grad(act, cot[:, :half_d], False), weight_grad(act, cot[:, half_d:], True)]
    grad_gate = (grad_act * up * sig * (1.0 + gate * (1.0 - sig))).astype(bf16)
    grad_up = (grad_act * (gate * sig)).astype(bf16)
    grad_gate_up = jnp.concatenate([grad_gate, grad_up], axis=-1)
    gate_up_terms = [weight_grad(h_mlp, grad_gate, False), weight_grad(h_mlp, grad_up, True)]
    grad_h_mlp = nt(grad_gate_up, full_gate_up)
    grad_mid_norm, gain_m_grad = norm_backward(grad_h_mlp, mid, scale_m, gain_m)
    grad_mid = cot.astype(f32) + grad_mid_norm
    grad_branch = grad_mid.astype(bf16)
    grad_attended = nt(grad_branch, full_out).astype(bf16)
    out_terms = [
        weight_grad(attended, grad_branch[:, :half_d], False),
        weight_grad(attended, grad_branch[:, half_d:], True),
    ]

    grad_qkv_parts = []
    for g in range(groups):
        qkv, low, bounds, mixed, lse = saved[g]
        grad = to_heads(grad_attended[g * micros * rows : (g + 1) * micros * rows], micros, heads)
        product = grad.astype(f32) * mixed.astype(f32)
        delta = jnp.sum(product.reshape(-1, heads, HD), axis=-1).T.reshape(heads, 1, -1)
        pieces = attend_back(qkv, grad, lse, delta, bounds, low, heads)
        grad_qkv_parts.append(to_rows(jnp.concatenate(pieces, axis=-1), micros, heads))
    grad_qkv = jnp.concatenate(grad_qkv_parts, axis=0)
    half_q = 3 * D // 2
    qkv_terms = [weight_grad(h_attn, grad_qkv[:, :half_q], False), weight_grad(h_attn, grad_qkv[:, half_q:], True)]
    grad_h_attn = nt(grad_qkv, full_qkv)
    grad_tok_norm, gain_a_grad = norm_backward(grad_h_attn, x, scale_a, gain_a)
    grad_tokens = grad_mid + grad_tok_norm
    gain_grads = scatter_small(jnp.stack([gain_a_grad, gain_m_grad]))

    return (
        layer_out.reshape(MB, 1, rows, D),
        grad_tokens.reshape(MB, 1, rows, D),
        jnp.concatenate(qkv_terms, axis=-1),
        jnp.concatenate(out_terms, axis=-1),
        jnp.concatenate(gate_up_terms, axis=-1),
        jnp.concatenate(down_terms, axis=-1),
        gain_grads[0],
        gain_grads[1],
    )


def solution(mesh):
    by_rows = P(("dp", "seq"), None)
    by_tokens = P(None, "dp", "seq", None)
    vector = P(("dp", "seq"))
    return jax.shard_map(
        shards,
        mesh=mesh,
        in_specs=(by_tokens, P(None, "dp", None), by_rows, by_rows, by_rows, by_rows, vector, vector, by_tokens),
        out_specs=(by_tokens, by_tokens, by_rows, by_rows, by_rows, by_rows, vector, vector),
        check_vma=False,
    )
```

time: 6710 us -> 2460 us (0.37)
  waiting for transfers between devices: 3400 us -> 1070 us
  blocking collectives: 1840 us -> 0 us
  matrix products: 921 us -> 514 us
  Pallas kernels: 0 us -> 213 us
  other arithmetic: 291 us -> 142 us
  local copies, waits for them, and re-layouts: 157 us -> 299 us
  starting transfers between devices: 52.7 us -> 184 us
    unnamed x3 -> x0, blocking collectives: 1840 us -> none
    reduce_scatter x3 -> x0, waiting for transfers between devices: 1180 us -> none  [the longest x1 1180 us: shards(): lax.psum_scatter(term_gate_up, ('dp', 'seq'), scatter_dimension=0, tiled=...]
    ppermute x16 -> x68, waiting for transfers between devices: 1610 us -> 484 us  [shift(): return lax.ppermute(block, axis, route)]
    dot_general x32 -> x41, matrix products: 921 us -> 514 us  [the longest x32 223 us: term(): return jnp.dot(side, cols_side, preferred_element_type=f32)]
    all_to_all x0 -> x8, waiting for transfers between devices: none -> 356 us  [the longest x4 309 us: to_heads(): got = lax.all_to_all(split, 'seq', 0, 0, tiled=True)]
    all_gather x4, waiting for transfers between devices: 570 us -> 227 us  [shards(): gather = lambda w: lax.all_gather(w, ('dp', 'seq'), axis=0, tiled=True)]
    pallas_call x0 -> x4, Pallas kernels: none -> 213 us  [the longest x2 122 us: attend_back(): pl.pallas_call(backward_kernel, grid_spec=pltpu.PrefetchScalarGridSpec(nu...]
    convert_element_type x7 -> x20, other arithmetic: 147 us -> 60.1 us  [the longest x8 35.3 us: weight_grad(): total = total.astype(bf16)]
  transfers between devices with their start and end apart: 24 -> 80, of which waited for: 11 -> 34; matrix products, arithmetic and copies ran while one was open for 40% -> 22% of each run, Pallas kernels for 0% -> 9%
where the time goes in v1:
time: 2460 us; the launch traced here: 2440 us
  waiting for transfers between devices  1070 us (43%)
  matrix products  514 us (21%)
  local copies, waits for them, and re-layouts  299 us (12%)
  Pallas kernels  213 us (9%)
  starting transfers between devices  184 us (7%)
  other arithmetic  142 us (6%)
    ppermute x68, waiting for transfers between devices, shift(): return lax.ppermute(block, axis, route)  484 us
    all_to_all x4, waiting for transfers between devices, to_heads(): got = lax.all_to_all(split, 'seq', 0, 0, tiled=True)  309 us
    all_gather x4, waiting for transfers between devices, shards(): gather = lambda w: lax.all_gather(w, ('dp', 'seq'), axis=0, tiled=True)  227 us
    dot_general x32, matrix products, term(): return jnp.dot(side, cols_side, preferred_element_type=f32)  223 us
    dot_general x4, matrix products, nt(): return jnp.einsum('re,de->rd', a, b, preferred_element_type=f32)  154 us
    ppermute x68, starting transfers between devices, shift(): return lax.ppermute(block, axis, route)  131 us
    pallas_call x2, Pallas kernels, attend_back(): pl.pallas_call(backward_kernel, grid_spec=pltpu.PrefetchScalarGridSpec(nu...  122 us
    pallas_call x2, Pallas kernels, attend(): pl.pallas_call(forward_kernel, grid_spec=pltpu.PrefetchScalarGridSpec(num...  90.7 us
  transfers between devices with their start and end apart: 80, of which 34 were waited for; matrix products, arithmetic and copies ran while one was open for 22% of the time, Pallas kernels for 9%

profile of v1, /device:TPU:0, one launch (start us, length us, event | category | flops | bytes accessed | tf_op | source)
XLA Modules:
  0.0 2437.9 jit_solution(9779797621073314111)
XLA Ops:
  36.5 131.9 %all-gather.6.cloned.1.call-done = bf16[2048,6144]{1,0:T(8,128)(2,1)} async-done(((bf16[64,6144]{1,0:T(8,128)(2,1)}), bf16[2048,6144]{1,0:T(8,128)(2,1)}) %all-gather.6.cloned.1.call-update) | async-done | bytes 25165840 | tf_op jit(solution)/shard_map/all_gather | solution.py:366
  168.4 18.6 convolution_convert_fusion.5
  191.9 8.9 copy.169
  205.8 18.6 convolution_convert_fusion.4
  229.3 9.0 copy.172
  238.3 195.3 %all-to-all-done = bf16[8,512,768]{1,2,0:T(8,128)(2,1)} async-done(((bf16[8,512,768]{1,2,0:T(8,128)(2,1)}), bf16[8,512,768]{1,2,0:T(8,128)(2,1)}, u32[]{:S(2)}, u32[]{:S(2)}) %all-to-all-start) | async-done | bytes 6291488 | tf_op jit(solution)/shard_map/all_to_all | solution.py:334
  443.9 8.7 copy.170
  455.4 45.2 %attend.2 = (bf16[4096,256]{1,0:T(8,128)(2,1)S(1)}, f32[2,1,4096]{2,1,0:T(1,128)S(1)}) custom-call(s32[4,8]{1,0:T(4,128)S(1)} %pad_add_fusion.bounds, bf16[4096,768]{1,0:T(8,128)(2,1)S(1)} %bitcast.484, bf16[4096,768]{1,0:T(8,128)(2,1)S(1)} %bitcast.485, bf16[4096,768]{1,0:T(8,128)(2,1)S(1)} %bitcast.486, s32[1,4096]{1,0:T(1,128)S(1)} %get-tuple-element.139.lo_ref), custom_call_target="tpu_custom_call" | custom-call | flops 7516192768 | bytes 8388608 | tf_op jit(solution)/shard_map/attend/pallas_call | solution.py:192
  503.3 113.5 %all-to-all-done.2 = bf16[8,512,768]{1,2,0:T(8,128)(2,1)} async-done(((bf16[8,512,768]{1,2,0:T(8,128)(2,1)}), bf16[8,512,768]{1,2,0:T(8,128)(2,1)}, u32[]{:S(2)}, u32[]{:S(2)}) %all-to-all-start.2) | async-done | bytes 6291488 | tf_op jit(solution)/shard_map/all_to_all | solution.py:334
  621.4 8.7 copy.173
  633.5 45.5 %attend.3 = (bf16[4096,256]{1,0:T(8,128)(2,1)S(1)}, f32[2,1,4096]{2,1,0:T(1,128)S(1)}) custom-call(s32[4,8]{1,0:T(4,128)S(1)} %pad_add_fusion.1.bounds, bf16[4096,768]{1,0:T(8,128)(2,1)S(1)} %bitcast.478, bf16[4096,768]{1,0:T(8,128)(2,1)S(1)} %bitcast.479, bf16[4096,768]{1,0:T(8,128)(2,1)S(1)} %bitcast.480, s32[1,4096]{1,0:T(1,128)S(1)} %get-tuple-element.104.lo_ref), custom_call_target="tpu_custom_call" | custom-call | flops 7516192768 | bytes 8388608 | tf_op jit(solution)/shard_map/attend/pallas_call | solution.py:192
  681.6 17.8 all-to-all-done.1
  704.0 11.6 copy.183
  715.6 11.8 reshape.710
  727.4 11.8 reshape.713
  751.4 22.1 reshape.729
  773.6 29.8 %all-to-all-done.3 = bf16[8,512,256]{1,2,0:T(8,128)(2,1)} async-done(((bf16[8,512,256]{1,2,0:T(8,128)(2,1)}), bf16[8,512,256]{1,2,0:T(8,128)(2,1)}, u32[]{:S(2)}, u32[]{:S(2)}) %all-to-all-start.3) | async-done | bytes 2097184 | tf_op jit(solution)/shard_map/all_to_all | solution.py:341
  803.4 14.4 multiply_reduce_fusion.4
  851.1 94.8 %all-gather.10.cloned.1.call-done = bf16[2048,11008]{1,0:T(8,128)(2,1)} async-done(((bf16[64,11008]{1,0:T(8,128)(2,1)}), bf16[2048,11008]{1,0:T(8,128)(2,1)}) %all-gather.10.cloned.1.call-update) | async-done | bytes 45088784 | tf_op jit(solution)/shard_map/all_gather | solution.py:366
  945.9 54.9 %fusion.225 = f32[1024,11008]{1,0:T(8,128)} fusion(bf16[1024,2048]{1,0:T(8,128)(2,1)} %multiply_convert_fusion.5, bf16[2048,11008]{1,0:T(8,128)(2,1)} %all-gather.10.cloned.1.call-done), kind=kOutput, calls=%fused_computation.434 | convolution fusion | flops 46170898432 | bytes 94371840 | tf_op jit(solution)/shard_map/dot_general | solution.py:398
  1000.8 44.6 %multiply_convert_fusion.1 = (bf16[1024,5504]{1,0:T(8,128)(2,1)}, bf16[1024,5504]{1,0:T(8,128)(2,1)}, bf16[1024,5504]{1,0:T(8,128)(2,1)}) fusion(f32[1024,11008]{1,0:T(8,128)} %fusion.225, bf16[1024,2048]{1,0:T(8,128)(2,1)} %bitcast.511, bf16[5504,2048]{1,0:T(8,128)(2,1)} %reshape.729), kind=kOutput, calls=%fused_computation.5 | convolution fusion | flops 23169990656 | bytes 105644032 | tf_op jit(solution)/shard_map/re,de->rd/dot_general | solution.py:360
  1045.4 15.6 copy.196
  1061.0 14.4 reshape.700
  1075.4 14.0 reshape.703
  1089.3 14.0 reshape.730
  1115.3 12.1 convolution_convert_fusion.2
  1127.4 12.1 convolution_convert_fusion.3
  1144.4 13.3 fusion.92
  1157.7 12.2 convolution_convert_fusion.1
  1169.9 13.1 fusion.84
  1183.0 61.0 %multiply_reduce_fusion = (f32[2048]{0:T(1024)S(1)}, f32[1024]{0:T(1024)S(1)}, f32[1024,2048]{1,0:T(8,128)}) fusion(f32[1024,2048]{1,0:T(8,128)} %copy-done.8, f32[1024]{0:T(1024)S(1)} %copy-done.51, f32[2048]{0:T(1024)S(1)} %bitcast.584, bf16[2048,11008]{1,0:T(8,128)(2,1)} %all-gather.10.cloned.1.call-done, bf16[1024,5504]{1,0:T(8,128)(2,1)} %get-tuple-element.109, ...), kind=kOutput, calls=%fused_computation.27 | convolution fusion | flops 46228570112 | bytes 84434944 | tf_op jit(solution)/shard_map/re,de->rd/dot_general | solution.py:360
  1259.6 31.5 %add_convert_fusion.4 = bf16[1024,2048]{1,0:T(8,128)(2,1)} fusion(f32[1024,2048]{1,0:T(8,128)S(1)} %bitcast.488, bf16[1024,5504]{1,0:T(8,128)(2,1)} %get-tuple-element.110, bf16[5504,2048]{1,0:T(8,128)(2,1)} %reshape.729), kind=kOutput, calls=%fused_computation.35 | convolution fusion | flops 23089643520 | bytes 46399488 | tf_op jit(solution)/shard_map/dot_general | solution.py:402
  1291.0 11.3 convolution_convert_fusion.10
  1309.7 9.9 copy.201
  1319.6 15.1 reshape.704
  1334.7 12.4 convolution_convert_fusion
  1370.4 13.9 collective-permute-done.22
  1448.8 60.7 %attend_back.2 = (bf16[4096,256]{1,0:T(8,128)(2,1)S(1)}, bf16[4096,256]{1,0:T(8,128)(2,1)S(1)}, bf16[4096,256]{1,0:T(8,128)(2,1)S(1)}) custom-call(s32[4,8]{1,0:T(4,128)S(1)} %copy-done.7, bf16[4096,768]{1,0:T(8,128)(2,1)} %bitcast.481, bf16[4096,768]{1,0:T(8,128)(2,1)} %bitcast.482, bf16[4096,768]{1,0:T(8,128)(2,1)} %bitcast.483, ...), custom_call_target="tpu_custom_call" | custom-call | flops 18790481920 | bytes 16777216 | tf_op jit(solution)/shard_map/attend_back/pallas_call | solution.py:276
  1512.4 8.7 copy.177
  1565.8 13.2 add_convert_fusion.3
  1579.0 21.1 collective-permute-done.50
  1613.9 13.2 add_convert_fusion.1
  1627.0 33.2 %collective-permute-done.57 = bf16[1376,1024]{1,0:T(8,128)(2,1)} collective-permute-done((bf16[1376,1024]{1,0:T(8,128)(2,1)}, bf16[1376,1024]{1,0:T(8,128)(2,1)}, u32[]{:S(2)}, u32[]{:S(2)}) %collective-permute-start.57) | collective-permute-done | bytes 2818080 | tf_op jit(solution)/shard_map/ppermute | solution.py:48
  1666.1 24.3 collective-permute-done.51
  1691.4 61.3 %attend_back.3 = (bf16[4096,256]{1,0:T(8,128)(2,1)S(1)}, bf16[4096,256]{1,0:T(8,128)(2,1)S(1)}, bf16[4096,256]{1,0:T(8,128)(2,1)S(1)}) custom-call(s32[4,8]{1,0:T(4,128)S(1)} %pad_add_fusion.1.bounds, bf16[4096,768]{1,0:T(8,128)(2,1)} %bitcast.475, bf16[4096,768]{1,0:T(8,128)(2,1)} %bitcast.476, bf16[4096,768]{1,0:T(8,128)(2,1)} %bitcast.477, ...), custom_call_target="tpu_custom_call" | custom-call | flops 18790481920 | bytes 16777216 | tf_op jit(solution)/shard_map/attend_back/pallas_call | solution.py:276
  1774.5 18.5 all-to-all-start.7
  1797.4 9.1 add_convert_fusion.2
  1808.9 31.5 %collective-permute-done.43 = bf16[512,5504]{1,0:T(8,128)(2,1)} collective-permute-done((bf16[512,5504]{1,0:T(8,128)(2,1)}, bf16[512,5504]{1,0:T(8,128)(2,1)}, u32[]{:S(2)}, u32[]{:S(2)}) %collective-permute-start.43) | collective-permute-done | bytes 5636128 | tf_op jit(solution)/shard_map/ppermute | solution.py:48
  1851.6 112.6 %collective-permute-done.53 = bf16[172,1024]{1,0:T(8,128)(2,1)S(1)} collective-permute-done((bf16[172,1024]{1,0:T(8,128)(2,1)}, bf16[172,1024]{1,0:T(8,128)(2,1)S(1)}, u32[]{:S(2)}, u32[]{:S(2)}) %collective-permute-start.53) | collective-permute-done | bytes 352288 | tf_op jit(solution)/shard_map/ppermute | solution.py:48
  1965.7 14.0 collective-permute-done.60
  1983.3 43.0 %collective-permute-done.44 = bf16[256,5504]{1,0:T(8,128)(2,1)S(1)} collective-permute-done((bf16[256,5504]{1,0:T(8,128)(2,1)S(1)}, bf16[256,5504]{1,0:T(8,128)(2,1)S(1)}, u32[]{:S(2)}, u32[]{:S(2)}) %collective-permute-start.44) | collective-permute-done | bytes 2818080 | tf_op jit(solution)/shard_map/ppermute | solution.py:48
  2047.6 36.7 %multiply_reduce_fusion.1 = (f32[2048]{0:T(1024)S(1)}, f32[1024]{0:T(1024)S(1)}, f32[1024,2048]{1,0:T(8,128)}) fusion(bf16[2,1,512,2048]{3,2,1,0:T(8,128)(2,1)S(1)} %copy-done.9, f32[1024]{0:T(1024)S(1)} %bitcast.596, f32[2048]{0:T(1024)S(1)} %bitcast.589, bf16[2048,6144]{1,0:T(8,128)(2,1)} %all-gather.6.cloned.1.call-done, ...), kind=kOutput, calls=%fused_computation.28 | convolution fusion | flops 25809645568 | bytes 50356224 | tf_op jit(solution)/shard_map/re,de->rd/dot_general | solution.py:360
  2099.7 11.8 multiply_add_fusion
  2120.1 9.3 fusion.116
  2165.1 28.5 %collective-permute-start.46 = (bf16[64,5504]{1,0:T(8,128)(2,1)}, bf16[64,5504]{1,0:T(8,128)(2,1)}, u32[]{:S(2)}, u32[]{:S(2)}) collective-permute-start(bf16[64,5504]{1,0:T(8,128)(2,1)} %get-tuple-element.120), channel_id=1, source_target_pairs={{0,4},{1,5},{2,6},{3,7},{4,0},{5,1},{6,2},{7,3},{8,12},{9,13},{10,... | collective-permute-start | bytes 2113544 | tf_op jit(solution)/shard_map/ppermute | solution.py:48
  2193.6 30.5 %collective-permute-done.39 = bf16[64,5504]{1,0:T(8,128)(2,1)} collective-permute-done((bf16[64,5504]{1,0:T(8,128)(2,1)}, bf16[64,5504]{1,0:T(8,128)(2,1)}, u32[]{:S(2)}, u32[]{:S(2)}) %collective-permute-start.39) | collective-permute-done | bytes 704544 | tf_op jit(solution)/shard_map/ppermute | solution.py:48
  2233.2 21.1 collective-permute-done.46
  2258.2 10.0 collective-permute-done.47
  2272.8 22.1 collective-permute-done.8
  2299.7 26.0 %collective-permute-done.15 = bf16[512,3072]{1,0:T(8,128)(2,1)} collective-permute-done((bf16[512,3072]{1,0:T(8,128)(2,1)}, bf16[512,3072]{1,0:T(8,128)(2,1)}, u32[]{:S(2)}, u32[]{:S(2)}) %collective-permute-start.15) | collective-permute-done | bytes 3145760 | tf_op jit(solution)/shard_map/ppermute | solution.py:48
  2334.0 22.4 collective-permute-done.9
  2357.1 12.2 collective-permute-start.10
  2387.5 11.5 collective-permute-done.11
  2407.5 22.2 collective-permute-done.18
  (473 shorter events, 500.3 us)
Async XLA Ops:
  7.2 161.2 %all-gather.6.cloned.1.call-start = ((), (), s32[]{:S(2)}) async-start(), calls=%async_computation.8 | async-start | bytes 25952256 | tf_op jit(solution)/shard_map/all_gather | solution.py:366
  7.9 743.5 %all-gather.12.cloned.1.call-start = ((), (), s32[]{:S(2)}) async-start(), calls=%async_computation.11 | async-start | bytes 23789568 | tf_op jit(solution)/shard_map/all_gather | solution.py:366
  8.7 764.9 %all-gather.8.cloned.1.call-start = ((), (), s32[]{:S(2)}) async-start(), calls=%async_computation.9 | async-start | bytes 8650752 | tf_op jit(solution)/shard_map/all_gather | solution.py:366
  9.4 936.5 %all-gather.10.cloned.1.call-start = ((), (), s32[]{:S(2)}) async-start(), calls=%async_computation.10 | async-start | bytes 46497792 | tf_op jit(solution)/shard_map/all_gather | solution.py:366
  200.8 232.8 %all-to-all-start = ((bf16[8,512,768]{1,2,0:T(8,128)(2,1)}), bf16[8,512,768]{1,2,0:T(8,128)(2,1)}, u32[]{:S(2)}, u32[]{:S(2)}) async-start(bf16[8,512,768]{1,2,0:T(8,128)(2,1)} %bitcast.496), calls=%async_computation | async-start | bytes 12582912 | tf_op jit(solution)/shard_map/all_to_all | solution.py:334
  433.6 183.2 %all-to-all-start.2 = ((bf16[8,512,768]{1,2,0:T(8,128)(2,1)}), bf16[8,512,768]{1,2,0:T(8,128)(2,1)}, u32[]{:S(2)}, u32[]{:S(2)}) async-start(bf16[8,512,768]{1,2,0:T(8,128)(2,1)} %bitcast.495), calls=%async_computation.2 | async-start | bytes 12582912 | tf_op jit(solution)/shard_map/all_to_all | solution.py:334
  616.8 82.6 %all-to-all-start.1 = ((bf16[8,512,256]{1,2,0:T(8,128)(2,1)}), bf16[8,512,256]{1,2,0:T(8,128)(2,1)}, u32[]{:S(2)}, u32[]{:S(2)}) async-start(bf16[8,512,256]{1,2,0:T(8,128)(2,1)} %copy.171), calls=%async_computation.1 | async-start | bytes 4194304 | tf_op jit(solution)/shard_map/all_to_all | solution.py:341
  699.4 104.0 %all-to-all-start.3 = ((bf16[8,512,256]{1,2,0:T(8,128)(2,1)}), bf16[8,512,256]{1,2,0:T(8,128)(2,1)}, u32[]{:S(2)}, u32[]{:S(2)}) async-start(bf16[8,512,256]{1,2,0:T(8,128)(2,1)} %copy.174), calls=%async_computation.3 | async-start | bytes 4194304 | tf_op jit(solution)/shard_map/all_to_all | solution.py:341
  1305.2 116.0 %all-to-all-start.4 = ((bf16[8,512,256]{2,1,0:T(8,128)(2,1)}), bf16[8,512,256]{2,1,0:T(8,128)(2,1)}, u32[]{:S(2)}, u32[]{:S(2)}) async-start(bf16[8,512,256]{2,1,0:T(8,128)(2,1)} %bitcast.470), calls=%async_computation.4 | async-start | bytes 4194304 | tf_op jit(solution)/shard_map/all_to_all | solution.py:334
  1347.3 23.1 collective-permute-start.20
  1348.8 12.9 collective-permute-start.28
  1358.9 25.4 %collective-permute-start.22 = (bf16[512,1024]{1,0:T(8,128)(2,1)S(1)}, bf16[512,1024]{1,0:T(8,128)(2,1)S(1)}, u32[]{:S(2)}, u32[]{:S(2)}) collective-permute-start(bf16[512,1024]{1,0:T(8,128)(2,1)S(1)} %add_convert_fusion.16), channel_id=1, source_target_pairs={{0,16},{8,24},{16,0},{24,8},{1,17},{9,25},{17,1},{25,9},{2,18},{10... | collective-permute-start | bytes 3145736 | tf_op jit(solution)/shard_map/ppermute | solution.py:48
  1361.6 25.9 %collective-permute-start.27 = (bf16[512,1024]{1,0:T(8,128)(2,1)}, bf16[512,1024]{1,0:T(8,128)(2,1)S(1)}, u32[]{:S(2)}, u32[]{:S(2)}) collective-permute-start(bf16[512,1024]{1,0:T(8,128)(2,1)} %convolution_convert_fusion.16), channel_id=1, source_target_pairs={{0,8},{8,0},{16,24},{24,16},{1,9},{9,1},{17,25},{25,17},{2,10},{10... | collective-permute-start | bytes 3145736 | tf_op jit(solution)/shard_map/ppermute | solution.py:48
  1364.0 26.2 %collective-permute-start.29 = (bf16[512,1024]{1,0:T(8,128)(2,1)}, bf16[512,1024]{1,0:T(8,128)(2,1)S(1)}, u32[]{:S(2)}, u32[]{:S(2)}) collective-permute-start(bf16[512,1024]{1,0:T(8,128)(2,1)} %add_convert_fusion.14), channel_id=1, source_target_pairs={{0,1},{1,0},{2,3},{3,2},{4,5},{5,4},{6,7},{7,6},{8,9},{9,8},{10,11... | collective-permute-start | bytes 3145736 | tf_op jit(solution)/shard_map/ppermute | solution.py:48
  1385.8 15.5 collective-permute-start.23
  1391.6 15.2 collective-permute-start.30
  1400.3 127.2 %collective-permute-start.49 = (bf16[1376,1024]{1,0:T(8,128)(2,1)}, bf16[1376,1024]{1,0:T(8,128)(2,1)}, u32[]{:S(2)}, u32[]{:S(2)}) collective-permute-start(bf16[1376,1024]{1,0:T(8,128)(2,1)} %convolution_convert_fusion.13), channel_id=1, source_target_pairs={{0,8},{8,0},{16,24},{24,16},{1,9},{9,1},{17,25},{25,17},{2,10},{10... | collective-permute-start | bytes 8454152 | tf_op jit(solution)/shard_map/ppermute | solution.py:48
  1400.3 178.7 %collective-permute-start.48 = (bf16[1376,1024]{1,0:T(8,128)(2,1)}, bf16[1376,1024]{1,0:T(8,128)(2,1)}, u32[]{:S(2)}, u32[]{:S(2)}) collective-permute-start(bf16[1376,1024]{1,0:T(8,128)(2,1)} %convolution_convert_fusion.14), channel_id=1, source_target_pairs={{0,8},{8,0},{16,24},{24,16},{1,9},{9,1},{17,25},{25,17},{2,10},{10... | collective-permute-start | bytes 8454152 | tf_op jit(solution)/shard_map/ppermute | solution.py:48
  1410.9 15.9 collective-permute-start.31
  1421.1 100.0 %all-to-all-start.6 = ((bf16[8,512,256]{2,1,0:T(8,128)(2,1)}), bf16[8,512,256]{2,1,0:T(8,128)(2,1)}, u32[]{:S(2)}, u32[]{:S(2)}) async-start(bf16[8,512,256]{2,1,0:T(8,128)(2,1)} %bitcast.530), calls=%async_computation.6 | async-start | bytes 4194304 | tf_op jit(solution)/shard_map/all_to_all | solution.py:334
  1426.9 109.8 %collective-permute-start.56 = (bf16[1376,1024]{1,0:T(8,128)(2,1)}, bf16[1376,1024]{1,0:T(8,128)(2,1)}, u32[]{:S(2)}, u32[]{:S(2)}) collective-permute-start(bf16[1376,1024]{1,0:T(8,128)(2,1)} %convolution_convert_fusion.11), channel_id=1, source_target_pairs={{0,8},{8,0},{16,24},{24,16},{1,9},{9,1},{17,25},{25,17},{2,10},{10... | collective-permute-start | bytes 8454152 | tf_op jit(solution)/shard_map/ppermute | solution.py:48
  1426.9 137.2 %collective-permute-start.35 = (bf16[512,5504]{1,0:T(8,128)(2,1)}, bf16[512,5504]{1,0:T(8,128)(2,1)}, u32[]{:S(2)}, u32[]{:S(2)}) collective-permute-start(bf16[512,5504]{1,0:T(8,128)(2,1)} %convolution_convert_fusion.2), channel_id=1, source_target_pairs={{0,8},{8,0},{16,24},{24,16},{1,9},{9,1},{17,25},{25,17},{2,10},{10... | collective-permute-start | bytes 16908296 | tf_op jit(solution)/shard_map/ppermute | solution.py:48
  1429.0 183.0 %collective-permute-start.42 = (bf16[512,5504]{1,0:T(8,128)(2,1)}, bf16[512,5504]{1,0:T(8,128)(2,1)}, u32[]{:S(2)}, u32[]{:S(2)}) collective-permute-start(bf16[512,5504]{1,0:T(8,128)(2,1)} %convolution_convert_fusion), channel_id=1, source_target_pairs={{0,8},{8,0},{16,24},{24,16},{1,9},{9,1},{17,25},{25,17},{2,10},{10... | collective-permute-start | bytes 16908296 | tf_op jit(solution)/shard_map/ppermute | solution.py:48
  1521.2 253.3 %all-to-all-start.5 = ((bf16[8,512,768]{1,2,0:T(8,128)(2,1)}), bf16[8,512,768]{1,2,0:T(8,128)(2,1)}, u32[]{:S(2)}, u32[]{:S(2)}) async-start(bf16[8,512,768]{1,2,0:T(8,128)(2,1)} %copy.177), calls=%async_computation.5 | async-start | bytes 12582912 | tf_op jit(solution)/shard_map/all_to_all | solution.py:341
  1527.5 99.6 %collective-permute-start.55 = (bf16[1376,1024]{1,0:T(8,128)(2,1)}, bf16[1376,1024]{1,0:T(8,128)(2,1)}, u32[]{:S(2)}, u32[]{:S(2)}) collective-permute-start(bf16[1376,1024]{1,0:T(8,128)(2,1)} %convolution_convert_fusion.12), channel_id=1, source_target_pairs={{0,8},{8,0},{16,24},{24,16},{1,9},{9,1},{17,25},{25,17},{2,10},{10... | collective-permute-start | bytes 8454152 | tf_op jit(solution)/shard_map/ppermute | solution.py:48
  1536.6 63.5 %collective-permute-start.50 = (bf16[1376,1024]{1,0:T(8,128)(2,1)}, bf16[1376,1024]{1,0:T(8,128)(2,1)}, u32[]{:S(2)}, u32[]{:S(2)}) collective-permute-start(bf16[1376,1024]{1,0:T(8,128)(2,1)} %add_convert_fusion.12), channel_id=1, source_target_pairs={{0,16},{8,24},{16,0},{24,8},{1,17},{9,25},{17,1},{25,9},{2,18},{10... | collective-permute-start | bytes 8454152 | tf_op jit(solution)/shard_map/ppermute | solution.py:48
  1564.1 96.1 %collective-permute-start.57 = (bf16[1376,1024]{1,0:T(8,128)(2,1)}, bf16[1376,1024]{1,0:T(8,128)(2,1)}, u32[]{:S(2)}, u32[]{:S(2)}) collective-permute-start(bf16[1376,1024]{1,0:T(8,128)(2,1)} %add_convert_fusion.10), channel_id=1, source_target_pairs={{0,1},{1,0},{2,3},{3,2},{4,5},{5,4},{6,7},{7,6},{8,9},{9,8},{10,11... | collective-permute-start | bytes 8454152 | tf_op jit(solution)/shard_map/ppermute | solution.py:48
  1579.0 214.0 %collective-permute-start.34 = (bf16[512,5504]{1,0:T(8,128)(2,1)}, bf16[512,5504]{1,0:T(8,128)(2,1)}, u32[]{:S(2)}, u32[]{:S(2)}) collective-permute-start(bf16[512,5504]{1,0:T(8,128)(2,1)} %convolution_convert_fusion.3), channel_id=1, source_target_pairs={{0,8},{8,0},{16,24},{24,16},{1,9},{9,1},{17,25},{25,17},{2,10},{10... | collective-permute-start | bytes 16908296 | tf_op jit(solution)/shard_map/ppermute | solution.py:48
  1600.1 196.4 %collective-permute-start.36 = (bf16[512,5504]{1,0:T(8,128)(2,1)}, bf16[512,5504]{1,0:T(8,128)(2,1)}, u32[]{:S(2)}, u32[]{:S(2)}) collective-permute-start(bf16[512,5504]{1,0:T(8,128)(2,1)} %add_convert_fusion.3), channel_id=1, source_target_pairs={{0,16},{8,24},{16,0},{24,8},{1,17},{9,25},{17,1},{25,9},{2,18},{10... | collective-permute-start | bytes 16908296 | tf_op jit(solution)/shard_map/ppermute | solution.py:48
  1612.0 78.3 %collective-permute-start.51 = (bf16[4,172,1024]{2,0,1:T(4,128)(2,1)S(1)}, bf16[4,172,1024]{2,0,1:T(4,128)(2,1)S(1)}, u32[]{:S(2)}, u32[]{:S(2)}) collective-permute-start(bf16[4,172,1024]{2,0,1:T(4,128)(2,1)S(1)} %copy.198), channel_id=1, source_target_pairs={{0,1},{1,0},{2,3},{3,2},{4,5},{5,4},{6,7},{7,6},{8,9},{9,8},{10,11... | collective-permute-start | bytes 4227080 | tf_op jit(solution)/shard_map/ppermute | solution.py:48
  1627.0 179.8 %collective-permute-start.41 = (bf16[512,5504]{1,0:T(8,128)(2,1)}, bf16[512,5504]{1,0:T(8,128)(2,1)}, u32[]{:S(2)}, u32[]{:S(2)}) collective-permute-start(bf16[512,5504]{1,0:T(8,128)(2,1)} %convolution_convert_fusion.1), channel_id=1, source_target_pairs={{0,8},{8,0},{16,24},{24,16},{1,9},{9,1},{17,25},{25,17},{2,10},{10... | collective-permute-start | bytes 16908296 | tf_op jit(solution)/shard_map/ppermute | solution.py:48
  1660.2 180.1 %collective-permute-start.43 = (bf16[512,5504]{1,0:T(8,128)(2,1)}, bf16[512,5504]{1,0:T(8,128)(2,1)}, u32[]{:S(2)}, u32[]{:S(2)}) collective-permute-start(bf16[512,5504]{1,0:T(8,128)(2,1)} %add_convert_fusion.1), channel_id=1, source_target_pairs={{0,1},{1,0},{2,3},{3,2},{4,5},{5,4},{6,7},{7,6},{8,9},{9,8},{10,11... | collective-permute-start | bytes 16908296 | tf_op jit(solution)/shard_map/ppermute | solution.py:48
  1690.3 78.4 %collective-permute-start.58 = (bf16[688,1024]{1,0:T(8,128)(2,1)}, bf16[688,1024]{1,0:T(8,128)(2,1)}, u32[]{:S(2)}, u32[]{:S(2)}) collective-permute-start(bf16[688,1024]{1,0:T(8,128)(2,1)} %dynamic-slice_bitcast_fusion.5), channel_id=1, source_target_pairs={{0,16},{8,24},{16,0},{24,8},{1,17},{9,25},{17,1},{25,9},{2,18},{10... | collective-permute-start | bytes 4227080 | tf_op jit(solution)/shard_map/ppermute | solution.py:48
  1768.7 79.8 %collective-permute-start.52 = (bf16[172,1024]{1,0:T(8,128)(2,1)}, bf16[172,1024]{1,0:T(8,128)(2,1)S(1)}, u32[]{:S(2)}, u32[]{:S(2)}) collective-permute-start(bf16[172,1024]{1,0:T(8,128)(2,1)} %get-tuple-element.127), channel_id=1, source_target_pairs={{0,2},{1,3},{2,4},{3,5},{4,6},{5,7},{6,0},{7,1},{8,10},{9,11},{10,... | collective-permute-start | bytes 1056776 | tf_op jit(solution)/shard_map/ppermute | solution.py:48
  1774.5 261.5 %all-to-all-start.7 = ((bf16[8,512,768]{1,2,0:T(8,128)(2,1)}), bf16[8,512,768]{1,2,0:T(8,128)(2,1)}, u32[]{:S(2)}, u32[]{:S(2)}) async-start(bf16[8,512,768]{1,2,0:T(8,128)(2,1)} %copy.181), calls=%async_computation.7 | async-start | bytes 12582912 | tf_op jit(solution)/shard_map/all_to_all | solution.py:341
  1793.0 171.2 %collective-permute-start.53 = (bf16[172,1024]{1,0:T(8,128)(2,1)}, bf16[172,1024]{1,0:T(8,128)(2,1)S(1)}, u32[]{:S(2)}, u32[]{:S(2)}) collective-permute-start(bf16[172,1024]{1,0:T(8,128)(2,1)} %get-tuple-element.129), channel_id=1, source_target_pairs={{0,4},{1,5},{2,6},{3,7},{4,0},{5,1},{6,2},{7,3},{8,12},{9,13},{10,... | collective-permute-start | bytes 1056776 | tf_op jit(solution)/shard_map/ppermute | solution.py:48
  1796.5 167.9 %collective-permute-start.54 = (bf16[172,1024]{1,0:T(8,128)(2,1)S(1)}, bf16[172,1024]{1,0:T(8,128)(2,1)S(1)}, u32[]{:S(2)}, u32[]{:S(2)}) collective-permute-start(bf16[172,1024]{1,0:T(8,128)(2,1)S(1)} %copy-done.40), channel_id=1, source_target_pairs={{0,6},{1,7},{2,0},{3,1},{4,2},{5,3},{6,4},{7,5},{8,14},{9,15},{10,... | collective-permute-start | bytes 1056776 | tf_op jit(solution)/shard_map/ppermute | solution.py:48
  1807.6 158.1 %collective-permute-start.59 = (bf16[172,1024]{1,0:T(8,128)(2,1)S(1)}, bf16[172,1024]{1,0:T(8,128)(2,1)S(1)}, u32[]{:S(2)}, u32[]{:S(2)}) collective-permute-start(bf16[172,1024]{1,0:T(8,128)(2,1)S(1)} %copy-done.41), channel_id=1, source_target_pairs={{0,2},{1,3},{2,4},{3,5},{4,6},{5,7},{6,0},{7,1},{8,10},{9,11},{10,... | collective-permute-start | bytes 1056776 | tf_op jit(solution)/shard_map/ppermute | solution.py:48
  1840.4 140.8 %collective-permute-start.37 = (bf16[4,64,5504]{2,1,0:T(8,128)(2,1)S(1)}, bf16[4,64,5504]{2,1,0:T(8,128)(2,1)S(1)}, u32[]{:S(2)}, u32[]{:S(2)}) collective-permute-start(bf16[4,64,5504]{2,1,0:T(8,128)(2,1)S(1)} %dynamic-slice_bitcast_fusion.1), channel_id=1, source_target_pairs={{0,1},{1,0},{2,3},{3,2},{4,5},{5,4},{6,7},{7,6},{8,9},{9,8},{10,11... | collective-permute-start | bytes 8454152 | tf_op jit(solution)/shard_map/ppermute | solution.py:48
  1848.5 131.2 %collective-permute-start.60 = (bf16[172,1024]{1,0:T(8,128)(2,1)S(1)}, bf16[172,1024]{1,0:T(8,128)(2,1)S(1)}, u32[]{:S(2)}, u32[]{:S(2)}) collective-permute-start(bf16[172,1024]{1,0:T(8,128)(2,1)S(1)} %get-tuple-element.132), channel_id=1, source_target_pairs={{0,4},{1,5},{2,6},{3,7},{4,0},{5,1},{6,2},{7,3},{8,12},{9,13},{10,... | collective-permute-start | bytes 1056776 | tf_op jit(solution)/shard_map/ppermute | solution.py:48
  1964.2 15.5 collective-permute-start.61
  1964.4 61.9 %collective-permute-start.44 = (bf16[256,5504]{1,0:T(8,128)(2,1)S(1)}, bf16[256,5504]{1,0:T(8,128)(2,1)S(1)}, u32[]{:S(2)}, u32[]{:S(2)}) collective-permute-start(bf16[256,5504]{1,0:T(8,128)(2,1)S(1)} %dynamic-slice_bitcast_fusion), channel_id=1, source_target_pairs={{0,16},{8,24},{16,0},{24,8},{1,17},{9,25},{17,1},{25,9},{2,18},{10... | collective-permute-start | bytes 8454152 | tf_op jit(solution)/shard_map/ppermute | solution.py:48
  2084.4 35.3 %collective-permute-start.62 = (f32[2,2,512]{2,1,0:T(2,128)S(1)}, f32[2,2,512]{2,1,0:T(2,128)S(1)}, u32[]{:S(2)}, u32[]{:S(2)}) collective-permute-start(f32[2,2,512]{2,1,0:T(2,128)S(1)} %bitcast.600), channel_id=1, source_target_pairs={{0,8},{8,0},{16,24},{24,16},{1,9},{9,1},{17,25},{25,17},{2,10},{10... | collective-permute-start | bytes 24584 | tf_op jit(solution)/shard_map/ppermute | solution.py:48
  2092.9 62.7 %collective-permute-start.7 = (bf16[512,3072]{1,0:T(8,128)(2,1)}, bf16[512,3072]{1,0:T(8,128)(2,1)}, u32[]{:S(2)}, u32[]{:S(2)}) collective-permute-start(bf16[512,3072]{1,0:T(8,128)(2,1)} %convolution_convert_fusion.8), channel_id=1, source_target_pairs={{0,8},{8,0},{16,24},{24,16},{1,9},{9,1},{17,25},{25,17},{2,10},{10... | collective-permute-start | bytes 9437192 | tf_op jit(solution)/shard_map/ppermute | solution.py:48
  2099.6 124.4 %collective-permute-start.14 = (bf16[512,3072]{1,0:T(8,128)(2,1)}, bf16[512,3072]{1,0:T(8,128)(2,1)}, u32[]{:S(2)}, u32[]{:S(2)}) collective-permute-start(bf16[512,3072]{1,0:T(8,128)(2,1)} %convolution_convert_fusion.6), channel_id=1, source_target_pairs={{0,8},{8,0},{16,24},{24,16},{1,9},{9,1},{17,25},{25,17},{2,10},{10... | collective-permute-start | bytes 9437192 | tf_op jit(solution)/shard_map/ppermute | solution.py:48
  2129.5 14.7 collective-permute-start.64
  2144.2 20.9 collective-permute-start.38
  2144.2 79.9 %collective-permute-start.39 = (bf16[64,5504]{1,0:T(8,128)(2,1)}, bf16[64,5504]{1,0:T(8,128)(2,1)}, u32[]{:S(2)}, u32[]{:S(2)}) collective-permute-start(bf16[64,5504]{1,0:T(8,128)(2,1)} %get-tuple-element.117), channel_id=1, source_target_pairs={{0,4},{1,5},{2,6},{3,7},{4,0},{5,1},{6,2},{7,3},{8,12},{9,13},{10,... | collective-permute-start | bytes 2113544 | tf_op jit(solution)/shard_map/ppermute | solution.py:48
  2153.6 77.2 %collective-permute-start.40 = (bf16[64,5504]{1,0:T(8,128)(2,1)}, bf16[64,5504]{1,0:T(8,128)(2,1)}, u32[]{:S(2)}, u32[]{:S(2)}) collective-permute-start(bf16[64,5504]{1,0:T(8,128)(2,1)} %get-tuple-element.116), channel_id=1, source_target_pairs={{0,6},{1,7},{2,0},{3,1},{4,2},{5,3},{6,4},{7,5},{8,14},{9,15},{10,... | collective-permute-start | bytes 2113544 | tf_op jit(solution)/shard_map/ppermute | solution.py:48
  2155.5 77.7 %collective-permute-start.45 = (bf16[64,5504]{1,0:T(8,128)(2,1)}, bf16[64,5504]{1,0:T(8,128)(2,1)}, u32[]{:S(2)}, u32[]{:S(2)}) collective-permute-start(bf16[64,5504]{1,0:T(8,128)(2,1)} %get-tuple-element.118), channel_id=1, source_target_pairs={{0,2},{1,3},{2,4},{3,5},{4,6},{5,7},{6,0},{7,1},{8,10},{9,11},{10,... | collective-permute-start | bytes 2113544 | tf_op jit(solution)/shard_map/ppermute | solution.py:48
  2165.1 89.2 %collective-permute-start.46 = (bf16[64,5504]{1,0:T(8,128)(2,1)}, bf16[64,5504]{1,0:T(8,128)(2,1)}, u32[]{:S(2)}, u32[]{:S(2)}) collective-permute-start(bf16[64,5504]{1,0:T(8,128)(2,1)} %get-tuple-element.120), channel_id=1, source_target_pairs={{0,4},{1,5},{2,6},{3,7},{4,0},{5,1},{6,2},{7,3},{8,12},{9,13},{10,... | collective-permute-start | bytes 2113544 | tf_op jit(solution)/shard_map/ppermute | solution.py:48
  2224.1 47.1 %collective-permute-start.6 = (bf16[512,3072]{1,0:T(8,128)(2,1)}, bf16[512,3072]{1,0:T(8,128)(2,1)S(1)}, u32[]{:S(2)}, u32[]{:S(2)}) collective-permute-start(bf16[512,3072]{1,0:T(8,128)(2,1)} %convolution_convert_fusion.9), channel_id=1, source_target_pairs={{0,8},{8,0},{16,24},{24,16},{1,9},{9,1},{17,25},{25,17},{2,10},{10... | collective-permute-start | bytes 9437192 | tf_op jit(solution)/shard_map/ppermute | solution.py:48
  2224.1 70.8 %collective-permute-start.8 = (bf16[512,3072]{1,0:T(8,128)(2,1)}, bf16[512,3072]{1,0:T(8,128)(2,1)}, u32[]{:S(2)}, u32[]{:S(2)}) collective-permute-start(bf16[512,3072]{1,0:T(8,128)(2,1)} %add_convert_fusion.8), channel_id=1, source_target_pairs={{0,16},{8,24},{16,0},{24,8},{1,17},{9,25},{17,1},{25,9},{2,18},{10... | collective-permute-start | bytes 9437192 | tf_op jit(solution)/shard_map/ppermute | solution.py:48
  2230.9 37.3 %collective-permute-start.47 = (bf16[64,5504]{1,0:T(8,128)(2,1)}, bf16[64,5504]{1,0:T(8,128)(2,1)S(1)}, u32[]{:S(2)}, u32[]{:S(2)}) collective-permute-start(bf16[64,5504]{1,0:T(8,128)(2,1)} %get-tuple-element.119), channel_id=1, source_target_pairs={{0,6},{1,7},{2,0},{3,1},{4,2},{5,3},{6,4},{7,5},{8,14},{9,15},{10,... | collective-permute-start | bytes 2113544 | tf_op jit(solution)/shard_map/ppermute | solution.py:48
  2233.2 66.5 %collective-permute-start.13 = (bf16[512,3072]{1,0:T(8,128)(2,1)}, bf16[512,3072]{1,0:T(8,128)(2,1)}, u32[]{:S(2)}, u32[]{:S(2)}) collective-permute-start(bf16[512,3072]{1,0:T(8,128)(2,1)} %convolution_convert_fusion.7), channel_id=1, source_target_pairs={{0,8},{8,0},{16,24},{24,16},{1,9},{9,1},{17,25},{25,17},{2,10},{10... | collective-permute-start | bytes 9437192 | tf_op jit(solution)/shard_map/ppermute | solution.py:48
  2254.3 71.4 %collective-permute-start.15 = (bf16[512,3072]{1,0:T(8,128)(2,1)}, bf16[512,3072]{1,0:T(8,128)(2,1)}, u32[]{:S(2)}, u32[]{:S(2)}) collective-permute-start(bf16[512,3072]{1,0:T(8,128)(2,1)} %add_convert_fusion.6), channel_id=1, source_target_pairs={{0,1},{1,0},{2,3},{3,2},{4,5},{5,4},{6,7},{7,6},{8,9},{9,8},{10,11... | collective-permute-start | bytes 9437192 | tf_op jit(solution)/shard_map/ppermute | solution.py:48
  2299.6 56.8 %collective-permute-start.9 = (bf16[4,64,3072]{2,1,0:T(8,128)(2,1)S(1)}, bf16[4,64,3072]{2,1,0:T(8,128)(2,1)S(1)}, u32[]{:S(2)}, u32[]{:S(2)}) collective-permute-start(bf16[4,64,3072]{2,1,0:T(8,128)(2,1)S(1)} %dynamic-slice_bitcast_fusion.3), channel_id=1, source_target_pairs={{0,1},{1,0},{2,3},{3,2},{4,5},{5,4},{6,7},{7,6},{8,9},{9,8},{10,11... | collective-permute-start | bytes 4718600 | tf_op jit(solution)/shard_map/ppermute | solution.py:48
  2330.3 42.3 %collective-permute-start.16 = (bf16[256,3072]{1,0:T(8,128)(2,1)S(1)}, bf16[256,3072]{1,0:T(8,128)(2,1)S(1)}, u32[]{:S(2)}, u32[]{:S(2)}) collective-permute-start(bf16[256,3072]{1,0:T(8,128)(2,1)S(1)} %dynamic-slice_bitcast_fusion.2), channel_id=1, source_target_pairs={{0,16},{8,24},{16,0},{24,8},{1,17},{9,25},{17,1},{25,9},{2,18},{10... | collective-permute-start | bytes 4718600 | tf_op jit(solution)/shard_map/ppermute | solution.py:48
  2357.1 25.1 %collective-permute-start.10 = (bf16[64,3072]{1,0:T(8,128)(2,1)S(1)}, bf16[64,3072]{1,0:T(8,128)(2,1)S(1)}, u32[]{:S(2)}, u32[]{:S(2)}) collective-permute-start(bf16[64,3072]{1,0:T(8,128)(2,1)S(1)} %get-tuple-element.121), channel_id=1, source_target_pairs={{0,2},{1,3},{2,4},{3,5},{4,6},{5,7},{6,0},{7,1},{8,10},{9,11},{10,... | collective-permute-start | bytes 1179656 | tf_op jit(solution)/shard_map/ppermute | solution.py:48
  2369.2 29.8 %collective-permute-start.11 = (bf16[64,3072]{1,0:T(8,128)(2,1)S(1)}, bf16[64,3072]{1,0:T(8,128)(2,1)S(1)}, u32[]{:S(2)}, u32[]{:S(2)}) collective-permute-start(bf16[64,3072]{1,0:T(8,128)(2,1)S(1)} %get-tuple-element.123), channel_id=1, source_target_pairs={{0,4},{1,5},{2,6},{3,7},{4,0},{5,1},{6,2},{7,3},{8,12},{9,13},{10,... | collective-permute-start | bytes 1179656 | tf_op jit(solution)/shard_map/ppermute | solution.py:48
  2372.6 26.5 %collective-permute-start.12 = (bf16[64,3072]{1,0:T(8,128)(2,1)S(1)}, bf16[64,3072]{1,0:T(8,128)(2,1)S(1)}, u32[]{:S(2)}, u32[]{:S(2)}) collective-permute-start(bf16[64,3072]{1,0:T(8,128)(2,1)S(1)} %get-tuple-element.122), channel_id=1, source_target_pairs={{0,6},{1,7},{2,0},{3,1},{4,2},{5,3},{6,4},{7,5},{8,14},{9,15},{10,... | collective-permute-start | bytes 1179656 | tf_op jit(solution)/shard_map/ppermute | solution.py:48
  2373.3 34.2 %collective-permute-start.17 = (bf16[64,3072]{1,0:T(8,128)(2,1)S(1)}, bf16[64,3072]{1,0:T(8,128)(2,1)S(1)}, u32[]{:S(2)}, u32[]{:S(2)}) collective-permute-start(bf16[64,3072]{1,0:T(8,128)(2,1)S(1)} %get-tuple-element.124), channel_id=1, source_target_pairs={{0,2},{1,3},{2,4},{3,5},{4,6},{5,7},{6,0},{7,1},{8,10},{9,11},{10,... | collective-permute-start | bytes 1179656 | tf_op jit(solution)/shard_map/ppermute | solution.py:48
  2375.4 54.3 %collective-permute-start.18 = (bf16[64,3072]{1,0:T(8,128)(2,1)S(1)}, bf16[64,3072]{1,0:T(8,128)(2,1)S(1)}, u32[]{:S(2)}, u32[]{:S(2)}) collective-permute-start(bf16[64,3072]{1,0:T(8,128)(2,1)S(1)} %get-tuple-element.126), channel_id=1, source_target_pairs={{0,4},{1,5},{2,6},{3,7},{4,0},{5,1},{6,2},{7,3},{8,12},{9,13},{10,... | collective-permute-start | bytes 1179656 | tf_op jit(solution)/shard_map/ppermute | solution.py:48
  2382.2 47.5 %collective-permute-start.19 = (bf16[64,3072]{1,0:T(8,128)(2,1)S(1)}, bf16[64,3072]{1,0:T(8,128)(2,1)S(1)}, u32[]{:S(2)}, u32[]{:S(2)}) collective-permute-start(bf16[64,3072]{1,0:T(8,128)(2,1)S(1)} %get-tuple-element.125), channel_id=1, source_target_pairs={{0,6},{1,7},{2,0},{3,1},{4,2},{5,3},{6,4},{7,5},{8,14},{9,15},{10,... | collective-permute-start | bytes 1179656 | tf_op jit(solution)/shard_map/ppermute | solution.py:48
  (94 other events, 3128.8 us)
Sparse Core Ops, SparseCore 0:
  11.0 157.3 all-gather.5
  171.3 263.6 all-gather.11
  437.9 181.8 all-gather.7
  622.6 323.2 all-gather.9

commit v2 on v1

v2 whole, which is shorter than its diff:
```python
import functools
import math

import jax
import jax.numpy as jnp
from jax import lax
from jax.experimental import pallas as pl
from jax.experimental.pallas import tpu as pltpu
from jax.sharding import PartitionSpec as P

D = 2048
H = 16
HD = 128
FF = 5504
WINDOW = 2048
MB = 2
TILE = 512

EPSILON = 1e-05
MASKED = -1e30
LOG2E = 1.4426950408889634
SCALE = 1.0 / math.sqrt(HD)

bf16 = jnp.bfloat16
f32 = jnp.float32


def digits_of(axis):
    size = lax.axis_size(axis)
    return [(axis, 1 << bit) for bit in reversed(range(size.bit_length() - 1))]


def digit_index(digit):
    axis, stride = digit
    return lax.rem(lax.axis_index(axis) // stride, 2)


def swap(block, digit):
    axis, stride = digit
    return lax.ppermute(block, axis, [(i, i ^ stride) for i in range(lax.axis_size(axis))])


def pick(array, index, dim):
    return lax.dynamic_index_in_dim(array, index, dim, keepdims=False)


def scatter_digit(parts, digit, dim, out_type):
    own = digit_index(digit)
    got = swap(pick(parts, 1 - own, dim), digit)
    return (pick(parts, own, dim).astype(f32) + got.astype(f32)).astype(out_type)


def gather_small(block):
    for digit in reversed(digits_of("dp") + digits_of("seq")):
        got = swap(block, digit)
        low = digit_index(digit) == 0
        block = jnp.concatenate([jnp.where(low, block, got), jnp.where(low, got, block)], axis=-1)
    return block


def scatter_small(terms):
    k = terms.shape[0]
    for digit in digits_of("dp") + digits_of("seq"):
        terms = scatter_digit(terms.reshape(k, 2, -1), digit, 1, f32)
    return terms


SLOTS = 8


def place_kernel(count, rows, widths, target, *refs):
    sources, outs = refs[: -3 - len(widths)], refs[-3 - len(widths) : -3]
    held, in_sems, out_sems = refs[-3:]
    per = sources[0].shape[0] // rows

    def read(n):
        source = sources[n // per].at[pl.ds((n % per) * rows, rows), :]
        return pltpu.make_async_copy(source, held.at[n % SLOTS], in_sems.at[n % SLOTS])

    def writes(n):
        start, left = pl.multiple_of(target[n], 16), 0
        copies = []
        for k, width in enumerate(widths):
            source = held.at[n % SLOTS, :, pl.ds(left, width)]
            copies.append(pltpu.make_async_copy(source, outs[k].at[pl.ds(start, rows), :], out_sems.at[n % SLOTS, k]))
            left += width
        return copies

    lag = SLOTS // 2
    for n in range(min(lag, count)):
        read(n).start()
    for n in range(count):
        if n >= lag:
            for copy in writes(n - lag):
                copy.wait()
        if n + lag < count:
            read(n + lag).start()
        read(n).wait()
        for copy in writes(n):
            copy.start()
    for n in range(max(count - lag, 0), count):
        for copy in writes(n):
            copy.wait()


class Gather:
    def __init__(self, blocks, seq_first):
        self.rows, self.widths = blocks[0].shape[0], [b.shape[1] for b in blocks]
        fast, height = digits_of("seq")[-1:], digits_of("dp")[:-1]
        self.far = digits_of("seq")[:-1]
        self.near = (fast + height if seq_first else height + fast) + digits_of("dp")[-1:]
        self.buffers = [(jnp.concatenate(blocks, axis=1), ())]

    def values(self):
        return [b for b, _ in self.buffers]

    def wait(self, *others):
        self.buffers = [(after(b, *others), d) for b, d in self.buffers]

    def far_step(self, n):
        (block, digits), digit = self.buffers[0], self.far[n]
        self.buffers = [(jnp.concatenate([block, swap(block, digit)], axis=0), digits + (digit,))]

    def near_step(self, n):
        digit = self.near[n]
        self.buffers = self.buffers + [(swap(b, digit), d + (digit,)) for b, d in self.buffers]

    def finish(self):
        offsets = []
        rows = self.rows
        stride_of = lambda digit: digit[1] * (lax.axis_size("seq") if digit[0] == "dp" else 1)
        for _, digits in self.buffers:
            near = sum(stride_of(d) for d in digits if d not in self.far)
            for n in range(1 << len(self.far)):
                offsets.append(near + sum(stride_of(d) for bit, d in enumerate(self.far) if n >> bit & 1))
        mine = lax.axis_index("dp") * lax.axis_size("seq") + lax.axis_index("seq")
        targets = lax.bitwise_xor(jnp.asarray(offsets, jnp.int32), mine.astype(jnp.int32)) * rows
        count = len(offsets)
        return pl.pallas_call(
            functools.partial(place_kernel, count, rows, self.widths),
            grid_spec=pltpu.PrefetchScalarGridSpec(
                num_scalar_prefetch=1,
                in_specs=[pl.BlockSpec(memory_space=pl.ANY)] * len(self.buffers),
                out_specs=[pl.BlockSpec(memory_space=pl.ANY)] * len(self.widths),
                scratch_shapes=[
                    pltpu.VMEM((SLOTS, rows, sum(self.widths)), bf16),
                    pltpu.SemaphoreType.DMA((SLOTS,)),
                    pltpu.SemaphoreType.DMA((SLOTS, len(self.widths))),
                ],
            ),
            out_shape=[jax.ShapeDtypeStruct((count * rows, width), bf16) for width in self.widths],
            compiler_params=pltpu.CompilerParams(vmem_limit_bytes=16 * 1024 * 1024),
            cost_estimate=pl.CostEstimate(flops=0, bytes_accessed=4 * count * rows * sum(self.widths), transcendentals=0),
            name="place",
        )(targets, *self.values())


def tn(a, b):
    return lax.dot_general(a, b, (((0,), (0,)), ((), ())), preferred_element_type=f32)


def after(value, *others):
    return lax.optimization_barrier((value,) + others)[0]


def pieces_of(side, seq_first):
    dp, seq = lax.axis_size("dp"), lax.axis_size("seq")
    tokens, total = side.shape
    if seq_first:
        pieces = side.reshape(tokens, dp // 2, 2, seq // 2, 2, -1).transpose(2, 0, 4, 1, 3, 5)
    else:
        pieces = side.reshape(tokens, dp // 2, 2, -1).transpose(2, 0, 1, 3)
    return pieces.reshape(2, tokens, total // 2)


class Reduce:
    def __init__(self, pieces, cols_side, seq_first, transposed=False):
        self.pieces, self.cols_side, self.seq_first, self.transposed = pieces, cols_side, seq_first, transposed
        self.half = pieces.shape[1 if transposed else 2] // 2
        self.own = self.half * 4 // (lax.axis_size("dp") * lax.axis_size("seq"))
        self.core, self.height = digits_of("dp")[-1], digits_of("dp")[0]
        self.fast, self.far = digits_of("seq")[-1], digits_of("seq")[:-1]
        self.first = self.fast if seq_first else self.height
        self.c, self.mine = digit_index(self.core), digit_index(self.first)

    def term(self, core_index, index, others):
        side = pick(after(self.pieces, *others), core_index, 0)
        if index is not None:
            side = lax.dynamic_slice_in_dim(side, index * self.half, self.half, 0 if self.transposed else 1)
        if self.transposed:
            return jnp.dot(side, self.cols_side, preferred_element_type=f32)
        return tn(side, self.cols_side)

    def cross(self, *others):
        term = self.term(1 - self.c, None, others).astype(bf16)
        self.got = swap(term, self.core)
        return term

    def got_part(self, index):
        return lax.dynamic_slice_in_dim(self.got, index * self.half, self.half, 0).astype(f32)

    def send(self, *others):
        away = (self.term(self.c, 1 - self.mine, others) + self.got_part(1 - self.mine)).astype(bf16)
        self.away = swap(away, self.first)
        return away

    def keep(self, *others):
        total = self.term(self.c, self.mine, others) + self.got_part(self.mine) + self.away.astype(f32)
        self.total = total.astype(bf16)
        return self.total

    def second(self, *others):
        cols = self.cols_side.shape[1]
        total = after(self.total, *others)
        if self.seq_first:
            self.total = scatter_digit(total.reshape(2, -1, cols), self.height, 0, bf16)
        else:
            self.total = scatter_digit(total.reshape(-1, 2, self.own, cols), self.fast, 1, bf16)
        return self.total


class Finish:
    def __init__(self, reduces, *others):
        self.reduces, self.far = reduces, reduces[0].far
        self.count = 1 << len(self.far)
        self.unit = D // (lax.axis_size("dp") * lax.axis_size("seq"))
        totals = [after(r.total, *others).reshape(self.count, self.unit, -1) for r in reduces]
        self.widths = [t.shape[2] for t in totals]
        self.total = jnp.concatenate(totals, axis=2)

    def step(self, n, *others):
        total = after(self.total, *others).reshape(-1, 2, self.unit, sum(self.widths))
        self.total = scatter_digit(total, self.far[-1 - n], 1, f32 if n == len(self.far) - 1 else bf16)
        return self.total

    def results(self):
        left = 0
        results = []
        for r, width in zip(self.reduces, self.widths):
            results.append(self.total[0, :, left : left + width].reshape(r.own, -1))
            left += width
        return results


def dot_nt(a, b):
    return lax.dot_general(a, b, (((1,), (1,)), ((), ())), preferred_element_type=f32)


def dot_tn(a, b):
    return lax.dot_general(a, b, (((0,), (0,)), ((), ())), preferred_element_type=f32)


def dot_nn(a, b):
    return lax.dot_general(a, b, (((1,), (0,)), ((), ())), preferred_element_type=f32)


def tile_of(ref, index):
    per = TILE // ref.shape[1]
    return ref[pl.ds(index * per, per)].reshape(TILE, HD)


def mask_of(i, j, lo):
    key = j * TILE + lax.broadcasted_iota(jnp.int32, (TILE, TILE), 0)
    query = i * TILE + lax.broadcasted_iota(jnp.int32, (TILE, TILE), 1)
    return (key >= lo) & (key <= query)


def forward_kernel(bounds, q_ref, k_ref, v_ref, lo_ref, o_ref, lse_ref, acc):
    pair, i = pl.program_id(0), pl.program_id(1)
    q = q_ref[...].reshape(TILE, HD)
    lo = lo_ref[...]
    factor = SCALE * LOG2E

    def step(j, carry, masked):
        m, l = carry
        s = dot_nt(tile_of(k_ref, j), q) * factor
        if masked:
            s = jnp.where(mask_of(i, j, lo), s, MASKED)
        new = jnp.maximum(m, jnp.max(s, axis=0, keepdims=True))
        p = jnp.exp2(s - new)
        old = jnp.exp2(m - new)
        acc[...] = acc[...] * old + dot_tn(tile_of(v_ref, j), p.astype(bf16))
        return new, l * old + jnp.sum(p, axis=0, keepdims=True)

    acc[...] = jnp.zeros_like(acc)
    carry = (jnp.full((1, TILE), MASKED, f32), jnp.zeros((1, TILE), f32))
    start = bounds[pair, 0, i]
    middle = bounds[pair, 1, i]
    carry = lax.fori_loop(start, middle, lambda j, c: step(j, c, True), carry)
    carry = lax.fori_loop(middle, i, lambda j, c: step(j, c, False), carry)
    m, l = step(i, carry, True)
    o_ref[...] = (acc[...] / l).T.astype(bf16).reshape(o_ref.shape)
    lse_ref[...] = m + jnp.log2(l)


def attend(qkv, bounds, low):
    seq, pairs, rows, _ = qkv.shape
    length = seq * rows
    blocks, per = length // TILE, TILE // rows
    whole = lambda part: pl.BlockSpec((seq, None, rows, HD), lambda p, i, b: (0, p, 0, part))
    line = pl.BlockSpec((None, 1, TILE), lambda p, i, b: (p, 0, i))
    block = pl.BlockSpec((per, None, rows, HD), lambda p, i, b: (i, p, 0, 0))
    return pl.pallas_call(
        forward_kernel,
        grid_spec=pltpu.PrefetchScalarGridSpec(
            num_scalar_prefetch=1,
            grid=(pairs, blocks),
            in_specs=[block, whole(1), whole(2), line],
            out_specs=[block, line],
            scratch_shapes=[pltpu.VMEM((HD, TILE), f32)],
        ),
        out_shape=[
            jax.ShapeDtypeStruct((seq, pairs, rows, HD), bf16),
            jax.ShapeDtypeStruct((pairs, 1, length), f32),
        ],
        compiler_params=pltpu.CompilerParams(vmem_limit_bytes=32 * 1024 * 1024),
        cost_estimate=pl.CostEstimate(
            flops=8 * pairs * length * 1792 * HD,
            bytes_accessed=8 * pairs * length * HD,
            transcendentals=pairs * length * 1792,
        ),
        name="attend",
    )(bounds, qkv, qkv, qkv, low)


def backward_kernel(bounds, q_ref, k_ref, v_ref, do_ref, o_ref, lse_ref, lo_ref, out_ref, dq, dk, dv, delta):
    pair, j = pl.program_id(0), pl.program_id(1)
    k = k_ref[...].reshape(TILE, HD)
    v = v_ref[...].reshape(TILE, HD)
    factor = SCALE * LOG2E

    def step(i, masked):
        rows = pl.ds(pl.multiple_of(i * TILE, TILE), TILE)
        q = tile_of(q_ref, i)
        do = tile_of(do_ref, i)
        s = dot_nt(k, q) * factor
        p = jnp.exp2(s - lse_ref[:, rows])
        if masked:
            p = jnp.where(mask_of(i, j, lo_ref[:, rows]), p, 0.0)
        dp = dot_nt(v, do)
        ds = (p * (dp - delta[:, rows])).astype(bf16)
        dv[...] += dot_nn(p.astype(bf16), do)
        dk[...] += dot_nn(ds, q)
        dq[rows, :] += dot_tn(ds, k)

    @pl.when(j == 0)
    def _():
        dq[...] = jnp.zeros_like(dq)

        @pl.loop(0, pl.num_programs(1))
        def _(i):
            rows = pl.ds(pl.multiple_of(i * TILE, TILE), TILE)
            product = tile_of(do_ref, i).astype(f32) * tile_of(o_ref, i).astype(f32)
            delta[:, rows] = jnp.sum(product.T, axis=0, keepdims=True)

    dk[...] = jnp.zeros_like(dk)
    dv[...] = jnp.zeros_like(dv)
    step(j, True)
    middle = bounds[pair, 2, j]
    end = bounds[pair, 3, j]

    @pl.loop(j + 1, middle)
    def _(i):
        step(i, False)

    @pl.loop(middle, end)
    def _(i):
        step(i, True)

    own = pl.ds(pl.multiple_of(j * TILE, TILE), TILE)
    shape = out_ref.shape[:-1] + (HD,)
    out_ref[:, :, :HD] = (dq[own, :] * SCALE).astype(bf16).reshape(shape)
    out_ref[:, :, HD : 2 * HD] = (dk[...] * SCALE).astype(bf16).reshape(shape)
    out_ref[:, :, 2 * HD :] = dv[...].astype(bf16).reshape(shape)


def attend_back(qkv, grad, mixed, lse, bounds, low):
    seq, pairs, rows, _ = qkv.shape
    length = seq * rows
    blocks, per = length // TILE, TILE // rows
    whole = pl.BlockSpec((seq, None, rows, HD), lambda p, j, b: (0, p, 0, 0))
    line = pl.BlockSpec((None, 1, length), lambda p, j, b: (p, 0, 0))
    block = lambda part: pl.BlockSpec((per, None, rows, HD), lambda p, j, b: (j, p, 0, part))
    return pl.pallas_call(
        backward_kernel,
        grid_spec=pltpu.PrefetchScalarGridSpec(
            num_scalar_prefetch=1,
            grid=(pairs, blocks),
            in_specs=[whole, block(1), block(2), whole, whole, line, line],
            out_specs=pl.BlockSpec((per, None, rows, 3 * HD), lambda p, j, b: (j, p, 0, 0)),
            scratch_shapes=[
                pltpu.VMEM((length, HD), f32),
                pltpu.VMEM((TILE, HD), f32),
                pltpu.VMEM((TILE, HD), f32),
                pltpu.VMEM((1, length), f32),
            ],
        ),
        out_shape=jax.ShapeDtypeStruct(qkv.shape, bf16),
        compiler_params=pltpu.CompilerParams(vmem_limit_bytes=40 * 1024 * 1024),
        cost_estimate=pl.CostEstimate(
            flops=20 * pairs * length * 1792 * HD,
            bytes_accessed=16 * pairs * length * HD,
            transcendentals=pairs * length * 1792,
        ),
        name="attend_back",
    )(bounds, qkv, qkv, qkv, grad, mixed, lse, low)


def key_bounds(segments):
    length = segments.shape[0]
    blocks = length // TILE
    place = jnp.arange(length, dtype=jnp.int32)
    start = jnp.zeros_like(place)
    for value in range(1, 4):
        earlier = jnp.sum(segments < value, dtype=jnp.int32)
        start = jnp.where(segments == value, earlier, start)
    low = jnp.maximum(start, place - (WINDOW - 1))
    index = jnp.arange(blocks, dtype=jnp.int32)
    first = low[::TILE]
    last = low[TILE - 1 :: TILE]
    begin = first // TILE
    middle = jnp.clip((last + TILE - 1) // TILE, begin, index)
    full = (last[None, :] <= index[:, None] * TILE) & (index[None, :] > index[:, None])
    some = (first[None, :] < (index[:, None] + 1) * TILE) & (index[None, :] > index[:, None])
    back_middle = index + 1 + jnp.sum(full, axis=1, dtype=jnp.int32)
    back_end = index + 1 + jnp.sum(some, axis=1, dtype=jnp.int32)
    return low[None], jnp.stack([begin, middle, back_middle, back_end])


def to_heads(rows, heads):
    seq = lax.axis_size("seq")
    parts = rows.shape[1] // (heads * HD)
    count = rows.shape[0] // MB
    split = rows.reshape(MB, count, parts, heads, HD).transpose(3, 0, 1, 2, 4)
    split = split.reshape(seq, heads * MB // seq, count, parts * HD)
    return lax.all_to_all(split, "seq", 0, 0, tiled=True)


def to_rows(whole, heads):
    got = lax.all_to_all(whole, "seq", 0, 0, tiled=True)
    count, parts = got.shape[2], got.shape[3] // HD
    got = got.reshape(heads, MB, count, parts, HD).transpose(1, 2, 3, 0, 4)
    return got.reshape(MB * count, parts * heads * HD)


def norm_scale(values):
    return lax.rsqrt(jnp.mean(values * values, axis=-1, keepdims=True) + EPSILON)


def norm_backward(grad_in, values, row_scale, gain):
    normed = values * row_scale
    gain_grad = jnp.sum(grad_in * normed, axis=0)
    scaled = grad_in * gain
    inner = jnp.mean(scaled * normed, axis=-1, keepdims=True)
    return row_scale * (scaled - normed * inner), gain_grad


def nt(a, b):
    return jnp.einsum("re,de->rd", a, b, preferred_element_type=f32)


def shards(tokens, segment_ids, w_qkv, w_out, w_gate_up, w_down, gain_attn, gain_mlp, cotangent):
    rows = tokens.shape[2]
    seq = lax.axis_size("seq")
    gather = lambda w: lax.all_gather(w, ("dp", "seq"), axis=0, tiled=True)
    groups = 2 if H * MB % (2 * seq) == 0 else 1
    heads = H // groups
    pairs = heads * MB // seq
    width = heads * HD

    x = tokens.reshape(MB * rows, D).astype(f32)
    cot = cotangent.reshape(MB * rows, D)
    bounds, low = [], []
    for k in range(pairs):
        micro = lax.rem(lax.axis_index("seq") * pairs + k, MB)
        pair_low, pair_bounds = key_bounds(pick(segment_ids[:, 0], micro, 0))
        bounds.append(pair_bounds)
        low.append(pair_low)
    bounds, low = jnp.stack(bounds), jnp.stack(low)

    order_qkv = w_qkv.reshape(-1, 3, groups, width).transpose(0, 2, 1, 3).reshape(w_qkv.shape)
    all_qkv = gather(order_qkv)
    full_qkv = [all_qkv[:, g * 3 * width : (g + 1) * 3 * width] for g in range(groups)]
    gains = gather_small(jnp.stack([gain_attn, gain_mlp])).astype(f32)
    gain_a, gain_m = gains[0], gains[1]
    scale_a = norm_scale(x)
    h_attn = (x * scale_a * gain_a).astype(bf16)
    gathers = [
        Gather([w_gate_up[:, FF:], w_down.reshape(w_qkv.shape[0], -1)], True),
        Gather([w_gate_up[:, :FF], w_out], False),
    ]
    values = lambda: [v for w in gathers for v in w.values()]

    def advance(step, *others):
        ready = values()
        for w in gathers:
            w.wait(*others, *ready)
            step(w)

    for n in range(len(gathers[0].far)):
        advance(lambda w: w.far_step(n))
    h_attn = after(h_attn, *values())
    advance(lambda w: w.near_step(0))
    arrived = []
    step_in = h_attn
    for g in range(groups):
        qkv_rows = jnp.dot(step_in, full_qkv[g], preferred_element_type=f32).astype(bf16)
        arrived.append(to_heads(qkv_rows, heads))
        step_in = after(h_attn, qkv_rows, *values())
    advance(lambda w: w.near_step(1))
    saved, attended = [], []
    last = None
    for g in range(groups):
        qkv = arrived[g] if last is None else after(arrived[g], last)
        last, lse = attend(qkv, bounds, low)
        saved.append((qkv, last, lse))
        attended.append(to_rows(last, heads))
    advance(lambda w: w.near_step(2), last)
    full_up, full_down = gathers[0].finish()
    full_gate, full_out = gathers[1].finish()
    attended = jnp.concatenate(attended, axis=1)

    mid = x + jnp.dot(attended, full_out, preferred_element_type=f32)
    scale_m = norm_scale(mid)
    h_mlp = (mid * scale_m * gain_m).astype(bf16)
    gate = jnp.dot(h_mlp, full_gate, preferred_element_type=f32)
    up = jnp.dot(h_mlp, full_up, preferred_element_type=f32)
    sig = jax.nn.sigmoid(gate)
    act = (gate * sig * up).astype(bf16)
    full_down = after(full_down, act).reshape(FF, D)
    grad_act = nt(cot, full_down)
    grad_gate = (grad_act * up * sig * (1.0 + gate * (1.0 - sig))).astype(bf16)
    grad_up = (grad_act * (gate * sig)).astype(bf16)
    grad_h_mlp = nt(grad_gate, full_gate) + nt(grad_up, full_up)
    grad_mid_norm, gain_m_grad = norm_backward(grad_h_mlp, mid, scale_m, gain_m)
    grad_mid = cot.astype(f32) + grad_mid_norm
    grad_branch = grad_mid.astype(bf16)
    grad_rows = [nt(grad_branch, full_out[g * width : (g + 1) * width]).astype(bf16) for g in range(groups)]
    grads = [to_heads(r, heads) for r in grad_rows]

    act_pieces = act.T.reshape(lax.axis_size("dp") // 2, 2, -1, MB * rows).transpose(1, 0, 2, 3)
    down = Reduce(act_pieces.reshape(2, FF // 2, MB * rows), cot, False, transposed=True)
    gate_r = Reduce(pieces_of(h_mlp, False), grad_gate, False)
    up_r = Reduce(pieces_of(h_mlp, True), grad_up, True)
    out_r = Reduce(pieces_of(attended, False), grad_branch, False)
    early = [gate_r, up_r, down, out_r]
    mark = tuple(grad_rows)
    for r in early:
        mark = (r.cross(*mark),)
    for r in early:
        mark = (r.send(*mark),)
    grad_heads = []
    for g in range(groups):
        qkv, mixed, lse = saved[g]
        back = attend_back(after(qkv, *mark), grads[g], mixed, lse, bounds, low)
        grad_heads.append(back)
        mark = (back,)
    grad_qkv = [to_rows(back, heads) for back in grad_heads]
    for r in early:
        mark = (r.keep(*mark),)
    layer_out = (mid + jnp.dot(after(act, *mark), full_down, preferred_element_type=f32)).astype(bf16)
    mark = (layer_out,)
    for r in early:
        r.second()

    h_sides = [pieces_of(h_attn, False), pieces_of(h_attn, True)]
    half = 3 * width // 2
    late = []
    grad_h_attn = 0.0
    for g in range(groups):
        final = g == groups - 1
        pair = [Reduce(h_sides[0], grad_qkv[g][:, :half], False), Reduce(h_sides[1], grad_qkv[g][:, half:], True)]
        for r in pair:
            mark = (r.cross(*mark),)
        part = nt(after(grad_qkv[g], *mark), full_qkv[g])
        grad_h_attn = grad_h_attn + part
        mark = (part,)
        for r in pair:
            mark = (r.send(*mark),)
        if final:
            first = Finish(early + late, *mark)
            first.step(0)
            grad_tok_norm, gain_a_grad = norm_backward(after(grad_h_attn, *mark), x, scale_a, gain_a)
            grad_tokens = grad_mid + grad_tok_norm
            mark = (grad_tokens,)
        late += pair
        for r in pair:
            mark = (r.keep(*mark),)
        for r in pair:
            r.second(*mark)
        if not final:
            mark = mark + tuple(r.total for r in early + pair)
    gain_grads = scatter_small(jnp.stack([gain_a_grad, gain_m_grad]))
    second = Finish(pair)
    far = len(first.far)
    for n in range(far):
        if n:
            first.step(n, *mark)
        second.step(n)
    results = first.results() + second.results()
    gate_grad, up_grad, down_grad, out_grad = results[:4]
    qkv_grads = [
        jnp.concatenate(results[4 + 2 * g : 6 + 2 * g], axis=1).reshape(-1, 3, 1, width) for g in range(groups)
    ]

    return (
        layer_out.reshape(MB, 1, rows, D),
        grad_tokens.reshape(MB, 1, rows, D),
        jnp.concatenate(qkv_grads, axis=2).reshape(-1, 3 * D),
        out_grad,
        jnp.concatenate([gate_grad, up_grad], axis=1),
        down_grad,
        gain_grads[0],
        gain_grads[1],
    )


def solution(mesh):
    by_rows = P(("dp", "seq"), None)
    by_tokens = P(None, "dp", "seq", None)
    vector = P(("dp", "seq"))
    return jax.shard_map(
        shards,
        mesh=mesh,
        in_specs=(by_tokens, P(None, "dp", None), by_rows, by_rows, by_rows, by_rows, vector, vector, by_tokens),
        out_specs=(by_tokens, by_tokens, by_rows, by_rows, by_rows, by_rows, vector, vector),
        check_vma=False,
    )
```

time: 2460 us -> 2430 us (0.988)
  starting transfers between devices: 184 us -> 100 us
  Pallas kernels: 213 us -> 269 us
  local copies, waits for them, and re-layouts: 299 us -> 330 us
    ppermute x68 -> x56, waiting for transfers between devices: 484 us -> 871 us  [swap(): lax.ppermute(block, axis, [(i, i ^ stride) for i in range(lax.axis_size(a...]
    all_gather x4 -> x1, waiting for transfers between devices: 227 us -> 0.01 us  [shards(): gather = lambda w: lax.all_gather(w, ('dp', 'seq'), axis=0, tiled=True)]
    all_to_all x8, waiting for transfers between devices: 356 us -> 188 us  [the longest x4 141 us: to_heads(): return lax.all_to_all(split, 'seq', 0, 0, tiled=True)]
    ppermute x68 -> x56, starting transfers between devices: 131 us -> 59.7 us  [swap(): lax.ppermute(block, axis, [(i, i ^ stride) for i in range(lax.axis_size(a...]
    pallas_call x0 -> x2, Pallas kernels: none -> 49.8 us  [finish(): pl.pallas_call(functools.partial(place_kernel, count, rows, self.widths),...]
    convert_element_type x16 -> x19, other arithmetic: 44.4 us -> 80.6 us  [the longest x8 34.2 us: keep(): self.total = total.astype(bf16)]
    reshape x19 -> x25, local copies, waits for them, and re-layouts: 116 us -> 152 us  [the longest x4 37.9 us: pieces_of(): pieces = side.reshape(tokens, dp // 2, 2, -1).transpose(2, 0, 1, 3)]
    convert_element_type x3 -> x0, local copies, waits for them, and re-layouts: 35.2 us -> none  [shards(): x = tokens.reshape(MB * rows, D).astype(f32)]
  transfers between devices with their start and end apart: 80 -> 65, of which waited for: 34 -> 19; matrix products, arithmetic and copies ran while one was open for 22% -> 26% of each run, Pallas kernels for 9% -> 10%
where the time goes in v2:
time: 2430 us; the launch traced here: 2420 us
  waiting for transfers between devices  1060 us (44%)
  matrix products  501 us (21%)
  local copies, waits for them, and re-layouts  330 us (14%)
  Pallas kernels  269 us (11%)
  other arithmetic  142 us (6%)
  starting transfers between devices  100 us (4%)
    ppermute x56, waiting for transfers between devices, swap(): lax.ppermute(block, axis, [(i, i ^ stride) for i in range(lax.axis_size(a...  871 us
    dot_general x7, matrix products, nt(): return jnp.einsum('re,de->rd', a, b, preferred_element_type=f32)  161 us
    dot_general x21, matrix products, tn(): lax.dot_general(a, b, (((0,), (0,)), ((), ())), preferred_element_type=f32)  158 us
    all_to_all x4, waiting for transfers between devices, to_heads(): return lax.all_to_all(split, 'seq', 0, 0, tiled=True)  141 us
    pallas_call x2, Pallas kernels, attend_back(): pl.pallas_call(backward_kernel, grid_spec=pltpu.PrefetchScalarGridSpec(nu...  126 us
    pallas_call x2, Pallas kernels, attend(): pl.pallas_call(forward_kernel, grid_spec=pltpu.PrefetchScalarGridSpec(num...  93.4 us
    ppermute x56, starting transfers between devices, swap(): lax.ppermute(block, axis, [(i, i ^ stride) for i in range(lax.axis_size(a...  59.7 us
    pallas_call x2, Pallas kernels, finish(): pl.pallas_call(functools.partial(place_kernel, count, rows, self.widths),...  49.8 us
  transfers between devices with their start and end apart: 65, of which 19 were waited for; matrix products, arithmetic and copies ran while one was open for 26% of the time, Pallas kernels for 10%

profile of v2, /device:TPU:0, one launch (start us, length us, event | category | flops | bytes accessed | tf_op | source)
XLA Modules:
  0.0 2417.6 jit_solution(7694349164614773827)
XLA Ops:
  25.9 56.5 %collective-permute-done.1 = bf16[2,128]{1,0:T(2,128)(2,1)S(1)} collective-permute-done((bf16[2,128]{1,0:T(2,128)(2,1)S(1)}, bf16[2,128]{1,0:T(2,128)(2,1)S(1)}, u32[]{:S(2)}, u32[]{:S(2)}) %collective-permute-start.1) | collective-permute-done | bytes 544 | tf_op jit(solution)/shard_map/ppermute | solution.py:40
  86.9 118.4 %collective-permute-done.2 = bf16[2,256]{1,0:T(2,128)(2,1)S(1)} collective-permute-done((bf16[2,256]{1,0:T(2,128)(2,1)S(1)}, bf16[2,256]{1,0:T(2,128)(2,1)S(1)}, u32[]{:S(2)}, u32[]{:S(2)}) %collective-permute-start.2) | collective-permute-done | bytes 1056 | tf_op jit(solution)/shard_map/ppermute | solution.py:40
  229.2 116.1 %collective-permute-done.8 = bf16[128,7552]{1,0:T(8,128)(2,1)S(1)} collective-permute-done((bf16[128,7552]{1,0:T(8,128)(2,1)S(1)}, bf16[128,7552]{1,0:T(8,128)(2,1)S(1)}, u32[]{:S(2)}, u32[]{:S(2)}) %collective-permute-start.8) | collective-permute-done | bytes 1933344 | tf_op jit(solution)/shard_map/ppermute | solution.py:40
  348.4 17.2 fusion.30
  370.3 8.9 copy.157
  379.2 8.6 copy.158
  396.1 83.7 %collective-permute-done.10.refs_1_ = bf16[256,7552]{1,0:T(8,128)(2,1)} collective-permute-done((bf16[256,7552]{1,0:T(8,128)(2,1)}, bf16[256,7552]{1,0:T(8,128)(2,1)}, u32[]{:S(2)}, u32[]{:S(2)}) %collective-permute-start.10) | collective-permute-done | bytes 3866656 | tf_op jit(solution)/shard_map/ppermute | solution.py:40
  479.8 103.9 %collective-permute-done.9.refs_1_ = bf16[256,11008]{1,0:T(8,128)(2,1)} collective-permute-done((bf16[256,11008]{1,0:T(8,128)(2,1)}, bf16[256,11008]{1,0:T(8,128)(2,1)}, u32[]{:S(2)}, u32[]{:S(2)}) %collective-permute-start.9) | collective-permute-done | bytes 5636128 | tf_op jit(solution)/shard_map/ppermute | solution.py:40
  583.7 17.0 convert_bitcast_fusion
  605.3 8.9 copy.160
  614.2 8.6 copy.161
  637.4 46.7 %attend.2 = (bf16[8,2,512,128]{3,2,1,0:T(8,128)(2,1)}, f32[2,1,4096]{2,1,0:T(1,128)S(1)}) custom-call(s32[2,4,8]{2,1,0:T(4,128)S(1)} %pad_add_fusion.1.bounds, bf16[8,2,512,384]{3,2,1,0:T(8,128)(2,1)} %all-to-all-done.q_ref.k_ref.v_ref, bf16[8,2,512,384]{3,2,1,0:T(8,128)(2,1)} %all-to-all-done.q_ref.k_ref.v_ref, ...), custom_call_target="tpu_custom_call" | custom-call | flops 15032385536 | bytes 8388608 | tf_op jit(solution)/shard_map/attend/pallas_call | solution.py:303
  684.1 82.3 %all-to-all-done.2.q_ref.k_ref.v_ref = bf16[8,2,512,384]{3,2,1,0:T(8,128)(2,1)} async-done(((bf16[8,2,512,384]{3,2,1,0:T(8,128)(2,1)}), bf16[8,2,512,384]{3,2,1,0:T(8,128)(2,1)}, u32[]{:S(2)}, u32[]{:S(2)}) %all-to-all-start.2) | async-done | bytes 6291488 | tf_op jit(solution)/shard_map/all_to_all | solution.py:436
  766.4 46.7 %attend.3 = (bf16[8,2,512,128]{3,2,1,0:T(8,128)(2,1)}, f32[2,1,4096]{2,1,0:T(1,128)S(1)}) custom-call(s32[2,4,8]{2,1,0:T(4,128)S(1)} %pad_add_fusion.1.bounds, bf16[8,2,512,384]{3,2,1,0:T(8,128)(2,1)} %all-to-all-done.2.q_ref.k_ref.v_ref, bf16[8,2,512,384]{3,2,1,0:T(8,128)(2,1)} %all-to-all-done.2.q_ref.k_ref.v_ref, ...), custom_call_target="tpu_custom_call" | custom-call | flops 15032385536 | bytes 8388608 | tf_op jit(solution)/shard_map/attend/pallas_call | solution.py:303
  817.3 64.3 %collective-permute-done.13.refs_2_ = bf16[256,7552]{1,0:T(8,128)(2,1)} collective-permute-done((bf16[256,7552]{1,0:T(8,128)(2,1)}, bf16[256,7552]{1,0:T(8,128)(2,1)}, u32[]{:S(2)}, u32[]{:S(2)}) %collective-permute-start.13) | collective-permute-done | bytes 3866656 | tf_op jit(solution)/shard_map/ppermute | solution.py:40
  893.6 44.7 %all-to-all-done.1 = bf16[8,2,512,128]{3,2,1,0:T(8,128)(2,1)} async-done(((bf16[8,2,512,128]{3,2,1,0:T(8,128)(2,1)}), bf16[8,2,512,128]{3,2,1,0:T(8,128)(2,1)}, u32[]{:S(2)}, u32[]{:S(2)}) %all-to-all-start.1) | async-done | bytes 2097184 | tf_op jit(solution)/shard_map/all_to_all | solution.py:440
  942.5 19.4 place.2
  965.3 11.5 multiply_reduce_fusion.2
  997.2 11.1 copy.170
  1013.2 34.0 %fusion.207 = f32[1024,5504]{1,0:T(8,128)} fusion(bf16[1024,2048]{1,0:T(8,128)(2,1)} %multiply_convert_fusion.1, bf16[2048,5504]{1,0:T(8,128)(2,1)} %get-tuple-element.99), kind=kOutput, calls=%fused_computation.365 | convolution fusion | flops 23085449216 | bytes 49283072 | tf_op jit(solution)/shard_map/dot_general | solution.py:526
  1047.2 30.4 %place.3 = (bf16[2048,5504]{1,0:T(8,128)(2,1)}, bf16[2048,5504]{1,0:T(8,128)(2,1)}) custom-call(s32[32]{0:T(128)S(1)} %xor_multiply_fusion.target, bf16[256,11008]{1,0:T(8,128)(2,1)} %constant_dynamic-update-slice_fusion.4.refs_0_, bf16[256,11008]{1,0:T(8,128)(2,1)} %collective-permute-done.9.refs_1_, bf16[256,11008]{1,0:T(8,128)(2,1)} %collective-permute-done.11.refs_2_, ...), custom_call_target="tpu_custom_call" | custom-call | bytes 90177536 | tf_op jit(solution)/shard_map/place/pallas_call | solution.py:139
  1077.6 37.9 %multiply_convert_fusion = (bf16[1024,5504]{1,0:T(8,128)(2,1)}, f32[1024,5504]{1,0:T(8,128)}) fusion(f32[1024,5504]{1,0:T(8,128)} %fusion.207, bf16[1024,2048]{1,0:T(8,128)(2,1)} %multiply_convert_fusion.1, bf16[2048,5504]{1,0:T(8,128)(2,1)} %get-tuple-element.104), kind=kOutput, calls=%fused_computation.13 | convolution fusion | flops 23119265792 | bytes 83099648 | tf_op jit(solution)/shard_map/dot_general | solution.py:527
  1115.6 31.2 %reshape.408 = bf16[5504,2048]{1,0:T(8,128)(2,1)} reshape(bf16[2048,5504]{1,0:T(8,128)(2,1)} %get-tuple-element.106) | data formatting | bytes 45088768 | tf_op jit(solution)/shard_map/reshape | solution.py:530
  1146.7 43.2 %fusion.2 = (bf16[1024,5504]{1,0:T(8,128)(2,1)}, bf16[1024,5504]{1,0:T(8,128)(2,1)}) fusion(f32[1024,5504]{1,0:T(8,128)} %get-tuple-element.258, f32[1024,5504]{1,0:T(8,128)} %fusion.207, bf16[5504,2048]{1,0:T(8,128)(2,1)} %reshape.408, bf16[1024,2048]{1,0:T(8,128)(2,1)} %bitcast.444), kind=kOutput, calls=%fused_computation.4 | convolution fusion | flops 23158718464 | bytes 94371840 | tf_op jit(solution)/shard_map/re,de->rd/dot_general | solution.py:459
  1189.9 31.8 %fusion.208 = f32[1024,2048]{1,0:T(8,128)} fusion(bf16[1024,5504]{1,0:T(8,128)(2,1)} %get-tuple-element.221, bf16[2048,5504]{1,0:T(8,128)(2,1)} %get-tuple-element.104), kind=kOutput, calls=%fused_computation.366 | convolution fusion | flops 23085449216 | bytes 42205184 | tf_op jit(solution)/shard_map/re,de->rd/dot_general | solution.py:459
  1221.7 36.0 %multiply_reduce_fusion = (f32[2048]{0:T(1024)}, f32[1024]{0:T(1024)S(1)}, f32[1024,2048]{1,0:T(8,128)}) fusion(f32[1024,2048]{1,0:T(8,128)} %copy-done.8, f32[1024]{0:T(1024)S(1)} %copy-done.52, f32[2048]{0:T(1024)S(1)} %bitcast.504, f32[1024,2048]{1,0:T(8,128)} %fusion.208, bf16[1024,5504]{1,0:T(8,128)(2,1)} %get-tuple-element.220, ...), kind=kOutput, calls=%fused_computation.49 | convolution fusion | flops 23100125184 | bytes 59006976 | tf_op jit(solution)/shard_map/re,de->rd/dot_general | solution.py:459
  1257.7 8.4 fusion.202
  1278.7 19.4 fusion.4
  1298.1 18.8 convolution_convert_fusion.2
  1317.2 18.4 convolution_convert_fusion.1
  1335.7 15.6 copy.166
  1357.6 14.0 convolution_convert_fusion
  1371.9 7.8 reshape.418
  1386.1 11.2 copy.178
  1409.0 9.9 maximum_bitcast_fusion
  1418.8 11.2 copy.165
  1430.0 9.5 convolution_convert_fusion.7
  1450.7 13.1 add_convert_fusion.5
  1465.2 13.1 add_convert_fusion.4
  1480.3 10.7 add_convert_fusion.3
  1507.7 62.8 %attend_back.2 = bf16[8,2,512,384]{3,2,1,0:T(8,128)(2,1)S(1)} custom-call(s32[2,4,8]{2,1,0:T(4,128)S(1)} %copy-done.5, bf16[8,2,512,384]{3,2,1,0:T(8,128)(2,1)} %all-to-all-done.q_ref.k_ref.v_ref, bf16[8,2,512,384]{3,2,1,0:T(8,128)(2,1)} %all-to-all-done.q_ref.k_ref.v_ref, bf16[8,2,512,384]{3,2,1,0:T(8,128)(2,1)} %all-to-all-done.q_ref.k_ref.v_ref, ...), custom_call_target="tpu_custom_call" | custom-call | flops 37580963840 | bytes 16777216 | tf_op jit(solution)/shard_map/attend_back/pallas_call | solution.py:384
  1573.2 55.2 %all-to-all-done.5.do_ref = bf16[8,2,512,128]{3,2,1,0:T(8,128)(2,1)} async-done(((bf16[8,2,512,128]{3,2,1,0:T(8,128)(2,1)}), bf16[8,2,512,128]{3,2,1,0:T(8,128)(2,1)}, u32[]{:S(2)}, u32[]{:S(2)}) %all-to-all-start.5) | async-done | bytes 2097184 | tf_op jit(solution)/shard_map/all_to_all | solution.py:436
  1635.9 63.4 %attend_back.3 = bf16[8,2,512,384]{3,2,1,0:T(8,128)(2,1)S(1)} custom-call(s32[2,4,8]{2,1,0:T(4,128)S(1)} %copy-done.5, bf16[8,2,512,384]{3,2,1,0:T(8,128)(2,1)} %all-to-all-done.2.q_ref.k_ref.v_ref, bf16[8,2,512,384]{3,2,1,0:T(8,128)(2,1)} %all-to-all-done.2.q_ref.k_ref.v_ref, bf16[8,2,512,384]{3,2,1,0:T(8,128)(2,1)} %all-to-all-done.2.q_ref.k_ref.v_ref, ...), custom_call_target="tpu_custom_call" | custom-call | flops 37580963840 | bytes 16777216 | tf_op jit(solution)/shard_map/attend_back/pallas_call | solution.py:384
  1699.4 11.7 fusion.131
  1716.5 11.4 fusion.129
  1728.0 8.8 add_convert_fusion.1
  1736.8 7.9 fusion.49
  1744.7 9.2 add_convert_fusion
  1765.0 31.3 %add_convert_fusion.6 = bf16[1024,2048]{1,0:T(8,128)(2,1)} fusion(f32[1024,2048]{1,0:T(8,128)S(1)} %bitcast.416, bf16[1024,5504]{1,0:T(8,128)(2,1)} %get-tuple-element.123, bf16[5504,2048]{1,0:T(8,128)(2,1)} %reshape.408), kind=kOutput, calls=%fused_computation.50 | convolution fusion | flops 23089643520 | bytes 46399488 | tf_op jit(solution)/shard_map/dot_general | solution.py:561
  1814.1 35.7 %collective-permute-done.38 = bf16[4,64,2048]{2,1,0:T(8,128)(2,1)} collective-permute-done((bf16[4,64,2048]{2,1,0:T(8,128)(2,1)}, bf16[4,64,2048]{2,1,0:T(8,128)(2,1)}, u32[]{:S(2)}, u32[]{:S(2)}) %collective-permute-start.38) | collective-permute-done | bytes 1048608 | tf_op jit(solution)/shard_map/ppermute | solution.py:40
  1862.5 8.6 copy.174
  1871.1 9.1 copy.175
  1880.3 10.3 reshape.415
  1900.9 17.4 fusion.13
  1931.9 26.0 %collective-permute-done.33 = bf16[512,1536]{1,0:T(8,128)(2,1)S(1)} collective-permute-done((bf16[512,1536]{1,0:T(8,128)(2,1)}, bf16[512,1536]{1,0:T(8,128)(2,1)S(1)}, u32[]{:S(2)}, u32[]{:S(2)}) %collective-permute-start.33) | collective-permute-done | bytes 1572896 | tf_op jit(solution)/shard_map/ppermute | solution.py:40
  1960.3 48.6 %collective-permute-done.34 = bf16[512,1536]{1,0:T(8,128)(2,1)S(1)} collective-permute-done((bf16[512,1536]{1,0:T(8,128)(2,1)S(1)}, bf16[512,1536]{1,0:T(8,128)(2,1)S(1)}, u32[]{:S(2)}, u32[]{:S(2)}) %collective-permute-start.34) | collective-permute-done | bytes 1572896 | tf_op jit(solution)/shard_map/ppermute | solution.py:40
  2017.3 8.7 copy.179
  2026.0 9.1 copy.180
  2035.1 10.3 reshape.421
  2063.1 21.2 fusion.206
  2121.7 11.8 fusion.26
  2155.9 84.1 %collective-permute-done.53 = f32[2,256]{1,0:T(2,128)S(1)} collective-permute-done((f32[2,256]{1,0:T(2,128)S(1)}, f32[2,256]{1,0:T(2,128)S(1)}, u32[]{:S(2)}, u32[]{:S(2)}) %collective-permute-start.53) | collective-permute-done | bytes 2080 | tf_op jit(solution)/shard_map/ppermute | solution.py:40
  2254.5 15.9 collective-permute-done.49
  2275.4 114.1 %collective-permute-done.50 = bf16[1,64,3072]{2,1,0:T(8,128)(2,1)S(1)} collective-permute-done((bf16[1,64,3072]{2,1,0:T(8,128)(2,1)S(1)}, bf16[1,64,3072]{2,1,0:T(8,128)(2,1)S(1)}, u32[]{:S(2)}, u32[]{:S(2)}) %collective-permute-start.50) | collective-permute-done | bytes 393248 | tf_op jit(solution)/shard_map/ppermute | solution.py:40
  (446 shorter events, 409.3 us)
Async XLA Ops:
  7.2 341.2 %all-gather.2.cloned.1.call-start = ((), (), s32[]{:S(2)}) async-start(), calls=%async_computation.8 | async-start | bytes 25952256 | tf_op jit(solution)/shard_map/all_gather | solution.py:465
  12.4 11.8 collective-permute-start
  19.7 200.0 %collective-permute-start.5 = (bf16[64,11008]{1,0:T(8,128)(2,1)}, bf16[64,11008]{1,0:T(8,128)(2,1)}, u32[]{:S(2)}, u32[]{:S(2)}) collective-permute-start(bf16[64,11008]{1,0:T(8,128)(2,1)} %pad_maximum_fusion.3), channel_id=1, source_target_pairs={{0,4},{1,5},{2,6},{3,7},{4,0},{5,1},{6,2},{7,3},{8,12},{9,13},{10,... | collective-permute-start | bytes 4227080 | tf_op jit(solution)/shard_map/ppermute | solution.py:40
  22.3 196.1 %collective-permute-start.6 = (bf16[64,7552]{1,0:T(8,128)(2,1)}, bf16[64,7552]{1,0:T(8,128)(2,1)}, u32[]{:S(2)}, u32[]{:S(2)}) collective-permute-start(bf16[64,7552]{1,0:T(8,128)(2,1)} %pad_maximum_fusion.4), channel_id=1, source_target_pairs={{0,4},{1,5},{2,6},{3,7},{4,0},{5,1},{6,2},{7,3},{8,12},{9,13},{10,... | collective-permute-start | bytes 2899976 | tf_op jit(solution)/shard_map/ppermute | solution.py:40
  24.3 58.0 %collective-permute-start.1 = (bf16[2,128]{1,0:T(2,128)(2,1)S(1)}, bf16[2,128]{1,0:T(2,128)(2,1)S(1)}, u32[]{:S(2)}, u32[]{:S(2)}) collective-permute-start(bf16[2,128]{1,0:T(2,128)(2,1)S(1)} %pad_maximum_fusion.11), channel_id=1, source_target_pairs={{0,2},{1,3},{2,0},{3,1},{4,6},{5,7},{6,4},{7,5},{8,10},{9,11},{10,... | collective-permute-start | bytes 1544 | tf_op jit(solution)/shard_map/ppermute | solution.py:40
  82.4 122.9 %collective-permute-start.2 = (bf16[2,256]{1,0:T(2,128)(2,1)S(1)}, bf16[2,256]{1,0:T(2,128)(2,1)S(1)}, u32[]{:S(2)}, u32[]{:S(2)}) collective-permute-start(bf16[2,256]{1,0:T(2,128)(2,1)S(1)} %pad_maximum_fusion.9), channel_id=1, source_target_pairs={{0,4},{1,5},{2,6},{3,7},{4,0},{5,1},{6,2},{7,3},{8,12},{9,13},{10,... | collective-permute-start | bytes 3080 | tf_op jit(solution)/shard_map/ppermute | solution.py:40
  208.5 3.7 collective-permute-start.4
  221.2 125.5 %collective-permute-start.7 = (bf16[128,11008]{1,0:T(8,128)(2,1)S(1)}, bf16[128,11008]{1,0:T(8,128)(2,1)S(1)}, u32[]{:S(2)}, u32[]{:S(2)}) collective-permute-start(bf16[128,11008]{1,0:T(8,128)(2,1)S(1)} %constant_dynamic-update-slice_fusion), channel_id=1, source_target_pairs={{0,2},{1,3},{2,0},{3,1},{4,6},{5,7},{6,4},{7,5},{8,10},{9,11},{10,... | collective-permute-start | bytes 8454152 | tf_op jit(solution)/shard_map/ppermute | solution.py:40
  225.8 119.5 %collective-permute-start.8 = (bf16[128,7552]{1,0:T(8,128)(2,1)S(1)}, bf16[128,7552]{1,0:T(8,128)(2,1)S(1)}, u32[]{:S(2)}, u32[]{:S(2)}) collective-permute-start(bf16[128,7552]{1,0:T(8,128)(2,1)S(1)} %constant_dynamic-update-slice_fusion.2), channel_id=1, source_target_pairs={{0,2},{1,3},{2,0},{3,1},{4,6},{5,7},{6,4},{7,5},{8,10},{9,11},{10,... | collective-permute-start | bytes 5799944 | tf_op jit(solution)/shard_map/ppermute | solution.py:40
  387.9 235.0 %all-to-all-start = ((bf16[8,2,512,384]{3,2,1,0:T(8,128)(2,1)}), bf16[8,2,512,384]{3,2,1,0:T(8,128)(2,1)}, u32[]{:S(2)}, u32[]{:S(2)}) async-start(bf16[8,2,512,384]{3,2,1,0:T(8,128)(2,1)} %copy.158), calls=%async_computation | async-start | bytes 12582912 | tf_op jit(solution)/shard_map/all_to_all | solution.py:436
  392.7 191.0 %collective-permute-start.9 = (bf16[256,11008]{1,0:T(8,128)(2,1)}, bf16[256,11008]{1,0:T(8,128)(2,1)}, u32[]{:S(2)}, u32[]{:S(2)}) collective-permute-start(bf16[256,11008]{1,0:T(8,128)(2,1)} %constant_dynamic-update-slice_fusion.4.refs_0_), channel_id=1, source_target_pairs={{0,1},{1,0},{2,3},{3,2},{4,5},{5,4},{6,7},{7,6},{8,9},{9,8},{10,11... | collective-permute-start | bytes 16908296 | tf_op jit(solution)/shard_map/ppermute | solution.py:40
  394.7 85.1 %collective-permute-start.10 = (bf16[256,7552]{1,0:T(8,128)(2,1)}, bf16[256,7552]{1,0:T(8,128)(2,1)}, u32[]{:S(2)}, u32[]{:S(2)}) collective-permute-start(bf16[256,7552]{1,0:T(8,128)(2,1)} %constant_dynamic-update-slice_fusion.6.refs_0_), channel_id=1, source_target_pairs={{0,16},{8,24},{16,0},{24,8},{1,17},{9,25},{17,1},{25,9},{2,18},{10... | collective-permute-start | bytes 11599880 | tf_op jit(solution)/shard_map/ppermute | solution.py:40
  622.9 143.6 %all-to-all-start.2 = ((bf16[8,2,512,384]{3,2,1,0:T(8,128)(2,1)}), bf16[8,2,512,384]{3,2,1,0:T(8,128)(2,1)}, u32[]{:S(2)}, u32[]{:S(2)}) async-start(bf16[8,2,512,384]{3,2,1,0:T(8,128)(2,1)} %copy.161), calls=%async_computation.2 | async-start | bytes 12582912 | tf_op jit(solution)/shard_map/all_to_all | solution.py:436
  633.3 184.0 %collective-permute-start.14 = (bf16[256,7552]{1,0:T(8,128)(2,1)}, bf16[256,7552]{1,0:T(8,128)(2,1)}, u32[]{:S(2)}, u32[]{:S(2)}) collective-permute-start(bf16[256,7552]{1,0:T(8,128)(2,1)} %collective-permute-done.10.refs_1_), channel_id=1, source_target_pairs={{0,1},{1,0},{2,3},{3,2},{4,5},{5,4},{6,7},{7,6},{8,9},{9,8},{10,11... | collective-permute-start | bytes 11599880 | tf_op jit(solution)/shard_map/ppermute | solution.py:40
  635.2 246.3 %collective-permute-start.12 = (bf16[256,11008]{1,0:T(8,128)(2,1)}, bf16[256,11008]{1,0:T(8,128)(2,1)}, u32[]{:S(2)}, u32[]{:S(2)}) collective-permute-start(bf16[256,11008]{1,0:T(8,128)(2,1)} %collective-permute-done.9.refs_1_), channel_id=1, source_target_pairs={{0,16},{8,24},{16,0},{24,8},{1,17},{9,25},{17,1},{25,9},{2,18},{10... | collective-permute-start | bytes 16908296 | tf_op jit(solution)/shard_map/ppermute | solution.py:40
  636.6 244.9 %collective-permute-start.11 = (bf16[256,11008]{1,0:T(8,128)(2,1)}, bf16[256,11008]{1,0:T(8,128)(2,1)}, u32[]{:S(2)}, u32[]{:S(2)}) collective-permute-start(bf16[256,11008]{1,0:T(8,128)(2,1)} %constant_dynamic-update-slice_fusion.4.refs_0_), channel_id=1, source_target_pairs={{0,16},{8,24},{16,0},{24,8},{1,17},{9,25},{17,1},{25,9},{2,18},{10... | collective-permute-start | bytes 16908296 | tf_op jit(solution)/shard_map/ppermute | solution.py:40
  637.3 244.3 %collective-permute-start.13 = (bf16[256,7552]{1,0:T(8,128)(2,1)}, bf16[256,7552]{1,0:T(8,128)(2,1)}, u32[]{:S(2)}, u32[]{:S(2)}) collective-permute-start(bf16[256,7552]{1,0:T(8,128)(2,1)} %constant_dynamic-update-slice_fusion.6.refs_0_), channel_id=1, source_target_pairs={{0,1},{1,0},{2,3},{3,2},{4,5},{5,4},{6,7},{7,6},{8,9},{9,8},{10,11... | collective-permute-start | bytes 11599880 | tf_op jit(solution)/shard_map/ppermute | solution.py:40
  813.1 72.3 %all-to-all-start.3 = ((bf16[8,2,512,128]{3,2,1,0:T(8,128)(2,1)}), bf16[8,2,512,128]{3,2,1,0:T(8,128)(2,1)S(1)}, u32[]{:S(2)}, u32[]{:S(2)}) async-start(bf16[8,2,512,128]{3,2,1,0:T(8,128)(2,1)} %get-tuple-element.89.o_ref), calls=%async_computation.3 | async-start | bytes 4194304 | tf_op jit(solution)/shard_map/all_to_all | solution.py:440
  881.6 60.3 %collective-permute-start.18 = (bf16[256,7552]{1,0:T(8,128)(2,1)}, bf16[256,7552]{1,0:T(8,128)(2,1)}, u32[]{:S(2)}, u32[]{:S(2)}) collective-permute-start(bf16[256,7552]{1,0:T(8,128)(2,1)} %collective-permute-done.14.refs_3_), channel_id=1, source_target_pairs={{0,8},{8,0},{16,24},{24,16},{1,9},{9,1},{17,25},{25,17},{2,10},{10... | collective-permute-start | bytes 11599880 | tf_op jit(solution)/shard_map/ppermute | solution.py:40
  881.6 60.3 %collective-permute-start.17 = (bf16[256,7552]{1,0:T(8,128)(2,1)}, bf16[256,7552]{1,0:T(8,128)(2,1)}, u32[]{:S(2)}, u32[]{:S(2)}) collective-permute-start(bf16[256,7552]{1,0:T(8,128)(2,1)} %collective-permute-done.13.refs_2_), channel_id=1, source_target_pairs={{0,8},{8,0},{16,24},{24,16},{1,9},{9,1},{17,25},{25,17},{2,10},{10... | collective-permute-start | bytes 11599880 | tf_op jit(solution)/shard_map/ppermute | solution.py:40
  882.1 60.3 %collective-permute-start.16 = (bf16[256,7552]{1,0:T(8,128)(2,1)}, bf16[256,7552]{1,0:T(8,128)(2,1)}, u32[]{:S(2)}, u32[]{:S(2)}) collective-permute-start(bf16[256,7552]{1,0:T(8,128)(2,1)} %collective-permute-done.10.refs_1_), channel_id=1, source_target_pairs={{0,8},{8,0},{16,24},{24,16},{1,9},{9,1},{17,25},{25,17},{2,10},{10... | collective-permute-start | bytes 11599880 | tf_op jit(solution)/shard_map/ppermute | solution.py:40
  882.1 60.4 %collective-permute-start.15 = (bf16[256,7552]{1,0:T(8,128)(2,1)}, bf16[256,7552]{1,0:T(8,128)(2,1)}, u32[]{:S(2)}, u32[]{:S(2)}) collective-permute-start(bf16[256,7552]{1,0:T(8,128)(2,1)} %constant_dynamic-update-slice_fusion.6.refs_0_), channel_id=1, source_target_pairs={{0,8},{8,0},{16,24},{24,16},{1,9},{9,1},{17,25},{25,17},{2,10},{10... | collective-permute-start | bytes 11599880 | tf_op jit(solution)/shard_map/ppermute | solution.py:40
  885.4 52.8 %all-to-all-start.1 = ((bf16[8,2,512,128]{3,2,1,0:T(8,128)(2,1)}), bf16[8,2,512,128]{3,2,1,0:T(8,128)(2,1)}, u32[]{:S(2)}, u32[]{:S(2)}) async-start(bf16[8,2,512,128]{3,2,1,0:T(8,128)(2,1)} %get-tuple-element.84.o_ref), calls=%async_computation.1 | async-start | bytes 4194304 | tf_op jit(solution)/shard_map/all_to_all | solution.py:440
  890.0 157.1 %collective-permute-start.22 = (bf16[256,11008]{1,0:T(8,128)(2,1)}, bf16[256,11008]{1,0:T(8,128)(2,1)}, u32[]{:S(2)}, u32[]{:S(2)}) collective-permute-start(bf16[256,11008]{1,0:T(8,128)(2,1)} %collective-permute-done.12.refs_3_), channel_id=1, source_target_pairs={{0,8},{8,0},{16,24},{24,16},{1,9},{9,1},{17,25},{25,17},{2,10},{10... | collective-permute-start | bytes 16908296 | tf_op jit(solution)/shard_map/ppermute | solution.py:40
  941.8 105.3 %collective-permute-start.21 = (bf16[256,11008]{1,0:T(8,128)(2,1)}, bf16[256,11008]{1,0:T(8,128)(2,1)}, u32[]{:S(2)}, u32[]{:S(2)}) collective-permute-start(bf16[256,11008]{1,0:T(8,128)(2,1)} %collective-permute-done.11.refs_2_), channel_id=1, source_target_pairs={{0,8},{8,0},{16,24},{24,16},{1,9},{9,1},{17,25},{25,17},{2,10},{10... | collective-permute-start | bytes 16908296 | tf_op jit(solution)/shard_map/ppermute | solution.py:40
  941.9 105.3 %collective-permute-start.20 = (bf16[256,11008]{1,0:T(8,128)(2,1)}, bf16[256,11008]{1,0:T(8,128)(2,1)}, u32[]{:S(2)}, u32[]{:S(2)}) collective-permute-start(bf16[256,11008]{1,0:T(8,128)(2,1)} %collective-permute-done.9.refs_1_), channel_id=1, source_target_pairs={{0,8},{8,0},{16,24},{24,16},{1,9},{9,1},{17,25},{25,17},{2,10},{10... | collective-permute-start | bytes 16908296 | tf_op jit(solution)/shard_map/ppermute | solution.py:40
  942.4 104.8 %collective-permute-start.19 = (bf16[256,11008]{1,0:T(8,128)(2,1)}, bf16[256,11008]{1,0:T(8,128)(2,1)}, u32[]{:S(2)}, u32[]{:S(2)}) collective-permute-start(bf16[256,11008]{1,0:T(8,128)(2,1)} %constant_dynamic-update-slice_fusion.4.refs_0_), channel_id=1, source_target_pairs={{0,8},{8,0},{16,24},{24,16},{1,9},{9,1},{17,25},{25,17},{2,10},{10... | collective-permute-start | bytes 16908296 | tf_op jit(solution)/shard_map/ppermute | solution.py:40
  1316.9 133.9 %collective-permute-start.23 = (bf16[1024,5504]{1,0:T(8,128)(2,1)}, bf16[1024,5504]{1,0:T(8,128)(2,1)}, u32[]{:S(2)}, u32[]{:S(2)}) collective-permute-start(bf16[1024,5504]{1,0:T(8,128)(2,1)} %convolution_convert_fusion.2), channel_id=1, source_target_pairs={{0,8},{8,0},{16,24},{24,16},{1,9},{9,1},{17,25},{25,17},{2,10},{10... | collective-permute-start | bytes 33816584 | tf_op jit(solution)/shard_map/ppermute | solution.py:40
  1357.4 107.9 %collective-permute-start.24 = (bf16[1024,5504]{1,0:T(8,128)(2,1)}, bf16[1024,5504]{1,0:T(8,128)(2,1)}, u32[]{:S(2)}, u32[]{:S(2)}) collective-permute-start(bf16[1024,5504]{1,0:T(8,128)(2,1)} %convolution_convert_fusion.1), channel_id=1, source_target_pairs={{0,8},{8,0},{16,24},{24,16},{1,9},{9,1},{17,25},{25,17},{2,10},{10... | collective-permute-start | bytes 33816584 | tf_op jit(solution)/shard_map/ppermute | solution.py:40
  1371.6 108.8 %collective-permute-start.25 = (bf16[2752,2048]{1,0:T(8,128)(2,1)}, bf16[2752,2048]{1,0:T(8,128)(2,1)}, u32[]{:S(2)}, u32[]{:S(2)}) collective-permute-start(bf16[2752,2048]{1,0:T(8,128)(2,1)} %convolution_convert_fusion), channel_id=1, source_target_pairs={{0,8},{8,0},{16,24},{24,16},{1,9},{9,1},{17,25},{25,17},{2,10},{10... | collective-permute-start | bytes 33816584 | tf_op jit(solution)/shard_map/ppermute | solution.py:40
  1439.5 59.9 %collective-permute-start.26 = (bf16[1024,2048]{1,0:T(8,128)(2,1)}, bf16[1024,2048]{1,0:T(8,128)(2,1)}, u32[]{:S(2)}, u32[]{:S(2)}) collective-permute-start(bf16[1024,2048]{1,0:T(8,128)(2,1)} %convolution_convert_fusion.7), channel_id=1, source_target_pairs={{0,8},{8,0},{16,24},{24,16},{1,9},{9,1},{17,25},{25,17},{2,10},{10... | collective-permute-start | bytes 12582920 | tf_op jit(solution)/shard_map/ppermute | solution.py:40
  1442.0 53.0 %all-to-all-start.4 = ((bf16[8,2,512,128]{3,2,1,0:T(8,128)(2,1)}), bf16[8,2,512,128]{3,2,1,0:T(8,128)(2,1)S(1)}, u32[]{:S(2)}, u32[]{:S(2)}) async-start(bf16[8,2,512,128]{3,2,1,0:T(8,128)(2,1)} %bitcast.456), calls=%async_computation.4 | async-start | bytes 4194304 | tf_op jit(solution)/shard_map/all_to_all | solution.py:436
  1463.8 247.2 %collective-permute-start.27 = (bf16[512,5504]{1,0:T(8,128)(2,1)}, bf16[512,5504]{1,0:T(8,128)(2,1)}, u32[]{:S(2)}, u32[]{:S(2)}) collective-permute-start(bf16[512,5504]{1,0:T(8,128)(2,1)} %add_convert_fusion.5), channel_id=1, source_target_pairs={{0,16},{8,24},{16,0},{24,8},{1,17},{9,25},{17,1},{25,9},{2,18},{10... | collective-permute-start | bytes 16908296 | tf_op jit(solution)/shard_map/ppermute | solution.py:40
  1478.3 249.7 %collective-permute-start.28 = (bf16[512,5504]{1,0:T(8,128)(2,1)}, bf16[512,5504]{1,0:T(8,128)(2,1)}, u32[]{:S(2)}, u32[]{:S(2)}) collective-permute-start(bf16[512,5504]{1,0:T(8,128)(2,1)} %add_convert_fusion.4), channel_id=1, source_target_pairs={{0,1},{1,0},{2,3},{3,2},{4,5},{5,4},{6,7},{7,6},{8,9},{9,8},{10,11... | collective-permute-start | bytes 16908296 | tf_op jit(solution)/shard_map/ppermute | solution.py:40
  1491.0 253.7 %collective-permute-start.29 = (bf16[1376,2048]{1,0:T(8,128)(2,1)}, bf16[1376,2048]{1,0:T(8,128)(2,1)}, u32[]{:S(2)}, u32[]{:S(2)}) collective-permute-start(bf16[1376,2048]{1,0:T(8,128)(2,1)} %add_convert_fusion.3), channel_id=1, source_target_pairs={{0,16},{8,24},{16,0},{24,8},{1,17},{9,25},{17,1},{25,9},{2,18},{10... | collective-permute-start | bytes 16908296 | tf_op jit(solution)/shard_map/ppermute | solution.py:40
  1495.1 133.3 %all-to-all-start.5 = ((bf16[8,2,512,128]{3,2,1,0:T(8,128)(2,1)}), bf16[8,2,512,128]{3,2,1,0:T(8,128)(2,1)}, u32[]{:S(2)}, u32[]{:S(2)}) async-start(bf16[8,2,512,128]{3,2,1,0:T(8,128)(2,1)} %bitcast.455), calls=%async_computation.5 | async-start | bytes 4194304 | tf_op jit(solution)/shard_map/all_to_all | solution.py:436
  1506.3 251.4 %collective-permute-start.30 = (bf16[512,2048]{1,0:T(8,128)(2,1)}, bf16[512,2048]{1,0:T(8,128)(2,1)}, u32[]{:S(2)}, u32[]{:S(2)}) collective-permute-start(bf16[512,2048]{1,0:T(8,128)(2,1)} %add_convert_fusion.8), channel_id=1, source_target_pairs={{0,16},{8,24},{16,0},{24,8},{1,17},{9,25},{17,1},{25,9},{2,18},{10... | collective-permute-start | bytes 6291464 | tf_op jit(solution)/shard_map/ppermute | solution.py:40
  1628.4 228.3 %all-to-all-start.6 = ((bf16[8,2,512,384]{3,2,1,0:T(8,128)(2,1)}), bf16[8,2,512,384]{3,2,1,0:T(8,128)(2,1)}, u32[]{:S(2)}, u32[]{:S(2)}) async-start(bf16[8,2,512,384]{3,2,1,0:T(8,128)(2,1)} %copy-done.1), calls=%async_computation.6 | async-start | bytes 12582912 | tf_op jit(solution)/shard_map/all_to_all | solution.py:440
  1763.0 89.4 %collective-permute-start.35 = (bf16[4,64,5504]{2,1,0:T(8,128)(2,1)}, bf16[4,64,5504]{2,1,0:T(8,128)(2,1)}, u32[]{:S(2)}, u32[]{:S(2)}) collective-permute-start(bf16[4,64,5504]{2,1,0:T(8,128)(2,1)} %dynamic-slice_bitcast_fusion.3), channel_id=1, source_target_pairs={{0,1},{1,0},{2,3},{3,2},{4,5},{5,4},{6,7},{7,6},{8,9},{9,8},{10,11... | collective-permute-start | bytes 8454152 | tf_op jit(solution)/shard_map/ppermute | solution.py:40
  1797.3 52.5 %collective-permute-start.38 = (bf16[4,64,2048]{2,1,0:T(8,128)(2,1)}, bf16[4,64,2048]{2,1,0:T(8,128)(2,1)}, u32[]{:S(2)}, u32[]{:S(2)}) collective-permute-start(bf16[4,64,2048]{2,1,0:T(8,128)(2,1)} %dynamic-slice_bitcast_fusion.4), channel_id=1, source_target_pairs={{0,1},{1,0},{2,3},{3,2},{4,5},{5,4},{6,7},{7,6},{8,9},{9,8},{10,11... | collective-permute-start | bytes 3145736 | tf_op jit(solution)/shard_map/ppermute | solution.py:40
  1809.8 203.7 %collective-permute-start.37 = (bf16[4,172,2048]{2,0,1:T(4,128)(2,1)}, bf16[4,172,2048]{2,0,1:T(4,128)(2,1)}, u32[]{:S(2)}, u32[]{:S(2)}) collective-permute-start(bf16[4,172,2048]{2,0,1:T(4,128)(2,1)} %copy.182), channel_id=1, source_target_pairs={{0,1},{1,0},{2,3},{3,2},{4,5},{5,4},{6,7},{7,6},{8,9},{9,8},{10,11... | collective-permute-start | bytes 8454152 | tf_op jit(solution)/shard_map/ppermute | solution.py:40
  1813.5 112.4 %collective-permute-start.36 = (bf16[256,5504]{1,0:T(8,128)(2,1)}, bf16[256,5504]{1,0:T(8,128)(2,1)}, u32[]{:S(2)}, u32[]{:S(2)}) collective-permute-start(bf16[256,5504]{1,0:T(8,128)(2,1)} %dynamic-slice_bitcast_fusion.2), channel_id=1, source_target_pairs={{0,16},{8,24},{16,0},{24,8},{1,17},{9,25},{17,1},{25,9},{2,18},{10... | collective-permute-start | bytes 8454152 | tf_op jit(solution)/shard_map/ppermute | solution.py:40
  1856.6 160.7 %all-to-all-start.7 = ((bf16[8,2,512,384]{3,2,1,0:T(8,128)(2,1)}), bf16[8,2,512,384]{3,2,1,0:T(8,128)(2,1)}, u32[]{:S(2)}, u32[]{:S(2)}) async-start(bf16[8,2,512,384]{3,2,1,0:T(8,128)(2,1)} %copy-done), calls=%async_computation.7 | async-start | bytes 12582912 | tf_op jit(solution)/shard_map/all_to_all | solution.py:440
  1896.6 21.8 collective-permute-start.31
  1900.4 21.6 collective-permute-start.32
  1921.4 36.5 %collective-permute-start.33 = (bf16[512,1536]{1,0:T(8,128)(2,1)}, bf16[512,1536]{1,0:T(8,128)(2,1)S(1)}, u32[]{:S(2)}, u32[]{:S(2)}) collective-permute-start(bf16[512,1536]{1,0:T(8,128)(2,1)} %add_convert_fusion.16), channel_id=1, source_target_pairs={{0,16},{8,24},{16,0},{24,8},{1,17},{9,25},{17,1},{25,9},{2,18},{10... | collective-permute-start | bytes 4718600 | tf_op jit(solution)/shard_map/ppermute | solution.py:40
  1923.8 85.1 %collective-permute-start.34 = (bf16[512,1536]{1,0:T(8,128)(2,1)S(1)}, bf16[512,1536]{1,0:T(8,128)(2,1)S(1)}, u32[]{:S(2)}, u32[]{:S(2)}) collective-permute-start(bf16[512,1536]{1,0:T(8,128)(2,1)S(1)} %add_convert_fusion.15), channel_id=1, source_target_pairs={{0,1},{1,0},{2,3},{3,2},{4,5},{5,4},{6,7},{7,6},{8,9},{9,8},{10,11... | collective-permute-start | bytes 4718600 | tf_op jit(solution)/shard_map/ppermute | solution.py:40
  2010.5 34.9 %collective-permute-start.40 = (bf16[256,1536]{1,0:T(8,128)(2,1)}, bf16[256,1536]{1,0:T(8,128)(2,1)}, u32[]{:S(2)}, u32[]{:S(2)}) collective-permute-start(bf16[256,1536]{1,0:T(8,128)(2,1)} %dynamic-slice_bitcast_fusion.8), channel_id=1, source_target_pairs={{0,16},{8,24},{16,0},{24,8},{1,17},{9,25},{17,1},{25,9},{2,18},{10... | collective-permute-start | bytes 2359304 | tf_op jit(solution)/shard_map/ppermute | solution.py:40
  2011.8 36.2 %collective-permute-start.39 = (bf16[4,64,1536]{2,1,0:T(8,128)(2,1)}, bf16[4,64,1536]{2,1,0:T(8,128)(2,1)}, u32[]{:S(2)}, u32[]{:S(2)}) collective-permute-start(bf16[4,64,1536]{2,1,0:T(8,128)(2,1)} %dynamic-slice_bitcast_fusion.9), channel_id=1, source_target_pairs={{0,1},{1,0},{2,3},{3,2},{4,5},{5,4},{6,7},{7,6},{8,9},{9,8},{10,11... | collective-permute-start | bytes 2359304 | tf_op jit(solution)/shard_map/ppermute | solution.py:40
  2057.7 26.6 %collective-permute-start.41 = (bf16[1024,1536]{1,0:T(8,128)(2,1)}, bf16[1024,1536]{1,0:T(8,128)(2,1)}, u32[]{:S(2)}, u32[]{:S(2)}) collective-permute-start(bf16[1024,1536]{1,0:T(8,128)(2,1)} %convolution_convert_fusion.4), channel_id=1, source_target_pairs={{0,8},{8,0},{16,24},{24,16},{1,9},{9,1},{17,25},{25,17},{2,10},{10... | collective-permute-start | bytes 9437192 | tf_op jit(solution)/shard_map/ppermute | solution.py:40
  2062.6 27.5 %collective-permute-start.42 = (bf16[1024,1536]{1,0:T(8,128)(2,1)}, bf16[1024,1536]{1,0:T(8,128)(2,1)}, u32[]{:S(2)}, u32[]{:S(2)}) collective-permute-start(bf16[1024,1536]{1,0:T(8,128)(2,1)} %convolution_convert_fusion.3), channel_id=1, source_target_pairs={{0,8},{8,0},{16,24},{24,16},{1,9},{9,1},{17,25},{25,17},{2,10},{10... | collective-permute-start | bytes 9437192 | tf_op jit(solution)/shard_map/ppermute | solution.py:40
  2095.9 43.4 %collective-permute-start.44 = (bf16[512,1536]{1,0:T(8,128)(2,1)}, bf16[512,1536]{1,0:T(8,128)(2,1)}, u32[]{:S(2)}, u32[]{:S(2)}) collective-permute-start(bf16[512,1536]{1,0:T(8,128)(2,1)} %add_convert_fusion.12), channel_id=1, source_target_pairs={{0,16},{8,24},{16,0},{24,8},{1,17},{9,25},{17,1},{25,9},{2,18},{10... | collective-permute-start | bytes 4718600 | tf_op jit(solution)/shard_map/ppermute | solution.py:40
  2097.6 49.2 %collective-permute-start.45 = (bf16[512,1536]{1,0:T(8,128)(2,1)}, bf16[512,1536]{1,0:T(8,128)(2,1)}, u32[]{:S(2)}, u32[]{:S(2)}) collective-permute-start(bf16[512,1536]{1,0:T(8,128)(2,1)} %add_convert_fusion.11), channel_id=1, source_target_pairs={{0,1},{1,0},{2,3},{3,2},{4,5},{5,4},{6,7},{7,6},{8,9},{9,8},{10,11... | collective-permute-start | bytes 4718600 | tf_op jit(solution)/shard_map/ppermute | solution.py:40
  2101.0 38.1 %collective-permute-start.51 = (f32[2,1024]{1,0:T(2,128)S(1)}, f32[2,1024]{1,0:T(2,128)S(1)}, u32[]{:S(2)}, u32[]{:S(2)}) collective-permute-start(f32[2,1024]{1,0:T(2,128)S(1)} %bitcast.515), channel_id=1, source_target_pairs={{0,16},{8,24},{16,0},{24,8},{1,17},{9,25},{17,1},{25,9},{2,18},{10... | collective-permute-start | bytes 24584 | tf_op jit(solution)/shard_map/ppermute | solution.py:40
  2119.9 125.2 %collective-permute-start.43 = (bf16[2,64,21632]{2,1,0:T(8,128)(2,1)}, bf16[2,64,21632]{2,1,0:T(8,128)(2,1)}, u32[]{:S(2)}, u32[]{:S(2)}) collective-permute-start(bf16[2,64,21632]{2,1,0:T(8,128)(2,1)} %dynamic-slice_bitcast_fusion), channel_id=1, source_target_pairs={{0,2},{1,3},{2,0},{3,1},{4,6},{5,7},{6,4},{7,5},{8,10},{9,11},{10,... | collective-permute-start | bytes 16613384 | tf_op jit(solution)/shard_map/ppermute | solution.py:40
  2139.2 12.4 collective-permute-start.52
  2150.2 93.0 %collective-permute-start.47 = (bf16[4,64,1536]{2,1,0:T(8,128)(2,1)}, bf16[4,64,1536]{2,1,0:T(8,128)(2,1)}, u32[]{:S(2)}, u32[]{:S(2)}) collective-permute-start(bf16[4,64,1536]{2,1,0:T(8,128)(2,1)} %dynamic-slice_bitcast_fusion.7), channel_id=1, source_target_pairs={{0,1},{1,0},{2,3},{3,2},{4,5},{5,4},{6,7},{7,6},{8,9},{9,8},{10,11... | collective-permute-start | bytes 2359304 | tf_op jit(solution)/shard_map/ppermute | solution.py:40
  2151.6 88.3 %collective-permute-start.53 = (f32[2,256]{1,0:T(2,128)S(1)}, f32[2,256]{1,0:T(2,128)S(1)}, u32[]{:S(2)}, u32[]{:S(2)}) collective-permute-start(f32[2,256]{1,0:T(2,128)S(1)} %bitcast.518), channel_id=1, source_target_pairs={{0,4},{1,5},{2,6},{3,7},{4,0},{5,1},{6,2},{7,3},{8,12},{9,13},{10,... | collective-permute-start | bytes 6152 | tf_op jit(solution)/shard_map/ppermute | solution.py:40
  2154.1 90.5 %collective-permute-start.48 = (bf16[256,1536]{1,0:T(8,128)(2,1)S(1)}, bf16[256,1536]{1,0:T(8,128)(2,1)S(1)}, u32[]{:S(2)}, u32[]{:S(2)}) collective-permute-start(bf16[256,1536]{1,0:T(8,128)(2,1)S(1)} %dynamic-slice_bitcast_fusion.6), channel_id=1, source_target_pairs={{0,16},{8,24},{16,0},{24,8},{1,17},{9,25},{17,1},{25,9},{2,18},{10... | collective-permute-start | bytes 2359304 | tf_op jit(solution)/shard_map/ppermute | solution.py:40
  2240.0 31.2 %collective-permute-start.54 = (f32[2,128]{1,0:T(2,128)S(1)}, f32[2,128]{1,0:T(2,128)S(1)}, u32[]{:S(2)}, u32[]{:S(2)}) collective-permute-start(f32[2,128]{1,0:T(2,128)S(1)} %fusion.200), channel_id=1, source_target_pairs={{0,2},{1,3},{2,0},{3,1},{4,6},{5,7},{6,4},{7,5},{8,10},{9,11},{10,... | collective-permute-start | bytes 3080 | tf_op jit(solution)/shard_map/ppermute | solution.py:40
  2245.1 25.4 %collective-permute-start.49 = (bf16[2,64,3072]{2,1,0:T(8,128)(2,1)S(1)}, bf16[2,64,3072]{2,1,0:T(8,128)(2,1)S(1)}, u32[]{:S(2)}, u32[]{:S(2)}) collective-permute-start(bf16[2,64,3072]{2,1,0:T(8,128)(2,1)S(1)} %dynamic-slice_bitcast_fusion.5), channel_id=1, source_target_pairs={{0,2},{1,3},{2,0},{3,1},{4,6},{5,7},{6,4},{7,5},{8,10},{9,11},{10,... | collective-permute-start | bytes 2359304 | tf_op jit(solution)/shard_map/ppermute | solution.py:40
  2252.5 137.7 %collective-permute-start.46 = (bf16[1,64,21632]{2,1,0:T(8,128)(2,1)}, bf16[1,64,21632]{2,1,0:T(8,128)(2,1)}, u32[]{:S(2)}, u32[]{:S(2)}) collective-permute-start(bf16[1,64,21632]{2,1,0:T(8,128)(2,1)} %constant_dynamic-slice_fusion.11), channel_id=1, source_target_pairs={{0,4},{1,5},{2,6},{3,7},{4,0},{5,1},{6,2},{7,3},{8,12},{9,13},{10,... | collective-permute-start | bytes 8306696 | tf_op jit(solution)/shard_map/ppermute | solution.py:40
  2270.7 118.8 %collective-permute-start.50 = (bf16[1,64,3072]{2,1,0:T(8,128)(2,1)S(1)}, bf16[1,64,3072]{2,1,0:T(8,128)(2,1)S(1)}, u32[]{:S(2)}, u32[]{:S(2)}) collective-permute-start(bf16[1,64,3072]{2,1,0:T(8,128)(2,1)S(1)} %constant_dynamic-slice_fusion.10), channel_id=1, source_target_pairs={{0,4},{1,5},{2,6},{3,7},{4,0},{5,1},{6,2},{7,3},{8,12},{9,13},{10,... | collective-permute-start | bytes 1179656 | tf_op jit(solution)/shard_map/ppermute | solution.py:40
  2271.3 3.6 collective-permute-start.55
  (79 other events, 1319.1 us)
Sparse Core Ops, SparseCore 0:
  12.5 240.0 all-gather.1

commit v3 on v2

--- a/solution.py
+++ b/solution.py
@@ -174,9 +174,9 @@
 
 
 class Reduce:
-    def __init__(self, pieces, cols_side, seq_first, transposed=False):
-        self.pieces, self.cols_side, self.seq_first, self.transposed = pieces, cols_side, seq_first, transposed
-        self.half = pieces.shape[1 if transposed else 2] // 2
+    def __init__(self, pieces, cols_side, seq_first, product=None):
+        self.pieces, self.cols_side, self.seq_first, self.product = pieces, cols_side, seq_first, product
+        self.half = product.shape[0] // 4 if pieces is None else pieces.shape[2] // 2
         self.own = self.half * 4 // (lax.axis_size("dp") * lax.axis_size("seq"))
         self.core, self.height = digits_of("dp")[-1], digits_of("dp")[0]
         self.fast, self.far = digits_of("seq")[-1], digits_of("seq")[:-1]
@@ -184,11 +184,12 @@
         self.c, self.mine = digit_index(self.core), digit_index(self.first)
 
     def term(self, core_index, index, others):
+        if self.pieces is None:
+            parts = pick(after(self.product, *others).reshape(2, 2, self.half, -1), core_index, 1)
+            return (parts.reshape(2 * self.half, -1) if index is None else pick(parts, index, 0)).astype(f32)
         side = pick(after(self.pieces, *others), core_index, 0)
         if index is not None:
-            side = lax.dynamic_slice_in_dim(side, index * self.half, self.half, 0 if self.transposed else 1)
-        if self.transposed:
-            return jnp.dot(side, self.cols_side, preferred_element_type=f32)
+            side = lax.dynamic_slice_in_dim(side, index * self.half, self.half, 1)
         return tn(side, self.cols_side)
 
     def cross(self, *others):
@@ -429,18 +430,19 @@
 
 def to_heads(rows, heads):
     seq = lax.axis_size("seq")
-    parts = rows.shape[1] // (heads * HD)
-    count = rows.shape[0] // MB
-    split = rows.reshape(MB, count, parts, heads, HD).transpose(3, 0, 1, 2, 4)
-    split = split.reshape(seq, heads * MB // seq, count, parts * HD)
+    count, width = rows.shape[0] // MB, rows.shape[1] // heads
+    split = rows.reshape(MB, count, heads, width).transpose(2, 0, 1, 3)
+    split = split.reshape(seq, heads * MB // seq, count, width)
     return lax.all_to_all(split, "seq", 0, 0, tiled=True)
 
 
-def to_rows(whole, heads):
-    got = lax.all_to_all(whole, "seq", 0, 0, tiled=True)
-    count, parts = got.shape[2], got.shape[3] // HD
-    got = got.reshape(heads, MB, count, parts, HD).transpose(1, 2, 3, 0, 4)
-    return got.reshape(MB * count, parts * heads * HD)
+def to_rows(whole):
+    return lax.all_to_all(whole, "seq", 0, 0, tiled=True)
+
+
+def rows_of(got, heads):
+    count, width = got.shape[2], got.shape[3]
+    return got.reshape(heads, MB, count, width).transpose(1, 2, 0, 3).reshape(MB * count, heads * width)
 
 
 def norm_scale(values):
@@ -478,90 +480,110 @@
         low.append(pair_low)
     bounds, low = jnp.stack(bounds), jnp.stack(low)
 
-    order_qkv = w_qkv.reshape(-1, 3, groups, width).transpose(0, 2, 1, 3).reshape(w_qkv.shape)
+    order_qkv = w_qkv.reshape(-1, 3, groups, heads, HD).transpose(0, 2, 3, 1, 4).reshape(w_qkv.shape)
     all_qkv = gather(order_qkv)
     full_qkv = [all_qkv[:, g * 3 * width : (g + 1) * 3 * width] for g in range(groups)]
-    gains = gather_small(jnp.stack([gain_attn, gain_mlp])).astype(f32)
+    all_gains = gather_small(jnp.stack([gain_attn, gain_mlp]))
+    gains = all_gains.astype(f32)
     gain_a, gain_m = gains[0], gains[1]
     scale_a = norm_scale(x)
     h_attn = (x * scale_a * gain_a).astype(bf16)
-    gathers = [
-        Gather([w_gate_up[:, FF:], w_down.reshape(w_qkv.shape[0], -1)], True),
-        Gather([w_gate_up[:, :FF], w_out], False),
-    ]
-    values = lambda: [v for w in gathers for v in w.values()]
-
-    def advance(step, *others):
-        ready = values()
-        for w in gathers:
-            w.wait(*others, *ready)
-            step(w)
-
-    for n in range(len(gathers[0].far)):
-        advance(lambda w: w.far_step(n))
-    h_attn = after(h_attn, *values())
-    advance(lambda w: w.near_step(0))
+    soon = Gather([w_gate_up[:, :FF], w_out], False)
+    later = Gather([w_gate_up[:, FF:], w_down.reshape(w_qkv.shape[0], -1)], True)
+    far = len(soon.far)
+
+    soon.wait(all_gains)
+    soon.far_step(0)
+    for n in range(1, far):
+        later.wait(*soon.values())
+        soon.far_step(n)
+        later.far_step(n - 1)
+    ready = soon.values() + later.values()
+    h_attn = after(h_attn, *ready)
+    soon.wait(*ready)
+    soon.near_step(0)
+    later.wait(*ready)
+    later.far_step(far - 1)
     arrived = []
     step_in = h_attn
     for g in range(groups):
         qkv_rows = jnp.dot(step_in, full_qkv[g], preferred_element_type=f32).astype(bf16)
         arrived.append(to_heads(qkv_rows, heads))
-        step_in = after(h_attn, qkv_rows, *values())
-    advance(lambda w: w.near_step(1))
+        ready = soon.values() + later.values()
+        step_in = after(h_attn, qkv_rows, *ready)
+    later.wait(*ready)
+    later.near_step(0)
+    soon.wait(*ready)
+    soon.near_step(1)
     saved, attended = [], []
     last = None
     for g in range(groups):
         qkv = arrived[g] if last is None else after(arrived[g], last)
         last, lse = attend(qkv, bounds, low)
         saved.append((qkv, last, lse))
-        attended.append(to_rows(last, heads))
-    advance(lambda w: w.near_step(2), last)
-    full_up, full_down = gathers[0].finish()
-    full_gate, full_out = gathers[1].finish()
+        attended.append(rows_of(to_rows(last), heads))
+        if g == 0:
+            later.wait(last)
+            later.near_step(1)
+    soon.wait(last)
+    soon.near_step(2)
+    full_gate, full_out = soon.finish()
     attended = jnp.concatenate(attended, axis=1)
 
     mid = x + jnp.dot(attended, full_out, preferred_element_type=f32)
     scale_m = norm_scale(mid)
     h_mlp = (mid * scale_m * gain_m).astype(bf16)
+    later.wait(h_mlp)
+    later.near_step(2)
     gate = jnp.dot(h_mlp, full_gate, preferred_element_type=f32)
+    full_up, full_down = later.finish()
+    full_down = full_down.reshape(FF, D)
     up = jnp.dot(h_mlp, full_up, preferred_element_type=f32)
     sig = jax.nn.sigmoid(gate)
     act = (gate * sig * up).astype(bf16)
-    full_down = after(full_down, act).reshape(FF, D)
-    grad_act = nt(cot, full_down)
+
+    down = Reduce(None, cot, False, product=tn(act, cot).astype(bf16))
+    mark = (down.cross(),)
+    grad_act = nt(after(cot, *mark), full_down)
     grad_gate = (grad_act * up * sig * (1.0 + gate * (1.0 - sig))).astype(bf16)
     grad_up = (grad_act * (gate * sig)).astype(bf16)
-    grad_h_mlp = nt(grad_gate, full_gate) + nt(grad_up, full_up)
+    mark = (down.send(grad_gate, grad_up),)
+    gate_r = Reduce(pieces_of(h_mlp, False), grad_gate, False)
+    up_r = Reduce(pieces_of(h_mlp, True), grad_up, True)
+    mark = (up_r.cross(*mark),)
+    mark = (gate_r.cross(*mark),)
+    half_grad = nt(after(grad_gate, *mark), full_gate)
+    mark = (up_r.send(half_grad),)
+    grad_h_mlp = half_grad + nt(after(grad_up, *mark), full_up)
     grad_mid_norm, gain_m_grad = norm_backward(grad_h_mlp, mid, scale_m, gain_m)
     grad_mid = cot.astype(f32) + grad_mid_norm
     grad_branch = grad_mid.astype(bf16)
     grad_rows = [nt(grad_branch, full_out[g * width : (g + 1) * width]).astype(bf16) for g in range(groups)]
     grads = [to_heads(r, heads) for r in grad_rows]
 
-    act_pieces = act.T.reshape(lax.axis_size("dp") // 2, 2, -1, MB * rows).transpose(1, 0, 2, 3)
-    down = Reduce(act_pieces.reshape(2, FF // 2, MB * rows), cot, False, transposed=True)
-    gate_r = Reduce(pieces_of(h_mlp, False), grad_gate, False)
-    up_r = Reduce(pieces_of(h_mlp, True), grad_up, True)
     out_r = Reduce(pieces_of(attended, False), grad_branch, False)
-    early = [gate_r, up_r, down, out_r]
-    mark = tuple(grad_rows)
-    for r in early:
-        mark = (r.cross(*mark),)
-    for r in early:
-        mark = (r.send(*mark),)
+    early = [down, up_r, gate_r, out_r]
+    mark = (gate_r.send(*grad_rows),)
+    mark = (out_r.cross(*mark),)
+    mark = (down.keep(*mark),)
+    down.second()
     grad_heads = []
     for g in range(groups):
         qkv, mixed, lse = saved[g]
         back = attend_back(after(qkv, *mark), grads[g], mixed, lse, bounds, low)
         grad_heads.append(back)
         mark = (back,)
-    grad_qkv = [to_rows(back, heads) for back in grad_heads]
-    for r in early:
+        if g == 0:
+            mark = (up_r.keep(*mark),)
+            up_r.second()
+            mark = (out_r.send(*mark),)
+    arrived = [to_rows(back) for back in grad_heads]
+    grad_qkv = []
+    for r in (gate_r, out_r):
         mark = (r.keep(*mark),)
+        r.second()
     layer_out = (mid + jnp.dot(after(act, *mark), full_down, preferred_element_type=f32)).astype(bf16)
     mark = (layer_out,)
-    for r in early:
-        r.second()
 
     h_sides = [pieces_of(h_attn, False), pieces_of(h_attn, True)]
     half = 3 * width // 2
@@ -569,44 +591,47 @@
     grad_h_attn = 0.0
     for g in range(groups):
         final = g == groups - 1
+        if final:
+            first = Finish(early, *mark)
+            mark = mark + (first.step(0),)
+        grad_qkv.append(rows_of(after(arrived[g], *mark), heads))
         pair = [Reduce(h_sides[0], grad_qkv[g][:, :half], False), Reduce(h_sides[1], grad_qkv[g][:, half:], True)]
         for r in pair:
             mark = (r.cross(*mark),)
+        if final:
+            for n in range(1, far):
+                first.step(n)
         part = nt(after(grad_qkv[g], *mark), full_qkv[g])
         grad_h_attn = grad_h_attn + part
         mark = (part,)
         for r in pair:
             mark = (r.send(*mark),)
         if final:
-            first = Finish(early + late, *mark)
-            first.step(0)
             grad_tok_norm, gain_a_grad = norm_backward(after(grad_h_attn, *mark), x, scale_a, gain_a)
             grad_tokens = grad_mid + grad_tok_norm
-            mark = (grad_tokens,)
-        late += pair
+            mark = (grad_tokens, first.total)
         for r in pair:
             mark = (r.keep(*mark),)
         for r in pair:
             r.second(*mark)
+        late += pair
         if not final:
             mark = mark + tuple(r.total for r in early + pair)
     gain_grads = scatter_small(jnp.stack([gain_a_grad, gain_m_grad]))
-    second = Finish(pair)
-    far = len(first.far)
+    second = Finish(late)
     for n in range(far):
-        if n:
-            first.step(n, *mark)
         second.step(n)
-    results = first.results() + second.results()
-    gate_grad, up_grad, down_grad, out_grad = results[:4]
+    down_grad, up_grad, gate_grad, out_grad = first.results()
+    terms = second.results()
     qkv_grads = [
-        jnp.concatenate(results[4 + 2 * g : 6 + 2 * g], axis=1).reshape(-1, 3, 1, width) for g in range(groups)
+        jnp.concatenate(terms[2 * g : 2 * g + 2], axis=1).reshape(-1, 1, heads, 3, HD) for g in range(groups)
     ]
+    qkv_grad = jnp.concatenate(qkv_grads, axis=1).transpose(0, 3, 1, 2, 4)
 
     return (
         layer_out.reshape(MB, 1, rows, D),
         grad_tokens.reshape(MB, 1, rows, D),
-        jnp.concatenate(qkv_grads, axis=2).reshape(-1, 3 * D),
+        qkv_grad.reshape(-1, 3 * D),
         out_grad,
         jnp.concatenate([gate_grad, up_grad], axis=1),
         down_grad,

time: 2430 us -> 2560 us (1.053)
  waiting for transfers between devices: 1060 us -> 1290 us
  local copies, waits for them, and re-layouts: 330 us -> 221 us
    ppermute x56, waiting for transfers between devices: 871 us -> 1130 us  [swap(): lax.ppermute(block, axis, [(i, i ^ stride) for i in range(lax.axis_size(a...]
    all_to_all x4, waiting for transfers between devices: 141 us -> 81.7 us  [to_heads(): return lax.all_to_all(split, 'seq', 0, 0, tiled=True)]
    reshape x15 -> x9, local copies, waits for them, and re-layouts: 101 us -> 45.4 us  [the longest x1 31.3 us: shards(): full_down = full_down.reshape(FF, D)]
    dot_general x3 -> x0, matrix products: 32.6 us -> none  [term(): return jnp.dot(side, self.cols_side, preferred_element_type=f32)]
    all_gather x1, waiting for transfers between devices: 0.01 us -> 25.7 us  [shards(): gather = lambda w: lax.all_gather(w, ('dp', 'seq'), axis=0, tiled=True)]
    dot_general x21 -> x22, matrix products: 158 us -> 180 us  [tn(): lax.dot_general(a, b, (((0,), (0,)), ((), ())), preferred_element_type=f32)]
  transfers between devices with their start and end apart: 65 -> 65, of which waited for: 19 -> 28; matrix products, arithmetic and copies ran while one was open for 26% -> 27% of each run, Pallas kernels for 10% -> 9%
where the time goes in v3:
time: 2560 us; the launch traced here: 2550 us
  waiting for transfers between devices  1290 us (50%)
  matrix products  491 us (19%)
  Pallas kernels  269 us (11%)
  local copies, waits for them, and re-layouts  221 us (9%)
  other arithmetic  144 us (6%)
  starting transfers between devices  118 us (5%)
    ppermute x56, waiting for transfers between devices, swap(): lax.ppermute(block, axis, [(i, i ^ stride) for i in range(lax.axis_size(a...  1130 us
    dot_general x22, matrix products, tn(): lax.dot_general(a, b, (((0,), (0,)), ((), ())), preferred_element_type=f32)  180 us
    dot_general x7, matrix products, nt(): return jnp.einsum('re,de->rd', a, b, preferred_element_type=f32)  163 us
    pallas_call x2, Pallas kernels, attend_back(): pl.pallas_call(backward_kernel, grid_spec=pltpu.PrefetchScalarGridSpec(nu...  126 us
    pallas_call x2, Pallas kernels, attend(): pl.pallas_call(forward_kernel, grid_spec=pltpu.PrefetchScalarGridSpec(num...  93.3 us
    all_to_all x4, waiting for transfers between devices, to_heads(): return lax.all_to_all(split, 'seq', 0, 0, tiled=True)  81.7 us
    ppermute x56, starting transfers between devices, swap(): lax.ppermute(block, axis, [(i, i ^ stride) for i in range(lax.axis_size(a...  69.2 us
    all_to_all x4, waiting for transfers between devices, to_rows(): return lax.all_to_all(whole, 'seq', 0, 0, tiled=True)  52.5 us
  transfers between devices with their start and end apart: 65, of which 28 were waited for; matrix products, arithmetic and copies ran while one was open for 27% of the time, Pallas kernels for 9%

profile of v3, /device:TPU:0, one launch (start us, length us, event | category | flops | bytes accessed | tf_op | source)
XLA Modules:
  0.0 2546.1 jit_solution(5085754380210124116)
XLA Ops:
  22.6 24.7 collective-permute-done.1
  51.2 36.8 %collective-permute-done.2 = bf16[2,256]{1,0:T(2,128)(2,1)S(1)} collective-permute-done((bf16[2,256]{1,0:T(2,128)(2,1)S(1)}, bf16[2,256]{1,0:T(2,128)(2,1)S(1)}, u32[]{:S(2)}, u32[]{:S(2)}) %collective-permute-start.2) | collective-permute-done | bytes 1056 | tf_op jit(solution)/shard_map/ppermute | solution.py:40
  101.9 9.6 collective-permute-start.6
  112.9 79.7 %collective-permute-done.7 = bf16[64,11008]{1,0:T(8,128)(2,1)S(1)} collective-permute-done((bf16[64,11008]{1,0:T(8,128)(2,1)}, bf16[64,11008]{1,0:T(8,128)(2,1)S(1)}, u32[]{:S(2)}, u32[]{:S(2)}) %collective-permute-start.7) | collective-permute-done | bytes 1409056 | tf_op jit(solution)/shard_map/ppermute | solution.py:40
  192.7 35.1 %collective-permute-done.6 = bf16[128,7552]{1,0:T(8,128)(2,1)S(1)} collective-permute-done((bf16[128,7552]{1,0:T(8,128)(2,1)S(1)}, bf16[128,7552]{1,0:T(8,128)(2,1)S(1)}, u32[]{:S(2)}, u32[]{:S(2)}) %collective-permute-start.6) | collective-permute-done | bytes 1933344 | tf_op jit(solution)/shard_map/ppermute | solution.py:40
  229.2 25.7 %all-gather.2.cloned.1.call-done = bf16[2048,6144]{1,0:T(8,128)(2,1)} async-done(((bf16[64,6144]{1,0:T(8,128)(2,1)}), bf16[2048,6144]{1,0:T(8,128)(2,1)}) %all-gather.2.cloned.1.call-update) | async-done | bytes 25165840 | tf_op jit(solution)/shard_map/all_gather | solution.py:467
  254.9 17.0 fusion.25
  277.2 9.5 all-to-all-start
  291.8 159.2 %collective-permute-done.9 = bf16[128,11008]{1,0:T(8,128)(2,1)S(1)} collective-permute-done((bf16[128,11008]{1,0:T(8,128)(2,1)S(1)}, bf16[128,11008]{1,0:T(8,128)(2,1)S(1)}, u32[]{:S(2)}, u32[]{:S(2)}) %collective-permute-start.9) | collective-permute-done | bytes 2818080 | tf_op jit(solution)/shard_map/ppermute | solution.py:40
  452.7 15.8 fusion.28
  488.3 46.7 %attend.2 = (bf16[8,2,512,128]{3,2,1,0:T(8,128)(2,1)}, f32[2,1,4096]{2,1,0:T(1,128)S(1)}) custom-call(s32[2,4,8]{2,1,0:T(4,128)S(1)} %pad_add_fusion.1.bounds, bf16[8,2,512,384]{3,2,1,0:T(8,128)(2,1)} %all-to-all-done.q_ref.k_ref.v_ref, bf16[8,2,512,384]{3,2,1,0:T(8,128)(2,1)} %all-to-all-done.q_ref.k_ref.v_ref, ...), custom_call_target="tpu_custom_call" | custom-call | flops 15032385536 | bytes 8388608 | tf_op jit(solution)/shard_map/attend/pallas_call | solution.py:304
  535.0 81.7 %all-to-all-done.2.q_ref.k_ref.v_ref = bf16[8,2,512,384]{3,2,1,0:T(8,128)(2,1)} async-done(((bf16[8,2,512,384]{3,2,1,0:T(8,128)(2,1)}), bf16[8,2,512,384]{3,2,1,0:T(8,128)(2,1)}, u32[]{:S(2)}, u32[]{:S(2)}) %all-to-all-start.2) | async-done | bytes 6291488 | tf_op jit(solution)/shard_map/all_to_all | solution.py:436
  616.7 46.7 %attend.3 = (bf16[8,2,512,128]{3,2,1,0:T(8,128)(2,1)}, f32[2,1,4096]{2,1,0:T(1,128)S(1)}) custom-call(s32[2,4,8]{2,1,0:T(4,128)S(1)} %pad_add_fusion.1.bounds, bf16[8,2,512,384]{3,2,1,0:T(8,128)(2,1)} %all-to-all-done.2.q_ref.k_ref.v_ref, bf16[8,2,512,384]{3,2,1,0:T(8,128)(2,1)} %all-to-all-done.2.q_ref.k_ref.v_ref, ...), custom_call_target="tpu_custom_call" | custom-call | flops 15032385536 | bytes 8388608 | tf_op jit(solution)/shard_map/attend/pallas_call | solution.py:304
  667.3 186.1 %collective-permute-done.10.refs_2_ = bf16[256,7552]{1,0:T(8,128)(2,1)} collective-permute-done((bf16[256,7552]{1,0:T(8,128)(2,1)}, bf16[256,7552]{1,0:T(8,128)(2,1)}, u32[]{:S(2)}, u32[]{:S(2)}) %collective-permute-start.10) | collective-permute-done | bytes 3866656 | tf_op jit(solution)/shard_map/ppermute | solution.py:40
  867.4 42.8 %all-to-all-done.1 = bf16[8,2,512,128]{3,2,1,0:T(8,128)(2,1)} async-done(((bf16[8,2,512,128]{3,2,1,0:T(8,128)(2,1)}), bf16[8,2,512,128]{3,2,1,0:T(8,128)(2,1)}, u32[]{:S(2)}, u32[]{:S(2)}) %all-to-all-start.1) | async-done | bytes 2097184 | tf_op jit(solution)/shard_map/all_to_all | solution.py:440
  914.4 19.4 place.2
  937.2 11.5 multiply_reduce_fusion.2
  953.8 32.9 %collective-permute-done.18.refs_3_ = bf16[256,11008]{1,0:T(8,128)(2,1)} collective-permute-done((bf16[256,11008]{1,0:T(8,128)(2,1)}, bf16[256,11008]{1,0:T(8,128)(2,1)}, u32[]{:S(2)}, u32[]{:S(2)}) %collective-permute-start.18) | collective-permute-done | bytes 5636128 | tf_op jit(solution)/shard_map/ppermute | solution.py:40
  986.8 119.2 %collective-permute-done.17.refs_2_ = bf16[256,11008]{1,0:T(8,128)(2,1)} collective-permute-done((bf16[256,11008]{1,0:T(8,128)(2,1)}, bf16[256,11008]{1,0:T(8,128)(2,1)}, u32[]{:S(2)}, u32[]{:S(2)}) %collective-permute-start.17) | collective-permute-done | bytes 5636128 | tf_op jit(solution)/shard_map/ppermute | solution.py:40
  1106.0 33.9 %fusion.191 = f32[1024,5504]{1,0:T(8,128)} fusion(bf16[1024,2048]{1,0:T(8,128)(2,1)} %multiply_convert_fusion.3, bf16[2048,5504]{1,0:T(8,128)(2,1)} %get-tuple-element.94), kind=kOutput, calls=%fused_computation.347 | convolution fusion | flops 23085449216 | bytes 49283072 | tf_op jit(solution)/shard_map/dot_general | solution.py:538
  1140.0 30.4 %place.3 = (bf16[2048,5504]{1,0:T(8,128)(2,1)}, bf16[2048,5504]{1,0:T(8,128)(2,1)}) custom-call(s32[32]{0:T(128)S(1)} %xor_multiply_fusion.target, bf16[256,11008]{1,0:T(8,128)(2,1)} %constant_dynamic-update-slice_fusion.7.refs_0_, bf16[256,11008]{1,0:T(8,128)(2,1)} %collective-permute-done.16.refs_1_, bf16[256,11008]{1,0:T(8,128)(2,1)} %collective-permute-done.17.refs_2_, ...), custom_call_target="tpu_custom_call" | custom-call | bytes 90177536 | tf_op jit(solution)/shard_map/place/pallas_call | solution.py:139
  1170.3 38.1 %multiply_convert_fusion.2 = (bf16[1024,5504]{1,0:T(8,128)(2,1)}, f32[1024,5504]{1,0:T(8,128)}) fusion(f32[1024,5504]{1,0:T(8,128)} %fusion.191, bf16[1024,2048]{1,0:T(8,128)(2,1)} %multiply_convert_fusion.3, bf16[2048,5504]{1,0:T(8,128)(2,1)} %get-tuple-element.102), kind=kOutput, calls=%fused_computation.3 | convolution fusion | flops 23119265792 | bytes 83099648 | tf_op jit(solution)/shard_map/dot_general | solution.py:541
  1208.4 31.3 %convolution_convert_fusion = bf16[5504,2048]{1,0:T(8,128)(2,1)} fusion(bf16[1024,5504]{1,0:T(8,128)(2,1)} %get-tuple-element.122, bf16[1024,2048]{1,0:T(8,128)(2,1)} %bitcast.407), kind=kOutput, calls=%fused_computation | convolution fusion | flops 23096721408 | bytes 38010880 | tf_op jit(solution)/shard_map/dot_general | solution.py:159
  1239.8 9.9 constant_dynamic-slice_fusion.12
  1261.5 31.3 %reshape.393 = bf16[5504,2048]{1,0:T(8,128)(2,1)} reshape(bf16[2048,5504]{1,0:T(8,128)(2,1)} %get-tuple-element.104) | data formatting | bytes 45088768 | tf_op jit(solution)/shard_map/reshape | solution.py:540
  1292.8 41.9 %multiply_convert_fusion = (bf16[1024,5504]{1,0:T(8,128)(2,1)}, bf16[1024,5504]{1,0:T(8,128)(2,1)}) fusion(f32[1024,5504]{1,0:T(8,128)} %fusion.191, f32[1024,5504]{1,0:T(8,128)} %get-tuple-element.260, bf16[1024,2048]{1,0:T(8,128)(2,1)} %bitcast.408, bf16[5504,2048]{1,0:T(8,128)(2,1)} %reshape.393), kind=kOutput, calls=%fused_computation.1 | convolution fusion | flops 23158718464 | bytes 94371840 | tf_op jit(solution)/shard_map/re,de->rd/dot_general | solution.py:461
  1334.8 10.1 fusion.3
  1344.9 18.7 convolution_convert_fusion.2
  1370.2 9.9 maximum_bitcast_fusion
  1380.0 11.2 copy.131
  1391.2 7.8 reshape.386
  1399.0 11.2 copy.132
  1410.2 19.6 convolution_convert_fusion.1
  1431.5 31.8 %fusion.192 = f32[1024,2048]{1,0:T(8,128)} fusion(bf16[1024,5504]{1,0:T(8,128)(2,1)} %get-tuple-element.108, bf16[2048,5504]{1,0:T(8,128)(2,1)} %get-tuple-element.94), kind=kOutput, calls=%fused_computation.348 | convolution fusion | flops 23085449216 | bytes 42205184 | tf_op jit(solution)/shard_map/re,de->rd/dot_general | solution.py:461
  1463.3 13.1 add_convert_fusion.3
  1476.4 35.7 %multiply_reduce_fusion = (f32[2048]{0:T(1024)}, f32[1024]{0:T(1024)S(1)}, f32[1024,2048]{1,0:T(8,128)}) fusion(f32[1024,2048]{1,0:T(8,128)} %copy-done.7, f32[1024]{0:T(1024)S(1)} %copy-done.47, f32[2048]{0:T(1024)S(1)} %bitcast.479, f32[1024,2048]{1,0:T(8,128)} %fusion.192, bf16[1024,5504]{1,0:T(8,128)(2,1)} %get-tuple-element.110, ...), kind=kOutput, calls=%fused_computation.42 | convolution fusion | flops 23100125184 | bytes 59006976 | tf_op jit(solution)/shard_map/re,de->rd/dot_general | solution.py:461
  1512.2 8.4 fusion.186
  1520.6 9.5 fusion.82
  1534.9 13.3 add_convert_fusion.2
  1562.6 13.0 fusion.2
  1589.3 7.8 reshape.402
  1603.6 11.2 copy.140
  1623.0 33.0 %collective-permute-done.35 = bf16[4,172,2048]{2,0,1:T(4,128)(2,1)} collective-permute-done((bf16[4,172,2048]{2,0,1:T(4,128)(2,1)}, bf16[4,172,2048]{2,0,1:T(4,128)(2,1)}, u32[]{:S(2)}, u32[]{:S(2)}) %collective-permute-start.35) | collective-permute-done | bytes 2818080 | tf_op jit(solution)/shard_map/ppermute | solution.py:40
  1661.3 7.8 all-to-all-start.5
  1669.2 62.8 %attend_back.2 = bf16[8,2,512,384]{3,2,1,0:T(8,128)(2,1)S(1)} custom-call(s32[2,4,8]{2,1,0:T(4,128)S(1)} %copy-done.5, bf16[8,2,512,384]{3,2,1,0:T(8,128)(2,1)} %all-to-all-done.q_ref.k_ref.v_ref, bf16[8,2,512,384]{3,2,1,0:T(8,128)(2,1)} %all-to-all-done.q_ref.k_ref.v_ref, bf16[8,2,512,384]{3,2,1,0:T(8,128)(2,1)} %all-to-all-done.q_ref.k_ref.v_ref, ...), custom_call_target="tpu_custom_call" | custom-call | flops 37580963840 | bytes 16777216 | tf_op jit(solution)/shard_map/attend_back/pallas_call | solution.py:385
  1732.0 11.7 fusion.121
  1743.7 49.9 %collective-permute-done.27 = bf16[512,5504]{1,0:T(8,128)(2,1)} collective-permute-done((bf16[512,5504]{1,0:T(8,128)(2,1)}, bf16[512,5504]{1,0:T(8,128)(2,1)}, u32[]{:S(2)}, u32[]{:S(2)}) %collective-permute-start.27) | collective-permute-done | bytes 5636128 | tf_op jit(solution)/shard_map/ppermute | solution.py:40
  1793.6 8.1 add_convert_fusion.1
  1815.6 63.4 %attend_back.3 = bf16[8,2,512,384]{3,2,1,0:T(8,128)(2,1)S(1)} custom-call(s32[2,4,8]{2,1,0:T(4,128)S(1)} %copy-done.5, bf16[8,2,512,384]{3,2,1,0:T(8,128)(2,1)} %all-to-all-done.2.q_ref.k_ref.v_ref, bf16[8,2,512,384]{3,2,1,0:T(8,128)(2,1)} %all-to-all-done.2.q_ref.k_ref.v_ref, bf16[8,2,512,384]{3,2,1,0:T(8,128)(2,1)} %all-to-all-done.2.q_ref.k_ref.v_ref, ...), custom_call_target="tpu_custom_call" | custom-call | flops 37580963840 | bytes 16777216 | tf_op jit(solution)/shard_map/attend_back/pallas_call | solution.py:385
  1879.0 11.7 fusion.115
  1910.9 32.1 %add_convert_fusion.4 = bf16[1024,2048]{1,0:T(8,128)(2,1)} fusion(f32[1024,2048]{1,0:T(8,128)S(1)} %bitcast.375, bf16[1024,5504]{1,0:T(8,128)(2,1)} %get-tuple-element.122, bf16[5504,2048]{1,0:T(8,128)(2,1)} %reshape.393), kind=kOutput, calls=%fused_computation.43 | convolution fusion | flops 23089643520 | bytes 46399488 | tf_op jit(solution)/shard_map/dot_general | solution.py:585
  1974.7 17.4 fusion.8
  2000.1 12.2 collective-permute-done.37
  2018.3 13.3 collective-permute-done.33
  2034.1 62.5 %collective-permute-done.34 = bf16[512,1536]{1,0:T(8,128)(2,1)S(1)} collective-permute-done((bf16[512,1536]{1,0:T(8,128)(2,1)S(1)}, bf16[512,1536]{1,0:T(8,128)(2,1)S(1)}, u32[]{:S(2)}, u32[]{:S(2)}) %collective-permute-start.34) | collective-permute-done | bytes 1572896 | tf_op jit(solution)/shard_map/ppermute | solution.py:40
  2134.3 9.2 collective-permute-start.41
  2143.6 101.0 %collective-permute-done.41 = bf16[2,64,18560]{2,1,0:T(8,128)(2,1)} collective-permute-done((bf16[2,64,18560]{2,1,0:T(8,128)(2,1)}, bf16[2,64,18560]{2,1,0:T(8,128)(2,1)}, u32[]{:S(2)}, u32[]{:S(2)}) %collective-permute-start.41) | collective-permute-done | bytes 4751392 | tf_op jit(solution)/shard_map/ppermute | solution.py:40
  2270.7 21.4 fusion.190
  2292.2 84.0 %collective-permute-done.44 = bf16[1,64,18560]{2,1,0:T(8,128)(2,1)} collective-permute-done((bf16[1,64,18560]{2,1,0:T(8,128)(2,1)S(1)}, bf16[1,64,18560]{2,1,0:T(8,128)(2,1)}, u32[]{:S(2)}, u32[]{:S(2)}) %collective-permute-start.44) | collective-permute-done | bytes 2375712 | tf_op jit(solution)/shard_map/ppermute | solution.py:40
  2396.7 17.0 fusion.21
  2413.8 8.3 collective-permute-done.51
  2438.7 17.0 collective-permute-done.47
  2462.0 32.3 %collective-permute-done.54 = f32[2,128]{1,0:T(2,128)S(1)} collective-permute-done((f32[2,128]{1,0:T(2,128)S(1)}, f32[2,128]{1,0:T(2,128)S(1)}, u32[]{:S(2)}, u32[]{:S(2)}) %collective-permute-start.54) | collective-permute-done | bytes 1056 | tf_op jit(solution)/shard_map/ppermute | solution.py:40
  2506.1 27.1 %collective-permute-done.50 = bf16[1,64,6144]{2,1,0:T(8,128)(2,1)S(1)} collective-permute-done((bf16[1,64,6144]{2,1,0:T(8,128)(2,1)S(1)}, bf16[1,64,6144]{2,1,0:T(8,128)(2,1)S(1)}, u32[]{:S(2)}, u32[]{:S(2)}) %collective-permute-start.50) | collective-permute-done | bytes 786464 | tf_op jit(solution)/shard_map/ppermute | solution.py:40
  (425 shorter events, 377.7 us)
Async XLA Ops:
  7.2 247.7 %all-gather.2.cloned.1.call-start = ((), (), s32[]{:S(2)}) async-start(), calls=%async_computation.8 | async-start | bytes 25952256 | tf_op jit(solution)/shard_map/all_gather | solution.py:467
  10.6 10.3 collective-permute-start
  15.1 79.8 %collective-permute-start.5 = (bf16[64,7552]{1,0:T(8,128)(2,1)S(1)}, bf16[64,7552]{1,0:T(8,128)(2,1)S(1)}, u32[]{:S(2)}, u32[]{:S(2)}) collective-permute-start(bf16[64,7552]{1,0:T(8,128)(2,1)S(1)} %pad_maximum_fusion.4), channel_id=1, source_target_pairs={{0,4},{1,5},{2,6},{3,7},{4,0},{5,1},{6,2},{7,3},{8,12},{9,13},{10,... | collective-permute-start | bytes 2899976 | tf_op jit(solution)/shard_map/ppermute | solution.py:40
  21.1 26.3 %collective-permute-start.1 = (bf16[2,128]{1,0:T(2,128)(2,1)S(1)}, bf16[2,128]{1,0:T(2,128)(2,1)S(1)}, u32[]{:S(2)}, u32[]{:S(2)}) collective-permute-start(bf16[2,128]{1,0:T(2,128)(2,1)S(1)} %pad_maximum_fusion.12), channel_id=1, source_target_pairs={{0,2},{1,3},{2,0},{3,1},{4,6},{5,7},{6,4},{7,5},{8,10},{9,11},{10,... | collective-permute-start | bytes 1544 | tf_op jit(solution)/shard_map/ppermute | solution.py:40
  47.5 40.5 %collective-permute-start.2 = (bf16[2,256]{1,0:T(2,128)(2,1)S(1)}, bf16[2,256]{1,0:T(2,128)(2,1)S(1)}, u32[]{:S(2)}, u32[]{:S(2)}) collective-permute-start(bf16[2,256]{1,0:T(2,128)(2,1)S(1)} %pad_maximum_fusion.10), channel_id=1, source_target_pairs={{0,4},{1,5},{2,6},{3,7},{4,0},{5,1},{6,2},{7,3},{8,12},{9,13},{10,... | collective-permute-start | bytes 3080 | tf_op jit(solution)/shard_map/ppermute | solution.py:40
  91.2 3.7 collective-permute-start.4
  96.5 96.1 %collective-permute-start.7 = (bf16[64,11008]{1,0:T(8,128)(2,1)}, bf16[64,11008]{1,0:T(8,128)(2,1)S(1)}, u32[]{:S(2)}, u32[]{:S(2)}) collective-permute-start(bf16[64,11008]{1,0:T(8,128)(2,1)} %pad_maximum_fusion.3), channel_id=1, source_target_pairs={{0,4},{1,5},{2,6},{3,7},{4,0},{5,1},{6,2},{7,3},{8,12},{9,13},{10,... | collective-permute-start | bytes 4227080 | tf_op jit(solution)/shard_map/ppermute | solution.py:40
  101.9 126.0 %collective-permute-start.6 = (bf16[128,7552]{1,0:T(8,128)(2,1)S(1)}, bf16[128,7552]{1,0:T(8,128)(2,1)S(1)}, u32[]{:S(2)}, u32[]{:S(2)}) collective-permute-start(bf16[128,7552]{1,0:T(8,128)(2,1)S(1)} %copy-done.36), channel_id=1, source_target_pairs={{0,2},{1,3},{2,0},{3,1},{4,6},{5,7},{6,4},{7,5},{8,10},{9,11},{10,... | collective-permute-start | bytes 5799944 | tf_op jit(solution)/shard_map/ppermute | solution.py:40
  277.2 196.7 %all-to-all-start = ((bf16[8,2,512,384]{3,2,1,0:T(8,128)(2,1)}), bf16[8,2,512,384]{3,2,1,0:T(8,128)(2,1)}, u32[]{:S(2)}, u32[]{:S(2)}) async-start(bf16[8,2,512,384]{3,2,1,0:T(8,128)(2,1)} %bitcast.381), calls=%async_computation | async-start | bytes 12582912 | tf_op jit(solution)/shard_map/all_to_all | solution.py:436
  286.7 164.3 %collective-permute-start.9 = (bf16[128,11008]{1,0:T(8,128)(2,1)S(1)}, bf16[128,11008]{1,0:T(8,128)(2,1)S(1)}, u32[]{:S(2)}, u32[]{:S(2)}) collective-permute-start(bf16[128,11008]{1,0:T(8,128)(2,1)S(1)} %constant_dynamic-update-slice_fusion.5), channel_id=1, source_target_pairs={{0,2},{1,3},{2,0},{3,1},{4,6},{5,7},{6,4},{7,5},{8,10},{9,11},{10,... | collective-permute-start | bytes 8454152 | tf_op jit(solution)/shard_map/ppermute | solution.py:40
  288.8 163.9 %collective-permute-start.8 = (bf16[256,7552]{1,0:T(8,128)(2,1)}, bf16[256,7552]{1,0:T(8,128)(2,1)}, u32[]{:S(2)}, u32[]{:S(2)}) collective-permute-start(bf16[256,7552]{1,0:T(8,128)(2,1)} %constant_dynamic-update-slice_fusion.2.refs_0_), channel_id=1, source_target_pairs={{0,16},{8,24},{16,0},{24,8},{1,17},{9,25},{17,1},{25,9},{2,18},{10... | collective-permute-start | bytes 11599880 | tf_op jit(solution)/shard_map/ppermute | solution.py:40
  473.9 142.8 %all-to-all-start.2 = ((bf16[8,2,512,384]{3,2,1,0:T(8,128)(2,1)}), bf16[8,2,512,384]{3,2,1,0:T(8,128)(2,1)}, u32[]{:S(2)}, u32[]{:S(2)}) async-start(bf16[8,2,512,384]{3,2,1,0:T(8,128)(2,1)} %bitcast.380), calls=%async_computation.2 | async-start | bytes 12582912 | tf_op jit(solution)/shard_map/all_to_all | solution.py:436
  484.4 182.8 %collective-permute-start.11 = (bf16[256,7552]{1,0:T(8,128)(2,1)}, bf16[256,7552]{1,0:T(8,128)(2,1)}, u32[]{:S(2)}, u32[]{:S(2)}) collective-permute-start(bf16[256,7552]{1,0:T(8,128)(2,1)} %collective-permute-done.8.refs_1_), channel_id=1, source_target_pairs={{0,1},{1,0},{2,3},{3,2},{4,5},{5,4},{6,7},{7,6},{8,9},{9,8},{10,11... | collective-permute-start | bytes 11599880 | tf_op jit(solution)/shard_map/ppermute | solution.py:40
  486.3 375.7 %collective-permute-start.16 = (bf16[256,11008]{1,0:T(8,128)(2,1)}, bf16[256,11008]{1,0:T(8,128)(2,1)}, u32[]{:S(2)}, u32[]{:S(2)}) collective-permute-start(bf16[256,11008]{1,0:T(8,128)(2,1)} %constant_dynamic-update-slice_fusion.7.refs_0_), channel_id=1, source_target_pairs={{0,1},{1,0},{2,3},{3,2},{4,5},{5,4},{6,7},{7,6},{8,9},{9,8},{10,11... | collective-permute-start | bytes 16908296 | tf_op jit(solution)/shard_map/ppermute | solution.py:40
  486.5 367.0 %collective-permute-start.10 = (bf16[256,7552]{1,0:T(8,128)(2,1)}, bf16[256,7552]{1,0:T(8,128)(2,1)}, u32[]{:S(2)}, u32[]{:S(2)}) collective-permute-start(bf16[256,7552]{1,0:T(8,128)(2,1)} %constant_dynamic-update-slice_fusion.2.refs_0_), channel_id=1, source_target_pairs={{0,1},{1,0},{2,3},{3,2},{4,5},{5,4},{6,7},{7,6},{8,9},{9,8},{10,11... | collective-permute-start | bytes 11599880 | tf_op jit(solution)/shard_map/ppermute | solution.py:40
  663.4 193.8 %all-to-all-start.3 = ((bf16[8,2,512,128]{3,2,1,0:T(8,128)(2,1)}), bf16[8,2,512,128]{3,2,1,0:T(8,128)(2,1)S(1)}, u32[]{:S(2)}, u32[]{:S(2)}) async-start(bf16[8,2,512,128]{3,2,1,0:T(8,128)(2,1)} %get-tuple-element.86.o_ref), calls=%async_computation.3 | async-start | bytes 4194304 | tf_op jit(solution)/shard_map/all_to_all | solution.py:440
  667.2 196.1 %collective-permute-start.15 = (bf16[256,7552]{1,0:T(8,128)(2,1)}, bf16[256,7552]{1,0:T(8,128)(2,1)}, u32[]{:S(2)}, u32[]{:S(2)}) collective-permute-start(bf16[256,7552]{1,0:T(8,128)(2,1)} %collective-permute-done.11.refs_3_), channel_id=1, source_target_pairs={{0,8},{8,0},{16,24},{24,16},{1,9},{9,1},{17,25},{25,17},{2,10},{10... | collective-permute-start | bytes 11599880 | tf_op jit(solution)/shard_map/ppermute | solution.py:40
  853.4 60.3 %collective-permute-start.14 = (bf16[256,7552]{1,0:T(8,128)(2,1)}, bf16[256,7552]{1,0:T(8,128)(2,1)}, u32[]{:S(2)}, u32[]{:S(2)}) collective-permute-start(bf16[256,7552]{1,0:T(8,128)(2,1)} %collective-permute-done.10.refs_2_), channel_id=1, source_target_pairs={{0,8},{8,0},{16,24},{24,16},{1,9},{9,1},{17,25},{25,17},{2,10},{10... | collective-permute-start | bytes 11599880 | tf_op jit(solution)/shard_map/ppermute | solution.py:40
  853.4 60.3 %collective-permute-start.13 = (bf16[256,7552]{1,0:T(8,128)(2,1)}, bf16[256,7552]{1,0:T(8,128)(2,1)}, u32[]{:S(2)}, u32[]{:S(2)}) collective-permute-start(bf16[256,7552]{1,0:T(8,128)(2,1)} %collective-permute-done.8.refs_1_), channel_id=1, source_target_pairs={{0,8},{8,0},{16,24},{24,16},{1,9},{9,1},{17,25},{25,17},{2,10},{10... | collective-permute-start | bytes 11599880 | tf_op jit(solution)/shard_map/ppermute | solution.py:40
  853.9 60.5 %collective-permute-start.12 = (bf16[256,7552]{1,0:T(8,128)(2,1)}, bf16[256,7552]{1,0:T(8,128)(2,1)}, u32[]{:S(2)}, u32[]{:S(2)}) collective-permute-start(bf16[256,7552]{1,0:T(8,128)(2,1)} %constant_dynamic-update-slice_fusion.2.refs_0_), channel_id=1, source_target_pairs={{0,8},{8,0},{16,24},{24,16},{1,9},{9,1},{17,25},{25,17},{2,10},{10... | collective-permute-start | bytes 11599880 | tf_op jit(solution)/shard_map/ppermute | solution.py:40
  857.1 53.0 %all-to-all-start.1 = ((bf16[8,2,512,128]{3,2,1,0:T(8,128)(2,1)}), bf16[8,2,512,128]{3,2,1,0:T(8,128)(2,1)}, u32[]{:S(2)}, u32[]{:S(2)}) async-start(bf16[8,2,512,128]{3,2,1,0:T(8,128)(2,1)} %get-tuple-element.81.o_ref), calls=%async_computation.1 | async-start | bytes 4194304 | tf_op jit(solution)/shard_map/all_to_all | solution.py:440
  862.0 124.8 %collective-permute-start.18 = (bf16[256,11008]{1,0:T(8,128)(2,1)}, bf16[256,11008]{1,0:T(8,128)(2,1)}, u32[]{:S(2)}, u32[]{:S(2)}) collective-permute-start(bf16[256,11008]{1,0:T(8,128)(2,1)} %collective-permute-done.16.refs_1_), channel_id=1, source_target_pairs={{0,16},{8,24},{16,0},{24,8},{1,17},{9,25},{17,1},{25,9},{2,18},{10... | collective-permute-start | bytes 16908296 | tf_op jit(solution)/shard_map/ppermute | solution.py:40
  863.3 242.7 %collective-permute-start.17 = (bf16[256,11008]{1,0:T(8,128)(2,1)}, bf16[256,11008]{1,0:T(8,128)(2,1)}, u32[]{:S(2)}, u32[]{:S(2)}) collective-permute-start(bf16[256,11008]{1,0:T(8,128)(2,1)} %constant_dynamic-update-slice_fusion.7.refs_0_), channel_id=1, source_target_pairs={{0,16},{8,24},{16,0},{24,8},{1,17},{9,25},{17,1},{25,9},{2,18},{10... | collective-permute-start | bytes 16908296 | tf_op jit(solution)/shard_map/ppermute | solution.py:40
  953.3 186.6 %collective-permute-start.20 = (bf16[256,11008]{1,0:T(8,128)(2,1)}, bf16[256,11008]{1,0:T(8,128)(2,1)}, u32[]{:S(2)}, u32[]{:S(2)}) collective-permute-start(bf16[256,11008]{1,0:T(8,128)(2,1)} %collective-permute-done.16.refs_1_), channel_id=1, source_target_pairs={{0,8},{8,0},{16,24},{24,16},{1,9},{9,1},{17,25},{25,17},{2,10},{10... | collective-permute-start | bytes 16908296 | tf_op jit(solution)/shard_map/ppermute | solution.py:40
  953.3 186.6 %collective-permute-start.19 = (bf16[256,11008]{1,0:T(8,128)(2,1)}, bf16[256,11008]{1,0:T(8,128)(2,1)}, u32[]{:S(2)}, u32[]{:S(2)}) collective-permute-start(bf16[256,11008]{1,0:T(8,128)(2,1)} %constant_dynamic-update-slice_fusion.7.refs_0_), channel_id=1, source_target_pairs={{0,8},{8,0},{16,24},{24,16},{1,9},{9,1},{17,25},{25,17},{2,10},{10... | collective-permute-start | bytes 16908296 | tf_op jit(solution)/shard_map/ppermute | solution.py:40
  986.8 153.2 %collective-permute-start.22 = (bf16[256,11008]{1,0:T(8,128)(2,1)}, bf16[256,11008]{1,0:T(8,128)(2,1)}, u32[]{:S(2)}, u32[]{:S(2)}) collective-permute-start(bf16[256,11008]{1,0:T(8,128)(2,1)} %collective-permute-done.18.refs_3_), channel_id=1, source_target_pairs={{0,8},{8,0},{16,24},{24,16},{1,9},{9,1},{17,25},{25,17},{2,10},{10... | collective-permute-start | bytes 16908296 | tf_op jit(solution)/shard_map/ppermute | solution.py:40
  1106.0 34.0 %collective-permute-start.21 = (bf16[256,11008]{1,0:T(8,128)(2,1)}, bf16[256,11008]{1,0:T(8,128)(2,1)}, u32[]{:S(2)}, u32[]{:S(2)}) collective-permute-start(bf16[256,11008]{1,0:T(8,128)(2,1)} %collective-permute-done.17.refs_2_), channel_id=1, source_target_pairs={{0,8},{8,0},{16,24},{24,16},{1,9},{9,1},{17,25},{25,17},{2,10},{10... | collective-permute-start | bytes 16908296 | tf_op jit(solution)/shard_map/ppermute | solution.py:40
  1249.7 85.1 %collective-permute-start.23 = (bf16[2752,2048]{1,0:T(8,128)(2,1)}, bf16[2752,2048]{1,0:T(8,128)(2,1)}, u32[]{:S(2)}, u32[]{:S(2)}) collective-permute-start(bf16[2752,2048]{1,0:T(8,128)(2,1)} %bitcast.32), channel_id=1, source_target_pairs={{0,8},{8,0},{16,24},{24,16},{1,9},{9,1},{17,25},{25,17},{2,10},{10... | collective-permute-start | bytes 33816584 | tf_op jit(solution)/shard_map/ppermute | solution.py:40
  1363.6 99.7 %collective-permute-start.24 = (bf16[1024,5504]{1,0:T(8,128)(2,1)}, bf16[1024,5504]{1,0:T(8,128)(2,1)}, u32[]{:S(2)}, u32[]{:S(2)}) collective-permute-start(bf16[1024,5504]{1,0:T(8,128)(2,1)} %convolution_convert_fusion.2), channel_id=1, source_target_pairs={{0,8},{8,0},{16,24},{24,16},{1,9},{9,1},{17,25},{25,17},{2,10},{10... | collective-permute-start | bytes 33816584 | tf_op jit(solution)/shard_map/ppermute | solution.py:40
  1429.8 105.1 %collective-permute-start.25 = (bf16[1024,5504]{1,0:T(8,128)(2,1)}, bf16[1024,5504]{1,0:T(8,128)(2,1)}, u32[]{:S(2)}, u32[]{:S(2)}) collective-permute-start(bf16[1024,5504]{1,0:T(8,128)(2,1)} %convolution_convert_fusion.1), channel_id=1, source_target_pairs={{0,8},{8,0},{16,24},{24,16},{1,9},{9,1},{17,25},{25,17},{2,10},{10... | collective-permute-start | bytes 33816584 | tf_op jit(solution)/shard_map/ppermute | solution.py:40
  1430.3 132.3 %collective-permute-start.26 = (bf16[1376,2048]{1,0:T(8,128)(2,1)}, bf16[1376,2048]{1,0:T(8,128)(2,1)}, u32[]{:S(2)}, u32[]{:S(2)}) collective-permute-start(bf16[1376,2048]{1,0:T(8,128)(2,1)} %fusion.3), channel_id=1, source_target_pairs={{0,16},{8,24},{16,0},{24,8},{1,17},{9,25},{17,1},{25,9},{2,18},{10... | collective-permute-start | bytes 16908296 | tf_op jit(solution)/shard_map/ppermute | solution.py:40
  1556.6 104.7 %all-to-all-start.4 = ((bf16[8,2,512,128]{3,2,1,0:T(8,128)(2,1)}), bf16[8,2,512,128]{3,2,1,0:T(8,128)(2,1)S(1)}, u32[]{:S(2)}, u32[]{:S(2)}) async-start(bf16[8,2,512,128]{3,2,1,0:T(8,128)(2,1)} %bitcast.414), calls=%async_computation.4 | async-start | bytes 4194304 | tf_op jit(solution)/shard_map/all_to_all | solution.py:436
  1587.3 68.7 %collective-permute-start.35 = (bf16[4,172,2048]{2,0,1:T(4,128)(2,1)}, bf16[4,172,2048]{2,0,1:T(4,128)(2,1)}, u32[]{:S(2)}, u32[]{:S(2)}) collective-permute-start(bf16[4,172,2048]{2,0,1:T(4,128)(2,1)} %copy.141), channel_id=1, source_target_pairs={{0,1},{1,0},{2,3},{3,2},{4,5},{5,4},{6,7},{7,6},{8,9},{9,8},{10,11... | collective-permute-start | bytes 8454152 | tf_op jit(solution)/shard_map/ppermute | solution.py:40
  1589.3 204.3 %collective-permute-start.27 = (bf16[512,5504]{1,0:T(8,128)(2,1)}, bf16[512,5504]{1,0:T(8,128)(2,1)}, u32[]{:S(2)}, u32[]{:S(2)}) collective-permute-start(bf16[512,5504]{1,0:T(8,128)(2,1)} %add_convert_fusion.3), channel_id=1, source_target_pairs={{0,1},{1,0},{2,3},{3,2},{4,5},{5,4},{6,7},{7,6},{8,9},{9,8},{10,11... | collective-permute-start | bytes 16908296 | tf_op jit(solution)/shard_map/ppermute | solution.py:40
  1619.8 181.9 %collective-permute-start.28 = (bf16[1024,2048]{1,0:T(8,128)(2,1)}, bf16[1024,2048]{1,0:T(8,128)(2,1)}, u32[]{:S(2)}, u32[]{:S(2)}) collective-permute-start(bf16[1024,2048]{1,0:T(8,128)(2,1)} %convolution_convert_fusion.7), channel_id=1, source_target_pairs={{0,8},{8,0},{16,24},{24,16},{1,9},{9,1},{17,25},{25,17},{2,10},{10... | collective-permute-start | bytes 12582920 | tf_op jit(solution)/shard_map/ppermute | solution.py:40
  1619.8 270.9 %collective-permute-start.29 = (bf16[512,5504]{1,0:T(8,128)(2,1)}, bf16[512,5504]{1,0:T(8,128)(2,1)}, u32[]{:S(2)}, u32[]{:S(2)}) collective-permute-start(bf16[512,5504]{1,0:T(8,128)(2,1)} %add_convert_fusion.2), channel_id=1, source_target_pairs={{0,16},{8,24},{16,0},{24,8},{1,17},{9,25},{17,1},{25,9},{2,18},{10... | collective-permute-start | bytes 16908296 | tf_op jit(solution)/shard_map/ppermute | solution.py:40
  1661.3 146.9 %all-to-all-start.5 = ((bf16[8,2,512,128]{3,2,1,0:T(8,128)(2,1)}), bf16[8,2,512,128]{3,2,1,0:T(8,128)(2,1)}, u32[]{:S(2)}, u32[]{:S(2)}) async-start(bf16[8,2,512,128]{3,2,1,0:T(8,128)(2,1)} %bitcast.416), calls=%async_computation.5 | async-start | bytes 4194304 | tf_op jit(solution)/shard_map/all_to_all | solution.py:436
  1807.4 100.1 %collective-permute-start.30 = (bf16[512,2048]{1,0:T(8,128)(2,1)}, bf16[512,2048]{1,0:T(8,128)(2,1)}, u32[]{:S(2)}, u32[]{:S(2)}) collective-permute-start(bf16[512,2048]{1,0:T(8,128)(2,1)} %add_convert_fusion.6), channel_id=1, source_target_pairs={{0,16},{8,24},{16,0},{24,8},{1,17},{9,25},{17,1},{25,9},{2,18},{10... | collective-permute-start | bytes 6291464 | tf_op jit(solution)/shard_map/ppermute | solution.py:40
  1808.2 143.6 %all-to-all-start.6 = ((bf16[8,2,512,384]{3,2,1,0:T(8,128)(2,1)}), bf16[8,2,512,384]{3,2,1,0:T(8,128)(2,1)}, u32[]{:S(2)}, u32[]{:S(2)}) async-start(bf16[8,2,512,384]{3,2,1,0:T(8,128)(2,1)} %copy-done.1), calls=%async_computation.6 | async-start | bytes 12582912 | tf_op jit(solution)/shard_map/all_to_all | solution.py:440
  1898.4 113.9 %collective-permute-start.37 = (bf16[4,64,5504]{2,1,0:T(8,128)(2,1)}, bf16[4,64,5504]{2,1,0:T(8,128)(2,1)}, u32[]{:S(2)}, u32[]{:S(2)}) collective-permute-start(bf16[4,64,5504]{2,1,0:T(8,128)(2,1)} %dynamic-slice_bitcast_fusion.2), channel_id=1, source_target_pairs={{0,1},{1,0},{2,3},{3,2},{4,5},{5,4},{6,7},{7,6},{8,9},{9,8},{10,11... | collective-permute-start | bytes 8454152 | tf_op jit(solution)/shard_map/ppermute | solution.py:40
  1902.2 196.4 %collective-permute-start.36 = (bf16[256,5504]{1,0:T(8,128)(2,1)}, bf16[256,5504]{1,0:T(8,128)(2,1)}, u32[]{:S(2)}, u32[]{:S(2)}) collective-permute-start(bf16[256,5504]{1,0:T(8,128)(2,1)} %dynamic-slice_bitcast_fusion.3), channel_id=1, source_target_pairs={{0,16},{8,24},{16,0},{24,8},{1,17},{9,25},{17,1},{25,9},{2,18},{10... | collective-permute-start | bytes 8454152 | tf_op jit(solution)/shard_map/ppermute | solution.py:40
  1944.1 161.3 %collective-permute-start.38 = (bf16[4,64,2048]{2,1,0:T(8,128)(2,1)}, bf16[4,64,2048]{2,1,0:T(8,128)(2,1)}, u32[]{:S(2)}, u32[]{:S(2)}) collective-permute-start(bf16[4,64,2048]{2,1,0:T(8,128)(2,1)} %dynamic-slice_bitcast_fusion.5), channel_id=1, source_target_pairs={{0,1},{1,0},{2,3},{3,2},{4,5},{5,4},{6,7},{7,6},{8,9},{9,8},{10,11... | collective-permute-start | bytes 3145736 | tf_op jit(solution)/shard_map/ppermute | solution.py:40
  1951.8 299.7 %all-to-all-start.7 = ((bf16[8,2,512,384]{3,2,1,0:T(8,128)(2,1)}), bf16[8,2,512,384]{3,2,1,0:T(8,128)(2,1)}, u32[]{:S(2)}, u32[]{:S(2)}) async-start(bf16[8,2,512,384]{3,2,1,0:T(8,128)(2,1)} %copy-done), calls=%async_computation.7 | async-start | bytes 12582912 | tf_op jit(solution)/shard_map/all_to_all | solution.py:440
  1969.2 22.9 collective-permute-start.31
  1974.2 22.1 collective-permute-start.32
  1995.1 36.6 %collective-permute-start.33 = (bf16[512,1536]{1,0:T(8,128)(2,1)}, bf16[512,1536]{1,0:T(8,128)(2,1)S(1)}, u32[]{:S(2)}, u32[]{:S(2)}) collective-permute-start(bf16[512,1536]{1,0:T(8,128)(2,1)} %add_convert_fusion.14), channel_id=1, source_target_pairs={{0,16},{8,24},{16,0},{24,8},{1,17},{9,25},{17,1},{25,9},{2,18},{10... | collective-permute-start | bytes 4718600 | tf_op jit(solution)/shard_map/ppermute | solution.py:40
  1998.1 98.5 %collective-permute-start.34 = (bf16[512,1536]{1,0:T(8,128)(2,1)S(1)}, bf16[512,1536]{1,0:T(8,128)(2,1)S(1)}, u32[]{:S(2)}, u32[]{:S(2)}) collective-permute-start(bf16[512,1536]{1,0:T(8,128)(2,1)S(1)} %add_convert_fusion.13), channel_id=1, source_target_pairs={{0,1},{1,0},{2,3},{3,2},{4,5},{5,4},{6,7},{7,6},{8,9},{9,8},{10,11... | collective-permute-start | bytes 4718600 | tf_op jit(solution)/shard_map/ppermute | solution.py:40
  2097.3 15.9 collective-permute-start.40
  2102.8 16.4 collective-permute-start.39
  2134.3 110.2 %collective-permute-start.41 = (bf16[2,64,18560]{2,1,0:T(8,128)(2,1)}, bf16[2,64,18560]{2,1,0:T(8,128)(2,1)}, u32[]{:S(2)}, u32[]{:S(2)}) collective-permute-start(bf16[2,64,18560]{2,1,0:T(8,128)(2,1)} %dynamic-slice_bitcast_fusion), channel_id=1, source_target_pairs={{0,2},{1,3},{2,0},{3,1},{4,6},{5,7},{6,4},{7,5},{8,10},{9,11},{10,... | collective-permute-start | bytes 14254088 | tf_op jit(solution)/shard_map/ppermute | solution.py:40
  2265.1 116.1 %collective-permute-start.42 = (bf16[1024,1536]{1,0:T(8,128)(2,1)}, bf16[1024,1536]{1,0:T(8,128)(2,1)}, u32[]{:S(2)}, u32[]{:S(2)}) collective-permute-start(bf16[1024,1536]{1,0:T(8,128)(2,1)} %convolution_convert_fusion.4), channel_id=1, source_target_pairs={{0,8},{8,0},{16,24},{24,16},{1,9},{9,1},{17,25},{25,17},{2,10},{10... | collective-permute-start | bytes 9437192 | tf_op jit(solution)/shard_map/ppermute | solution.py:40
  2270.0 117.0 %collective-permute-start.43 = (bf16[1024,1536]{1,0:T(8,128)(2,1)}, bf16[1024,1536]{1,0:T(8,128)(2,1)}, u32[]{:S(2)}, u32[]{:S(2)}) collective-permute-start(bf16[1024,1536]{1,0:T(8,128)(2,1)} %convolution_convert_fusion.3), channel_id=1, source_target_pairs={{0,8},{8,0},{16,24},{24,16},{1,9},{9,1},{17,25},{25,17},{2,10},{10... | collective-permute-start | bytes 9437192 | tf_op jit(solution)/shard_map/ppermute | solution.py:40
  2270.6 105.5 %collective-permute-start.44 = (bf16[1,64,18560]{2,1,0:T(8,128)(2,1)S(1)}, bf16[1,64,18560]{2,1,0:T(8,128)(2,1)}, u32[]{:S(2)}, u32[]{:S(2)}) collective-permute-start(bf16[1,64,18560]{2,1,0:T(8,128)(2,1)S(1)} %constant_dynamic-slice_fusion.11), channel_id=1, source_target_pairs={{0,4},{1,5},{2,6},{3,7},{4,0},{5,1},{6,2},{7,3},{8,12},{9,13},{10,... | collective-permute-start | bytes 7127048 | tf_op jit(solution)/shard_map/ppermute | solution.py:40
  2386.1 40.3 %collective-permute-start.45 = (bf16[512,1536]{1,0:T(8,128)(2,1)}, bf16[512,1536]{1,0:T(8,128)(2,1)}, u32[]{:S(2)}, u32[]{:S(2)}) collective-permute-start(bf16[512,1536]{1,0:T(8,128)(2,1)} %add_convert_fusion.10), channel_id=1, source_target_pairs={{0,16},{8,24},{16,0},{24,8},{1,17},{9,25},{17,1},{25,9},{2,18},{10... | collective-permute-start | bytes 4718600 | tf_op jit(solution)/shard_map/ppermute | solution.py:40
  2392.1 40.9 %collective-permute-start.46 = (bf16[512,1536]{1,0:T(8,128)(2,1)}, bf16[512,1536]{1,0:T(8,128)(2,1)}, u32[]{:S(2)}, u32[]{:S(2)}) collective-permute-start(bf16[512,1536]{1,0:T(8,128)(2,1)} %add_convert_fusion.9), channel_id=1, source_target_pairs={{0,1},{1,0},{2,3},{3,2},{4,5},{5,4},{6,7},{7,6},{8,9},{9,8},{10,11... | collective-permute-start | bytes 4718600 | tf_op jit(solution)/shard_map/ppermute | solution.py:40
  2395.3 26.7 %collective-permute-start.51 = (f32[2,1024]{1,0:T(2,128)S(1)}, f32[2,1024]{1,0:T(2,128)S(1)}, u32[]{:S(2)}, u32[]{:S(2)}) collective-permute-start(f32[2,1024]{1,0:T(2,128)S(1)} %bitcast.490), channel_id=1, source_target_pairs={{0,16},{8,24},{16,0},{24,8},{1,17},{9,25},{17,1},{25,9},{2,18},{10... | collective-permute-start | bytes 24584 | tf_op jit(solution)/shard_map/ppermute | solution.py:40
  2422.1 4.1 collective-permute-start.52
  2426.3 12.5 collective-permute-start.53
  2435.7 20.0 collective-permute-start.47
  2436.4 19.7 collective-permute-start.48
  2457.9 36.5 %collective-permute-start.49 = (bf16[2,64,6144]{2,1,0:T(8,128)(2,1)}, bf16[2,64,6144]{2,1,0:T(8,128)(2,1)}, u32[]{:S(2)}, u32[]{:S(2)}) collective-permute-start(bf16[2,64,6144]{2,1,0:T(8,128)(2,1)} %dynamic-slice_bitcast_fusion.4), channel_id=1, source_target_pairs={{0,2},{1,3},{2,0},{3,1},{4,6},{5,7},{6,4},{7,5},{8,10},{9,11},{10,... | collective-permute-start | bytes 4718600 | tf_op jit(solution)/shard_map/ppermute | solution.py:40
  2460.2 34.1 %collective-permute-start.54 = (f32[2,128]{1,0:T(2,128)S(1)}, f32[2,128]{1,0:T(2,128)S(1)}, u32[]{:S(2)}, u32[]{:S(2)}) collective-permute-start(f32[2,128]{1,0:T(2,128)S(1)} %fusion.183), channel_id=1, source_target_pairs={{0,2},{1,3},{2,0},{3,1},{4,6},{5,7},{6,4},{7,5},{8,10},{9,11},{10,... | collective-permute-start | bytes 3080 | tf_op jit(solution)/shard_map/ppermute | solution.py:40
  2497.4 35.8 %collective-permute-start.50 = (bf16[1,64,6144]{2,1,0:T(8,128)(2,1)S(1)}, bf16[1,64,6144]{2,1,0:T(8,128)(2,1)S(1)}, u32[]{:S(2)}, u32[]{:S(2)}) collective-permute-start(bf16[1,64,6144]{2,1,0:T(8,128)(2,1)S(1)} %constant_dynamic-slice_fusion.10), channel_id=1, source_target_pairs={{0,4},{1,5},{2,6},{3,7},{4,0},{5,1},{6,2},{7,3},{8,12},{9,13},{10,... | collective-permute-start | bytes 2359304 | tf_op jit(solution)/shard_map/ppermute | solution.py:40
  2499.6 6.0 collective-permute-start.55
  (75 other events, 2602.1 us)
Sparse Core Ops, SparseCore 0:
  11.6 243.3 all-gather.1

commit v4 on v3

--- a/solution.py
+++ b/solution.py
@@ -44,9 +44,11 @@
     return lax.dynamic_index_in_dim(array, index, dim, keepdims=False)
 
 
-def scatter_digit(parts, digit, dim, out_type):
+def scatter_digit(parts, digit, dim, out_type, hold=()):
     own = digit_index(digit)
     got = swap(pick(parts, 1 - own, dim), digit)
+    if hold:
+        got = lax.optimization_barrier((got,) + tuple(hold))[0]
     return (pick(parts, own, dim).astype(f32) + got.astype(f32)).astype(out_type)
 
 
@@ -229,9 +231,9 @@
         self.widths = [t.shape[2] for t in totals]
         self.total = jnp.concatenate(totals, axis=2)
 
-    def step(self, n, *others):
+    def step(self, n, *others, hold=()):
         total = after(self.total, *others).reshape(-1, 2, self.unit, sum(self.widths))
-        self.total = scatter_digit(total, self.far[-1 - n], 1, f32 if n == len(self.far) - 1 else bf16)
+        self.total = scatter_digit(total, self.far[-1 - n], 1, f32 if n == len(self.far) - 1 else bf16, hold)
         return self.total
 
     def results(self):
@@ -324,8 +326,8 @@
     )(bounds, qkv, qkv, qkv, low)
 
 
-def backward_kernel(bounds, q_ref, k_ref, v_ref, do_ref, o_ref, lse_ref, lo_ref, out_ref, dq, dk, dv, delta):
-    pair, j = pl.program_id(0), pl.program_id(1)
+def backward_kernel(pair, bounds, q_ref, k_ref, v_ref, do_ref, o_ref, lse_ref, lo_ref, out_ref, dq, dk, dv, delta):
+    j = pl.program_id(0)
     k = k_ref[...].reshape(TILE, HD)
     v = v_ref[...].reshape(TILE, HD)
     factor = SCALE * LOG2E
@@ -348,7 +350,7 @@
     def _():
         dq[...] = jnp.zeros_like(dq)
 
-        @pl.loop(0, pl.num_programs(1))
+        @pl.loop(0, pl.num_programs(0))
         def _(i):
             rows = pl.ds(pl.multiple_of(i * TILE, TILE), TILE)
             product = tile_of(do_ref, i).astype(f32) * tile_of(o_ref, i).astype(f32)
@@ -375,20 +377,20 @@
     out_ref[:, :, 2 * HD :] = dv[...].astype(bf16).reshape(shape)
 
 
-def attend_back(qkv, grad, mixed, lse, bounds, low):
-    seq, pairs, rows, _ = qkv.shape
+def attend_back(pair, qkv, grad, mixed, lse, bounds, low):
+    seq, _, rows, _ = qkv.shape
     length = seq * rows
     blocks, per = length // TILE, TILE // rows
-    whole = pl.BlockSpec((seq, None, rows, HD), lambda p, j, b: (0, p, 0, 0))
-    line = pl.BlockSpec((None, 1, length), lambda p, j, b: (p, 0, 0))
-    block = lambda part: pl.BlockSpec((per, None, rows, HD), lambda p, j, b: (j, p, 0, part))
+    whole = pl.BlockSpec((seq, None, rows, HD), lambda j, b: (0, pair, 0, 0))
+    line = pl.BlockSpec((None, 1, length), lambda j, b: (pair, 0, 0))
+    block = lambda part: pl.BlockSpec((per, None, rows, HD), lambda j, b: (j, pair, 0, part))
     return pl.pallas_call(
-        backward_kernel,
+        functools.partial(backward_kernel, pair),
         grid_spec=pltpu.PrefetchScalarGridSpec(
             num_scalar_prefetch=1,
-            grid=(pairs, blocks),
+            grid=(blocks,),
             in_specs=[whole, block(1), block(2), whole, whole, line, line],
-            out_specs=pl.BlockSpec((per, None, rows, 3 * HD), lambda p, j, b: (j, p, 0, 0)),
+            out_specs=pl.BlockSpec((per, None, rows, 3 * HD), lambda j, b: (j, 0, 0, 0)),
             scratch_shapes=[
                 pltpu.VMEM((length, HD), f32),
                 pltpu.VMEM((TILE, HD), f32),
@@ -396,12 +398,12 @@
                 pltpu.VMEM((1, length), f32),
             ],
         ),
-        out_shape=jax.ShapeDtypeStruct(qkv.shape, bf16),
+        out_shape=jax.ShapeDtypeStruct((seq, 1, rows, 3 * HD), bf16),
         compiler_params=pltpu.CompilerParams(vmem_limit_bytes=40 * 1024 * 1024),
         cost_estimate=pl.CostEstimate(
-            flops=20 * pairs * length * 1792 * HD,
-            bytes_accessed=16 * pairs * length * HD,
-            transcendentals=pairs * length * 1792,
+            flops=20 * length * 1792 * HD,
+            bytes_accessed=16 * length * HD,
+            transcendentals=length * 1792,
         ),
         name="attend_back",
     )(bounds, qkv, qkv, qkv, grad, mixed, lse, low)
@@ -428,11 +430,11 @@
     return low[None], jnp.stack([begin, middle, back_middle, back_end])
 
 
-def to_heads(rows, heads):
+def to_heads(rows, micros):
     seq = lax.axis_size("seq")
-    count, width = rows.shape[0] // MB, rows.shape[1] // heads
-    split = rows.reshape(MB, count, heads, width).transpose(2, 0, 1, 3)
-    split = split.reshape(seq, heads * MB // seq, count, width)
+    count, width = rows.shape[0] // micros, rows.shape[1] // H
+    split = rows.reshape(micros, count, H, width).transpose(2, 0, 1, 3)
+    split = split.reshape(seq, H * micros // seq, count, width)
     return lax.all_to_all(split, "seq", 0, 0, tiled=True)
 
 
@@ -440,9 +442,9 @@
     return lax.all_to_all(whole, "seq", 0, 0, tiled=True)
 
 
-def rows_of(got, heads):
+def rows_of(got, micros):
     count, width = got.shape[2], got.shape[3]
-    return got.reshape(heads, MB, count, width).transpose(1, 2, 0, 3).reshape(MB * count, heads * width)
+    return got.reshape(H, micros, count, width).transpose(1, 2, 0, 3).reshape(micros * count, H * width)
 
 
 def norm_scale(values):
@@ -465,24 +467,25 @@
     rows = tokens.shape[2]
     seq = lax.axis_size("seq")
     gather = lambda w: lax.all_gather(w, ("dp", "seq"), axis=0, tiled=True)
-    groups = 2 if H * MB % (2 * seq) == 0 else 1
-    heads = H // groups
-    pairs = heads * MB // seq
-    width = heads * HD
+    groups = MB if H % seq == 0 else 1
+    micros = MB // groups
+    pairs = H * micros // seq
+    size = micros * rows
+    of = lambda array, g: array[g * size : (g + 1) * size]
 
     x = tokens.reshape(MB * rows, D).astype(f32)
     cot = cotangent.reshape(MB * rows, D)
     bounds, low = [], []
-    for k in range(pairs):
-        micro = lax.rem(lax.axis_index("seq") * pairs + k, MB)
-        pair_low, pair_bounds = key_bounds(pick(segment_ids[:, 0], micro, 0))
-        bounds.append(pair_bounds)
-        low.append(pair_low)
-    bounds, low = jnp.stack(bounds), jnp.stack(low)
-
-    order_qkv = w_qkv.reshape(-1, 3, groups, heads, HD).transpose(0, 2, 3, 1, 4).reshape(w_qkv.shape)
-    all_qkv = gather(order_qkv)
-    full_qkv = [all_qkv[:, g * 3 * width : (g + 1) * 3 * width] for g in range(groups)]
+    for g in range(groups):
+        made = []
+        for k in range(pairs):
+            micro = g if micros == 1 else lax.rem(lax.axis_index("seq") * pairs + k, micros)
+            made.append(key_bounds(segment_ids[g, 0] if micros == 1 else pick(segment_ids[:, 0], micro, 0)))
+        low.append(jnp.stack([m[0] for m in made]))
+        bounds.append(jnp.stack([m[1] for m in made]))
+
+    order_qkv = w_qkv.reshape(-1, 3, H, HD).transpose(0, 2, 1, 3).reshape(w_qkv.shape)
+    full_qkv = gather(order_qkv)
     all_gains = gather_small(jnp.stack([gain_attn, gain_mlp]))
     gains = all_gains.astype(f32)
     gain_a, gain_m = gains[0], gains[1]
@@ -499,138 +502,173 @@
         soon.far_step(n)
         later.far_step(n - 1)
     ready = soon.values() + later.values()
-    h_attn = after(h_attn, *ready)
     soon.wait(*ready)
     soon.near_step(0)
     later.wait(*ready)
     later.far_step(far - 1)
-    arrived = []
-    step_in = h_attn
+    step_in = after(h_attn, *later.values())
+    later.near_step(0)
+    saved, attended, arrived = [], [], []
     for g in range(groups):
-        qkv_rows = jnp.dot(step_in, full_qkv[g], preferred_element_type=f32).astype(bf16)
-        arrived.append(to_heads(qkv_rows, heads))
-        ready = soon.values() + later.values()
-        step_in = after(h_attn, qkv_rows, *ready)
-    later.wait(*ready)
-    later.near_step(0)
-    soon.wait(*ready)
-    soon.near_step(1)
-    saved, attended = [], []
-    last = None
-    for g in range(groups):
-        qkv = arrived[g] if last is None else after(arrived[g], last)
-        last, lse = attend(qkv, bounds, low)
-        saved.append((qkv, last, lse))
-        attended.append(rows_of(to_rows(last), heads))
+        qkv_rows = jnp.dot(of(step_in, g), full_qkv, preferred_element_type=f32).astype(bf16)
+        qkv = to_heads(qkv_rows, micros)
         if g == 0:
-            later.wait(last)
+            ready = soon.values() + later.values()
+            qkv = after(qkv, *ready)
+            soon.wait(*ready)
+            soon.near_step(1)
+            later.wait(*ready)
             later.near_step(1)
-    soon.wait(last)
-    soon.near_step(2)
-    full_gate, full_out = soon.finish()
-    attended = jnp.concatenate(attended, axis=1)
-
-    mid = x + jnp.dot(attended, full_out, preferred_element_type=f32)
-    scale_m = norm_scale(mid)
-    h_mlp = (mid * scale_m * gain_m).astype(bf16)
-    later.wait(h_mlp)
-    later.near_step(2)
-    gate = jnp.dot(h_mlp, full_gate, preferred_element_type=f32)
+        else:
+            qkv = after(qkv, gate_first)
+        mixed, lse = attend(qkv, bounds[g], low[g])
+        saved.append((qkv, mixed, lse))
+        attended.append(rows_of(to_rows(mixed), micros))
+        if g == 0:
+            step_in = after(h_attn, attended[0])
+            soon.near_step(2)
+            full_gate, full_out = soon.finish()
+
+            mid_first = of(x, 0) + jnp.dot(attended[0], full_out, preferred_element_type=f32)
+            scale_first = norm_scale(mid_first)
+            h_first = (mid_first * scale_first * gain_m).astype(bf16)
+            gate_first = jnp.dot(h_first, full_gate, preferred_element_type=f32)
+            later.near_step(2)
+    later.wait(gate_first)
     full_up, full_down = later.finish()
     full_down = full_down.reshape(FF, D)
-    up = jnp.dot(h_mlp, full_up, preferred_element_type=f32)
-    sig = jax.nn.sigmoid(gate)
-    act = (gate * sig * up).astype(bf16)
-
-    down = Reduce(None, cot, False, product=tn(act, cot).astype(bf16))
-    mark = (down.cross(),)
-    grad_act = nt(after(cot, *mark), full_down)
-    grad_gate = (grad_act * up * sig * (1.0 + gate * (1.0 - sig))).astype(bf16)
-    grad_up = (grad_act * (gate * sig)).astype(bf16)
-    mark = (down.send(grad_gate, grad_up),)
-    gate_r = Reduce(pieces_of(h_mlp, False), grad_gate, False)
-    up_r = Reduce(pieces_of(h_mlp, True), grad_up, True)
-    mark = (up_r.cross(*mark),)
-    mark = (gate_r.cross(*mark),)
-    half_grad = nt(after(grad_gate, *mark), full_gate)
-    mark = (up_r.send(half_grad),)
-    grad_h_mlp = half_grad + nt(after(grad_up, *mark), full_up)
-    grad_mid_norm, gain_m_grad = norm_backward(grad_h_mlp, mid, scale_m, gain_m)
-    grad_mid = cot.astype(f32) + grad_mid_norm
-    grad_branch = grad_mid.astype(bf16)
-    grad_rows = [nt(grad_branch, full_out[g * width : (g + 1) * width]).astype(bf16) for g in range(groups)]
-    grads = [to_heads(r, heads) for r in grad_rows]
-
-    out_r = Reduce(pieces_of(attended, False), grad_branch, False)
+
+    parts = []
+    grads = []
+    rows_grad = []
+    mark = (mixed,)
+
+    def back_of(g, *others):
+        qkv, mixed, lse = saved[g]
+        pieces = []
+        for k in range(pairs):
+            back = attend_back(k, after(qkv, *others), grads[g], mixed, lse, bounds[g], low[g])
+            others = (back,)
+            pieces.append(to_rows(back))
+        rows_grad.append(pieces)
+        return back
+
+    for g in range(groups):
+        final = g == groups - 1
+        if g == 0:
+            mid, scale_m, h_mlp, gate = mid_first, scale_first, h_first, gate_first
+        else:
+            mid = of(x, g) + jnp.dot(after(attended[g], *mark), full_out, preferred_element_type=f32)
+            scale_m = norm_scale(mid)
+            h_mlp = (mid * scale_m * gain_m).astype(bf16)
+            gate = jnp.dot(h_mlp, full_gate, preferred_element_type=f32)
+        up = jnp.dot(after(h_mlp, *mark), full_up, preferred_element_type=f32)
+        sig = jax.nn.sigmoid(gate)
+        act = (gate * sig * up).astype(bf16)
+        parts.append([mid, scale_m, h_mlp, act])
+        mark = (act,)
+        if g:
+            mark = (back_of(g - 1, *mark),)
+        if final:
+            acts = jnp.concatenate([p[3] for p in parts], axis=0)
+            sides = jnp.concatenate([p[2] for p in parts], axis=0)
+            down = Reduce(None, cot, False, product=tn(after(acts, *mark), cot).astype(bf16))
+            mark = (down.cross(),)
+        if g:
+            mark = mark + (rows_grad[-1][0],)
+        cot_part = of(cot, g)
+        grad_act = nt(after(cot_part, *mark), full_down)
+        grad_gate = (grad_act * up * sig * (1.0 + gate * (1.0 - sig))).astype(bf16)
+        grad_up = (grad_act * (gate * sig)).astype(bf16)
+        parts[g] += [grad_gate, grad_up]
+        mark = (grad_gate, grad_up)
+        if final:
+            mark = (down.send(*mark),)
+            gate_r = Reduce(pieces_of(sides, False), jnp.concatenate([p[4] for p in parts], axis=0), False)
+            up_r = Reduce(pieces_of(sides, True), jnp.concatenate([p[5] for p in parts], axis=0), True)
+            mark = (up_r.cross(*mark),)
+            mark = (gate_r.cross(*mark),)
+        half_grad = nt(after(grad_gate, *mark), full_gate)
+        mark = (half_grad,)
+        if final:
+            mark = (up_r.send(*mark),)
+        grad_h_mlp = half_grad + nt(after(grad_up, *mark), full_up)
+        grad_mid_norm, gain_part = norm_backward(grad_h_mlp, mid, scale_m, gain_m)
+        grad_mid = cot_part.astype(f32) + grad_mid_norm
+        grad_branch = grad_mid.astype(bf16)
+        grad_rows = nt(after(grad_branch, *[r for pieces in rows_grad for r in pieces]), full_out).astype(bf16)
+        grads.append(to_heads(grad_rows, micros))
+        parts[g] += [grad_mid, grad_branch, gain_part]
+        mark = (grad_rows,)
+
+    attended_all = jnp.concatenate(attended, axis=0)
+    out_r = Reduce(pieces_of(attended_all, False), jnp.concatenate([p[7] for p in parts], axis=0), False)
     early = [down, up_r, gate_r, out_r]
-    mark = (gate_r.send(*grad_rows),)
+    mark = (gate_r.send(*mark),)
     mark = (out_r.cross(*mark),)
     mark = (down.keep(*mark),)
     down.second()
-    grad_heads = []
-    for g in range(groups):
-        qkv, mixed, lse = saved[g]
-        back = attend_back(after(qkv, *mark), grads[g], mixed, lse, bounds, low)
-        grad_heads.append(back)
-        mark = (back,)
-        if g == 0:
-            mark = (up_r.keep(*mark),)
-            up_r.second()
-            mark = (out_r.send(*mark),)
-    arrived = [to_rows(back) for back in grad_heads]
-    grad_qkv = []
+    mark = (back_of(groups - 1, *mark),)
+    mark = (up_r.keep(*mark),)
+    up_r.second()
+    mark = (out_r.send(*mark), rows_grad[-1][0])
     for r in (gate_r, out_r):
         mark = (r.keep(*mark),)
         r.second()
-    layer_out = (mid + jnp.dot(after(act, *mark), full_down, preferred_element_type=f32)).astype(bf16)
-    mark = (layer_out,)
-
+    layer_outs, grad_qkv, grad_tokens, gain_a_parts = [], [], [], []
+
+    def finish_tokens(g, *others):
+        grad_h_attn = nt(after(grad_qkv[g], *others), full_qkv)
+        grad_norm, gain_part = norm_backward(grad_h_attn, of(x, g), of(scale_a, g), gain_a)
+        grad_tokens.append(parts[g][6] + grad_norm)
+        gain_a_parts.append(gain_part)
+        return grad_tokens[-1]
+
+    for g in range(groups):
+        act = after(parts[g][3], *mark)
+        layer_outs.append((parts[g][0] + jnp.dot(act, full_down, preferred_element_type=f32)).astype(bf16))
+        mark = (layer_outs[-1],)
+    mark = mark + tuple(rows_grad[-1])
+    first = Finish(early, *mark)
+    first.step(0)
     h_sides = [pieces_of(h_attn, False), pieces_of(h_attn, True)]
-    half = 3 * width // 2
-    late = []
-    grad_h_attn = 0.0
-    for g in range(groups):
-        final = g == groups - 1
-        if final:
-            first = Finish(early, *mark)
-            mark = mark + (first.step(0),)
-        grad_qkv.append(rows_of(after(arrived[g], *mark), heads))
-        pair = [Reduce(h_sides[0], grad_qkv[g][:, :half], False), Reduce(h_sides[1], grad_qkv[g][:, half:], True)]
-        for r in pair:
-            mark = (r.cross(*mark),)
-        if final:
-            for n in range(1, far):
-                first.step(n)
-        part = nt(after(grad_qkv[g], *mark), full_qkv[g])
-        grad_h_attn = grad_h_attn + part
-        mark = (part,)
-        for r in pair:
-            mark = (r.send(*mark),)
-        if final:
-            grad_tok_norm, gain_a_grad = norm_backward(after(grad_h_attn, *mark), x, scale_a, gain_a)
-            grad_tokens = grad_mid + grad_tok_norm
-            mark = (grad_tokens, first.total)
-        for r in pair:
-            mark = (r.keep(*mark),)
-        for r in pair:
-            r.second(*mark)
-        late += pair
-        if not final:
-            mark = mark + tuple(r.total for r in early + pair)
-    gain_grads = scatter_small(jnp.stack([gain_a_grad, gain_m_grad]))
+    for g in range(groups - 1):
+        grad_qkv.append(rows_of(jnp.concatenate(rows_grad[g], axis=1), micros))
+    grad_qkv.append(rows_of(jnp.concatenate([after(r, *mark) for r in rows_grad[-1]], axis=1), micros))
+    last_rows = grad_qkv[-1]
+    all_qkv = jnp.concatenate(grad_qkv, axis=0)
+    half = 3 * D // 2
+    late = [Reduce(h_sides[0], all_qkv[:, :half], False), Reduce(h_sides[1], all_qkv[:, half:], True)]
+    for r in late:
+        mark = (r.cross(*mark),)
+    for g in range(groups - 1):
+        mark = (finish_tokens(g, *mark),)
+    for r in late:
+        mark = (r.send(*mark),)
+    mark = mark + (first.total,)
+    g = groups - 1
+    grad_h_attn = nt(after(last_rows, *mark), full_qkv)
+    grad_norm, gain_part = norm_backward(grad_h_attn, of(x, g), of(scale_a, g), gain_a)
+    grad_tokens.append(parts[g][6] + grad_norm)
+    gain_a_parts.append(gain_part)
+    mark = (grad_tokens[-1],)
+    for r in late:
+        mark = (r.keep(*mark),)
+    for r in late:
+        r.second(*mark)
+    gain_grads = scatter_small(jnp.stack([sum(gain_a_parts), sum(p[8] for p in parts)]))
     second = Finish(late)
     for n in range(far):
+        if n:
+            first.step(n, hold=mark)
         second.step(n)
     down_grad, up_grad, gate_grad, out_grad = first.results()
-    terms = second.results()
-    qkv_grads = [
-        jnp.concatenate(terms[2 * g : 2 * g + 2], axis=1).reshape(-1, 1, heads, 3, HD) for g in range(groups)
-    ]
-    qkv_grad = jnp.concatenate(qkv_grads, axis=1).transpose(0, 3, 1, 2, 4)
+    qkv_grad = jnp.concatenate(second.results(), axis=1).reshape(-1, H, 3, HD).transpose(0, 2, 1, 3)
+    join = lambda arrays: jnp.concatenate(arrays, axis=0).reshape(MB, 1, rows, D)
 
     return (
-        layer_out.reshape(MB, 1, rows, D),
-        grad_tokens.reshape(MB, 1, rows, D),
+        join(layer_outs),
+        join(grad_tokens),
         qkv_grad.reshape(-1, 3 * D),
         out_grad,
         jnp.concatenate([gate_grad, up_grad], axis=1),

time: 2560 us -> 2420 us (0.945)
  waiting for transfers between devices: 1290 us -> 1020 us
  matrix products: 491 us -> 555 us
    ppermute x56 -> x50, waiting for transfers between devices: 1130 us -> 878 us  [swap(): lax.ppermute(block, axis, [(i, i ^ stride) for i in range(lax.axis_size(a...]
    all_to_all x4 -> x6, waiting for transfers between devices: 52.5 us -> 110 us  [to_rows(): return lax.all_to_all(whole, 'seq', 0, 0, tiled=True)]
    dot_general x5 -> x9, matrix products: 114 us -> 167 us  [the longest x2 51.3 us: shards(): up = jnp.dot(after(h_mlp, *mark), full_up, preferred_element_type=f32)]
    all_to_all x4, waiting for transfers between devices: 81.7 us -> 35.5 us  [to_heads(): return lax.all_to_all(split, 'seq', 0, 0, tiled=True)]
    convert_element_type x1 -> x4, local copies, waits for them, and re-layouts: 6.39 us -> 48.1 us  [shards(): x = tokens.reshape(MB * rows, D).astype(f32)]
    concatenate x2 -> x6, other arithmetic: 1.1 us -> 37.6 us  [the longest x1 11.5 us: shards(): acts = jnp.concatenate([p[3] for p in parts], axis=0)]
    all_gather x1, waiting for transfers between devices: 25.7 us -> 0.01 us  [shards(): gather = lambda w: lax.all_gather(w, ('dp', 'seq'), axis=0, tiled=True)]
    dot_general x7 -> x10, matrix products: 163 us -> 186 us  [nt(): return jnp.einsum('re,de->rd', a, b, preferred_element_type=f32)]
  transfers between devices with their start and end apart: 65 -> 61, of which waited for: 28 -> 24; matrix products, arithmetic and copies ran while one was open for 27% -> 35% of each run, Pallas kernels for 9% -> 5%
where the time goes in v4:
time: 2420 us; the launch traced here: 2410 us
  waiting for transfers between devices  1020 us (42%)
  matrix products  555 us (23%)
  Pallas kernels  276 us (11%)
  local copies, waits for them, and re-layouts  246 us (10%)
  other arithmetic  169 us (7%)
  starting transfers between devices  121 us (5%)
    ppermute x50, waiting for transfers between devices, swap(): lax.ppermute(block, axis, [(i, i ^ stride) for i in range(lax.axis_size(a...  878 us
    dot_general x10, matrix products, nt(): return jnp.einsum('re,de->rd', a, b, preferred_element_type=f32)  186 us
    dot_general x16, matrix products, tn(): lax.dot_general(a, b, (((0,), (0,)), ((), ())), preferred_element_type=f32)  184 us
    pallas_call x4, Pallas kernels, attend_back(): pl.pallas_call(functools.partial(backward_kernel, pair), grid_spec=pltpu....  132 us
    all_to_all x6, waiting for transfers between devices, to_rows(): return lax.all_to_all(whole, 'seq', 0, 0, tiled=True)  110 us
    pallas_call x2, Pallas kernels, attend(): pl.pallas_call(forward_kernel, grid_spec=pltpu.PrefetchScalarGridSpec(num...  93.6 us
    ppermute x50, starting transfers between devices, swap(): lax.ppermute(block, axis, [(i, i ^ stride) for i in range(lax.axis_size(a...  60.6 us
    dot_general x2, matrix products, shards(): up = jnp.dot(after(h_mlp, *mark), full_up, preferred_element_type=f32)  51.3 us
  transfers between devices with their start and end apart: 61, of which 24 were waited for; matrix products, arithmetic and copies ran while one was open for 35% of the time, Pallas kernels for 5%

profile of v4, /device:TPU:0, one launch (start us, length us, event | category | flops | bytes accessed | tf_op | source)
XLA Modules:
  0.0 2406.9 jit_solution(1657410646489158071)
XLA Ops:
  27.1 19.0 collective-permute-done.1
  48.5 34.0 %collective-permute-done.2 = bf16[2,256]{1,0:T(2,128)(2,1)S(1)} collective-permute-done((bf16[2,256]{1,0:T(2,128)(2,1)S(1)}, bf16[2,256]{1,0:T(2,128)(2,1)S(1)}, u32[]{:S(2)}, u32[]{:S(2)}) %collective-permute-start.2) | collective-permute-done | bytes 1056 | tf_op jit(solution)/shard_map/ppermute | solution.py:40
  87.4 11.7 collective-permute-start.7
  100.6 83.5 %collective-permute-done.6 = bf16[64,11008]{1,0:T(8,128)(2,1)S(1)} collective-permute-done((bf16[64,11008]{1,0:T(8,128)(2,1)}, bf16[64,11008]{1,0:T(8,128)(2,1)S(1)}, u32[]{:S(2)}, u32[]{:S(2)}) %collective-permute-start.6) | collective-permute-done | bytes 1409056 | tf_op jit(solution)/shard_map/ppermute | solution.py:40
  184.2 29.8 %collective-permute-done.7 = bf16[128,7552]{1,0:T(8,128)(2,1)S(1)} collective-permute-done((bf16[128,7552]{1,0:T(8,128)(2,1)}, bf16[128,7552]{1,0:T(8,128)(2,1)S(1)}, u32[]{:S(2)}, u32[]{:S(2)}) %collective-permute-start.7) | collective-permute-done | bytes 1933344 | tf_op jit(solution)/shard_map/ppermute | solution.py:40
  223.7 84.7 %collective-permute-done.8 = bf16[128,11008]{1,0:T(8,128)(2,1)} collective-permute-done((bf16[128,11008]{1,0:T(8,128)(2,1)S(1)}, bf16[128,11008]{1,0:T(8,128)(2,1)}, u32[]{:S(2)}, u32[]{:S(2)}) %collective-permute-start.8) | collective-permute-done | bytes 2818080 | tf_op jit(solution)/shard_map/ppermute | solution.py:40
  312.0 18.7 convolution_convert_fusion.4
  336.5 10.9 all-to-all-start
  356.5 77.6 %collective-permute-done.9.refs_1_ = bf16[256,7552]{1,0:T(8,128)(2,1)} collective-permute-done((bf16[256,7552]{1,0:T(8,128)(2,1)}, bf16[256,7552]{1,0:T(8,128)(2,1)}, u32[]{:S(2)}, u32[]{:S(2)}) %collective-permute-start.9) | collective-permute-done | bytes 3866656 | tf_op jit(solution)/shard_map/ppermute | solution.py:40
  434.1 103.9 %collective-permute-done.10.refs_1_ = bf16[256,11008]{1,0:T(8,128)(2,1)} collective-permute-done((bf16[256,11008]{1,0:T(8,128)(2,1)}, bf16[256,11008]{1,0:T(8,128)(2,1)}, u32[]{:S(2)}, u32[]{:S(2)}) %collective-permute-start.10) | collective-permute-done | bytes 5636128 | tf_op jit(solution)/shard_map/ppermute | solution.py:40
  538.0 46.9 %attend.2 = (bf16[8,2,512,128]{3,2,1,0:T(8,128)(2,1)}, f32[2,1,4096]{2,1,0:T(1,128)S(1)}) custom-call(s32[2,4,8]{2,1,0:T(4,128)S(1)} %pad_add_fusion.2.bounds, bf16[8,2,512,384]{3,2,1,0:T(8,128)(2,1)} %all-to-all-done.q_ref.k_ref.v_ref, bf16[8,2,512,384]{3,2,1,0:T(8,128)(2,1)} %all-to-all-done.q_ref.k_ref.v_ref, ...), custom_call_target="tpu_custom_call" | custom-call | flops 15032385536 | bytes 8388608 | tf_op jit(solution)/shard_map/attend/pallas_call | solution.py:306
  593.5 43.9 %all-to-all-done.1 = bf16[8,2,512,128]{3,2,1,0:T(8,128)(2,1)S(1)} async-done(((bf16[8,2,512,128]{3,2,1,0:T(8,128)(2,1)}), bf16[8,2,512,128]{3,2,1,0:T(8,128)(2,1)S(1)}, u32[]{:S(2)}, u32[]{:S(2)}) %all-to-all-start.1) | async-done | bytes 2097184 | tf_op jit(solution)/shard_map/all_to_all | solution.py:442
  641.6 19.3 convolution_convert_fusion.3
  672.0 59.5 %collective-permute-done.12.refs_3_ = bf16[256,7552]{1,0:T(8,128)(2,1)} collective-permute-done((bf16[256,7552]{1,0:T(8,128)(2,1)}, bf16[256,7552]{1,0:T(8,128)(2,1)}, u32[]{:S(2)}, u32[]{:S(2)}) %collective-permute-start.12) | collective-permute-done | bytes 3866656 | tf_op jit(solution)/shard_map/ppermute | solution.py:40
  731.4 100.7 %collective-permute-done.11.refs_2_ = bf16[256,7552]{1,0:T(8,128)(2,1)} collective-permute-done((bf16[256,7552]{1,0:T(8,128)(2,1)}, bf16[256,7552]{1,0:T(8,128)(2,1)}, u32[]{:S(2)}, u32[]{:S(2)}) %collective-permute-start.11) | collective-permute-done | bytes 3866656 | tf_op jit(solution)/shard_map/ppermute | solution.py:40
  850.7 19.3 place.2
  880.6 19.7 fusion.120
  900.3 30.4 %place.3 = (bf16[2048,5504]{1,0:T(8,128)(2,1)}, bf16[2048,5504]{1,0:T(8,128)(2,1)}) custom-call(s32[32]{0:T(128)S(1)} %xor_multiply_fusion.target, bf16[256,11008]{1,0:T(8,128)(2,1)} %constant_dynamic-update-slice_fusion.7.refs_0_, bf16[256,11008]{1,0:T(8,128)(2,1)} %collective-permute-done.10.refs_1_, bf16[256,11008]{1,0:T(8,128)(2,1)} %collective-permute-done.17.refs_2_, ...), custom_call_target="tpu_custom_call" | custom-call | bytes 90177536 | tf_op jit(solution)/shard_map/place/pallas_call | solution.py:141
  930.8 31.1 %reshape.490 = bf16[5504,2048]{1,0:T(8,128)(2,1)} reshape(bf16[2048,5504]{1,0:T(8,128)(2,1)} %get-tuple-element.108) | data formatting | bytes 45088768 | tf_op jit(solution)/shard_map/reshape | solution.py:539
  961.9 46.7 %attend.3 = (bf16[8,2,512,128]{3,2,1,0:T(8,128)(2,1)}, f32[2,1,4096]{2,1,0:T(1,128)S(1)}) custom-call(s32[2,4,8]{2,1,0:T(4,128)S(1)} %pad_add_fusion.3.bounds, bf16[8,2,512,384]{3,2,1,0:T(8,128)(2,1)} %all-to-all-done.2.q_ref.k_ref.v_ref, bf16[8,2,512,384]{3,2,1,0:T(8,128)(2,1)} %all-to-all-done.2.q_ref.k_ref.v_ref, ...), custom_call_target="tpu_custom_call" | custom-call | flops 15032385536 | bytes 8388608 | tf_op jit(solution)/shard_map/attend/pallas_call | solution.py:306
  1013.1 26.0 %multiply_convert_fusion.5 = (bf16[512,5504]{1,0:T(8,128)(2,1)}, f32[512,5504]{1,0:T(8,128)}) fusion(f32[512,5504]{1,0:T(8,128)} %fusion.120, bf16[512,2048]{1,0:T(8,128)(2,1)S(1)} %multiply_convert_fusion.9, bf16[2048,5504]{1,0:T(8,128)(2,1)} %get-tuple-element.106), kind=kOutput, calls=%fused_computation.24 | convolution fusion | flops 11559632896 | bytes 52822016 | tf_op jit(solution)/shard_map/dot_general | solution.py:565
  1039.1 25.3 %multiply_convert_fusion.3 = (bf16[512,5504]{1,0:T(8,128)(2,1)}, bf16[512,5504]{1,0:T(8,128)(2,1)}) fusion(f32[512,5504]{1,0:T(8,128)} %fusion.120, f32[512,5504]{1,0:T(8,128)} %get-tuple-element.277, bf16[512,2048]{1,0:T(8,128)(2,1)} %get-tuple-element.107, bf16[5504,2048]{1,0:T(8,128)(2,1)} %reshape.490), kind=kOutput, calls=%fused_computation.22 | convolution fusion | flops 11579359232 | bytes 58458112 | tf_op jit(solution)/shard_map/re,de->rd/dot_general | solution.py:463
  1064.4 19.6 fusion.121
  1084.0 19.6 multiply_reduce_fusion.2
  1127.2 10.3 multiply_reduce_fusion.8
  1141.2 19.0 fusion.122
  1160.2 25.3 %multiply_convert_fusion.2 = (bf16[512,5504]{1,0:T(8,128)(2,1)}, f32[512,5504]{1,0:T(8,128)}) fusion(f32[512,5504]{1,0:T(8,128)} %fusion.122, bf16[512,2048]{1,0:T(8,128)(2,1)} %copy-done.38, bf16[2048,5504]{1,0:T(8,128)(2,1)} %get-tuple-element.106), kind=kOutput, calls=%fused_computation.19 | convolution fusion | flops 11559632896 | bytes 52822016 | tf_op jit(solution)/shard_map/dot_general | solution.py:565
  1185.6 11.5 pad_maximum_fusion
  1197.0 33.1 %attend_back.4 = bf16[8,1,512,384]{3,2,1,0:T(8,128)(2,1)} custom-call(s32[2,4,8]{2,1,0:T(4,128)S(1)} %copy-done.8, bf16[8,2,512,384]{3,2,1,0:T(8,128)(2,1)} %all-to-all-done.q_ref.k_ref.v_ref, bf16[8,2,512,384]{3,2,1,0:T(8,128)(2,1)} %all-to-all-done.q_ref.k_ref.v_ref, bf16[8,2,512,384]{3,2,1,0:T(8,128)(2,1)} %all-to-all-done.q_ref.k_ref.v_ref, ...), custom_call_target="tpu_custom_call" | custom-call | flops 18790481920 | bytes 8388608 | tf_op jit(solution)/shard_map/attend_back/pallas_call | solution.py:387
  1230.2 33.4 %attend_back.5 = bf16[8,1,512,384]{3,2,1,0:T(8,128)(2,1)} custom-call(s32[2,4,8]{2,1,0:T(4,128)S(1)} %copy-done.8, bf16[8,2,512,384]{3,2,1,0:T(8,128)(2,1)} %all-to-all-done.q_ref.k_ref.v_ref, bf16[8,2,512,384]{3,2,1,0:T(8,128)(2,1)} %all-to-all-done.q_ref.k_ref.v_ref, bf16[8,2,512,384]{3,2,1,0:T(8,128)(2,1)} %all-to-all-done.q_ref.k_ref.v_ref, ...), custom_call_target="tpu_custom_call" | custom-call | flops 18790481920 | bytes 8388608 | tf_op jit(solution)/shard_map/attend_back/pallas_call | solution.py:387
  1263.6 31.2 %convolution_convert_fusion = bf16[5504,2048]{1,0:T(8,128)(2,1)} fusion(bf16[1024,5504]{1,0:T(8,128)(2,1)} %pad_maximum_fusion, bf16[1024,2048]{1,0:T(8,128)(2,1)S(1)} %bitcast.357), kind=kOutput, calls=%fused_computation | convolution fusion | flops 23096721408 | bytes 38010880 | tf_op jit(solution)/shard_map/dot_general | solution.py:161
  1327.3 55.1 %all-to-all-done.5 = bf16[8,1,512,384]{3,2,1,0:T(8,128)(2,1)S(1)} async-done(((bf16[8,1,512,384]{3,2,1,0:T(8,128)(2,1)}), bf16[8,1,512,384]{3,2,1,0:T(8,128)(2,1)S(1)}, u32[]{:S(2)}, u32[]{:S(2)}) %all-to-all-start.5) | async-done | bytes 3145760 | tf_op jit(solution)/shard_map/all_to_all | solution.py:442
  1382.5 26.2 %multiply_convert_fusion = (bf16[512,5504]{1,0:T(8,128)(2,1)}, bf16[512,5504]{1,0:T(8,128)(2,1)}) fusion(f32[512,5504]{1,0:T(8,128)} %fusion.122, f32[512,5504]{1,0:T(8,128)} %get-tuple-element.282, bf16[512,2048]{1,0:T(8,128)(2,1)} %get-tuple-element.117, bf16[5504,2048]{1,0:T(8,128)(2,1)} %reshape.490), kind=kOutput, calls=%fused_computation.17 | convolution fusion | flops 11579359232 | bytes 58458112 | tf_op jit(solution)/shard_map/re,de->rd/dot_general | solution.py:463
  1418.6 19.7 convolution_convert_fusion.2
  1446.2 11.2 copy.125
  1457.3 19.3 convolution_convert_fusion.1
  1487.4 19.5 fusion.123
  1506.9 12.0 add_convert_fusion.3
  1520.9 18.1 multiply_reduce_fusion.1
  1542.4 10.7 all-to-all-done.6
  1567.8 11.8 add_convert_fusion.2
  1585.8 24.4 %collective-permute-done.26 = bf16[1376,2048]{1,0:T(8,128)(2,1)} collective-permute-done((bf16[1376,2048]{1,0:T(8,128)(2,1)}, bf16[1376,2048]{1,0:T(8,128)(2,1)}, u32[]{:S(2)}, u32[]{:S(2)}) %collective-permute-start.26) | collective-permute-done | bytes 5636128 | tf_op jit(solution)/shard_map/ppermute | solution.py:40
  1610.2 13.4 fusion.1
  1637.5 35.5 %all-to-all-done.7.do_ref = bf16[8,2,512,128]{3,2,1,0:T(8,128)(2,1)S(1)} async-done(((bf16[8,2,512,128]{3,2,1,0:T(8,128)(2,1)}), bf16[8,2,512,128]{3,2,1,0:T(8,128)(2,1)S(1)}, u32[]{:S(2)}, u32[]{:S(2)}) %all-to-all-start.7) | async-done | bytes 2097184 | tf_op jit(solution)/shard_map/all_to_all | solution.py:438
  1673.0 33.0 %attend_back.6 = bf16[8,1,512,384]{3,2,1,0:T(8,128)(2,1)} custom-call(s32[2,4,8]{2,1,0:T(4,128)S(1)} %copy-done.6, bf16[8,2,512,384]{3,2,1,0:T(8,128)(2,1)} %all-to-all-done.2.q_ref.k_ref.v_ref, bf16[8,2,512,384]{3,2,1,0:T(8,128)(2,1)} %all-to-all-done.2.q_ref.k_ref.v_ref, bf16[8,2,512,384]{3,2,1,0:T(8,128)(2,1)} %all-to-all-done.2.q_ref.k_ref.v_ref, ...), custom_call_target="tpu_custom_call" | custom-call | flops 18790481920 | bytes 8388608 | tf_op jit(solution)/shard_map/attend_back/pallas_call | solution.py:387
  1713.9 32.8 %attend_back.7 = bf16[8,1,512,384]{3,2,1,0:T(8,128)(2,1)} custom-call(s32[2,4,8]{2,1,0:T(4,128)S(1)} %copy-done.6, bf16[8,2,512,384]{3,2,1,0:T(8,128)(2,1)} %all-to-all-done.2.q_ref.k_ref.v_ref, bf16[8,2,512,384]{3,2,1,0:T(8,128)(2,1)} %all-to-all-done.2.q_ref.k_ref.v_ref, bf16[8,2,512,384]{3,2,1,0:T(8,128)(2,1)} %all-to-all-done.2.q_ref.k_ref.v_ref, ...), custom_call_target="tpu_custom_call" | custom-call | flops 18790481920 | bytes 8388608 | tf_op jit(solution)/shard_map/attend_back/pallas_call | solution.py:387
  1767.5 11.5 reshape.531
  1779.0 11.6 copy.131
  1790.6 13.2 copy.133
  1803.8 11.8 reshape.530
  1864.2 11.8 fusion.17
  1889.1 13.6 collective-permute-done.30
  1906.1 19.9 add_convert_fusion.9
  1930.9 19.3 add_convert_fusion.8
  1964.1 11.3 convolution_convert_fusion.6
  1975.4 10.6 convolution_convert_fusion.5
  1991.0 21.1 collective-permute-done.36
  2028.3 20.4 multiply_reduce_fusion.4
  2077.0 52.1 %collective-permute-done.37 = bf16[2,64,18560]{2,1,0:T(8,128)(2,1)} collective-permute-done((bf16[2,64,18560]{2,1,0:T(8,128)(2,1)}, bf16[2,64,18560]{2,1,0:T(8,128)(2,1)}, u32[]{:S(2)}, u32[]{:S(2)}) %collective-permute-start.37) | collective-permute-done | bytes 4751392 | tf_op jit(solution)/shard_map/ppermute | solution.py:40
  2134.7 20.1 multiply_reduce_fusion.3
  2198.3 84.7 %collective-permute-done.47 = f32[2,256]{1,0:T(2,128)S(1)} collective-permute-done((f32[2,256]{1,0:T(2,128)S(1)}, f32[2,256]{1,0:T(2,128)S(1)}, u32[]{:S(2)}, u32[]{:S(2)}) %collective-permute-start.47) | collective-permute-done | bytes 2080 | tf_op jit(solution)/shard_map/ppermute | solution.py:40
  2298.1 22.5 collective-permute-done.41
  2327.3 30.8 %collective-permute-done.42 = bf16[2,64,6144]{2,1,0:T(8,128)(2,1)S(1)} collective-permute-done((bf16[2,64,6144]{2,1,0:T(8,128)(2,1)S(1)}, bf16[2,64,6144]{2,1,0:T(8,128)(2,1)S(1)}, u32[]{:S(2)}, u32[]{:S(2)}) %collective-permute-start.42) | collective-permute-done | bytes 1572896 | tf_op jit(solution)/shard_map/ppermute | solution.py:40
  2366.6 28.3 %collective-permute-done.43 = bf16[1,64,6144]{2,1,0:T(8,128)(2,1)} collective-permute-done((bf16[1,64,6144]{2,1,0:T(8,128)(2,1)}, bf16[1,64,6144]{2,1,0:T(8,128)(2,1)}, u32[]{:S(2)}, u32[]{:S(2)}) %collective-permute-start.43) | collective-permute-done | bytes 786464 | tf_op jit(solution)/shard_map/ppermute | solution.py:40
  (469 shorter events, 488.0 us)
Async XLA Ops:
  7.2 304.8 %all-gather.2.cloned.1.call-start = ((), (), s32[]{:S(2)}) async-start(), calls=%async_computation.10 | async-start | bytes 25952256 | tf_op jit(solution)/shard_map/all_gather | solution.py:469
  12.1 70.5 %collective-permute-start.5 = (bf16[64,7552]{1,0:T(8,128)(2,1)S(1)}, bf16[64,7552]{1,0:T(8,128)(2,1)S(1)}, u32[]{:S(2)}, u32[]{:S(2)}) collective-permute-start(bf16[64,7552]{1,0:T(8,128)(2,1)S(1)} %pad_maximum_fusion.29), channel_id=1, source_target_pairs={{0,4},{1,5},{2,6},{3,7},{4,0},{5,1},{6,2},{7,3},{8,12},{9,13},{10,... | collective-permute-start | bytes 2899976 | tf_op jit(solution)/shard_map/ppermute | solution.py:40
  16.2 9.2 collective-permute-start
  25.5 20.5 collective-permute-start.1
  46.1 36.3 %collective-permute-start.2 = (bf16[2,256]{1,0:T(2,128)(2,1)S(1)}, bf16[2,256]{1,0:T(2,128)(2,1)S(1)}, u32[]{:S(2)}, u32[]{:S(2)}) collective-permute-start(bf16[2,256]{1,0:T(2,128)(2,1)S(1)} %pad_maximum_fusion.33), channel_id=1, source_target_pairs={{0,4},{1,5},{2,6},{3,7},{4,0},{5,1},{6,2},{7,3},{8,12},{9,13},{10,... | collective-permute-start | bytes 3080 | tf_op jit(solution)/shard_map/ppermute | solution.py:40
  82.5 1.5 collective-permute-start.3
  83.9 100.2 %collective-permute-start.6 = (bf16[64,11008]{1,0:T(8,128)(2,1)}, bf16[64,11008]{1,0:T(8,128)(2,1)S(1)}, u32[]{:S(2)}, u32[]{:S(2)}) collective-permute-start(bf16[64,11008]{1,0:T(8,128)(2,1)} %pad_maximum_fusion.23), channel_id=1, source_target_pairs={{0,4},{1,5},{2,6},{3,7},{4,0},{5,1},{6,2},{7,3},{8,12},{9,13},{10,... | collective-permute-start | bytes 4227080 | tf_op jit(solution)/shard_map/ppermute | solution.py:40
  84.0 132.1 %collective-permute-start.4 = (bf16[2,1024]{1,0:T(2,128)(2,1)S(1)}, bf16[2,1024]{1,0:T(2,128)(2,1)S(1)}, u32[]{:S(2)}, u32[]{:S(2)}) collective-permute-start(bf16[2,1024]{1,0:T(2,128)(2,1)S(1)} %pad_maximum_fusion.31), channel_id=1, source_target_pairs={{0,16},{8,24},{16,0},{24,8},{1,17},{9,25},{17,1},{25,9},{2,18},{10... | collective-permute-start | bytes 12296 | tf_op jit(solution)/shard_map/ppermute | solution.py:40
  87.4 126.6 %collective-permute-start.7 = (bf16[128,7552]{1,0:T(8,128)(2,1)}, bf16[128,7552]{1,0:T(8,128)(2,1)S(1)}, u32[]{:S(2)}, u32[]{:S(2)}) collective-permute-start(bf16[128,7552]{1,0:T(8,128)(2,1)} %get-tuple-element.242), channel_id=1, source_target_pairs={{0,2},{1,3},{2,0},{3,1},{4,6},{5,7},{6,4},{7,5},{8,10},{9,11},{10,... | collective-permute-start | bytes 5799944 | tf_op jit(solution)/shard_map/ppermute | solution.py:40
  215.4 93.0 %collective-permute-start.8 = (bf16[128,11008]{1,0:T(8,128)(2,1)S(1)}, bf16[128,11008]{1,0:T(8,128)(2,1)}, u32[]{:S(2)}, u32[]{:S(2)}) collective-permute-start(bf16[128,11008]{1,0:T(8,128)(2,1)S(1)} %constant_dynamic-update-slice_fusion.2), channel_id=1, source_target_pairs={{0,2},{1,3},{2,0},{3,1},{4,6},{5,7},{6,4},{7,5},{8,10},{9,11},{10,... | collective-permute-start | bytes 8454152 | tf_op jit(solution)/shard_map/ppermute | solution.py:40
  216.7 661.5 %copy-start.54 = (f32[1,2048]{1,0:T(1,128)}, f32[1,2048]{1,0:T(1,128)S(1)}, u32[]{:S(2)}) copy-start(f32[1,2048]{1,0:T(1,128)S(1)} %get-tuple-element.250) | copy-start | bytes 24580
  336.5 201.4 %all-to-all-start = ((bf16[8,2,512,384]{3,2,1,0:T(8,128)(2,1)}), bf16[8,2,512,384]{3,2,1,0:T(8,128)(2,1)}, u32[]{:S(2)}, u32[]{:S(2)}) async-start(bf16[8,2,512,384]{3,2,1,0:T(8,128)(2,1)} %bitcast.359), calls=%async_computation | async-start | bytes 12582912 | tf_op jit(solution)/shard_map/all_to_all | solution.py:438
  347.4 190.5 %collective-permute-start.10 = (bf16[256,11008]{1,0:T(8,128)(2,1)}, bf16[256,11008]{1,0:T(8,128)(2,1)}, u32[]{:S(2)}, u32[]{:S(2)}) collective-permute-start(bf16[256,11008]{1,0:T(8,128)(2,1)} %constant_dynamic-update-slice_fusion.7.refs_0_), channel_id=1, source_target_pairs={{0,1},{1,0},{2,3},{3,2},{4,5},{5,4},{6,7},{7,6},{8,9},{9,8},{10,11... | collective-permute-start | bytes 16908296 | tf_op jit(solution)/shard_map/ppermute | solution.py:40
  349.5 84.7 %collective-permute-start.9 = (bf16[256,7552]{1,0:T(8,128)(2,1)}, bf16[256,7552]{1,0:T(8,128)(2,1)}, u32[]{:S(2)}, u32[]{:S(2)}) collective-permute-start(bf16[256,7552]{1,0:T(8,128)(2,1)} %constant_dynamic-update-slice_fusion.4.refs_0_), channel_id=1, source_target_pairs={{0,16},{8,24},{16,0},{24,8},{1,17},{9,25},{17,1},{25,9},{2,18},{10... | collective-permute-start | bytes 11599880 | tf_op jit(solution)/shard_map/ppermute | solution.py:40
  356.4 228.4 %copy-start.7 = (s32[2,4,8]{2,1,0:T(4,128)}, s32[2,4,8]{2,1,0:T(4,128)S(1)}, u32[]{:S(2)}) copy-start(s32[2,4,8]{2,1,0:T(4,128)S(1)} %pad_add_fusion.2.bounds) | copy-start | bytes 772
  356.5 605.4 %copy-start.1 = (s32[2,1,4096]{2,1,0:T(1,128)}, s32[2,1,4096]{2,1,0:T(1,128)S(1)}, u32[]{:S(2)}) copy-start(s32[2,1,4096]{2,1,0:T(1,128)S(1)} %get-tuple-element.291.lo_ref) | copy-start | bytes 98308
  584.9 52.6 %all-to-all-start.1 = ((bf16[8,2,512,128]{3,2,1,0:T(8,128)(2,1)}), bf16[8,2,512,128]{3,2,1,0:T(8,128)(2,1)S(1)}, u32[]{:S(2)}, u32[]{:S(2)}) async-start(bf16[8,2,512,128]{3,2,1,0:T(8,128)(2,1)} %get-tuple-element.87.o_ref), calls=%async_computation.1 | async-start | bytes 4194304 | tf_op jit(solution)/shard_map/all_to_all | solution.py:442
  589.4 142.0 %collective-permute-start.12 = (bf16[256,7552]{1,0:T(8,128)(2,1)}, bf16[256,7552]{1,0:T(8,128)(2,1)}, u32[]{:S(2)}, u32[]{:S(2)}) collective-permute-start(bf16[256,7552]{1,0:T(8,128)(2,1)} %collective-permute-done.9.refs_1_), channel_id=1, source_target_pairs={{0,1},{1,0},{2,3},{3,2},{4,5},{5,4},{6,7},{7,6},{8,9},{9,8},{10,11... | collective-permute-start | bytes 11599880 | tf_op jit(solution)/shard_map/ppermute | solution.py:40
  591.4 240.7 %collective-permute-start.14 = (bf16[256,7552]{1,0:T(8,128)(2,1)}, bf16[256,7552]{1,0:T(8,128)(2,1)}, u32[]{:S(2)}, u32[]{:S(2)}) collective-permute-start(bf16[256,7552]{1,0:T(8,128)(2,1)} %collective-permute-done.9.refs_1_), channel_id=1, source_target_pairs={{0,8},{8,0},{16,24},{24,16},{1,9},{9,1},{17,25},{25,17},{2,10},{10... | collective-permute-start | bytes 11599880 | tf_op jit(solution)/shard_map/ppermute | solution.py:40
  591.4 240.7 %collective-permute-start.11 = (bf16[256,7552]{1,0:T(8,128)(2,1)}, bf16[256,7552]{1,0:T(8,128)(2,1)}, u32[]{:S(2)}, u32[]{:S(2)}) collective-permute-start(bf16[256,7552]{1,0:T(8,128)(2,1)} %constant_dynamic-update-slice_fusion.4.refs_0_), channel_id=1, source_target_pairs={{0,1},{1,0},{2,3},{3,2},{4,5},{5,4},{6,7},{7,6},{8,9},{9,8},{10,11... | collective-permute-start | bytes 11599880 | tf_op jit(solution)/shard_map/ppermute | solution.py:40
  591.5 241.2 %collective-permute-start.18 = (bf16[256,11008]{1,0:T(8,128)(2,1)}, bf16[256,11008]{1,0:T(8,128)(2,1)}, u32[]{:S(2)}, u32[]{:S(2)}) collective-permute-start(bf16[256,11008]{1,0:T(8,128)(2,1)} %collective-permute-done.10.refs_1_), channel_id=1, source_target_pairs={{0,16},{8,24},{16,0},{24,8},{1,17},{9,25},{17,1},{25,9},{2,18},{10... | collective-permute-start | bytes 16908296 | tf_op jit(solution)/shard_map/ppermute | solution.py:40
  592.7 243.7 %collective-permute-start.17 = (bf16[256,11008]{1,0:T(8,128)(2,1)}, bf16[256,11008]{1,0:T(8,128)(2,1)}, u32[]{:S(2)}, u32[]{:S(2)}) collective-permute-start(bf16[256,11008]{1,0:T(8,128)(2,1)} %constant_dynamic-update-slice_fusion.7.refs_0_), channel_id=1, source_target_pairs={{0,16},{8,24},{16,0},{24,8},{1,17},{9,25},{17,1},{25,9},{2,18},{10... | collective-permute-start | bytes 16908296 | tf_op jit(solution)/shard_map/ppermute | solution.py:40
  666.7 295.3 %all-to-all-start.2 = ((bf16[8,2,512,384]{3,2,1,0:T(8,128)(2,1)}), bf16[8,2,512,384]{3,2,1,0:T(8,128)(2,1)}, u32[]{:S(2)}, u32[]{:S(2)}) async-start(bf16[8,2,512,384]{3,2,1,0:T(8,128)(2,1)} %bitcast.358), calls=%async_computation.2 | async-start | bytes 12582912 | tf_op jit(solution)/shard_map/all_to_all | solution.py:438
  731.4 101.3 %collective-permute-start.13 = (bf16[256,7552]{1,0:T(8,128)(2,1)}, bf16[256,7552]{1,0:T(8,128)(2,1)}, u32[]{:S(2)}, u32[]{:S(2)}) collective-permute-start(bf16[256,7552]{1,0:T(8,128)(2,1)} %constant_dynamic-update-slice_fusion.4.refs_0_), channel_id=1, source_target_pairs={{0,8},{8,0},{16,24},{24,16},{1,9},{9,1},{17,25},{25,17},{2,10},{10... | collective-permute-start | bytes 11599880 | tf_op jit(solution)/shard_map/ppermute | solution.py:40
  832.1 7.0 collective-permute-start.16
  832.1 18.6 collective-permute-start.15
  832.7 67.7 %collective-permute-start.20 = (bf16[256,11008]{1,0:T(8,128)(2,1)}, bf16[256,11008]{1,0:T(8,128)(2,1)}, u32[]{:S(2)}, u32[]{:S(2)}) collective-permute-start(bf16[256,11008]{1,0:T(8,128)(2,1)} %collective-permute-done.10.refs_1_), channel_id=1, source_target_pairs={{0,8},{8,0},{16,24},{24,16},{1,9},{9,1},{17,25},{25,17},{2,10},{10... | collective-permute-start | bytes 16908296 | tf_op jit(solution)/shard_map/ppermute | solution.py:40
  832.8 67.6 %collective-permute-start.19 = (bf16[256,11008]{1,0:T(8,128)(2,1)}, bf16[256,11008]{1,0:T(8,128)(2,1)}, u32[]{:S(2)}, u32[]{:S(2)}) collective-permute-start(bf16[256,11008]{1,0:T(8,128)(2,1)} %constant_dynamic-update-slice_fusion.7.refs_0_), channel_id=1, source_target_pairs={{0,8},{8,0},{16,24},{24,16},{1,9},{9,1},{17,25},{25,17},{2,10},{10... | collective-permute-start | bytes 16908296 | tf_op jit(solution)/shard_map/ppermute | solution.py:40
  836.4 63.9 %collective-permute-start.22 = (bf16[256,11008]{1,0:T(8,128)(2,1)}, bf16[256,11008]{1,0:T(8,128)(2,1)}, u32[]{:S(2)}, u32[]{:S(2)}) collective-permute-start(bf16[256,11008]{1,0:T(8,128)(2,1)} %collective-permute-done.18.refs_3_), channel_id=1, source_target_pairs={{0,8},{8,0},{16,24},{24,16},{1,9},{9,1},{17,25},{25,17},{2,10},{10... | collective-permute-start | bytes 16908296 | tf_op jit(solution)/shard_map/ppermute | solution.py:40
  839.1 61.2 %collective-permute-start.21 = (bf16[256,11008]{1,0:T(8,128)(2,1)}, bf16[256,11008]{1,0:T(8,128)(2,1)}, u32[]{:S(2)}, u32[]{:S(2)}) collective-permute-start(bf16[256,11008]{1,0:T(8,128)(2,1)} %collective-permute-done.17.refs_2_), channel_id=1, source_target_pairs={{0,8},{8,0},{16,24},{24,16},{1,9},{9,1},{17,25},{25,17},{2,10},{10... | collective-permute-start | bytes 16908296 | tf_op jit(solution)/shard_map/ppermute | solution.py:40
  1008.6 108.3 %all-to-all-start.3 = ((bf16[8,2,512,128]{3,2,1,0:T(8,128)(2,1)}), bf16[8,2,512,128]{3,2,1,0:T(8,128)(2,1)}, u32[]{:S(2)}, u32[]{:S(2)}) async-start(bf16[8,2,512,128]{3,2,1,0:T(8,128)(2,1)} %get-tuple-element.94.o_ref), calls=%async_computation.3 | async-start | bytes 4194304 | tf_op jit(solution)/shard_map/all_to_all | solution.py:442
  1116.9 80.1 %all-to-all-start.4 = ((bf16[8,2,512,128]{3,2,1,0:T(8,128)(2,1)}), bf16[8,2,512,128]{3,2,1,0:T(8,128)(2,1)S(1)}, u32[]{:S(2)}, u32[]{:S(2)}) async-start(bf16[8,2,512,128]{3,2,1,0:T(8,128)(2,1)} %bitcast.390), calls=%async_computation.4 | async-start | bytes 4194304 | tf_op jit(solution)/shard_map/all_to_all | solution.py:438
  1304.8 103.8 %collective-permute-start.23 = (bf16[2752,2048]{1,0:T(8,128)(2,1)}, bf16[2752,2048]{1,0:T(8,128)(2,1)}, u32[]{:S(2)}, u32[]{:S(2)}) collective-permute-start(bf16[2752,2048]{1,0:T(8,128)(2,1)} %bitcast.47), channel_id=1, source_target_pairs={{0,8},{8,0},{16,24},{24,16},{1,9},{9,1},{17,25},{25,17},{2,10},{10... | collective-permute-start | bytes 33816584 | tf_op jit(solution)/shard_map/ppermute | solution.py:40
  1304.8 77.6 %all-to-all-start.5 = ((bf16[8,1,512,384]{3,2,1,0:T(8,128)(2,1)}), bf16[8,1,512,384]{3,2,1,0:T(8,128)(2,1)S(1)}, u32[]{:S(2)}, u32[]{:S(2)}) async-start(bf16[8,1,512,384]{3,2,1,0:T(8,128)(2,1)} %attend_back.4), calls=%async_computation.5 | async-start | bytes 6291456 | tf_op jit(solution)/shard_map/all_to_all | solution.py:442
  1438.3 68.6 %collective-permute-start.24 = (bf16[1024,5504]{1,0:T(8,128)(2,1)}, bf16[1024,5504]{1,0:T(8,128)(2,1)}, u32[]{:S(2)}, u32[]{:S(2)}) collective-permute-start(bf16[1024,5504]{1,0:T(8,128)(2,1)} %convolution_convert_fusion.2), channel_id=1, source_target_pairs={{0,8},{8,0},{16,24},{24,16},{1,9},{9,1},{17,25},{25,17},{2,10},{10... | collective-permute-start | bytes 33816584 | tf_op jit(solution)/shard_map/ppermute | solution.py:40
  1476.6 91.2 %collective-permute-start.25 = (bf16[1024,5504]{1,0:T(8,128)(2,1)}, bf16[1024,5504]{1,0:T(8,128)(2,1)}, u32[]{:S(2)}, u32[]{:S(2)}) collective-permute-start(bf16[1024,5504]{1,0:T(8,128)(2,1)} %convolution_convert_fusion.1), channel_id=1, source_target_pairs={{0,8},{8,0},{16,24},{24,16},{1,9},{9,1},{17,25},{25,17},{2,10},{10... | collective-permute-start | bytes 33816584 | tf_op jit(solution)/shard_map/ppermute | solution.py:40
  1477.1 76.0 %all-to-all-start.6 = ((bf16[8,1,512,384]{3,2,1,0:T(8,128)(2,1)}), bf16[8,1,512,384]{3,2,1,0:T(8,128)(2,1)}, u32[]{:S(2)}, u32[]{:S(2)}) async-start(bf16[8,1,512,384]{3,2,1,0:T(8,128)(2,1)} %attend_back.5), calls=%async_computation.6 | async-start | bytes 6291456 | tf_op jit(solution)/shard_map/all_to_all | solution.py:442
  1486.5 123.7 %collective-permute-start.26 = (bf16[1376,2048]{1,0:T(8,128)(2,1)}, bf16[1376,2048]{1,0:T(8,128)(2,1)}, u32[]{:S(2)}, u32[]{:S(2)}) collective-permute-start(bf16[1376,2048]{1,0:T(8,128)(2,1)} %fusion.2), channel_id=1, source_target_pairs={{0,16},{8,24},{16,0},{24,8},{1,17},{9,25},{17,1},{25,9},{2,18},{10... | collective-permute-start | bytes 16908296 | tf_op jit(solution)/shard_map/ppermute | solution.py:40
  1518.9 237.3 %collective-permute-start.27 = (bf16[512,5504]{1,0:T(8,128)(2,1)}, bf16[512,5504]{1,0:T(8,128)(2,1)}, u32[]{:S(2)}, u32[]{:S(2)}) collective-permute-start(bf16[512,5504]{1,0:T(8,128)(2,1)} %add_convert_fusion.3), channel_id=1, source_target_pairs={{0,1},{1,0},{2,3},{3,2},{4,5},{5,4},{6,7},{7,6},{8,9},{9,8},{10,11... | collective-permute-start | bytes 16908296 | tf_op jit(solution)/shard_map/ppermute | solution.py:40
  1563.7 109.3 %all-to-all-start.7 = ((bf16[8,2,512,128]{3,2,1,0:T(8,128)(2,1)}), bf16[8,2,512,128]{3,2,1,0:T(8,128)(2,1)S(1)}, u32[]{:S(2)}, u32[]{:S(2)}) async-start(bf16[8,2,512,128]{3,2,1,0:T(8,128)(2,1)} %bitcast.388), calls=%async_computation.7 | async-start | bytes 4194304 | tf_op jit(solution)/shard_map/all_to_all | solution.py:438
  1623.6 226.0 %collective-permute-start.28 = (bf16[1024,2048]{1,0:T(8,128)(2,1)}, bf16[1024,2048]{1,0:T(8,128)(2,1)}, u32[]{:S(2)}, u32[]{:S(2)}) collective-permute-start(bf16[1024,2048]{1,0:T(8,128)(2,1)} %convolution_convert_fusion.7), channel_id=1, source_target_pairs={{0,8},{8,0},{16,24},{24,16},{1,9},{9,1},{17,25},{25,17},{2,10},{10... | collective-permute-start | bytes 12582920 | tf_op jit(solution)/shard_map/ppermute | solution.py:40
  1623.6 252.4 %collective-permute-start.29 = (bf16[512,5504]{1,0:T(8,128)(2,1)}, bf16[512,5504]{1,0:T(8,128)(2,1)}, u32[]{:S(2)}, u32[]{:S(2)}) collective-permute-start(bf16[512,5504]{1,0:T(8,128)(2,1)} %add_convert_fusion.2), channel_id=1, source_target_pairs={{0,16},{8,24},{16,0},{24,8},{1,17},{9,25},{17,1},{25,9},{2,18},{10... | collective-permute-start | bytes 16908296 | tf_op jit(solution)/shard_map/ppermute | solution.py:40
  1635.8 207.6 %collective-permute-start.33 = (bf16[4,172,2048]{2,0,1:T(4,128)(2,1)}, bf16[4,172,2048]{2,0,1:T(4,128)(2,1)}, u32[]{:S(2)}, u32[]{:S(2)}) collective-permute-start(bf16[4,172,2048]{2,0,1:T(4,128)(2,1)} %copy.136), channel_id=1, source_target_pairs={{0,1},{1,0},{2,3},{3,2},{4,5},{5,4},{6,7},{7,6},{8,9},{9,8},{10,11... | collective-permute-start | bytes 8454152 | tf_op jit(solution)/shard_map/ppermute | solution.py:40
  1706.0 152.3 %all-to-all-start.8 = ((bf16[8,1,512,384]{3,2,1,0:T(8,128)(2,1)}), bf16[8,1,512,384]{3,2,1,0:T(8,128)(2,1)}, u32[]{:S(2)}, u32[]{:S(2)}) async-start(bf16[8,1,512,384]{3,2,1,0:T(8,128)(2,1)} %attend_back.6), calls=%async_computation.8 | async-start | bytes 6291456 | tf_op jit(solution)/shard_map/all_to_all | solution.py:442
  1766.0 89.9 %collective-permute-start.34 = (bf16[256,5504]{1,0:T(8,128)(2,1)}, bf16[256,5504]{1,0:T(8,128)(2,1)S(1)}, u32[]{:S(2)}, u32[]{:S(2)}) collective-permute-start(bf16[256,5504]{1,0:T(8,128)(2,1)} %dynamic-slice_bitcast_fusion.3), channel_id=1, source_target_pairs={{0,16},{8,24},{16,0},{24,8},{1,17},{9,25},{17,1},{25,9},{2,18},{10... | collective-permute-start | bytes 8454152 | tf_op jit(solution)/shard_map/ppermute | solution.py:40
  1855.4 47.3 %collective-permute-start.30 = (bf16[512,2048]{1,0:T(8,128)(2,1)}, bf16[512,2048]{1,0:T(8,128)(2,1)}, u32[]{:S(2)}, u32[]{:S(2)}) collective-permute-start(bf16[512,2048]{1,0:T(8,128)(2,1)} %add_convert_fusion.11), channel_id=1, source_target_pairs={{0,16},{8,24},{16,0},{24,8},{1,17},{9,25},{17,1},{25,9},{2,18},{10... | collective-permute-start | bytes 6291464 | tf_op jit(solution)/shard_map/ppermute | solution.py:40
  1858.3 91.9 %all-to-all-start.9 = ((bf16[8,1,512,384]{3,2,1,0:T(8,128)(2,1)}), bf16[8,1,512,384]{3,2,1,0:T(8,128)(2,1)S(1)}, u32[]{:S(2)}, u32[]{:S(2)}) async-start(bf16[8,1,512,384]{3,2,1,0:T(8,128)(2,1)} %attend_back.7), calls=%async_computation.9 | async-start | bytes 6291456 | tf_op jit(solution)/shard_map/all_to_all | solution.py:442
  1927.8 86.3 %collective-permute-start.35 = (bf16[4,64,5504]{2,1,0:T(8,128)(2,1)}, bf16[4,64,5504]{2,1,0:T(8,128)(2,1)}, u32[]{:S(2)}, u32[]{:S(2)}) collective-permute-start(bf16[4,64,5504]{2,1,0:T(8,128)(2,1)} %dynamic-slice_bitcast_fusion.2), channel_id=1, source_target_pairs={{0,1},{1,0},{2,3},{3,2},{4,5},{5,4},{6,7},{7,6},{8,9},{9,8},{10,11... | collective-permute-start | bytes 8454152 | tf_op jit(solution)/shard_map/ppermute | solution.py:40
  1930.5 81.6 %collective-permute-start.36 = (bf16[4,64,2048]{2,1,0:T(8,128)(2,1)}, bf16[4,64,2048]{2,1,0:T(8,128)(2,1)}, u32[]{:S(2)}, u32[]{:S(2)}) collective-permute-start(bf16[4,64,2048]{2,1,0:T(8,128)(2,1)} %dynamic-slice_bitcast_fusion.7), channel_id=1, source_target_pairs={{0,1},{1,0},{2,3},{3,2},{4,5},{5,4},{6,7},{7,6},{8,9},{9,8},{10,11... | collective-permute-start | bytes 3145736 | tf_op jit(solution)/shard_map/ppermute | solution.py:40
  1975.4 82.5 %collective-permute-start.31 = (bf16[1024,3072]{1,0:T(8,128)(2,1)}, bf16[1024,3072]{1,0:T(8,128)(2,1)}, u32[]{:S(2)}, u32[]{:S(2)}) collective-permute-start(bf16[1024,3072]{1,0:T(8,128)(2,1)} %convolution_convert_fusion.6), channel_id=1, source_target_pairs={{0,8},{8,0},{16,24},{24,16},{1,9},{9,1},{17,25},{25,17},{2,10},{10... | collective-permute-start | bytes 18874376 | tf_op jit(solution)/shard_map/ppermute | solution.py:40
  1986.1 81.3 %collective-permute-start.32 = (bf16[1024,3072]{1,0:T(8,128)(2,1)}, bf16[1024,3072]{1,0:T(8,128)(2,1)}, u32[]{:S(2)}, u32[]{:S(2)}) collective-permute-start(bf16[1024,3072]{1,0:T(8,128)(2,1)} %convolution_convert_fusion.5), channel_id=1, source_target_pairs={{0,8},{8,0},{16,24},{24,16},{1,9},{9,1},{17,25},{25,17},{2,10},{10... | collective-permute-start | bytes 18874376 | tf_op jit(solution)/shard_map/ppermute | solution.py:40
  2024.5 104.7 %collective-permute-start.37 = (bf16[2,64,18560]{2,1,0:T(8,128)(2,1)}, bf16[2,64,18560]{2,1,0:T(8,128)(2,1)}, u32[]{:S(2)}, u32[]{:S(2)}) collective-permute-start(bf16[2,64,18560]{2,1,0:T(8,128)(2,1)} %dynamic-slice_bitcast_fusion), channel_id=1, source_target_pairs={{0,2},{1,3},{2,0},{3,1},{4,6},{5,7},{6,4},{7,5},{8,10},{9,11},{10,... | collective-permute-start | bytes 14254088 | tf_op jit(solution)/shard_map/ppermute | solution.py:40
  2065.6 114.3 %collective-permute-start.38 = (bf16[512,3072]{1,0:T(8,128)(2,1)}, bf16[512,3072]{1,0:T(8,128)(2,1)}, u32[]{:S(2)}, u32[]{:S(2)}) collective-permute-start(bf16[512,3072]{1,0:T(8,128)(2,1)} %add_convert_fusion.7), channel_id=1, source_target_pairs={{0,16},{8,24},{16,0},{24,8},{1,17},{9,25},{17,1},{25,9},{2,18},{10... | collective-permute-start | bytes 9437192 | tf_op jit(solution)/shard_map/ppermute | solution.py:40
  2076.7 115.0 %collective-permute-start.39 = (bf16[512,3072]{1,0:T(8,128)(2,1)}, bf16[512,3072]{1,0:T(8,128)(2,1)}, u32[]{:S(2)}, u32[]{:S(2)}) collective-permute-start(bf16[512,3072]{1,0:T(8,128)(2,1)} %add_convert_fusion.6), channel_id=1, source_target_pairs={{0,1},{1,0},{2,3},{3,2},{4,5},{5,4},{6,7},{7,6},{8,9},{9,8},{10,11... | collective-permute-start | bytes 9437192 | tf_op jit(solution)/shard_map/ppermute | solution.py:40
  2154.9 14.0 collective-permute-start.45
  2169.0 7.9 collective-permute-start.46
  2176.8 119.1 %collective-permute-start.44 = (bf16[1,64,18560]{2,1,0:T(8,128)(2,1)}, bf16[1,64,18560]{2,1,0:T(8,128)(2,1)}, u32[]{:S(2)}, u32[]{:S(2)}) collective-permute-start(bf16[1,64,18560]{2,1,0:T(8,128)(2,1)} %constant_dynamic-slice_fusion.10), channel_id=1, source_target_pairs={{0,4},{1,5},{2,6},{3,7},{4,0},{5,1},{6,2},{7,3},{8,12},{9,13},{10,... | collective-permute-start | bytes 7127048 | tf_op jit(solution)/shard_map/ppermute | solution.py:40
  2176.9 106.1 %collective-permute-start.47 = (f32[2,256]{1,0:T(2,128)S(1)}, f32[2,256]{1,0:T(2,128)S(1)}, u32[]{:S(2)}, u32[]{:S(2)}) collective-permute-start(f32[2,256]{1,0:T(2,128)S(1)} %bitcast.463), channel_id=1, source_target_pairs={{0,4},{1,5},{2,6},{3,7},{4,0},{5,1},{6,2},{7,3},{8,12},{9,13},{10,... | collective-permute-start | bytes 6152 | tf_op jit(solution)/shard_map/ppermute | solution.py:40
  2197.7 98.1 %collective-permute-start.40 = (bf16[4,64,3072]{2,1,0:T(8,128)(2,1)}, bf16[4,64,3072]{2,1,0:T(8,128)(2,1)}, u32[]{:S(2)}, u32[]{:S(2)}) collective-permute-start(bf16[4,64,3072]{2,1,0:T(8,128)(2,1)} %dynamic-slice_bitcast_fusion.6), channel_id=1, source_target_pairs={{0,1},{1,0},{2,3},{3,2},{4,5},{5,4},{6,7},{7,6},{8,9},{9,8},{10,11... | collective-permute-start | bytes 4718600 | tf_op jit(solution)/shard_map/ppermute | solution.py:40
  2283.0 3.6 collective-permute-start.48
  2284.3 36.3 %collective-permute-start.41 = (bf16[256,3072]{1,0:T(8,128)(2,1)}, bf16[256,3072]{1,0:T(8,128)(2,1)}, u32[]{:S(2)}, u32[]{:S(2)}) collective-permute-start(bf16[256,3072]{1,0:T(8,128)(2,1)} %dynamic-slice_bitcast_fusion.5), channel_id=1, source_target_pairs={{0,16},{8,24},{16,0},{24,8},{1,17},{9,25},{17,1},{25,9},{2,18},{10... | collective-permute-start | bytes 4718600 | tf_op jit(solution)/shard_map/ppermute | solution.py:40
  2286.7 8.6 collective-permute-start.49
  2323.0 35.2 %collective-permute-start.42 = (bf16[2,64,6144]{2,1,0:T(8,128)(2,1)S(1)}, bf16[2,64,6144]{2,1,0:T(8,128)(2,1)S(1)}, u32[]{:S(2)}, u32[]{:S(2)}) collective-permute-start(bf16[2,64,6144]{2,1,0:T(8,128)(2,1)S(1)} %dynamic-slice_bitcast_fusion.4), channel_id=1, source_target_pairs={{0,2},{1,3},{2,0},{3,1},{4,6},{5,7},{6,4},{7,5},{8,10},{9,11},{10,... | collective-permute-start | bytes 4718600 | tf_op jit(solution)/shard_map/ppermute | solution.py:40
  2359.5 35.4 %collective-permute-start.43 = (bf16[1,64,6144]{2,1,0:T(8,128)(2,1)}, bf16[1,64,6144]{2,1,0:T(8,128)(2,1)}, u32[]{:S(2)}, u32[]{:S(2)}) collective-permute-start(bf16[1,64,6144]{2,1,0:T(8,128)(2,1)} %constant_dynamic-slice_fusion.11), channel_id=1, source_target_pairs={{0,4},{1,5},{2,6},{3,7},{4,0},{5,1},{6,2},{7,3},{8,12},{9,13},{10,... | collective-permute-start | bytes 2359304 | tf_op jit(solution)/shard_map/ppermute | solution.py:40
  (93 other events, 2235.8 us)
Sparse Core Ops, SparseCore 0:
  11.6 260.4 all-gather.1

commit v5 on v4

--- a/solution.py
+++ b/solution.py
@@ -21,6 +21,8 @@
 LOG2E = 1.4426950408889634
 SCALE = 1.0 / math.sqrt(HD)
 
+QUICK = pl.CostEstimate(flops=1024, bytes_accessed=1024, transcendentals=0)
+
 bf16 = jnp.bfloat16
 f32 = jnp.float32
 
@@ -60,11 +62,17 @@
     return block
 
 
-def scatter_small(terms):
-    k = terms.shape[0]
-    for digit in digits_of("dp") + digits_of("seq"):
-        terms = scatter_digit(terms.reshape(k, 2, -1), digit, 1, f32)
-    return terms
+class ScatterSmall:
+    def __init__(self, terms):
+        self.digits = digits_of("dp") + digits_of("seq")
+        self.terms = terms.reshape((terms.shape[0],) + (2,) * len(self.digits) + (-1,))
+        for digit in digits_of("dp")[::-1] + digits_of("seq")[-1:]:
+            self.step(digit)
+
+    def step(self, digit, *others):
+        dim = 1 + self.digits.index(digit)
+        self.digits = [d for d in self.digits if d != digit]
+        self.terms = scatter_digit(after(self.terms, *others), digit, dim, f32)
 
 
 SLOTS = 8
@@ -152,7 +160,7 @@
             ),
             out_shape=[jax.ShapeDtypeStruct((count * rows, width), bf16) for width in self.widths],
             compiler_params=pltpu.CompilerParams(vmem_limit_bytes=16 * 1024 * 1024),
-            cost_estimate=pl.CostEstimate(flops=0, bytes_accessed=4 * count * rows * sum(self.widths), transcendentals=0),
+            cost_estimate=QUICK,
             name="place",
         )(targets, *self.values())
 
@@ -317,11 +325,7 @@
             jax.ShapeDtypeStruct((pairs, 1, length), f32),
         ],
         compiler_params=pltpu.CompilerParams(vmem_limit_bytes=32 * 1024 * 1024),
-        cost_estimate=pl.CostEstimate(
-            flops=8 * pairs * length * 1792 * HD,
-            bytes_accessed=8 * pairs * length * HD,
-            transcendentals=pairs * length * 1792,
-        ),
+        cost_estimate=QUICK,
         name="attend",
     )(bounds, qkv, qkv, qkv, low)
 
@@ -400,11 +404,7 @@
         ),
         out_shape=jax.ShapeDtypeStruct((seq, 1, rows, 3 * HD), bf16),
         compiler_params=pltpu.CompilerParams(vmem_limit_bytes=40 * 1024 * 1024),
-        cost_estimate=pl.CostEstimate(
-            flops=20 * length * 1792 * HD,
-            bytes_accessed=16 * length * HD,
-            transcendentals=length * 1792,
-        ),
+        cost_estimate=QUICK,
         name="attend_back",
     )(bounds, qkv, qkv, qkv, grad, mixed, lse, low)
 
@@ -506,35 +506,34 @@
     soon.near_step(0)
     later.wait(*ready)
     later.far_step(far - 1)
-    step_in = after(h_attn, *later.values())
+    later.wait(*soon.values())
     later.near_step(0)
+    h_kept = step_in = after(h_attn, *later.values())
     saved, attended, arrived = [], [], []
     for g in range(groups):
         qkv_rows = jnp.dot(of(step_in, g), full_qkv, preferred_element_type=f32).astype(bf16)
         qkv = to_heads(qkv_rows, micros)
         if g == 0:
             ready = soon.values() + later.values()
-            qkv = after(qkv, *ready)
-            soon.wait(*ready)
-            soon.near_step(1)
-            later.wait(*ready)
-            later.near_step(1)
+            for w in (soon, later):
+                w.wait(*ready)
+                w.near_step(1)
+            qkv = after(qkv, *soon.values(), *later.values())
         else:
             qkv = after(qkv, gate_first)
         mixed, lse = attend(qkv, bounds[g], low[g])
         saved.append((qkv, mixed, lse))
         attended.append(rows_of(to_rows(mixed), micros))
         if g == 0:
-            step_in = after(h_attn, attended[0])
             soon.near_step(2)
+            later.near_step(2)
+            step_in = after(h_kept, attended[0], *soon.values(), *later.values())
             full_gate, full_out = soon.finish()
 
             mid_first = of(x, 0) + jnp.dot(attended[0], full_out, preferred_element_type=f32)
             scale_first = norm_scale(mid_first)
             h_first = (mid_first * scale_first * gain_m).astype(bf16)
             gate_first = jnp.dot(h_first, full_gate, preferred_element_type=f32)
-            later.near_step(2)
-    later.wait(gate_first)
     full_up, full_down = later.finish()
     full_down = full_down.reshape(FF, D)
 
@@ -567,13 +566,15 @@
         act = (gate * sig * up).astype(bf16)
         parts.append([mid, scale_m, h_mlp, act])
         mark = (act,)
+        if final:
+            acts = jnp.concatenate([p[3] for p in parts], axis=0)
+            sides = jnp.concatenate([p[2] for p in parts], axis=0)
+            down = Reduce(None, cot, False, product=tn(after(acts, *mark, *grads), cot).astype(bf16))
+            mark = (down.cross(),)
         if g:
             mark = (back_of(g - 1, *mark),)
         if final:
-            acts = jnp.concatenate([p[3] for p in parts], axis=0)
-            sides = jnp.concatenate([p[2] for p in parts], axis=0)
-            down = Reduce(None, cot, False, product=tn(after(acts, *mark), cot).astype(bf16))
-            mark = (down.cross(),)
+            mark = (down.send(*mark),)
         if g:
             mark = mark + (rows_grad[-1][0],)
         cot_part = of(cot, g)
@@ -583,20 +584,23 @@
         parts[g] += [grad_gate, grad_up]
         mark = (grad_gate, grad_up)
         if final:
-            mark = (down.send(*mark),)
             gate_r = Reduce(pieces_of(sides, False), jnp.concatenate([p[4] for p in parts], axis=0), False)
             up_r = Reduce(pieces_of(sides, True), jnp.concatenate([p[5] for p in parts], axis=0), True)
             mark = (up_r.cross(*mark),)
             mark = (gate_r.cross(*mark),)
+        if final:
+            mark = mark + (down.away,) + tuple(r for pieces in rows_grad for r in pieces)
         half_grad = nt(after(grad_gate, *mark), full_gate)
         mark = (half_grad,)
         if final:
+            mark = (down.keep(*mark),)
+            down.second()
             mark = (up_r.send(*mark),)
         grad_h_mlp = half_grad + nt(after(grad_up, *mark), full_up)
         grad_mid_norm, gain_part = norm_backward(grad_h_mlp, mid, scale_m, gain_m)
         grad_mid = cot_part.astype(f32) + grad_mid_norm
         grad_branch = grad_mid.astype(bf16)
-        grad_rows = nt(after(grad_branch, *[r for pieces in rows_grad for r in pieces]), full_out).astype(bf16)
+        grad_rows = nt(grad_branch, full_out).astype(bf16)
         grads.append(to_heads(grad_rows, micros))
         parts[g] += [grad_mid, grad_branch, gain_part]
         mark = (grad_rows,)
@@ -606,8 +610,6 @@
     early = [down, up_r, gate_r, out_r]
     mark = (gate_r.send(*mark),)
     mark = (out_r.cross(*mark),)
-    mark = (down.keep(*mark),)
-    down.second()
     mark = (back_of(groups - 1, *mark),)
     mark = (up_r.keep(*mark),)
     up_r.second()
@@ -631,7 +633,7 @@
     mark = mark + tuple(rows_grad[-1])
     first = Finish(early, *mark)
     first.step(0)
-    h_sides = [pieces_of(h_attn, False), pieces_of(h_attn, True)]
+    h_sides = [pieces_of(h_kept, False), pieces_of(h_kept, True)]
     for g in range(groups - 1):
         grad_qkv.append(rows_of(jnp.concatenate(rows_grad[g], axis=1), micros))
     grad_qkv.append(rows_of(jnp.concatenate([after(r, *mark) for r in rows_grad[-1]], axis=1), micros))
@@ -656,12 +658,14 @@
         mark = (r.keep(*mark),)
     for r in late:
         r.second(*mark)
-    gain_grads = scatter_small(jnp.stack([sum(gain_a_parts), sum(p[8] for p in parts)]))
+    gain_sums = ScatterSmall(jnp.stack([sum(gain_a_parts), sum(p[8] for p in parts)]))
     second = Finish(late)
     for n in range(far):
         if n:
             first.step(n, hold=mark)
+        gain_sums.step(digits_of("seq")[-2 - n], second.total)
         second.step(n)
+    gain_grads = gain_sums.terms
     down_grad, up_grad, gate_grad, out_grad = first.results()
     qkv_grad = jnp.concatenate(second.results(), axis=1).reshape(-1, H, 3, HD).transpose(0, 2, 1, 3)
     join = lambda arrays: jnp.concatenate(arrays, axis=0).reshape(MB, 1, rows, D)

time: 2420 us -> 2450 us (1.012)
  blocking collectives: 0 us -> 54.8 us
  local copies, waits for them, and re-layouts: 246 us -> 212 us
  waiting for transfers between devices: 1020 us -> 1050 us
    all_to_all x6 -> x5, waiting for transfers between devices: 110 us -> 45.5 us  [to_rows(): return lax.all_to_all(whole, 'seq', 0, 0, tiled=True)]
    all_to_all x0 -> x1, blocking collectives: none -> 54.8 us  [to_rows(): return lax.all_to_all(whole, 'seq', 0, 0, tiled=True)]
    all_to_all x4, waiting for transfers between devices: 35.5 us -> 85.7 us  [to_heads(): return lax.all_to_all(split, 'seq', 0, 0, tiled=True)]
    ppermute x50, waiting for transfers between devices: 878 us -> 924 us  [swap(): lax.ppermute(block, axis, [(i, i ^ stride) for i in range(lax.axis_size(a...]
    convert_element_type x4 -> x1, local copies, waits for them, and re-layouts: 48.1 us -> 9.23 us  [shards(): x = tokens.reshape(MB * rows, D).astype(f32)]
  transfers between devices with their start and end apart: 61 -> 60, of which waited for: 24 -> 23; matrix products, arithmetic and copies ran while one was open for 35% -> 31% of each run, Pallas kernels for 5% -> 9%
where the time goes in v5:
time: 2450 us; the launch traced here: 2440 us
  waiting for transfers between devices  1050 us (43%)
  matrix products  555 us (23%)
  Pallas kernels  271 us (11%)
  local copies, waits for them, and re-layouts  212 us (9%)
  other arithmetic  160 us (7%)
  starting transfers between devices  116 us (5%)
  blocking collectives  54.8 us (2%)
    ppermute x50, waiting for transfers between devices, swap(): lax.ppermute(block, axis, [(i, i ^ stride) for i in range(lax.axis_size(a...  924 us
    dot_general x16, matrix products, tn(): lax.dot_general(a, b, (((0,), (0,)), ((), ())), preferred_element_type=f32)  188 us
    dot_general x10, matrix products, nt(): return jnp.einsum('re,de->rd', a, b, preferred_element_type=f32)  182 us
    pallas_call x4, Pallas kernels, attend_back(): pl.pallas_call(functools.partial(backward_kernel, pair), grid_spec=pltpu....  130 us
    pallas_call x2, Pallas kernels, attend(): pl.pallas_call(forward_kernel, grid_spec=pltpu.PrefetchScalarGridSpec(num...  92.7 us
    all_to_all x4, waiting for transfers between devices, to_heads(): return lax.all_to_all(split, 'seq', 0, 0, tiled=True)  85.7 us
    ppermute x50, starting transfers between devices, swap(): lax.ppermute(block, axis, [(i, i ^ stride) for i in range(lax.axis_size(a...  69.3 us
    all_to_all x1, blocking collectives, to_rows(): return lax.all_to_all(whole, 'seq', 0, 0, tiled=True)  54.8 us
  transfers between devices with their start and end apart: 60, of which 23 were waited for; matrix products, arithmetic and copies ran while one was open for 31% of the time, Pallas kernels for 9%

profile of v5, /device:TPU:0, one launch (start us, length us, event | category | flops | bytes accessed | tf_op | source)
XLA Modules:
  0.0 2439.6 jit_solution(17417890586136064317)
XLA Ops:
  18.4 64.0 %collective-permute-done.5 = bf16[64,7552]{1,0:T(8,128)(2,1)S(1)} collective-permute-done((bf16[64,7552]{1,0:T(8,128)(2,1)S(1)}, bf16[64,7552]{1,0:T(8,128)(2,1)S(1)}, u32[]{:S(2)}, u32[]{:S(2)}) %collective-permute-start.5) | collective-permute-done | bytes 966688 | tf_op jit(solution)/shard_map/ppermute | solution.py:42
  82.7 19.3 collective-permute-start.7
  102.1 81.8 %collective-permute-done.6 = bf16[64,11008]{1,0:T(8,128)(2,1)S(1)} collective-permute-done((bf16[64,11008]{1,0:T(8,128)(2,1)S(1)}, bf16[64,11008]{1,0:T(8,128)(2,1)S(1)}, u32[]{:S(2)}, u32[]{:S(2)}) %collective-permute-start.6) | collective-permute-done | bytes 1409056 | tf_op jit(solution)/shard_map/ppermute | solution.py:42
  184.0 30.1 %collective-permute-done.7 = bf16[128,7552]{1,0:T(8,128)(2,1)S(1)} collective-permute-done((bf16[128,7552]{1,0:T(8,128)(2,1)S(1)}, bf16[128,7552]{1,0:T(8,128)(2,1)S(1)}, u32[]{:S(2)}, u32[]{:S(2)}) %collective-permute-start.7) | collective-permute-done | bytes 1933344 | tf_op jit(solution)/shard_map/ppermute | solution.py:42
  217.7 90.6 %collective-permute-done.8 = bf16[128,11008]{1,0:T(8,128)(2,1)S(1)} collective-permute-done((bf16[128,11008]{1,0:T(8,128)(2,1)S(1)}, bf16[128,11008]{1,0:T(8,128)(2,1)S(1)}, u32[]{:S(2)}, u32[]{:S(2)}) %collective-permute-start.8) | collective-permute-done | bytes 2818080 | tf_op jit(solution)/shard_map/ppermute | solution.py:42
  315.1 120.7 %collective-permute-done = bf16[2,64]{1,0:T(2,128)(2,1)S(1)} collective-permute-done((bf16[2,64]{1,0:T(2,128)(2,1)S(1)}, bf16[2,64]{1,0:T(2,128)(2,1)S(1)}, u32[]{:S(2)}, u32[]{:S(2)}) %collective-permute-start) | collective-permute-done | bytes 288 | tf_op jit(solution)/shard_map/ppermute | solution.py:42
  439.5 9.2 collective-permute-start.2
  460.9 9.2 copy.145
  475.4 19.0 convolution_convert_fusion.4
  509.9 150.0 %collective-permute-done.12.refs_3_ = bf16[256,7552]{1,0:T(8,128)(2,1)} collective-permute-done((bf16[256,7552]{1,0:T(8,128)(2,1)}, bf16[256,7552]{1,0:T(8,128)(2,1)}, u32[]{:S(2)}, u32[]{:S(2)}) %collective-permute-start.12) | collective-permute-done | bytes 3866656 | tf_op jit(solution)/shard_map/ppermute | solution.py:42
  659.9 81.8 %collective-permute-done.11.refs_2_ = bf16[256,7552]{1,0:T(8,128)(2,1)} collective-permute-done((bf16[256,7552]{1,0:T(8,128)(2,1)}, bf16[256,7552]{1,0:T(8,128)(2,1)}, u32[]{:S(2)}, u32[]{:S(2)}) %collective-permute-start.11) | collective-permute-done | bytes 3866656 | tf_op jit(solution)/shard_map/ppermute | solution.py:42
  753.2 46.0 %attend.2 = (bf16[8,2,512,128]{3,2,1,0:T(8,128)(2,1)S(1)}, f32[2,1,4096]{2,1,0:T(1,128)S(1)}) custom-call(s32[2,4,8]{2,1,0:T(4,128)S(1)} %pad_add_fusion.2.bounds, bf16[8,2,512,384]{3,2,1,0:T(8,128)(2,1)} %all-to-all-done.q_ref.k_ref.v_ref, bf16[8,2,512,384]{3,2,1,0:T(8,128)(2,1)} %all-to-all-done.q_ref.k_ref.v_ref, ...), custom_call_target="tpu_custom_call" | custom-call | flops 1024 | bytes 1024 | tf_op jit(solution)/shard_map/attend/pallas_call | solution.py:314
  799.2 54.8 %all_to_all.50 = bf16[8,2,512,128]{3,2,1,0:T(8,128)(2,1)} all-to-all(bf16[8,2,512,128]{3,2,1,0:T(8,128)(2,1)S(1)} %get-tuple-element.86.o_ref), channel_id=1, replica_groups=mesh['dp'=4,'seq'=8] {'seq'}, dimensions={0} | all-to-all | bytes 4194304 | tf_op jit(solution)/shard_map/all_to_all | solution.py:442
  858.3 19.5 convolution_convert_fusion.3
  899.8 18.1 place.2
  921.2 30.4 %place.3 = (bf16[2048,5504]{1,0:T(8,128)(2,1)}, bf16[2048,5504]{1,0:T(8,128)(2,1)}) custom-call(s32[32]{0:T(128)S(1)} %xor_multiply_fusion.target, bf16[256,11008]{1,0:T(8,128)(2,1)} %pad_maximum_fusion.8.refs_0_, bf16[256,11008]{1,0:T(8,128)(2,1)} %collective-permute-done.10.refs_1_, bf16[256,11008]{1,0:T(8,128)(2,1)} %collective-permute-done.13.refs_2_, ...), custom_call_target="tpu_custom_call" | custom-call | flops 1024 | bytes 1024 | tf_op jit(solution)/shard_map/place/pallas_call | solution.py:149
  951.6 31.1 %reshape.456 = bf16[5504,2048]{1,0:T(8,128)(2,1)} reshape(bf16[2048,5504]{1,0:T(8,128)(2,1)} %get-tuple-element.95) | data formatting | bytes 45088768 | tf_op jit(solution)/shard_map/reshape | solution.py:538
  994.1 19.7 fusion.120
  1013.8 12.6 all-to-all-done.2.q_ref.k_ref.v_ref
  1026.4 46.7 %attend.3 = (bf16[8,2,512,128]{3,2,1,0:T(8,128)(2,1)}, f32[2,1,4096]{2,1,0:T(1,128)S(1)}) custom-call(s32[2,4,8]{2,1,0:T(4,128)S(1)} %pad_add_fusion.3.bounds, bf16[8,2,512,384]{3,2,1,0:T(8,128)(2,1)} %all-to-all-done.2.q_ref.k_ref.v_ref, bf16[8,2,512,384]{3,2,1,0:T(8,128)(2,1)} %all-to-all-done.2.q_ref.k_ref.v_ref, ...), custom_call_target="tpu_custom_call" | custom-call | flops 1024 | bytes 1024 | tf_op jit(solution)/shard_map/attend/pallas_call | solution.py:314
  1076.8 25.2 %multiply_convert_fusion.5 = (bf16[512,5504]{1,0:T(8,128)(2,1)}, f32[512,5504]{1,0:T(8,128)}) fusion(f32[512,5504]{1,0:T(8,128)} %fusion.120, bf16[512,2048]{1,0:T(8,128)(2,1)} %copy-done.43, bf16[2048,5504]{1,0:T(8,128)(2,1)} %get-tuple-element.93), kind=kOutput, calls=%fused_computation.24 | convolution fusion | flops 11559632896 | bytes 52822016 | tf_op jit(solution)/shard_map/dot_general | solution.py:564
  1101.9 25.2 %multiply_convert_fusion.3 = (bf16[512,5504]{1,0:T(8,128)(2,1)}, bf16[512,5504]{1,0:T(8,128)(2,1)}) fusion(f32[512,5504]{1,0:T(8,128)} %fusion.120, f32[512,5504]{1,0:T(8,128)} %get-tuple-element.268, bf16[512,2048]{1,0:T(8,128)(2,1)} %get-tuple-element.94, bf16[5504,2048]{1,0:T(8,128)(2,1)} %reshape.456), kind=kOutput, calls=%fused_computation.22 | convolution fusion | flops 11579359232 | bytes 58458112 | tf_op jit(solution)/shard_map/re,de->rd/dot_general | solution.py:463
  1127.1 19.8 fusion.121
  1146.9 19.4 multiply_reduce_fusion.2
  1191.1 10.3 multiply_reduce_fusion.8
  1205.1 19.0 fusion.122
  1224.1 25.4 %multiply_convert_fusion.2 = (bf16[512,5504]{1,0:T(8,128)(2,1)}, f32[512,5504]{1,0:T(8,128)}) fusion(f32[512,5504]{1,0:T(8,128)} %fusion.122, bf16[512,2048]{1,0:T(8,128)(2,1)} %copy-done.45, bf16[2048,5504]{1,0:T(8,128)(2,1)} %get-tuple-element.93), kind=kOutput, calls=%fused_computation.19 | convolution fusion | flops 11559632896 | bytes 52822016 | tf_op jit(solution)/shard_map/dot_general | solution.py:564
  1249.4 11.5 pad_maximum_fusion
  1260.9 32.1 %convolution_convert_fusion = bf16[5504,2048]{1,0:T(8,128)(2,1)} fusion(bf16[1024,5504]{1,0:T(8,128)(2,1)} %pad_maximum_fusion, bf16[1024,2048]{1,0:T(8,128)(2,1)} %bitcast.348), kind=kOutput, calls=%fused_computation | convolution fusion | flops 23096721408 | bytes 38010880 | tf_op jit(solution)/shard_map/dot_general | solution.py:169
  1293.1 10.6 constant_dynamic-slice_fusion.10
  1303.7 32.0 %attend_back.4 = bf16[8,1,512,384]{3,2,1,0:T(8,128)(2,1)S(1)} custom-call(s32[2,4,8]{2,1,0:T(4,128)S(1)} %copy-done.21, bf16[8,2,512,384]{3,2,1,0:T(8,128)(2,1)} %all-to-all-done.q_ref.k_ref.v_ref, bf16[8,2,512,384]{3,2,1,0:T(8,128)(2,1)} %all-to-all-done.q_ref.k_ref.v_ref, bf16[8,2,512,384]{3,2,1,0:T(8,128)(2,1)} %all-to-all-done.q_ref.k_ref.v_ref, ...), custom_call_target="tpu_custom_call" | custom-call | flops 1024 | bytes 1024 | tf_op jit(solution)/shard_map/attend_back/pallas_call | solution.py:391
  1345.5 33.1 %attend_back.5 = bf16[8,1,512,384]{3,2,1,0:T(8,128)(2,1)} custom-call(s32[2,4,8]{2,1,0:T(4,128)S(1)} %copy-done.21, bf16[8,2,512,384]{3,2,1,0:T(8,128)(2,1)} %all-to-all-done.q_ref.k_ref.v_ref, bf16[8,2,512,384]{3,2,1,0:T(8,128)(2,1)} %all-to-all-done.q_ref.k_ref.v_ref, bf16[8,2,512,384]{3,2,1,0:T(8,128)(2,1)} %all-to-all-done.q_ref.k_ref.v_ref, ...), custom_call_target="tpu_custom_call" | custom-call | flops 1024 | bytes 1024 | tf_op jit(solution)/shard_map/attend_back/pallas_call | solution.py:391
  1392.5 10.1 fusion.2
  1402.6 12.7 all-to-all-done.5
  1415.3 24.5 %multiply_convert_fusion = (bf16[512,5504]{1,0:T(8,128)(2,1)}, bf16[512,5504]{1,0:T(8,128)(2,1)}) fusion(f32[512,5504]{1,0:T(8,128)} %fusion.122, f32[512,5504]{1,0:T(8,128)} %get-tuple-element.273, bf16[512,2048]{1,0:T(8,128)(2,1)S(1)} %copy-done.59, bf16[5504,2048]{1,0:T(8,128)(2,1)} %reshape.456), kind=kOutput, calls=%fused_computation.17 | convolution fusion | flops 11579359232 | bytes 58458112 | tf_op jit(solution)/shard_map/re,de->rd/dot_general | solution.py:463
  1439.8 19.4 convolution_convert_fusion.2
  1473.5 11.2 copy.152
  1484.7 19.3 convolution_convert_fusion.1
  1504.2 32.8 %all-to-all-done.6 = bf16[8,1,512,384]{3,2,1,0:T(8,128)(2,1)} async-done(((bf16[8,1,512,384]{3,2,1,0:T(8,128)(2,1)}), bf16[8,1,512,384]{3,2,1,0:T(8,128)(2,1)}, u32[]{:S(2)}, u32[]{:S(2)}) %all-to-all-start.6) | async-done | bytes 3145760 | tf_op jit(solution)/shard_map/all_to_all | solution.py:442
  1537.0 46.6 %collective-permute-done.24 = bf16[1376,2048]{1,0:T(8,128)(2,1)} collective-permute-done((bf16[1376,2048]{1,0:T(8,128)(2,1)}, bf16[1376,2048]{1,0:T(8,128)(2,1)}, u32[]{:S(2)}, u32[]{:S(2)}) %collective-permute-start.24) | collective-permute-done | bytes 5636128 | tf_op jit(solution)/shard_map/ppermute | solution.py:42
  1583.6 19.6 fusion.123
  1603.1 13.3 fusion.1
  1616.5 12.4 add_convert_fusion.3
  1630.3 19.2 multiply_reduce_fusion.1
  1682.9 12.2 add_convert_fusion.2
  1702.7 73.2 %all-to-all-done.7.do_ref = bf16[8,2,512,128]{3,2,1,0:T(8,128)(2,1)S(1)} async-done(((bf16[8,2,512,128]{3,2,1,0:T(8,128)(2,1)}), bf16[8,2,512,128]{3,2,1,0:T(8,128)(2,1)S(1)}, u32[]{:S(2)}, u32[]{:S(2)}) %all-to-all-start.7) | async-done | bytes 2097184 | tf_op jit(solution)/shard_map/all_to_all | solution.py:438
  1775.9 32.1 %attend_back.6 = bf16[8,1,512,384]{3,2,1,0:T(8,128)(2,1)S(1)} custom-call(s32[2,4,8]{2,1,0:T(4,128)S(1)} %copy-done.19, bf16[8,2,512,384]{3,2,1,0:T(8,128)(2,1)} %all-to-all-done.2.q_ref.k_ref.v_ref, bf16[8,2,512,384]{3,2,1,0:T(8,128)(2,1)} %all-to-all-done.2.q_ref.k_ref.v_ref, bf16[8,2,512,384]{3,2,1,0:T(8,128)(2,1)} %all-to-all-done.2.q_ref.k_ref.v_ref, ...), custom_call_target="tpu_custom_call" | custom-call | flops 1024 | bytes 1024 | tf_op jit(solution)/shard_map/attend_back/pallas_call | solution.py:391
  1814.3 32.9 %attend_back.7 = bf16[8,1,512,384]{3,2,1,0:T(8,128)(2,1)} custom-call(s32[2,4,8]{2,1,0:T(4,128)S(1)} %copy-done.19, bf16[8,2,512,384]{3,2,1,0:T(8,128)(2,1)} %all-to-all-done.2.q_ref.k_ref.v_ref, bf16[8,2,512,384]{3,2,1,0:T(8,128)(2,1)} %all-to-all-done.2.q_ref.k_ref.v_ref, bf16[8,2,512,384]{3,2,1,0:T(8,128)(2,1)} %all-to-all-done.2.q_ref.k_ref.v_ref, ...), custom_call_target="tpu_custom_call" | custom-call | flops 1024 | bytes 1024 | tf_op jit(solution)/shard_map/attend_back/pallas_call | solution.py:391
  1847.2 9.4 fusion.16
  1904.6 26.3 %collective-permute-done.34 = bf16[256,5504]{1,0:T(8,128)(2,1)} collective-permute-done((bf16[256,5504]{1,0:T(8,128)(2,1)}, bf16[256,5504]{1,0:T(8,128)(2,1)}, u32[]{:S(2)}, u32[]{:S(2)}) %collective-permute-start.34) | collective-permute-done | bytes 2818080 | tf_op jit(solution)/shard_map/ppermute | solution.py:42
  1941.2 11.8 fusion.14
  1975.5 19.9 add_convert_fusion.9
  2000.3 19.3 add_convert_fusion.8
  2033.4 11.3 convolution_convert_fusion.6
  2044.8 10.7 convolution_convert_fusion.5
  2060.3 20.4 collective-permute-done.36
  2095.4 20.3 multiply_reduce_fusion.4
  2134.3 9.2 add_convert_fusion.6
  2143.6 52.1 %collective-permute-done.37 = bf16[2,64,18560]{2,1,0:T(8,128)(2,1)} collective-permute-done((bf16[2,64,18560]{2,1,0:T(8,128)(2,1)}, bf16[2,64,18560]{2,1,0:T(8,128)(2,1)}, u32[]{:S(2)}, u32[]{:S(2)}) %collective-permute-start.37) | collective-permute-done | bytes 4751392 | tf_op jit(solution)/shard_map/ppermute | solution.py:42
  2201.3 20.2 multiply_reduce_fusion.3
  2268.8 81.9 %collective-permute-done.44 = bf16[1,64,18560]{2,1,0:T(8,128)(2,1)S(1)} collective-permute-done((bf16[1,64,18560]{2,1,0:T(8,128)(2,1)S(1)}, bf16[1,64,18560]{2,1,0:T(8,128)(2,1)S(1)}, u32[]{:S(2)}, u32[]{:S(2)}) %collective-permute-start.44) | collective-permute-done | bytes 2375712 | tf_op jit(solution)/shard_map/ppermute | solution.py:42
  2357.0 32.5 %collective-permute-done.48 = f32[2,2,64]{2,0,1:T(2,128)S(1)} collective-permute-done((f32[2,2,64]{2,0,1:T(2,128)S(1)}, f32[2,2,64]{2,0,1:T(2,128)S(1)}, u32[]{:S(2)}, u32[]{:S(2)}) %collective-permute-start.48) | collective-permute-done | bytes 1056 | tf_op jit(solution)/shard_map/ppermute | solution.py:42
  2396.2 15.0 collective-permute-done.49
  2411.7 16.0 collective-permute-done.43
  (473 shorter events, 437.9 us)
Async XLA Ops:
  7.2 468.2 %all-gather.2.cloned.1.call-start = ((), (), s32[]{:S(2)}) async-start(), calls=%async_computation.10 | async-start | bytes 25952256 | tf_op jit(solution)/shard_map/all_gather | solution.py:469
  12.0 70.3 %collective-permute-start.5 = (bf16[64,7552]{1,0:T(8,128)(2,1)S(1)}, bf16[64,7552]{1,0:T(8,128)(2,1)S(1)}, u32[]{:S(2)}, u32[]{:S(2)}) collective-permute-start(bf16[64,7552]{1,0:T(8,128)(2,1)S(1)} %pad_maximum_fusion.30), channel_id=1, source_target_pairs={{0,4},{1,5},{2,6},{3,7},{4,0},{5,1},{6,2},{7,3},{8,12},{9,13},{10,... | collective-permute-start | bytes 2899976 | tf_op jit(solution)/shard_map/ppermute | solution.py:42
  82.6 101.3 %collective-permute-start.6 = (bf16[64,11008]{1,0:T(8,128)(2,1)S(1)}, bf16[64,11008]{1,0:T(8,128)(2,1)S(1)}, u32[]{:S(2)}, u32[]{:S(2)}) collective-permute-start(bf16[64,11008]{1,0:T(8,128)(2,1)S(1)} %pad_maximum_fusion.24), channel_id=1, source_target_pairs={{0,4},{1,5},{2,6},{3,7},{4,0},{5,1},{6,2},{7,3},{8,12},{9,13},{10,... | collective-permute-start | bytes 4227080 | tf_op jit(solution)/shard_map/ppermute | solution.py:42
  82.7 131.4 %collective-permute-start.7 = (bf16[128,7552]{1,0:T(8,128)(2,1)S(1)}, bf16[128,7552]{1,0:T(8,128)(2,1)S(1)}, u32[]{:S(2)}, u32[]{:S(2)}) collective-permute-start(bf16[128,7552]{1,0:T(8,128)(2,1)S(1)} %get-tuple-element.238), channel_id=1, source_target_pairs={{0,2},{1,3},{2,0},{3,1},{4,6},{5,7},{6,4},{7,5},{8,10},{9,11},{10,... | collective-permute-start | bytes 5799944 | tf_op jit(solution)/shard_map/ppermute | solution.py:42
  214.3 94.0 %collective-permute-start.8 = (bf16[128,11008]{1,0:T(8,128)(2,1)S(1)}, bf16[128,11008]{1,0:T(8,128)(2,1)S(1)}, u32[]{:S(2)}, u32[]{:S(2)}) collective-permute-start(bf16[128,11008]{1,0:T(8,128)(2,1)S(1)} %constant_dynamic-update-slice_fusion.2), channel_id=1, source_target_pairs={{0,2},{1,3},{2,0},{3,1},{4,6},{5,7},{6,4},{7,5},{8,10},{9,11},{10,... | collective-permute-start | bytes 8454152 | tf_op jit(solution)/shard_map/ppermute | solution.py:42
  214.4 96.6 %collective-permute-start.9 = (bf16[256,7552]{1,0:T(8,128)(2,1)S(1)}, bf16[256,7552]{1,0:T(8,128)(2,1)S(1)}, u32[]{:S(2)}, u32[]{:S(2)}) collective-permute-start(bf16[256,7552]{1,0:T(8,128)(2,1)S(1)} %constant_dynamic-update-slice_fusion.4.refs_0_), channel_id=1, source_target_pairs={{0,16},{8,24},{16,0},{24,8},{1,17},{9,25},{17,1},{25,9},{2,18},{10... | collective-permute-start | bytes 11599880 | tf_op jit(solution)/shard_map/ppermute | solution.py:42
  313.0 162.4 %collective-permute-start.10 = (bf16[256,11008]{1,0:T(8,128)(2,1)}, bf16[256,11008]{1,0:T(8,128)(2,1)}, u32[]{:S(2)}, u32[]{:S(2)}) collective-permute-start(bf16[256,11008]{1,0:T(8,128)(2,1)} %pad_maximum_fusion.8.refs_0_), channel_id=1, source_target_pairs={{0,1},{1,0},{2,3},{3,2},{4,5},{5,4},{6,7},{7,6},{8,9},{9,8},{10,11... | collective-permute-start | bytes 16908296 | tf_op jit(solution)/shard_map/ppermute | solution.py:42
  314.5 121.3 %collective-permute-start = (bf16[2,64]{1,0:T(2,128)(2,1)S(1)}, bf16[2,64]{1,0:T(2,128)(2,1)S(1)}, u32[]{:S(2)}, u32[]{:S(2)}) collective-permute-start(bf16[2,64]{1,0:T(2,128)(2,1)S(1)} %pad_maximum_fusion.36), channel_id=1, source_target_pairs={{0,1},{1,0},{2,3},{3,2},{4,5},{5,4},{6,7},{7,6},{8,9},{9,8},{10,11... | collective-permute-start | bytes 776 | tf_op jit(solution)/shard_map/ppermute | solution.py:42
  435.9 3.5 collective-permute-start.1
  439.5 10.8 collective-permute-start.2
  450.3 3.2 collective-permute-start.3
  453.5 16.6 collective-permute-start.4
  470.2 731.2 %copy-start.62 = (f32[1,2048]{1,0:T(1,128)}, f32[1,2048]{1,0:T(1,128)S(1)}, u32[]{:S(2)}) copy-start(f32[1,2048]{1,0:T(1,128)S(1)} %get-tuple-element.243) | copy-start | bytes 24580
  500.1 241.6 %copy-start.68 = (s32[2,1,4096]{2,1,0:T(1,128)S(1)}, s32[2,1,4096]{2,1,0:T(1,128)}, u32[]{:S(2)}) copy-start(s32[2,1,4096]{2,1,0:T(1,128)} %param.12) | copy-start | bytes 98308
  500.1 253.0 %all-to-all-start = ((bf16[8,2,512,384]{3,2,1,0:T(8,128)(2,1)}), bf16[8,2,512,384]{3,2,1,0:T(8,128)(2,1)}, u32[]{:S(2)}, u32[]{:S(2)}) async-start(bf16[8,2,512,384]{3,2,1,0:T(8,128)(2,1)} %bitcast.351), calls=%async_computation | async-start | bytes 12582912 | tf_op jit(solution)/shard_map/all_to_all | solution.py:438
  505.8 154.1 %collective-permute-start.12 = (bf16[256,7552]{1,0:T(8,128)(2,1)}, bf16[256,7552]{1,0:T(8,128)(2,1)}, u32[]{:S(2)}, u32[]{:S(2)}) collective-permute-start(bf16[256,7552]{1,0:T(8,128)(2,1)} %copy-done.10), channel_id=1, source_target_pairs={{0,1},{1,0},{2,3},{3,2},{4,5},{5,4},{6,7},{7,6},{8,9},{9,8},{10,11... | collective-permute-start | bytes 11599880 | tf_op jit(solution)/shard_map/ppermute | solution.py:42
  507.8 233.9 %collective-permute-start.11 = (bf16[256,7552]{1,0:T(8,128)(2,1)}, bf16[256,7552]{1,0:T(8,128)(2,1)}, u32[]{:S(2)}, u32[]{:S(2)}) collective-permute-start(bf16[256,7552]{1,0:T(8,128)(2,1)} %copy-done.8), channel_id=1, source_target_pairs={{0,1},{1,0},{2,3},{3,2},{4,5},{5,4},{6,7},{7,6},{8,9},{9,8},{10,11... | collective-permute-start | bytes 11599880 | tf_op jit(solution)/shard_map/ppermute | solution.py:42
  507.9 241.1 %collective-permute-start.14 = (bf16[256,11008]{1,0:T(8,128)(2,1)}, bf16[256,11008]{1,0:T(8,128)(2,1)}, u32[]{:S(2)}, u32[]{:S(2)}) collective-permute-start(bf16[256,11008]{1,0:T(8,128)(2,1)} %collective-permute-done.10.refs_1_), channel_id=1, source_target_pairs={{0,16},{8,24},{16,0},{24,8},{1,17},{9,25},{17,1},{25,9},{2,18},{10... | collective-permute-start | bytes 16908296 | tf_op jit(solution)/shard_map/ppermute | solution.py:42
  509.1 242.6 %collective-permute-start.13 = (bf16[256,11008]{1,0:T(8,128)(2,1)}, bf16[256,11008]{1,0:T(8,128)(2,1)}, u32[]{:S(2)}, u32[]{:S(2)}) collective-permute-start(bf16[256,11008]{1,0:T(8,128)(2,1)} %pad_maximum_fusion.8.refs_0_), channel_id=1, source_target_pairs={{0,16},{8,24},{16,0},{24,8},{1,17},{9,25},{17,1},{25,9},{2,18},{10... | collective-permute-start | bytes 16908296 | tf_op jit(solution)/shard_map/ppermute | solution.py:42
  509.9 236.6 %collective-permute-start.16 = (bf16[256,7552]{1,0:T(8,128)(2,1)}, bf16[256,7552]{1,0:T(8,128)(2,1)S(1)}, u32[]{:S(2)}, u32[]{:S(2)}) collective-permute-start(bf16[256,7552]{1,0:T(8,128)(2,1)} %copy-done.10), channel_id=1, source_target_pairs={{0,8},{8,0},{16,24},{24,16},{1,9},{9,1},{17,25},{25,17},{2,10},{10... | collective-permute-start | bytes 11599880 | tf_op jit(solution)/shard_map/ppermute | solution.py:42
  659.9 93.1 %collective-permute-start.20 = (bf16[256,11008]{1,0:T(8,128)(2,1)}, bf16[256,11008]{1,0:T(8,128)(2,1)}, u32[]{:S(2)}, u32[]{:S(2)}) collective-permute-start(bf16[256,11008]{1,0:T(8,128)(2,1)} %collective-permute-done.10.refs_1_), channel_id=1, source_target_pairs={{0,8},{8,0},{16,24},{24,16},{1,9},{9,1},{17,25},{25,17},{2,10},{10... | collective-permute-start | bytes 16908296 | tf_op jit(solution)/shard_map/ppermute | solution.py:42
  741.8 10.7 collective-permute-start.15
  748.5 109.8 %collective-permute-start.19 = (bf16[256,11008]{1,0:T(8,128)(2,1)}, bf16[256,11008]{1,0:T(8,128)(2,1)}, u32[]{:S(2)}, u32[]{:S(2)}) collective-permute-start(bf16[256,11008]{1,0:T(8,128)(2,1)} %pad_maximum_fusion.8.refs_0_), channel_id=1, source_target_pairs={{0,8},{8,0},{16,24},{24,16},{1,9},{9,1},{17,25},{25,17},{2,10},{10... | collective-permute-start | bytes 16908296 | tf_op jit(solution)/shard_map/ppermute | solution.py:42
  749.0 109.3 %collective-permute-start.22 = (bf16[256,11008]{1,0:T(8,128)(2,1)}, bf16[256,11008]{1,0:T(8,128)(2,1)}, u32[]{:S(2)}, u32[]{:S(2)}) collective-permute-start(bf16[256,11008]{1,0:T(8,128)(2,1)} %collective-permute-done.14.refs_3_), channel_id=1, source_target_pairs={{0,8},{8,0},{16,24},{24,16},{1,9},{9,1},{17,25},{25,17},{2,10},{10... | collective-permute-start | bytes 16908296 | tf_op jit(solution)/shard_map/ppermute | solution.py:42
  751.7 106.6 %collective-permute-start.21 = (bf16[256,11008]{1,0:T(8,128)(2,1)}, bf16[256,11008]{1,0:T(8,128)(2,1)}, u32[]{:S(2)}, u32[]{:S(2)}) collective-permute-start(bf16[256,11008]{1,0:T(8,128)(2,1)} %collective-permute-done.13.refs_2_), channel_id=1, source_target_pairs={{0,8},{8,0},{16,24},{24,16},{1,9},{9,1},{17,25},{25,17},{2,10},{10... | collective-permute-start | bytes 16908296 | tf_op jit(solution)/shard_map/ppermute | solution.py:42
  752.4 274.0 %copy-start.14 = (s32[2,1,4096]{2,1,0:T(1,128)}, s32[2,1,4096]{2,1,0:T(1,128)S(1)}, u32[]{:S(2)}) copy-start(s32[2,1,4096]{2,1,0:T(1,128)S(1)} %get-tuple-element.282.lo_ref) | copy-start | bytes 98308
  752.5 105.8 %collective-permute-start.18 = (bf16[256,7552]{1,0:T(8,128)(2,1)}, bf16[256,7552]{1,0:T(8,128)(2,1)}, u32[]{:S(2)}, u32[]{:S(2)}) collective-permute-start(bf16[256,7552]{1,0:T(8,128)(2,1)} %collective-permute-done.12.refs_3_), channel_id=1, source_target_pairs={{0,8},{8,0},{16,24},{24,16},{1,9},{9,1},{17,25},{25,17},{2,10},{10... | collective-permute-start | bytes 11599880 | tf_op jit(solution)/shard_map/ppermute | solution.py:42
  753.0 105.2 %collective-permute-start.17 = (bf16[256,7552]{1,0:T(8,128)(2,1)}, bf16[256,7552]{1,0:T(8,128)(2,1)}, u32[]{:S(2)}, u32[]{:S(2)}) collective-permute-start(bf16[256,7552]{1,0:T(8,128)(2,1)} %collective-permute-done.11.refs_2_), channel_id=1, source_target_pairs={{0,8},{8,0},{16,24},{24,16},{1,9},{9,1},{17,25},{25,17},{2,10},{10... | collective-permute-start | bytes 11599880 | tf_op jit(solution)/shard_map/ppermute | solution.py:42
  883.4 143.0 %all-to-all-start.2 = ((bf16[8,2,512,384]{3,2,1,0:T(8,128)(2,1)}), bf16[8,2,512,384]{3,2,1,0:T(8,128)(2,1)}, u32[]{:S(2)}, u32[]{:S(2)}) async-start(bf16[8,2,512,384]{3,2,1,0:T(8,128)(2,1)} %bitcast.352), calls=%async_computation.2 | async-start | bytes 12582912 | tf_op jit(solution)/shard_map/all_to_all | solution.py:438
  991.8 174.6 %copy-start.73 = (f32[512]{0:T(512)}, f32[512]{0:T(512)S(1)}, u32[]{:S(2)}) copy-start(f32[512]{0:T(512)S(1)} %add_rsqrt_fusion.2) | copy-start | bytes 6148
  1073.1 106.5 %all-to-all-start.3 = ((bf16[8,2,512,128]{3,2,1,0:T(8,128)(2,1)}), bf16[8,2,512,128]{3,2,1,0:T(8,128)(2,1)S(1)}, u32[]{:S(2)}, u32[]{:S(2)}) async-start(bf16[8,2,512,128]{3,2,1,0:T(8,128)(2,1)} %get-tuple-element.91.o_ref), calls=%async_computation.3 | async-start | bytes 4194304 | tf_op jit(solution)/shard_map/all_to_all | solution.py:442
  1180.9 80.0 %all-to-all-start.4 = ((bf16[8,2,512,128]{3,2,1,0:T(8,128)(2,1)}), bf16[8,2,512,128]{3,2,1,0:T(8,128)(2,1)S(1)}, u32[]{:S(2)}, u32[]{:S(2)}) async-start(bf16[8,2,512,128]{3,2,1,0:T(8,128)(2,1)} %bitcast.383), calls=%async_computation.4 | async-start | bytes 4194304 | tf_op jit(solution)/shard_map/all_to_all | solution.py:438
  1303.7 88.8 %collective-permute-start.23 = (bf16[2752,2048]{1,0:T(8,128)(2,1)}, bf16[2752,2048]{1,0:T(8,128)(2,1)}, u32[]{:S(2)}, u32[]{:S(2)}) collective-permute-start(bf16[2752,2048]{1,0:T(8,128)(2,1)} %bitcast.47), channel_id=1, source_target_pairs={{0,8},{8,0},{16,24},{24,16},{1,9},{9,1},{17,25},{25,17},{2,10},{10... | collective-permute-start | bytes 33816584 | tf_op jit(solution)/shard_map/ppermute | solution.py:42
  1337.4 77.9 %all-to-all-start.5 = ((bf16[8,1,512,384]{3,2,1,0:T(8,128)(2,1)}), bf16[8,1,512,384]{3,2,1,0:T(8,128)(2,1)}, u32[]{:S(2)}, u32[]{:S(2)}) async-start(bf16[8,1,512,384]{3,2,1,0:T(8,128)(2,1)} %copy-done.7), calls=%async_computation.5 | async-start | bytes 6291456 | tf_op jit(solution)/shard_map/all_to_all | solution.py:442
  1459.2 157.2 %collective-permute-start.25 = (bf16[1024,5504]{1,0:T(8,128)(2,1)}, bf16[1024,5504]{1,0:T(8,128)(2,1)}, u32[]{:S(2)}, u32[]{:S(2)}) collective-permute-start(bf16[1024,5504]{1,0:T(8,128)(2,1)} %convolution_convert_fusion.2), channel_id=1, source_target_pairs={{0,8},{8,0},{16,24},{24,16},{1,9},{9,1},{17,25},{25,17},{2,10},{10... | collective-permute-start | bytes 33816584 | tf_op jit(solution)/shard_map/ppermute | solution.py:42
  1459.2 124.4 %collective-permute-start.24 = (bf16[1376,2048]{1,0:T(8,128)(2,1)}, bf16[1376,2048]{1,0:T(8,128)(2,1)}, u32[]{:S(2)}, u32[]{:S(2)}) collective-permute-start(bf16[1376,2048]{1,0:T(8,128)(2,1)} %fusion.2), channel_id=1, source_target_pairs={{0,16},{8,24},{16,0},{24,8},{1,17},{9,25},{17,1},{25,9},{2,18},{10... | collective-permute-start | bytes 16908296 | tf_op jit(solution)/shard_map/ppermute | solution.py:42
  1461.1 75.9 %all-to-all-start.6 = ((bf16[8,1,512,384]{3,2,1,0:T(8,128)(2,1)}), bf16[8,1,512,384]{3,2,1,0:T(8,128)(2,1)}, u32[]{:S(2)}, u32[]{:S(2)}) async-start(bf16[8,1,512,384]{3,2,1,0:T(8,128)(2,1)} %attend_back.5), calls=%async_computation.6 | async-start | bytes 6291456 | tf_op jit(solution)/shard_map/all_to_all | solution.py:442
  1504.0 178.9 %collective-permute-start.26 = (bf16[1024,5504]{1,0:T(8,128)(2,1)}, bf16[1024,5504]{1,0:T(8,128)(2,1)}, u32[]{:S(2)}, u32[]{:S(2)}) collective-permute-start(bf16[1024,5504]{1,0:T(8,128)(2,1)} %convolution_convert_fusion.1), channel_id=1, source_target_pairs={{0,8},{8,0},{16,24},{24,16},{1,9},{9,1},{17,25},{25,17},{2,10},{10... | collective-permute-start | bytes 33816584 | tf_op jit(solution)/shard_map/ppermute | solution.py:42
  1628.8 227.8 %collective-permute-start.27 = (bf16[512,5504]{1,0:T(8,128)(2,1)}, bf16[512,5504]{1,0:T(8,128)(2,1)}, u32[]{:S(2)}, u32[]{:S(2)}) collective-permute-start(bf16[512,5504]{1,0:T(8,128)(2,1)} %add_convert_fusion.3), channel_id=1, source_target_pairs={{0,1},{1,0},{2,3},{3,2},{4,5},{5,4},{6,7},{7,6},{8,9},{9,8},{10,11... | collective-permute-start | bytes 16908296 | tf_op jit(solution)/shard_map/ppermute | solution.py:42
  1660.3 115.7 %all-to-all-start.7 = ((bf16[8,2,512,128]{3,2,1,0:T(8,128)(2,1)}), bf16[8,2,512,128]{3,2,1,0:T(8,128)(2,1)S(1)}, u32[]{:S(2)}, u32[]{:S(2)}) async-start(bf16[8,2,512,128]{3,2,1,0:T(8,128)(2,1)} %bitcast.381), calls=%async_computation.7 | async-start | bytes 4194304 | tf_op jit(solution)/shard_map/all_to_all | solution.py:438
  1680.9 210.3 %collective-permute-start.33 = (bf16[4,172,2048]{2,0,1:T(4,128)(2,1)}, bf16[4,172,2048]{2,0,1:T(4,128)(2,1)}, u32[]{:S(2)}, u32[]{:S(2)}) collective-permute-start(bf16[4,172,2048]{2,0,1:T(4,128)(2,1)} %copy.161), channel_id=1, source_target_pairs={{0,1},{1,0},{2,3},{3,2},{4,5},{5,4},{6,7},{7,6},{8,9},{9,8},{10,11... | collective-permute-start | bytes 8454152 | tf_op jit(solution)/shard_map/ppermute | solution.py:42
  1701.3 196.9 %collective-permute-start.28 = (bf16[1024,2048]{1,0:T(8,128)(2,1)}, bf16[1024,2048]{1,0:T(8,128)(2,1)}, u32[]{:S(2)}, u32[]{:S(2)}) collective-permute-start(bf16[1024,2048]{1,0:T(8,128)(2,1)} %convolution_convert_fusion.7), channel_id=1, source_target_pairs={{0,8},{8,0},{16,24},{24,16},{1,9},{9,1},{17,25},{25,17},{2,10},{10... | collective-permute-start | bytes 12582920 | tf_op jit(solution)/shard_map/ppermute | solution.py:42
  1701.3 251.7 %collective-permute-start.29 = (bf16[512,5504]{1,0:T(8,128)(2,1)}, bf16[512,5504]{1,0:T(8,128)(2,1)}, u32[]{:S(2)}, u32[]{:S(2)}) collective-permute-start(bf16[512,5504]{1,0:T(8,128)(2,1)} %add_convert_fusion.2), channel_id=1, source_target_pairs={{0,16},{8,24},{16,0},{24,8},{1,17},{9,25},{17,1},{25,9},{2,18},{10... | collective-permute-start | bytes 16908296 | tf_op jit(solution)/shard_map/ppermute | solution.py:42
  1809.6 125.2 %all-to-all-start.8 = ((bf16[8,1,512,384]{3,2,1,0:T(8,128)(2,1)}), bf16[8,1,512,384]{3,2,1,0:T(8,128)(2,1)}, u32[]{:S(2)}, u32[]{:S(2)}) async-start(bf16[8,1,512,384]{3,2,1,0:T(8,128)(2,1)} %copy-done.6), calls=%async_computation.8 | async-start | bytes 6291456 | tf_op jit(solution)/shard_map/all_to_all | solution.py:442
  1866.5 64.3 %collective-permute-start.34 = (bf16[256,5504]{1,0:T(8,128)(2,1)}, bf16[256,5504]{1,0:T(8,128)(2,1)}, u32[]{:S(2)}, u32[]{:S(2)}) collective-permute-start(bf16[256,5504]{1,0:T(8,128)(2,1)} %dynamic-slice_bitcast_fusion.3), channel_id=1, source_target_pairs={{0,16},{8,24},{16,0},{24,8},{1,17},{9,25},{17,1},{25,9},{2,18},{10... | collective-permute-start | bytes 8454152 | tf_op jit(solution)/shard_map/ppermute | solution.py:42
  1904.5 67.6 %collective-permute-start.30 = (bf16[512,2048]{1,0:T(8,128)(2,1)}, bf16[512,2048]{1,0:T(8,128)(2,1)}, u32[]{:S(2)}, u32[]{:S(2)}) collective-permute-start(bf16[512,2048]{1,0:T(8,128)(2,1)} %add_convert_fusion.11), channel_id=1, source_target_pairs={{0,16},{8,24},{16,0},{24,8},{1,17},{9,25},{17,1},{25,9},{2,18},{10... | collective-permute-start | bytes 6291464 | tf_op jit(solution)/shard_map/ppermute | solution.py:42
  1934.8 84.8 %all-to-all-start.9 = ((bf16[8,1,512,384]{3,2,1,0:T(8,128)(2,1)}), bf16[8,1,512,384]{3,2,1,0:T(8,128)(2,1)S(1)}, u32[]{:S(2)}, u32[]{:S(2)}) async-start(bf16[8,1,512,384]{3,2,1,0:T(8,128)(2,1)} %attend_back.7), calls=%async_computation.9 | async-start | bytes 6291456 | tf_op jit(solution)/shard_map/all_to_all | solution.py:442
  1997.2 85.5 %collective-permute-start.35 = (bf16[4,64,5504]{2,1,0:T(8,128)(2,1)}, bf16[4,64,5504]{2,1,0:T(8,128)(2,1)}, u32[]{:S(2)}, u32[]{:S(2)}) collective-permute-start(bf16[4,64,5504]{2,1,0:T(8,128)(2,1)} %dynamic-slice_bitcast_fusion.2), channel_id=1, source_target_pairs={{0,1},{1,0},{2,3},{3,2},{4,5},{5,4},{6,7},{7,6},{8,9},{9,8},{10,11... | collective-permute-start | bytes 8454152 | tf_op jit(solution)/shard_map/ppermute | solution.py:42
  1999.9 80.9 %collective-permute-start.36 = (bf16[4,64,2048]{2,1,0:T(8,128)(2,1)}, bf16[4,64,2048]{2,1,0:T(8,128)(2,1)}, u32[]{:S(2)}, u32[]{:S(2)}) collective-permute-start(bf16[4,64,2048]{2,1,0:T(8,128)(2,1)} %dynamic-slice_bitcast_fusion.7), channel_id=1, source_target_pairs={{0,1},{1,0},{2,3},{3,2},{4,5},{5,4},{6,7},{7,6},{8,9},{9,8},{10,11... | collective-permute-start | bytes 3145736 | tf_op jit(solution)/shard_map/ppermute | solution.py:42
  2044.8 80.1 %collective-permute-start.31 = (bf16[1024,3072]{1,0:T(8,128)(2,1)}, bf16[1024,3072]{1,0:T(8,128)(2,1)}, u32[]{:S(2)}, u32[]{:S(2)}) collective-permute-start(bf16[1024,3072]{1,0:T(8,128)(2,1)} %convolution_convert_fusion.6), channel_id=1, source_target_pairs={{0,8},{8,0},{16,24},{24,16},{1,9},{9,1},{17,25},{25,17},{2,10},{10... | collective-permute-start | bytes 18874376 | tf_op jit(solution)/shard_map/ppermute | solution.py:42
  2055.4 78.9 %collective-permute-start.32 = (bf16[1024,3072]{1,0:T(8,128)(2,1)}, bf16[1024,3072]{1,0:T(8,128)(2,1)}, u32[]{:S(2)}, u32[]{:S(2)}) collective-permute-start(bf16[1024,3072]{1,0:T(8,128)(2,1)} %convolution_convert_fusion.5), channel_id=1, source_target_pairs={{0,8},{8,0},{16,24},{24,16},{1,9},{9,1},{17,25},{25,17},{2,10},{10... | collective-permute-start | bytes 18874376 | tf_op jit(solution)/shard_map/ppermute | solution.py:42
  2093.1 102.6 %collective-permute-start.37 = (bf16[2,64,18560]{2,1,0:T(8,128)(2,1)}, bf16[2,64,18560]{2,1,0:T(8,128)(2,1)}, u32[]{:S(2)}, u32[]{:S(2)}) collective-permute-start(bf16[2,64,18560]{2,1,0:T(8,128)(2,1)} %dynamic-slice_bitcast_fusion), channel_id=1, source_target_pairs={{0,2},{1,3},{2,0},{3,1},{4,6},{5,7},{6,4},{7,5},{8,10},{9,11},{10,... | collective-permute-start | bytes 14254088 | tf_op jit(solution)/shard_map/ppermute | solution.py:42
  2132.6 113.7 %collective-permute-start.38 = (bf16[512,3072]{1,0:T(8,128)(2,1)}, bf16[512,3072]{1,0:T(8,128)(2,1)}, u32[]{:S(2)}, u32[]{:S(2)}) collective-permute-start(bf16[512,3072]{1,0:T(8,128)(2,1)} %add_convert_fusion.7), channel_id=1, source_target_pairs={{0,16},{8,24},{16,0},{24,8},{1,17},{9,25},{17,1},{25,9},{2,18},{10... | collective-permute-start | bytes 9437192 | tf_op jit(solution)/shard_map/ppermute | solution.py:42
  2143.5 117.8 %collective-permute-start.39 = (bf16[512,3072]{1,0:T(8,128)(2,1)}, bf16[512,3072]{1,0:T(8,128)(2,1)}, u32[]{:S(2)}, u32[]{:S(2)}) collective-permute-start(bf16[512,3072]{1,0:T(8,128)(2,1)} %add_convert_fusion.6), channel_id=1, source_target_pairs={{0,1},{1,0},{2,3},{3,2},{4,5},{5,4},{6,7},{7,6},{8,9},{9,8},{10,11... | collective-permute-start | bytes 9437192 | tf_op jit(solution)/shard_map/ppermute | solution.py:42
  2221.7 10.2 collective-permute-start.45
  2231.9 8.4 collective-permute-start.46
  2240.3 6.0 collective-permute-start.47
  2246.3 104.4 %collective-permute-start.44 = (bf16[1,64,18560]{2,1,0:T(8,128)(2,1)S(1)}, bf16[1,64,18560]{2,1,0:T(8,128)(2,1)S(1)}, u32[]{:S(2)}, u32[]{:S(2)}) collective-permute-start(bf16[1,64,18560]{2,1,0:T(8,128)(2,1)S(1)} %constant_dynamic-slice_fusion.8), channel_id=1, source_target_pairs={{0,4},{1,5},{2,6},{3,7},{4,0},{5,1},{6,2},{7,3},{8,12},{9,13},{10,... | collective-permute-start | bytes 7127048 | tf_op jit(solution)/shard_map/ppermute | solution.py:42
  2267.5 84.0 %collective-permute-start.40 = (bf16[4,64,3072]{2,1,0:T(8,128)(2,1)S(1)}, bf16[4,64,3072]{2,1,0:T(8,128)(2,1)S(1)}, u32[]{:S(2)}, u32[]{:S(2)}) collective-permute-start(bf16[4,64,3072]{2,1,0:T(8,128)(2,1)S(1)} %dynamic-slice_bitcast_fusion.6), channel_id=1, source_target_pairs={{0,1},{1,0},{2,3},{3,2},{4,5},{5,4},{6,7},{7,6},{8,9},{9,8},{10,11... | collective-permute-start | bytes 4718600 | tf_op jit(solution)/shard_map/ppermute | solution.py:42
  2267.8 84.3 %collective-permute-start.41 = (bf16[256,3072]{1,0:T(8,128)(2,1)S(1)}, bf16[256,3072]{1,0:T(8,128)(2,1)S(1)}, u32[]{:S(2)}, u32[]{:S(2)}) collective-permute-start(bf16[256,3072]{1,0:T(8,128)(2,1)S(1)} %dynamic-slice_bitcast_fusion.5), channel_id=1, source_target_pairs={{0,16},{8,24},{16,0},{24,8},{1,17},{9,25},{17,1},{25,9},{2,18},{10... | collective-permute-start | bytes 4718600 | tf_op jit(solution)/shard_map/ppermute | solution.py:42
  2353.1 36.4 %collective-permute-start.42 = (bf16[2,64,6144]{2,1,0:T(8,128)(2,1)S(1)}, bf16[2,64,6144]{2,1,0:T(8,128)(2,1)S(1)}, u32[]{:S(2)}, u32[]{:S(2)}) collective-permute-start(bf16[2,64,6144]{2,1,0:T(8,128)(2,1)S(1)} %dynamic-slice_bitcast_fusion.4), channel_id=1, source_target_pairs={{0,2},{1,3},{2,0},{3,1},{4,6},{5,7},{6,4},{7,5},{8,10},{9,11},{10,... | collective-permute-start | bytes 4718600 | tf_op jit(solution)/shard_map/ppermute | solution.py:42
  2353.2 36.3 %collective-permute-start.48 = (f32[2,2,64]{2,0,1:T(2,128)S(1)}, f32[2,2,64]{2,0,1:T(2,128)S(1)}, u32[]{:S(2)}, u32[]{:S(2)}) collective-permute-start(f32[2,2,64]{2,0,1:T(2,128)S(1)} %bitcast.457), channel_id=1, source_target_pairs={{0,2},{1,3},{2,0},{3,1},{4,6},{5,7},{6,4},{7,5},{8,10},{9,11},{10,... | collective-permute-start | bytes 3080 | tf_op jit(solution)/shard_map/ppermute | solution.py:42
  2389.9 21.2 collective-permute-start.49
  2391.0 36.7 %collective-permute-start.43 = (bf16[1,64,6144]{2,1,0:T(8,128)(2,1)}, bf16[1,64,6144]{2,1,0:T(8,128)(2,1)}, u32[]{:S(2)}, u32[]{:S(2)}) collective-permute-start(bf16[1,64,6144]{2,1,0:T(8,128)(2,1)} %constant_dynamic-slice_fusion.9), channel_id=1, source_target_pairs={{0,4},{1,5},{2,6},{3,7},{4,0},{5,1},{6,2},{7,3},{8,12},{9,13},{10,... | collective-permute-start | bytes 2359304 | tf_op jit(solution)/shard_map/ppermute | solution.py:42
  (100 other events, 2228.6 us)
Sparse Core Ops, SparseCore 0:
  11.6 260.7 all-gather.1

commit v6 on v5

--- a/solution.py
+++ b/solution.py
@@ -495,7 +495,7 @@
     later = Gather([w_gate_up[:, FF:], w_down.reshape(w_qkv.shape[0], -1)], True)
     far = len(soon.far)
 
-    soon.wait(all_gains)
+    soon.wait(all_gains, h_attn)
     soon.far_step(0)
     for n in range(1, far):
         later.wait(*soon.values())
@@ -510,37 +510,36 @@
     later.near_step(0)
     h_kept = step_in = after(h_attn, *later.values())
     saved, attended, arrived = [], [], []
-    for g in range(groups):
-        qkv_rows = jnp.dot(of(step_in, g), full_qkv, preferred_element_type=f32).astype(bf16)
-        qkv = to_heads(qkv_rows, micros)
-        if g == 0:
-            ready = soon.values() + later.values()
-            for w in (soon, later):
-                w.wait(*ready)
-                w.near_step(1)
-            qkv = after(qkv, *soon.values(), *later.values())
-        else:
-            qkv = after(qkv, gate_first)
+
+    def project(g, *others):
+        qkv_rows = jnp.dot(of(after(h_kept, *others), g), full_qkv, preferred_element_type=f32).astype(bf16)
+        arrived.append(to_heads(qkv_rows, micros))
+
+    def attention(g, others):
+        qkv = after(arrived[g], *others)
         mixed, lse = attend(qkv, bounds[g], low[g])
         saved.append((qkv, mixed, lse))
-        attended.append(rows_of(to_rows(mixed), micros))
-        if g == 0:
-            soon.near_step(2)
-            later.near_step(2)
-            step_in = after(h_kept, attended[0], *soon.values(), *later.values())
-            full_gate, full_out = soon.finish()
-
-            mid_first = of(x, 0) + jnp.dot(attended[0], full_out, preferred_element_type=f32)
-            scale_first = norm_scale(mid_first)
-            h_first = (mid_first * scale_first * gain_m).astype(bf16)
-            gate_first = jnp.dot(h_first, full_gate, preferred_element_type=f32)
+        return to_rows(mixed)
+
+    project(0)
+    ready = soon.values() + later.values()
+    for w in (soon, later):
+        w.wait(*ready)
+        w.near_step(1)
+    back_rows = attention(0, soon.values() + later.values())
+    soon.near_step(2)
+    later.near_step(2)
+    full_gate, full_out = soon.finish()
     full_up, full_down = later.finish()
     full_down = full_down.reshape(FF, D)
+    attended.append(rows_of(after(back_rows, full_gate, full_out, full_up, full_down), micros))
+    if groups > 1:
+        project(1, attended[0])
 
     parts = []
     grads = []
     rows_grad = []
-    mark = (mixed,)
+    mark = ()
 
     def back_of(g, *others):
         qkv, mixed, lse = saved[g]
@@ -554,13 +553,10 @@
 
     for g in range(groups):
         final = g == groups - 1
-        if g == 0:
-            mid, scale_m, h_mlp, gate = mid_first, scale_first, h_first, gate_first
-        else:
-            mid = of(x, g) + jnp.dot(after(attended[g], *mark), full_out, preferred_element_type=f32)
-            scale_m = norm_scale(mid)
-            h_mlp = (mid * scale_m * gain_m).astype(bf16)
-            gate = jnp.dot(h_mlp, full_gate, preferred_element_type=f32)
+        mid = of(x, g) + jnp.dot(after(attended[g], *mark), full_out, preferred_element_type=f32)
+        scale_m = norm_scale(mid)
+        h_mlp = (mid * scale_m * gain_m).astype(bf16)
+        gate = jnp.dot(h_mlp, full_gate, preferred_element_type=f32)
         up = jnp.dot(after(h_mlp, *mark), full_up, preferred_element_type=f32)
         sig = jax.nn.sigmoid(gate)
         act = (gate * sig * up).astype(bf16)
@@ -583,24 +579,26 @@
         grad_up = (grad_act * (gate * sig)).astype(bf16)
         parts[g] += [grad_gate, grad_up]
         mark = (grad_gate, grad_up)
+        if not final:
+            back_rows = attention(g + 1, mark)
+            mark = (saved[-1][1],)
         if final:
             gate_r = Reduce(pieces_of(sides, False), jnp.concatenate([p[4] for p in parts], axis=0), False)
             up_r = Reduce(pieces_of(sides, True), jnp.concatenate([p[5] for p in parts], axis=0), True)
             mark = (up_r.cross(*mark),)
             mark = (gate_r.cross(*mark),)
         if final:
-            mark = mark + (down.away,) + tuple(r for pieces in rows_grad for r in pieces)
+            mark = (up_r.send(*mark),)
         half_grad = nt(after(grad_gate, *mark), full_gate)
         mark = (half_grad,)
-        if final:
-            mark = (down.keep(*mark),)
-            down.second()
-            mark = (up_r.send(*mark),)
         grad_h_mlp = half_grad + nt(after(grad_up, *mark), full_up)
         grad_mid_norm, gain_part = norm_backward(grad_h_mlp, mid, scale_m, gain_m)
         grad_mid = cot_part.astype(f32) + grad_mid_norm
         grad_branch = grad_mid.astype(bf16)
-        grad_rows = nt(grad_branch, full_out).astype(bf16)
+        arrivals = [r for pieces in rows_grad for r in pieces]
+        grad_rows = nt(after(grad_branch, *arrivals), full_out).astype(bf16)
+        if not final:
+            attended.append(rows_of(after(back_rows, grad_rows), micros))
         grads.append(to_heads(grad_rows, micros))
         parts[g] += [grad_mid, grad_branch, gain_part]
         mark = (grad_rows,)
@@ -610,6 +608,8 @@
     early = [down, up_r, gate_r, out_r]
     mark = (gate_r.send(*mark),)
     mark = (out_r.cross(*mark),)
+    mark = (down.keep(*mark),)
+    down.second(grads[-1])
     mark = (back_of(groups - 1, *mark),)
     mark = (up_r.keep(*mark),)
     up_r.second()
@@ -647,13 +647,12 @@
         mark = (finish_tokens(g, *mark),)
     for r in late:
         mark = (r.send(*mark),)
-    mark = mark + (first.total,)
     g = groups - 1
     grad_h_attn = nt(after(last_rows, *mark), full_qkv)
     grad_norm, gain_part = norm_backward(grad_h_attn, of(x, g), of(scale_a, g), gain_a)
     grad_tokens.append(parts[g][6] + grad_norm)
     gain_a_parts.append(gain_part)
-    mark = (grad_tokens[-1],)
+    mark = (grad_tokens[-1], first.total)
     for r in late:
         mark = (r.keep(*mark),)
     for r in late:

time: 2450 us -> 2380 us (0.971)
  blocking collectives: 54.8 us -> 0 us
    all_to_all x1 -> x0, blocking collectives: 54.8 us -> none  [to_rows(): return lax.all_to_all(whole, 'seq', 0, 0, tiled=True)]
    dot_general x4 -> x2, matrix products: 67.2 us -> 38.1 us  [project(): jnp.dot(of(after(h_kept, *others), g), full_qkv, preferred_element_type=f32)]
  transfers between devices with their start and end apart: 60 -> 61, of which waited for: 23 -> 28; matrix products, arithmetic and copies ran while one was open for 31% -> 31% of each run, Pallas kernels for 9% -> 9%
where the time goes in v6:
time: 2380 us; the launch traced here: 2370 us
  waiting for transfers between devices  1050 us (44%)
  matrix products  556 us (23%)
  Pallas kernels  271 us (11%)
  local copies, waits for them, and re-layouts  211 us (9%)
  other arithmetic  165 us (7%)
  starting transfers between devices  104 us (4%)
    ppermute x50, waiting for transfers between devices, swap(): lax.ppermute(block, axis, [(i, i ^ stride) for i in range(lax.axis_size(a...  923 us
    dot_general x10, matrix products, nt(): return jnp.einsum('re,de->rd', a, b, preferred_element_type=f32)  186 us
    dot_general x16, matrix products, tn(): lax.dot_general(a, b, (((0,), (0,)), ((), ())), preferred_element_type=f32)  185 us
    pallas_call x4, Pallas kernels, attend_back(): pl.pallas_call(functools.partial(backward_kernel, pair), grid_spec=pltpu....  131 us
    all_to_all x4, waiting for transfers between devices, to_heads(): return lax.all_to_all(split, 'seq', 0, 0, tiled=True)  97.1 us
    pallas_call x2, Pallas kernels, attend(): pl.pallas_call(forward_kernel, grid_spec=pltpu.PrefetchScalarGridSpec(num...  93.4 us
    dot_general x2, matrix products, shards(): up = jnp.dot(after(h_mlp, *mark), full_up, preferred_element_type=f32)  50.7 us
    ppermute x50, starting transfers between devices, swap(): lax.ppermute(block, axis, [(i, i ^ stride) for i in range(lax.axis_size(a...  49.5 us
  transfers between devices with their start and end apart: 61, of which 28 were waited for; matrix products, arithmetic and copies ran while one was open for 31% of the time, Pallas kernels for 9%

profile of v6, /device:TPU:0, one launch (start us, length us, event | category | flops | bytes accessed | tf_op | source)
XLA Modules:
  0.0 2371.5 jit_solution(10448315392357666652)
XLA Ops:
  36.2 9.4 copy.145
  55.2 71.9 %collective-permute-done.5 = bf16[64,7552]{1,0:T(8,128)(2,1)S(1)} collective-permute-done((bf16[64,7552]{1,0:T(8,128)(2,1)S(1)}, bf16[64,7552]{1,0:T(8,128)(2,1)S(1)}, u32[]{:S(2)}, u32[]{:S(2)}) %collective-permute-start.5) | collective-permute-done | bytes 966688 | tf_op jit(solution)/shard_map/ppermute | solution.py:42
  129.4 121.8 %collective-permute-done.6 = bf16[64,11008]{1,0:T(8,128)(2,1)S(1)} collective-permute-done((bf16[64,11008]{1,0:T(8,128)(2,1)S(1)}, bf16[64,11008]{1,0:T(8,128)(2,1)S(1)}, u32[]{:S(2)}, u32[]{:S(2)}) %collective-permute-start.6) | collective-permute-done | bytes 1409056 | tf_op jit(solution)/shard_map/ppermute | solution.py:42
  251.2 16.3 collective-permute-done.7
  269.9 60.8 %collective-permute-done.8 = bf16[128,11008]{1,0:T(8,128)(2,1)} collective-permute-done((bf16[128,11008]{1,0:T(8,128)(2,1)S(1)}, bf16[128,11008]{1,0:T(8,128)(2,1)}, u32[]{:S(2)}, u32[]{:S(2)}) %collective-permute-start.8) | collective-permute-done | bytes 2818080 | tf_op jit(solution)/shard_map/ppermute | solution.py:42
  332.9 20.4 collective-permute-done.9.refs_1_
  355.1 120.4 %collective-permute-done.10.refs_1_ = bf16[256,11008]{1,0:T(8,128)(2,1)} collective-permute-done((bf16[256,11008]{1,0:T(8,128)(2,1)S(1)}, bf16[256,11008]{1,0:T(8,128)(2,1)}, u32[]{:S(2)}, u32[]{:S(2)}) %collective-permute-start.10) | collective-permute-done | bytes 5636128 | tf_op jit(solution)/shard_map/ppermute | solution.py:42
  475.5 18.9 convolution_convert_fusion.4
  509.3 149.1 %collective-permute-done.12.refs_3_ = bf16[256,7552]{1,0:T(8,128)(2,1)} collective-permute-done((bf16[256,7552]{1,0:T(8,128)(2,1)}, bf16[256,7552]{1,0:T(8,128)(2,1)}, u32[]{:S(2)}, u32[]{:S(2)}) %collective-permute-start.12) | collective-permute-done | bytes 3866656 | tf_op jit(solution)/shard_map/ppermute | solution.py:42
  658.4 80.4 %collective-permute-done.11.refs_2_ = bf16[256,7552]{1,0:T(8,128)(2,1)} collective-permute-done((bf16[256,7552]{1,0:T(8,128)(2,1)}, bf16[256,7552]{1,0:T(8,128)(2,1)}, u32[]{:S(2)}, u32[]{:S(2)}) %collective-permute-start.11) | collective-permute-done | bytes 3866656 | tf_op jit(solution)/shard_map/ppermute | solution.py:42
  750.2 46.9 %attend.2 = (bf16[8,2,512,128]{3,2,1,0:T(8,128)(2,1)}, f32[2,1,4096]{2,1,0:T(1,128)S(1)}) custom-call(s32[2,4,8]{2,1,0:T(4,128)S(1)} %pad_add_fusion.2.bounds, bf16[8,2,512,384]{3,2,1,0:T(8,128)(2,1)} %all-to-all-done.q_ref.k_ref.v_ref, bf16[8,2,512,384]{3,2,1,0:T(8,128)(2,1)} %all-to-all-done.q_ref.k_ref.v_ref, ...), custom_call_target="tpu_custom_call" | custom-call | flops 1024 | bytes 1024 | tf_op jit(solution)/shard_map/attend/pallas_call | solution.py:314
  814.5 17.0 place.2
  834.9 29.4 %place.3 = (bf16[2048,5504]{1,0:T(8,128)(2,1)}, bf16[2048,5504]{1,0:T(8,128)(2,1)}) custom-call(s32[32]{0:T(128)S(1)} %xor_multiply_fusion.target, bf16[256,11008]{1,0:T(8,128)(2,1)S(1)} %bitcast.340, bf16[256,11008]{1,0:T(8,128)(2,1)} %collective-permute-done.10.refs_1_, bf16[256,11008]{1,0:T(8,128)(2,1)} %collective-permute-done.13.refs_2_, ...), custom_call_target="tpu_custom_call" | custom-call | flops 1024 | bytes 1024 | tf_op jit(solution)/shard_map/place/pallas_call | solution.py:149
  864.3 31.1 %reshape.449 = bf16[5504,2048]{1,0:T(8,128)(2,1)} reshape(bf16[2048,5504]{1,0:T(8,128)(2,1)} %get-tuple-element.93) | data formatting | bytes 45088768 | tf_op jit(solution)/shard_map/reshape | solution.py:534
  899.4 19.2 convolution_convert_fusion.3
  930.2 10.3 multiply_reduce_fusion.10
  944.2 19.0 fusion.120
  963.2 25.4 %multiply_convert_fusion.5 = (bf16[512,5504]{1,0:T(8,128)(2,1)}, f32[512,5504]{1,0:T(8,128)}) fusion(f32[512,5504]{1,0:T(8,128)} %fusion.120, bf16[512,2048]{1,0:T(8,128)(2,1)} %copy-done.38, bf16[2048,5504]{1,0:T(8,128)(2,1)} %get-tuple-element.92), kind=kOutput, calls=%fused_computation.24 | convolution fusion | flops 11559632896 | bytes 52822016 | tf_op jit(solution)/shard_map/dot_general | solution.py:560
  988.6 25.2 %multiply_convert_fusion.3 = (bf16[512,5504]{1,0:T(8,128)(2,1)}, bf16[512,5504]{1,0:T(8,128)(2,1)}) fusion(f32[512,5504]{1,0:T(8,128)} %fusion.120, f32[512,5504]{1,0:T(8,128)} %get-tuple-element.274, bf16[512,2048]{1,0:T(8,128)(2,1)} %get-tuple-element.96, bf16[5504,2048]{1,0:T(8,128)(2,1)} %reshape.449), kind=kOutput, calls=%fused_computation.22 | convolution fusion | flops 11579359232 | bytes 58458112 | tf_op jit(solution)/shard_map/re,de->rd/dot_general | solution.py:463
  1013.7 54.3 %all-to-all-done.2.q_ref.k_ref.v_ref = bf16[8,2,512,384]{3,2,1,0:T(8,128)(2,1)} async-done(((bf16[8,2,512,384]{3,2,1,0:T(8,128)(2,1)}), bf16[8,2,512,384]{3,2,1,0:T(8,128)(2,1)}, u32[]{:S(2)}, u32[]{:S(2)}) %all-to-all-start.2) | async-done | bytes 6291488 | tf_op jit(solution)/shard_map/all_to_all | solution.py:438
  1068.0 46.5 %attend.3 = (bf16[8,2,512,128]{3,2,1,0:T(8,128)(2,1)}, f32[2,1,4096]{2,1,0:T(1,128)S(1)}) custom-call(s32[2,4,8]{2,1,0:T(4,128)S(1)} %pad_add_fusion.3.bounds, bf16[8,2,512,384]{3,2,1,0:T(8,128)(2,1)} %all-to-all-done.2.q_ref.k_ref.v_ref, bf16[8,2,512,384]{3,2,1,0:T(8,128)(2,1)} %all-to-all-done.2.q_ref.k_ref.v_ref, ...), custom_call_target="tpu_custom_call" | custom-call | flops 1024 | bytes 1024 | tf_op jit(solution)/shard_map/attend/pallas_call | solution.py:314
  1118.4 19.4 fusion.121
  1137.8 19.4 multiply_reduce_fusion.2
  1182.2 10.3 multiply_reduce_fusion.8
  1196.2 19.0 fusion.122
  1215.2 25.3 %multiply_convert_fusion.2 = (bf16[512,5504]{1,0:T(8,128)(2,1)}, f32[512,5504]{1,0:T(8,128)}) fusion(f32[512,5504]{1,0:T(8,128)} %fusion.122, bf16[512,2048]{1,0:T(8,128)(2,1)} %copy-done.40, bf16[2048,5504]{1,0:T(8,128)(2,1)} %get-tuple-element.92), kind=kOutput, calls=%fused_computation.19 | convolution fusion | flops 11559632896 | bytes 52822016 | tf_op jit(solution)/shard_map/dot_general | solution.py:560
  1240.5 11.5 pad_maximum_fusion
  1252.0 31.4 %convolution_convert_fusion = bf16[5504,2048]{1,0:T(8,128)(2,1)} fusion(bf16[1024,5504]{1,0:T(8,128)(2,1)} %pad_maximum_fusion, bf16[1024,2048]{1,0:T(8,128)(2,1)} %bitcast.350), kind=kOutput, calls=%fused_computation | convolution fusion | flops 23096721408 | bytes 38010880 | tf_op jit(solution)/shard_map/dot_general | solution.py:169
  1283.3 9.9 constant_dynamic-slice_fusion.10
  1293.3 32.3 %attend_back.4 = bf16[8,1,512,384]{3,2,1,0:T(8,128)(2,1)S(1)} custom-call(s32[2,4,8]{2,1,0:T(4,128)S(1)} %copy-done.19, bf16[8,2,512,384]{3,2,1,0:T(8,128)(2,1)} %all-to-all-done.q_ref.k_ref.v_ref, bf16[8,2,512,384]{3,2,1,0:T(8,128)(2,1)} %all-to-all-done.q_ref.k_ref.v_ref, bf16[8,2,512,384]{3,2,1,0:T(8,128)(2,1)} %all-to-all-done.q_ref.k_ref.v_ref, ...), custom_call_target="tpu_custom_call" | custom-call | flops 1024 | bytes 1024 | tf_op jit(solution)/shard_map/attend_back/pallas_call | solution.py:391
  1333.7 33.4 %attend_back.5 = bf16[8,1,512,384]{3,2,1,0:T(8,128)(2,1)} custom-call(s32[2,4,8]{2,1,0:T(4,128)S(1)} %copy-done.19, bf16[8,2,512,384]{3,2,1,0:T(8,128)(2,1)} %all-to-all-done.q_ref.k_ref.v_ref, bf16[8,2,512,384]{3,2,1,0:T(8,128)(2,1)} %all-to-all-done.q_ref.k_ref.v_ref, bf16[8,2,512,384]{3,2,1,0:T(8,128)(2,1)} %all-to-all-done.q_ref.k_ref.v_ref, ...), custom_call_target="tpu_custom_call" | custom-call | flops 1024 | bytes 1024 | tf_op jit(solution)/shard_map/attend_back/pallas_call | solution.py:391
  1380.9 10.1 fusion.2
  1391.0 14.0 all-to-all-done.5
  1405.0 24.6 %multiply_convert_fusion = (bf16[512,5504]{1,0:T(8,128)(2,1)}, bf16[512,5504]{1,0:T(8,128)(2,1)}) fusion(f32[512,5504]{1,0:T(8,128)} %fusion.122, f32[512,5504]{1,0:T(8,128)} %get-tuple-element.279, bf16[512,2048]{1,0:T(8,128)(2,1)S(1)} %copy-done.52, bf16[5504,2048]{1,0:T(8,128)(2,1)} %reshape.449), kind=kOutput, calls=%fused_computation.17 | convolution fusion | flops 11579359232 | bytes 58458112 | tf_op jit(solution)/shard_map/re,de->rd/dot_general | solution.py:463
  1429.7 19.7 convolution_convert_fusion.2
  1457.1 11.2 copy.152
  1468.3 19.3 convolution_convert_fusion.1
  1494.3 11.8 add_convert_fusion.3
  1508.0 19.4 fusion.123
  1527.4 18.8 multiply_reduce_fusion.1
  1549.6 14.3 all-to-all-done.6
  1581.9 13.3 add_convert_fusion.2
  1602.8 14.7 collective-permute-done.26
  1617.5 13.0 fusion.1
  1630.5 42.8 %all-to-all-done.7.do_ref = bf16[8,2,512,128]{3,2,1,0:T(8,128)(2,1)S(1)} async-done(((bf16[8,2,512,128]{3,2,1,0:T(8,128)(2,1)}), bf16[8,2,512,128]{3,2,1,0:T(8,128)(2,1)S(1)}, u32[]{:S(2)}, u32[]{:S(2)}) %all-to-all-start.7) | async-done | bytes 2097184 | tf_op jit(solution)/shard_map/all_to_all | solution.py:438
  1673.3 32.0 %attend_back.6 = bf16[8,1,512,384]{3,2,1,0:T(8,128)(2,1)S(1)} custom-call(s32[2,4,8]{2,1,0:T(4,128)S(1)} %copy-done.17, bf16[8,2,512,384]{3,2,1,0:T(8,128)(2,1)} %all-to-all-done.2.q_ref.k_ref.v_ref, bf16[8,2,512,384]{3,2,1,0:T(8,128)(2,1)} %all-to-all-done.2.q_ref.k_ref.v_ref, bf16[8,2,512,384]{3,2,1,0:T(8,128)(2,1)} %all-to-all-done.2.q_ref.k_ref.v_ref, ...), custom_call_target="tpu_custom_call" | custom-call | flops 1024 | bytes 1024 | tf_op jit(solution)/shard_map/attend_back/pallas_call | solution.py:391
  1715.3 32.9 %attend_back.7 = bf16[8,1,512,384]{3,2,1,0:T(8,128)(2,1)} custom-call(s32[2,4,8]{2,1,0:T(4,128)S(1)} %copy-done.17, bf16[8,2,512,384]{3,2,1,0:T(8,128)(2,1)} %all-to-all-done.2.q_ref.k_ref.v_ref, bf16[8,2,512,384]{3,2,1,0:T(8,128)(2,1)} %all-to-all-done.2.q_ref.k_ref.v_ref, bf16[8,2,512,384]{3,2,1,0:T(8,128)(2,1)} %all-to-all-done.2.q_ref.k_ref.v_ref, ...), custom_call_target="tpu_custom_call" | custom-call | flops 1024 | bytes 1024 | tf_op jit(solution)/shard_map/attend_back/pallas_call | solution.py:391
  1813.6 14.0 collective-permute-done.33
  1832.7 12.4 collective-permute-done.34
  1854.5 9.4 fusion.14
  1876.6 10.2 collective-permute-done.30
  1891.5 19.2 add_convert_fusion.9
  1910.7 19.3 add_convert_fusion.8
  1943.9 11.3 convolution_convert_fusion.6
  1955.2 11.6 convolution_convert_fusion.5
  1972.2 21.1 multiply_reduce_fusion.4
  2010.9 44.0 %collective-permute-done.36 = bf16[4,64,2048]{2,1,0:T(8,128)(2,1)} collective-permute-done((bf16[4,64,2048]{2,1,0:T(8,128)(2,1)}, bf16[4,64,2048]{2,1,0:T(8,128)(2,1)}, u32[]{:S(2)}, u32[]{:S(2)}) %collective-permute-start.36) | collective-permute-done | bytes 1048608 | tf_op jit(solution)/shard_map/ppermute | solution.py:42
  2085.9 20.3 multiply_reduce_fusion.3
  2109.1 9.9 multiply_add_fusion
  2119.0 26.7 %collective-permute-done.46 = f32[2,2,2,2,64]{4,3,2,1,0:T(2,128)S(1)} collective-permute-done((f32[2,2,2,2,64]{4,3,2,1,0:T(2,128)S(1)}, f32[2,2,2,2,64]{4,3,2,1,0:T(2,128)S(1)}, u32[]{:S(2)}, u32[]{:S(2)}) %collective-permute-start.46) | collective-permute-done | bytes 4128 | tf_op jit(solution)/shard_map/ppermute | solution.py:42
  2154.3 17.0 collective-permute-done.37
  2207.3 71.6 %collective-permute-done.44 = bf16[1,64,18560]{2,1,0:T(8,128)(2,1)} collective-permute-done((bf16[1,64,18560]{2,1,0:T(8,128)(2,1)S(1)}, bf16[1,64,18560]{2,1,0:T(8,128)(2,1)}, u32[]{:S(2)}, u32[]{:S(2)}) %collective-permute-start.44) | collective-permute-done | bytes 2375712 | tf_op jit(solution)/shard_map/ppermute | solution.py:42
  2286.8 31.5 %collective-permute-done.48 = f32[2,2,64]{2,0,1:T(2,128)S(1)} collective-permute-done((f32[2,2,64]{2,0,1:T(2,128)S(1)}, f32[2,2,64]{2,0,1:T(2,128)S(1)}, u32[]{:S(2)}, u32[]{:S(2)}) %collective-permute-start.48) | collective-permute-done | bytes 1056 | tf_op jit(solution)/shard_map/ppermute | solution.py:42
  2325.7 33.9 %collective-permute-done.43 = bf16[1,64,6144]{2,1,0:T(8,128)(2,1)} collective-permute-done((bf16[1,64,6144]{2,1,0:T(8,128)(2,1)}, bf16[1,64,6144]{2,1,0:T(8,128)(2,1)}, u32[]{:S(2)}, u32[]{:S(2)}) %collective-permute-start.43) | collective-permute-done | bytes 786464 | tf_op jit(solution)/shard_map/ppermute | solution.py:42
  (472 shorter events, 455.0 us)
Async XLA Ops:
  7.2 468.3 %all-gather.2.cloned.1.call-start = ((), (), s32[]{:S(2)}) async-start(), calls=%async_computation.10 | async-start | bytes 25952256 | tf_op jit(solution)/shard_map/all_gather | solution.py:469
  10.6 4.5 collective-permute-start
  15.2 3.6 collective-permute-start.1
  18.9 4.6 collective-permute-start.2
  23.6 3.4 collective-permute-start.3
  27.0 19.4 collective-permute-start.4
  46.5 1146.0 %copy-start.54 = (f32[1,2048]{1,0:T(1,128)}, f32[1,2048]{1,0:T(1,128)S(1)}, u32[]{:S(2)}) copy-start(f32[1,2048]{1,0:T(1,128)S(1)} %get-tuple-element.249) | copy-start | bytes 24580
  52.9 74.3 %collective-permute-start.5 = (bf16[64,7552]{1,0:T(8,128)(2,1)S(1)}, bf16[64,7552]{1,0:T(8,128)(2,1)S(1)}, u32[]{:S(2)}, u32[]{:S(2)}) collective-permute-start(bf16[64,7552]{1,0:T(8,128)(2,1)S(1)} %pad_maximum_fusion.30), channel_id=1, source_target_pairs={{0,4},{1,5},{2,6},{3,7},{4,0},{5,1},{6,2},{7,3},{8,12},{9,13},{10,... | collective-permute-start | bytes 2899976 | tf_op jit(solution)/shard_map/ppermute | solution.py:42
  127.4 123.7 %collective-permute-start.6 = (bf16[64,11008]{1,0:T(8,128)(2,1)S(1)}, bf16[64,11008]{1,0:T(8,128)(2,1)S(1)}, u32[]{:S(2)}, u32[]{:S(2)}) collective-permute-start(bf16[64,11008]{1,0:T(8,128)(2,1)S(1)} %pad_maximum_fusion.24), channel_id=1, source_target_pairs={{0,4},{1,5},{2,6},{3,7},{4,0},{5,1},{6,2},{7,3},{8,12},{9,13},{10,... | collective-permute-start | bytes 4227080 | tf_op jit(solution)/shard_map/ppermute | solution.py:42
  127.5 140.0 %collective-permute-start.7 = (bf16[128,7552]{1,0:T(8,128)(2,1)S(1)}, bf16[128,7552]{1,0:T(8,128)(2,1)S(1)}, u32[]{:S(2)}, u32[]{:S(2)}) collective-permute-start(bf16[128,7552]{1,0:T(8,128)(2,1)S(1)} %get-tuple-element.244), channel_id=1, source_target_pairs={{0,2},{1,3},{2,0},{3,1},{4,6},{5,7},{6,4},{7,5},{8,10},{9,11},{10,... | collective-permute-start | bytes 5799944 | tf_op jit(solution)/shard_map/ppermute | solution.py:42
  267.8 62.9 %collective-permute-start.8 = (bf16[128,11008]{1,0:T(8,128)(2,1)S(1)}, bf16[128,11008]{1,0:T(8,128)(2,1)}, u32[]{:S(2)}, u32[]{:S(2)}) collective-permute-start(bf16[128,11008]{1,0:T(8,128)(2,1)S(1)} %constant_dynamic-update-slice_fusion.2), channel_id=1, source_target_pairs={{0,2},{1,3},{2,0},{3,1},{4,6},{5,7},{6,4},{7,5},{8,10},{9,11},{10,... | collective-permute-start | bytes 8454152 | tf_op jit(solution)/shard_map/ppermute | solution.py:42
  268.2 85.1 %collective-permute-start.9 = (bf16[256,7552]{1,0:T(8,128)(2,1)S(1)}, bf16[256,7552]{1,0:T(8,128)(2,1)S(1)}, u32[]{:S(2)}, u32[]{:S(2)}) collective-permute-start(bf16[256,7552]{1,0:T(8,128)(2,1)S(1)} %constant_dynamic-update-slice_fusion.4.refs_0_), channel_id=1, source_target_pairs={{0,16},{8,24},{16,0},{24,8},{1,17},{9,25},{17,1},{25,9},{2,18},{10... | collective-permute-start | bytes 11599880 | tf_op jit(solution)/shard_map/ppermute | solution.py:42
  353.3 122.2 %collective-permute-start.10 = (bf16[256,11008]{1,0:T(8,128)(2,1)S(1)}, bf16[256,11008]{1,0:T(8,128)(2,1)}, u32[]{:S(2)}, u32[]{:S(2)}) collective-permute-start(bf16[256,11008]{1,0:T(8,128)(2,1)S(1)} %pad_maximum_fusion.8.refs_0_), channel_id=1, source_target_pairs={{0,1},{1,0},{2,3},{3,2},{4,5},{5,4},{6,7},{7,6},{8,9},{9,8},{10,11... | collective-permute-start | bytes 16908296 | tf_op jit(solution)/shard_map/ppermute | solution.py:42
  500.1 250.1 %all-to-all-start = ((bf16[8,2,512,384]{3,2,1,0:T(8,128)(2,1)}), bf16[8,2,512,384]{3,2,1,0:T(8,128)(2,1)}, u32[]{:S(2)}, u32[]{:S(2)}) async-start(bf16[8,2,512,384]{3,2,1,0:T(8,128)(2,1)} %bitcast.353), calls=%async_computation | async-start | bytes 12582912 | tf_op jit(solution)/shard_map/all_to_all | solution.py:438
  505.2 153.2 %collective-permute-start.12 = (bf16[256,7552]{1,0:T(8,128)(2,1)}, bf16[256,7552]{1,0:T(8,128)(2,1)}, u32[]{:S(2)}, u32[]{:S(2)}) collective-permute-start(bf16[256,7552]{1,0:T(8,128)(2,1)} %copy-done.6), channel_id=1, source_target_pairs={{0,1},{1,0},{2,3},{3,2},{4,5},{5,4},{6,7},{7,6},{8,9},{9,8},{10,11... | collective-permute-start | bytes 11599880 | tf_op jit(solution)/shard_map/ppermute | solution.py:42
  507.2 231.5 %collective-permute-start.11 = (bf16[256,7552]{1,0:T(8,128)(2,1)}, bf16[256,7552]{1,0:T(8,128)(2,1)}, u32[]{:S(2)}, u32[]{:S(2)}) collective-permute-start(bf16[256,7552]{1,0:T(8,128)(2,1)} %copy-done.4), channel_id=1, source_target_pairs={{0,1},{1,0},{2,3},{3,2},{4,5},{5,4},{6,7},{7,6},{8,9},{9,8},{10,11... | collective-permute-start | bytes 11599880 | tf_op jit(solution)/shard_map/ppermute | solution.py:42
  507.3 240.6 %collective-permute-start.14 = (bf16[256,11008]{1,0:T(8,128)(2,1)}, bf16[256,11008]{1,0:T(8,128)(2,1)}, u32[]{:S(2)}, u32[]{:S(2)}) collective-permute-start(bf16[256,11008]{1,0:T(8,128)(2,1)} %collective-permute-done.10.refs_1_), channel_id=1, source_target_pairs={{0,16},{8,24},{16,0},{24,8},{1,17},{9,25},{17,1},{25,9},{2,18},{10... | collective-permute-start | bytes 16908296 | tf_op jit(solution)/shard_map/ppermute | solution.py:42
  508.7 240.2 %collective-permute-start.13 = (bf16[256,11008]{1,0:T(8,128)(2,1)}, bf16[256,11008]{1,0:T(8,128)(2,1)}, u32[]{:S(2)}, u32[]{:S(2)}) collective-permute-start(bf16[256,11008]{1,0:T(8,128)(2,1)} %copy-done.1), channel_id=1, source_target_pairs={{0,16},{8,24},{16,0},{24,8},{1,17},{9,25},{17,1},{25,9},{2,18},{10... | collective-permute-start | bytes 16908296 | tf_op jit(solution)/shard_map/ppermute | solution.py:42
  509.3 234.2 %collective-permute-start.16 = (bf16[256,7552]{1,0:T(8,128)(2,1)}, bf16[256,7552]{1,0:T(8,128)(2,1)S(1)}, u32[]{:S(2)}, u32[]{:S(2)}) collective-permute-start(bf16[256,7552]{1,0:T(8,128)(2,1)} %copy-done.6), channel_id=1, source_target_pairs={{0,8},{8,0},{16,24},{24,16},{1,9},{9,1},{17,25},{25,17},{2,10},{10... | collective-permute-start | bytes 11599880 | tf_op jit(solution)/shard_map/ppermute | solution.py:42
  658.4 87.5 %collective-permute-start.15 = (bf16[256,7552]{1,0:T(8,128)(2,1)}, bf16[256,7552]{1,0:T(8,128)(2,1)S(1)}, u32[]{:S(2)}, u32[]{:S(2)}) collective-permute-start(bf16[256,7552]{1,0:T(8,128)(2,1)} %copy-done.4), channel_id=1, source_target_pairs={{0,8},{8,0},{16,24},{24,16},{1,9},{9,1},{17,25},{25,17},{2,10},{10... | collective-permute-start | bytes 11599880 | tf_op jit(solution)/shard_map/ppermute | solution.py:42
  738.7 10.8 collective-permute-start.18
  745.4 89.4 %collective-permute-start.20 = (bf16[256,11008]{1,0:T(8,128)(2,1)}, bf16[256,11008]{1,0:T(8,128)(2,1)}, u32[]{:S(2)}, u32[]{:S(2)}) collective-permute-start(bf16[256,11008]{1,0:T(8,128)(2,1)} %collective-permute-done.10.refs_1_), channel_id=1, source_target_pairs={{0,8},{8,0},{16,24},{24,16},{1,9},{9,1},{17,25},{25,17},{2,10},{10... | collective-permute-start | bytes 16908296 | tf_op jit(solution)/shard_map/ppermute | solution.py:42
  747.8 87.0 %collective-permute-start.19 = (bf16[256,11008]{1,0:T(8,128)(2,1)}, bf16[256,11008]{1,0:T(8,128)(2,1)}, u32[]{:S(2)}, u32[]{:S(2)}) collective-permute-start(bf16[256,11008]{1,0:T(8,128)(2,1)} %copy-done.1), channel_id=1, source_target_pairs={{0,8},{8,0},{16,24},{24,16},{1,9},{9,1},{17,25},{25,17},{2,10},{10... | collective-permute-start | bytes 16908296 | tf_op jit(solution)/shard_map/ppermute | solution.py:42
  747.8 87.0 %collective-permute-start.22 = (bf16[256,11008]{1,0:T(8,128)(2,1)}, bf16[256,11008]{1,0:T(8,128)(2,1)}, u32[]{:S(2)}, u32[]{:S(2)}) collective-permute-start(bf16[256,11008]{1,0:T(8,128)(2,1)} %collective-permute-done.14.refs_3_), channel_id=1, source_target_pairs={{0,8},{8,0},{16,24},{24,16},{1,9},{9,1},{17,25},{25,17},{2,10},{10... | collective-permute-start | bytes 16908296 | tf_op jit(solution)/shard_map/ppermute | solution.py:42
  748.8 86.0 %collective-permute-start.21 = (bf16[256,11008]{1,0:T(8,128)(2,1)}, bf16[256,11008]{1,0:T(8,128)(2,1)}, u32[]{:S(2)}, u32[]{:S(2)}) collective-permute-start(bf16[256,11008]{1,0:T(8,128)(2,1)} %collective-permute-done.13.refs_2_), channel_id=1, source_target_pairs={{0,8},{8,0},{16,24},{24,16},{1,9},{9,1},{17,25},{25,17},{2,10},{10... | collective-permute-start | bytes 16908296 | tf_op jit(solution)/shard_map/ppermute | solution.py:42
  749.6 318.4 %copy-start.12 = (s32[2,1,4096]{2,1,0:T(1,128)}, s32[2,1,4096]{2,1,0:T(1,128)S(1)}, u32[]{:S(2)}) copy-start(s32[2,1,4096]{2,1,0:T(1,128)S(1)} %get-tuple-element.288.lo_ref) | copy-start | bytes 98308
  749.6 58.5 %collective-permute-start.17 = (bf16[256,7552]{1,0:T(8,128)(2,1)}, bf16[256,7552]{1,0:T(8,128)(2,1)}, u32[]{:S(2)}, u32[]{:S(2)}) collective-permute-start(bf16[256,7552]{1,0:T(8,128)(2,1)} %collective-permute-done.11.refs_2_), channel_id=1, source_target_pairs={{0,8},{8,0},{16,24},{24,16},{1,9},{9,1},{17,25},{25,17},{2,10},{10... | collective-permute-start | bytes 11599880 | tf_op jit(solution)/shard_map/ppermute | solution.py:42
  797.1 98.3 %all-to-all-start.1 = ((bf16[8,2,512,128]{3,2,1,0:T(8,128)(2,1)}), bf16[8,2,512,128]{3,2,1,0:T(8,128)(2,1)}, u32[]{:S(2)}, u32[]{:S(2)}) async-start(bf16[8,2,512,128]{3,2,1,0:T(8,128)(2,1)} %get-tuple-element.89.o_ref), calls=%async_computation.1 | async-start | bytes 4194304 | tf_op jit(solution)/shard_map/all_to_all | solution.py:442
  803.1 264.9 %copy-start.16 = (s32[2,4,8]{2,1,0:T(4,128)}, s32[2,4,8]{2,1,0:T(4,128)S(1)}, u32[]{:S(2)}) copy-start(s32[2,4,8]{2,1,0:T(4,128)S(1)} %pad_add_fusion.3.bounds) | copy-start | bytes 772
  924.2 143.8 %all-to-all-start.2 = ((bf16[8,2,512,384]{3,2,1,0:T(8,128)(2,1)}), bf16[8,2,512,384]{3,2,1,0:T(8,128)(2,1)}, u32[]{:S(2)}, u32[]{:S(2)}) async-start(bf16[8,2,512,384]{3,2,1,0:T(8,128)(2,1)} %bitcast.354), calls=%async_computation.2 | async-start | bytes 12582912 | tf_op jit(solution)/shard_map/all_to_all | solution.py:438
  1114.5 56.0 %all-to-all-start.3 = ((bf16[8,2,512,128]{3,2,1,0:T(8,128)(2,1)}), bf16[8,2,512,128]{3,2,1,0:T(8,128)(2,1)S(1)}, u32[]{:S(2)}, u32[]{:S(2)}) async-start(bf16[8,2,512,128]{3,2,1,0:T(8,128)(2,1)} %get-tuple-element.98.o_ref), calls=%async_computation.3 | async-start | bytes 4194304 | tf_op jit(solution)/shard_map/all_to_all | solution.py:442
  1171.8 80.2 %all-to-all-start.4 = ((bf16[8,2,512,128]{3,2,1,0:T(8,128)(2,1)}), bf16[8,2,512,128]{3,2,1,0:T(8,128)(2,1)S(1)}, u32[]{:S(2)}, u32[]{:S(2)}) async-start(bf16[8,2,512,128]{3,2,1,0:T(8,128)(2,1)} %bitcast.387), calls=%async_computation.4 | async-start | bytes 4194304 | tf_op jit(solution)/shard_map/all_to_all | solution.py:438
  1293.3 87.7 %collective-permute-start.23 = (bf16[2752,2048]{1,0:T(8,128)(2,1)}, bf16[2752,2048]{1,0:T(8,128)(2,1)}, u32[]{:S(2)}, u32[]{:S(2)}) collective-permute-start(bf16[2752,2048]{1,0:T(8,128)(2,1)} %bitcast.47), channel_id=1, source_target_pairs={{0,8},{8,0},{16,24},{24,16},{1,9},{9,1},{17,25},{25,17},{2,10},{10... | collective-permute-start | bytes 33816584 | tf_op jit(solution)/shard_map/ppermute | solution.py:42
  1327.4 77.7 %all-to-all-start.5 = ((bf16[8,1,512,384]{3,2,1,0:T(8,128)(2,1)}), bf16[8,1,512,384]{3,2,1,0:T(8,128)(2,1)}, u32[]{:S(2)}, u32[]{:S(2)}) async-start(bf16[8,1,512,384]{3,2,1,0:T(8,128)(2,1)} %copy-done.3), calls=%async_computation.5 | async-start | bytes 6291456 | tf_op jit(solution)/shard_map/all_to_all | solution.py:442
  1449.3 45.0 %collective-permute-start.24 = (bf16[1024,5504]{1,0:T(8,128)(2,1)}, bf16[1024,5504]{1,0:T(8,128)(2,1)}, u32[]{:S(2)}, u32[]{:S(2)}) collective-permute-start(bf16[1024,5504]{1,0:T(8,128)(2,1)} %convolution_convert_fusion.2), channel_id=1, source_target_pairs={{0,8},{8,0},{16,24},{24,16},{1,9},{9,1},{17,25},{25,17},{2,10},{10... | collective-permute-start | bytes 33816584 | tf_op jit(solution)/shard_map/ppermute | solution.py:42
  1487.6 94.3 %collective-permute-start.25 = (bf16[1024,5504]{1,0:T(8,128)(2,1)}, bf16[1024,5504]{1,0:T(8,128)(2,1)}, u32[]{:S(2)}, u32[]{:S(2)}) collective-permute-start(bf16[1024,5504]{1,0:T(8,128)(2,1)} %convolution_convert_fusion.1), channel_id=1, source_target_pairs={{0,8},{8,0},{16,24},{24,16},{1,9},{9,1},{17,25},{25,17},{2,10},{10... | collective-permute-start | bytes 33816584 | tf_op jit(solution)/shard_map/ppermute | solution.py:42
  1488.1 75.8 %all-to-all-start.6 = ((bf16[8,1,512,384]{3,2,1,0:T(8,128)(2,1)}), bf16[8,1,512,384]{3,2,1,0:T(8,128)(2,1)}, u32[]{:S(2)}, u32[]{:S(2)}) async-start(bf16[8,1,512,384]{3,2,1,0:T(8,128)(2,1)} %attend_back.5), calls=%async_computation.6 | async-start | bytes 6291456 | tf_op jit(solution)/shard_map/all_to_all | solution.py:442
  1492.7 124.7 %collective-permute-start.26 = (bf16[1376,2048]{1,0:T(8,128)(2,1)}, bf16[1376,2048]{1,0:T(8,128)(2,1)}, u32[]{:S(2)}, u32[]{:S(2)}) collective-permute-start(bf16[1376,2048]{1,0:T(8,128)(2,1)} %fusion.2), channel_id=1, source_target_pairs={{0,16},{8,24},{16,0},{24,8},{1,17},{9,25},{17,1},{25,9},{2,18},{10... | collective-permute-start | bytes 16908296 | tf_op jit(solution)/shard_map/ppermute | solution.py:42
  1506.1 264.8 %collective-permute-start.27 = (bf16[512,5504]{1,0:T(8,128)(2,1)}, bf16[512,5504]{1,0:T(8,128)(2,1)}, u32[]{:S(2)}, u32[]{:S(2)}) collective-permute-start(bf16[512,5504]{1,0:T(8,128)(2,1)} %add_convert_fusion.3), channel_id=1, source_target_pairs={{0,1},{1,0},{2,3},{3,2},{4,5},{5,4},{6,7},{7,6},{8,9},{9,8},{10,11... | collective-permute-start | bytes 16908296 | tf_op jit(solution)/shard_map/ppermute | solution.py:42
  1574.9 98.3 %all-to-all-start.7 = ((bf16[8,2,512,128]{3,2,1,0:T(8,128)(2,1)}), bf16[8,2,512,128]{3,2,1,0:T(8,128)(2,1)S(1)}, u32[]{:S(2)}, u32[]{:S(2)}) async-start(bf16[8,2,512,128]{3,2,1,0:T(8,128)(2,1)} %bitcast.385), calls=%async_computation.7 | async-start | bytes 4194304 | tf_op jit(solution)/shard_map/all_to_all | solution.py:438
  1601.3 203.8 %collective-permute-start.28 = (bf16[1024,2048]{1,0:T(8,128)(2,1)}, bf16[1024,2048]{1,0:T(8,128)(2,1)}, u32[]{:S(2)}, u32[]{:S(2)}) collective-permute-start(bf16[1024,2048]{1,0:T(8,128)(2,1)} %convolution_convert_fusion.7), channel_id=1, source_target_pairs={{0,8},{8,0},{16,24},{24,16},{1,9},{9,1},{17,25},{25,17},{2,10},{10... | collective-permute-start | bytes 12582920 | tf_op jit(solution)/shard_map/ppermute | solution.py:42
  1601.3 262.7 %collective-permute-start.29 = (bf16[512,5504]{1,0:T(8,128)(2,1)}, bf16[512,5504]{1,0:T(8,128)(2,1)}, u32[]{:S(2)}, u32[]{:S(2)}) collective-permute-start(bf16[512,5504]{1,0:T(8,128)(2,1)} %add_convert_fusion.2), channel_id=1, source_target_pairs={{0,16},{8,24},{16,0},{24,8},{1,17},{9,25},{17,1},{25,9},{2,18},{10... | collective-permute-start | bytes 16908296 | tf_op jit(solution)/shard_map/ppermute | solution.py:42
  1707.0 143.0 %all-to-all-start.8 = ((bf16[8,1,512,384]{3,2,1,0:T(8,128)(2,1)}), bf16[8,1,512,384]{3,2,1,0:T(8,128)(2,1)}, u32[]{:S(2)}, u32[]{:S(2)}) async-start(bf16[8,1,512,384]{3,2,1,0:T(8,128)(2,1)} %copy-done.2), calls=%async_computation.8 | async-start | bytes 6291456 | tf_op jit(solution)/shard_map/all_to_all | solution.py:442
  1760.1 67.4 %collective-permute-start.33 = (bf16[4,172,2048]{2,0,1:T(4,128)(2,1)}, bf16[4,172,2048]{2,0,1:T(4,128)(2,1)}, u32[]{:S(2)}, u32[]{:S(2)}) collective-permute-start(bf16[4,172,2048]{2,0,1:T(4,128)(2,1)} %copy.161), channel_id=1, source_target_pairs={{0,1},{1,0},{2,3},{3,2},{4,5},{5,4},{6,7},{7,6},{8,9},{9,8},{10,11... | collective-permute-start | bytes 8454152 | tf_op jit(solution)/shard_map/ppermute | solution.py:42
  1780.8 64.3 %collective-permute-start.34 = (bf16[256,5504]{1,0:T(8,128)(2,1)}, bf16[256,5504]{1,0:T(8,128)(2,1)}, u32[]{:S(2)}, u32[]{:S(2)}) collective-permute-start(bf16[256,5504]{1,0:T(8,128)(2,1)} %dynamic-slice_bitcast_fusion.3), channel_id=1, source_target_pairs={{0,16},{8,24},{16,0},{24,8},{1,17},{9,25},{17,1},{25,9},{2,18},{10... | collective-permute-start | bytes 8454152 | tf_op jit(solution)/shard_map/ppermute | solution.py:42
  1812.1 74.6 %collective-permute-start.30 = (bf16[512,2048]{1,0:T(8,128)(2,1)}, bf16[512,2048]{1,0:T(8,128)(2,1)}, u32[]{:S(2)}, u32[]{:S(2)}) collective-permute-start(bf16[512,2048]{1,0:T(8,128)(2,1)} %add_convert_fusion.11), channel_id=1, source_target_pairs={{0,16},{8,24},{16,0},{24,8},{1,17},{9,25},{17,1},{25,9},{2,18},{10... | collective-permute-start | bytes 6291464 | tf_op jit(solution)/shard_map/ppermute | solution.py:42
  1850.0 80.1 %all-to-all-start.9 = ((bf16[8,1,512,384]{3,2,1,0:T(8,128)(2,1)}), bf16[8,1,512,384]{3,2,1,0:T(8,128)(2,1)S(1)}, u32[]{:S(2)}, u32[]{:S(2)}) async-start(bf16[8,1,512,384]{3,2,1,0:T(8,128)(2,1)} %attend_back.7), calls=%async_computation.9 | async-start | bytes 6291456 | tf_op jit(solution)/shard_map/all_to_all | solution.py:442
  1955.2 113.7 %collective-permute-start.31 = (bf16[1024,3072]{1,0:T(8,128)(2,1)}, bf16[1024,3072]{1,0:T(8,128)(2,1)}, u32[]{:S(2)}, u32[]{:S(2)}) collective-permute-start(bf16[1024,3072]{1,0:T(8,128)(2,1)} %convolution_convert_fusion.6), channel_id=1, source_target_pairs={{0,8},{8,0},{16,24},{24,16},{1,9},{9,1},{17,25},{25,17},{2,10},{10... | collective-permute-start | bytes 18874376 | tf_op jit(solution)/shard_map/ppermute | solution.py:42
  1966.8 110.2 %collective-permute-start.32 = (bf16[1024,3072]{1,0:T(8,128)(2,1)}, bf16[1024,3072]{1,0:T(8,128)(2,1)}, u32[]{:S(2)}, u32[]{:S(2)}) collective-permute-start(bf16[1024,3072]{1,0:T(8,128)(2,1)} %convolution_convert_fusion.5), channel_id=1, source_target_pairs={{0,8},{8,0},{16,24},{24,16},{1,9},{9,1},{17,25},{25,17},{2,10},{10... | collective-permute-start | bytes 18874376 | tf_op jit(solution)/shard_map/ppermute | solution.py:42
  1969.1 87.5 %collective-permute-start.35 = (bf16[4,64,5504]{2,1,0:T(8,128)(2,1)}, bf16[4,64,5504]{2,1,0:T(8,128)(2,1)}, u32[]{:S(2)}, u32[]{:S(2)}) collective-permute-start(bf16[4,64,5504]{2,1,0:T(8,128)(2,1)} %dynamic-slice_bitcast_fusion.2), channel_id=1, source_target_pairs={{0,1},{1,0},{2,3},{3,2},{4,5},{5,4},{6,7},{7,6},{8,9},{9,8},{10,11... | collective-permute-start | bytes 8454152 | tf_op jit(solution)/shard_map/ppermute | solution.py:42
  1970.4 84.5 %collective-permute-start.36 = (bf16[4,64,2048]{2,1,0:T(8,128)(2,1)}, bf16[4,64,2048]{2,1,0:T(8,128)(2,1)}, u32[]{:S(2)}, u32[]{:S(2)}) collective-permute-start(bf16[4,64,2048]{2,1,0:T(8,128)(2,1)} %dynamic-slice_bitcast_fusion.7), channel_id=1, source_target_pairs={{0,1},{1,0},{2,3},{3,2},{4,5},{5,4},{6,7},{7,6},{8,9},{9,8},{10,11... | collective-permute-start | bytes 3145736 | tf_op jit(solution)/shard_map/ppermute | solution.py:42
  2067.4 103.9 %collective-permute-start.37 = (bf16[2,64,18560]{2,1,0:T(8,128)(2,1)}, bf16[2,64,18560]{2,1,0:T(8,128)(2,1)}, u32[]{:S(2)}, u32[]{:S(2)}) collective-permute-start(bf16[2,64,18560]{2,1,0:T(8,128)(2,1)} %dynamic-slice_bitcast_fusion), channel_id=1, source_target_pairs={{0,2},{1,3},{2,0},{3,1},{4,6},{5,7},{6,4},{7,5},{8,10},{9,11},{10,... | collective-permute-start | bytes 14254088 | tf_op jit(solution)/shard_map/ppermute | solution.py:42
  2076.4 108.9 %collective-permute-start.38 = (bf16[512,3072]{1,0:T(8,128)(2,1)}, bf16[512,3072]{1,0:T(8,128)(2,1)}, u32[]{:S(2)}, u32[]{:S(2)}) collective-permute-start(bf16[512,3072]{1,0:T(8,128)(2,1)} %add_convert_fusion.7), channel_id=1, source_target_pairs={{0,16},{8,24},{16,0},{24,8},{1,17},{9,25},{17,1},{25,9},{2,18},{10... | collective-permute-start | bytes 9437192 | tf_op jit(solution)/shard_map/ppermute | solution.py:42
  2085.3 114.5 %collective-permute-start.39 = (bf16[512,3072]{1,0:T(8,128)(2,1)}, bf16[512,3072]{1,0:T(8,128)(2,1)}, u32[]{:S(2)}, u32[]{:S(2)}) collective-permute-start(bf16[512,3072]{1,0:T(8,128)(2,1)} %add_convert_fusion.6), channel_id=1, source_target_pairs={{0,1},{1,0},{2,3},{3,2},{4,5},{5,4},{6,7},{7,6},{8,9},{9,8},{10,11... | collective-permute-start | bytes 9437192 | tf_op jit(solution)/shard_map/ppermute | solution.py:42
  2106.3 1.2 collective-permute-start.45
  2107.6 38.2 %collective-permute-start.46 = (f32[2,2,2,2,64]{4,3,2,1,0:T(2,128)S(1)}, f32[2,2,2,2,64]{4,3,2,1,0:T(2,128)S(1)}, u32[]{:S(2)}, u32[]{:S(2)}) collective-permute-start(f32[2,2,2,2,64]{4,3,2,1,0:T(2,128)S(1)} %fusion.91), channel_id=1, source_target_pairs={{0,16},{8,24},{16,0},{24,8},{1,17},{9,25},{17,1},{25,9},{2,18},{10... | collective-permute-start | bytes 12296 | tf_op jit(solution)/shard_map/ppermute | solution.py:42
  2145.8 8.5 collective-permute-start.47
  2175.1 103.8 %collective-permute-start.44 = (bf16[1,64,18560]{2,1,0:T(8,128)(2,1)S(1)}, bf16[1,64,18560]{2,1,0:T(8,128)(2,1)}, u32[]{:S(2)}, u32[]{:S(2)}) collective-permute-start(bf16[1,64,18560]{2,1,0:T(8,128)(2,1)S(1)} %constant_dynamic-slice_fusion.8), channel_id=1, source_target_pairs={{0,4},{1,5},{2,6},{3,7},{4,0},{5,1},{6,2},{7,3},{8,12},{9,13},{10,... | collective-permute-start | bytes 7127048 | tf_op jit(solution)/shard_map/ppermute | solution.py:42
  2206.0 75.3 %collective-permute-start.40 = (bf16[4,64,3072]{2,1,0:T(8,128)(2,1)S(1)}, bf16[4,64,3072]{2,1,0:T(8,128)(2,1)S(1)}, u32[]{:S(2)}, u32[]{:S(2)}) collective-permute-start(bf16[4,64,3072]{2,1,0:T(8,128)(2,1)S(1)} %dynamic-slice_bitcast_fusion.6), channel_id=1, source_target_pairs={{0,1},{1,0},{2,3},{3,2},{4,5},{5,4},{6,7},{7,6},{8,9},{9,8},{10,11... | collective-permute-start | bytes 4718600 | tf_op jit(solution)/shard_map/ppermute | solution.py:42
  2206.7 75.2 %collective-permute-start.41 = (bf16[256,3072]{1,0:T(8,128)(2,1)S(1)}, bf16[256,3072]{1,0:T(8,128)(2,1)S(1)}, u32[]{:S(2)}, u32[]{:S(2)}) collective-permute-start(bf16[256,3072]{1,0:T(8,128)(2,1)S(1)} %dynamic-slice_bitcast_fusion.5), channel_id=1, source_target_pairs={{0,16},{8,24},{16,0},{24,8},{1,17},{9,25},{17,1},{25,9},{2,18},{10... | collective-permute-start | bytes 4718600 | tf_op jit(solution)/shard_map/ppermute | solution.py:42
  2282.9 35.5 %collective-permute-start.42 = (bf16[2,64,6144]{2,1,0:T(8,128)(2,1)S(1)}, bf16[2,64,6144]{2,1,0:T(8,128)(2,1)S(1)}, u32[]{:S(2)}, u32[]{:S(2)}) collective-permute-start(bf16[2,64,6144]{2,1,0:T(8,128)(2,1)S(1)} %dynamic-slice_bitcast_fusion.4), channel_id=1, source_target_pairs={{0,2},{1,3},{2,0},{3,1},{4,6},{5,7},{6,4},{7,5},{8,10},{9,11},{10,... | collective-permute-start | bytes 4718600 | tf_op jit(solution)/shard_map/ppermute | solution.py:42
  2283.3 35.0 %collective-permute-start.48 = (f32[2,2,64]{2,0,1:T(2,128)S(1)}, f32[2,2,64]{2,0,1:T(2,128)S(1)}, u32[]{:S(2)}, u32[]{:S(2)}) collective-permute-start(f32[2,2,64]{2,0,1:T(2,128)S(1)} %bitcast.458), channel_id=1, source_target_pairs={{0,2},{1,3},{2,0},{3,1},{4,6},{5,7},{6,4},{7,5},{8,10},{9,11},{10,... | collective-permute-start | bytes 3080 | tf_op jit(solution)/shard_map/ppermute | solution.py:42
  2318.8 6.4 collective-permute-start.49
  2322.8 36.7 %collective-permute-start.43 = (bf16[1,64,6144]{2,1,0:T(8,128)(2,1)}, bf16[1,64,6144]{2,1,0:T(8,128)(2,1)}, u32[]{:S(2)}, u32[]{:S(2)}) collective-permute-start(bf16[1,64,6144]{2,1,0:T(8,128)(2,1)} %constant_dynamic-slice_fusion.9), channel_id=1, source_target_pairs={{0,4},{1,5},{2,6},{3,7},{4,0},{5,1},{6,2},{7,3},{8,12},{9,13},{10,... | collective-permute-start | bytes 2359304 | tf_op jit(solution)/shard_map/ppermute | solution.py:42
  (99 other events, 2187.7 us)
Sparse Core Ops, SparseCore 0:
  11.6 250.1 all-gather.1

commit v7 on v6

--- a/solution.py
+++ b/solution.py
@@ -506,9 +506,8 @@
     soon.near_step(0)
     later.wait(*ready)
     later.far_step(far - 1)
-    later.wait(*soon.values())
     later.near_step(0)
-    h_kept = step_in = after(h_attn, *later.values())
+    h_kept = after(h_attn, *later.values(), *soon.values())
     saved, attended, arrived = [], [], []
 
     def project(g, *others):
@@ -530,9 +529,8 @@
     soon.near_step(2)
     later.near_step(2)
     full_gate, full_out = soon.finish()
-    full_up, full_down = later.finish()
-    full_down = full_down.reshape(FF, D)
-    attended.append(rows_of(after(back_rows, full_gate, full_out, full_up, full_down), micros))
+    full_up, flat_down = later.finish()
+    attended.append(rows_of(after(back_rows, full_gate, full_out, full_up, flat_down), micros))
     if groups > 1:
         project(1, attended[0])
 
@@ -562,6 +560,8 @@
         act = (gate * sig * up).astype(bf16)
         parts.append([mid, scale_m, h_mlp, act])
         mark = (act,)
+        if g == 0:
+            full_down = after(flat_down, act).reshape(FF, D)
         if final:
             acts = jnp.concatenate([p[3] for p in parts], axis=0)
             sides = jnp.concatenate([p[2] for p in parts], axis=0)
@@ -588,7 +588,7 @@
             mark = (up_r.cross(*mark),)
             mark = (gate_r.cross(*mark),)
         if final:
-            mark = (up_r.send(*mark),)
+            mark = (up_r.send(*mark, *[r for pieces in rows_grad for r in pieces]),)
         half_grad = nt(after(grad_gate, *mark), full_gate)
         mark = (half_grad,)
         grad_h_mlp = half_grad + nt(after(grad_up, *mark), full_up)
@@ -630,9 +630,8 @@
         act = after(parts[g][3], *mark)
         layer_outs.append((parts[g][0] + jnp.dot(act, full_down, preferred_element_type=f32)).astype(bf16))
         mark = (layer_outs[-1],)
-    mark = mark + tuple(rows_grad[-1])
+    mark = mark + tuple(rows_grad[-1]) + tuple(r.total for r in early)
     first = Finish(early, *mark)
-    first.step(0)
     h_sides = [pieces_of(h_kept, False), pieces_of(h_kept, True)]
     for g in range(groups - 1):
         grad_qkv.append(rows_of(jnp.concatenate(rows_grad[g], axis=1), micros))
@@ -647,6 +646,7 @@
         mark = (finish_tokens(g, *mark),)
     for r in late:
         mark = (r.send(*mark),)
+    first.step(0, hold=mark)
     g = groups - 1
     grad_h_attn = nt(after(last_rows, *mark), full_qkv)
     grad_norm, gain_part = norm_backward(grad_h_attn, of(x, g), of(scale_a, g), gain_a)

time: 2380 us -> 2360 us (level)
  transfers between devices with their start and end apart: 61 -> 61, of which waited for: 28 -> 24; matrix products, arithmetic and copies ran while one was open for 31% -> 30% of each run, Pallas kernels for 9% -> 10%
where the time goes in v7:
time: 2360 us; the launch traced here: 2350 us
  waiting for transfers between devices  1030 us (44%)
  matrix products  554 us (23%)
  Pallas kernels  271 us (11%)
  local copies, waits for them, and re-layouts  218 us (9%)
  other arithmetic  156 us (7%)
  starting transfers between devices  106 us (4%)
    ppermute x50, waiting for transfers between devices, swap(): lax.ppermute(block, axis, [(i, i ^ stride) for i in range(lax.axis_size(a...  914 us
    dot_general x10, matrix products, nt(): return jnp.einsum('re,de->rd', a, b, preferred_element_type=f32)  186 us
    dot_general x16, matrix products, tn(): lax.dot_general(a, b, (((0,), (0,)), ((), ())), preferred_element_type=f32)  184 us
    pallas_call x4, Pallas kernels, attend_back(): pl.pallas_call(functools.partial(backward_kernel, pair), grid_spec=pltpu....  131 us
    pallas_call x2, Pallas kernels, attend(): pl.pallas_call(forward_kernel, grid_spec=pltpu.PrefetchScalarGridSpec(num...  93.8 us
    all_to_all x4, waiting for transfers between devices, to_heads(): return lax.all_to_all(split, 'seq', 0, 0, tiled=True)  73.6 us
    ppermute x50, starting transfers between devices, swap(): lax.ppermute(block, axis, [(i, i ^ stride) for i in range(lax.axis_size(a...  54.9 us
    dot_general x2, matrix products, shards(): up = jnp.dot(after(h_mlp, *mark), full_up, preferred_element_type=f32)  50.6 us
  transfers between devices with their start and end apart: 61, of which 24 were waited for; matrix products, arithmetic and copies ran while one was open for 30% of the time, Pallas kernels for 10%

profile of v7, /device:TPU:0, one launch (start us, length us, event | category | flops | bytes accessed | tf_op | source)
XLA Modules:
  0.0 2353.0 jit_solution(18438047000911538285)
XLA Ops:
  36.2 9.3 copy.145
  55.2 72.0 %collective-permute-done.5 = bf16[64,7552]{1,0:T(8,128)(2,1)S(1)} collective-permute-done((bf16[64,7552]{1,0:T(8,128)(2,1)S(1)}, bf16[64,7552]{1,0:T(8,128)(2,1)S(1)}, u32[]{:S(2)}, u32[]{:S(2)}) %collective-permute-start.5) | collective-permute-done | bytes 966688 | tf_op jit(solution)/shard_map/ppermute | solution.py:42
  129.4 121.8 %collective-permute-done.6 = bf16[64,11008]{1,0:T(8,128)(2,1)S(1)} collective-permute-done((bf16[64,11008]{1,0:T(8,128)(2,1)S(1)}, bf16[64,11008]{1,0:T(8,128)(2,1)S(1)}, u32[]{:S(2)}, u32[]{:S(2)}) %collective-permute-start.6) | collective-permute-done | bytes 1409056 | tf_op jit(solution)/shard_map/ppermute | solution.py:42
  251.2 16.3 collective-permute-done.7
  268.4 62.2 %collective-permute-done.8 = bf16[128,11008]{1,0:T(8,128)(2,1)S(1)} collective-permute-done((bf16[128,11008]{1,0:T(8,128)(2,1)S(1)}, bf16[128,11008]{1,0:T(8,128)(2,1)S(1)}, u32[]{:S(2)}, u32[]{:S(2)}) %collective-permute-start.8) | collective-permute-done | bytes 2818080 | tf_op jit(solution)/shard_map/ppermute | solution.py:42
  336.1 82.7 %collective-permute-done.10.refs_1_ = bf16[256,7552]{1,0:T(8,128)(2,1)S(1)} collective-permute-done((bf16[256,7552]{1,0:T(8,128)(2,1)S(1)}, bf16[256,7552]{1,0:T(8,128)(2,1)S(1)}, u32[]{:S(2)}, u32[]{:S(2)}) %collective-permute-start.10) | collective-permute-done | bytes 3866656 | tf_op jit(solution)/shard_map/ppermute | solution.py:42
  420.7 35.0 %collective-permute-done.9.refs_1_ = bf16[256,11008]{1,0:T(8,128)(2,1)} collective-permute-done((bf16[256,11008]{1,0:T(8,128)(2,1)S(1)}, bf16[256,11008]{1,0:T(8,128)(2,1)}, u32[]{:S(2)}, u32[]{:S(2)}) %collective-permute-start.9) | collective-permute-done | bytes 5636128 | tf_op jit(solution)/shard_map/ppermute | solution.py:42
  455.6 19.0 convolution_convert_fusion.4
  489.3 149.0 %collective-permute-done.12.refs_3_ = bf16[256,7552]{1,0:T(8,128)(2,1)} collective-permute-done((bf16[256,7552]{1,0:T(8,128)(2,1)}, bf16[256,7552]{1,0:T(8,128)(2,1)}, u32[]{:S(2)}, u32[]{:S(2)}) %collective-permute-start.12) | collective-permute-done | bytes 3866656 | tf_op jit(solution)/shard_map/ppermute | solution.py:42
  638.3 80.8 %collective-permute-done.11.refs_2_ = bf16[256,7552]{1,0:T(8,128)(2,1)} collective-permute-done((bf16[256,7552]{1,0:T(8,128)(2,1)}, bf16[256,7552]{1,0:T(8,128)(2,1)}, u32[]{:S(2)}, u32[]{:S(2)}) %collective-permute-start.11) | collective-permute-done | bytes 3866656 | tf_op jit(solution)/shard_map/ppermute | solution.py:42
  730.6 46.9 %attend.2 = (bf16[8,2,512,128]{3,2,1,0:T(8,128)(2,1)}, f32[2,1,4096]{2,1,0:T(1,128)S(1)}) custom-call(s32[2,4,8]{2,1,0:T(4,128)S(1)} %pad_add_fusion.2.bounds, bf16[8,2,512,384]{3,2,1,0:T(8,128)(2,1)} %all-to-all-done.q_ref.k_ref.v_ref, bf16[8,2,512,384]{3,2,1,0:T(8,128)(2,1)} %all-to-all-done.q_ref.k_ref.v_ref, ...), custom_call_target="tpu_custom_call" | custom-call | flops 1024 | bytes 1024 | tf_op jit(solution)/shard_map/attend/pallas_call | solution.py:314
  795.1 17.0 place.2
  815.4 29.4 %place.3 = (bf16[2048,5504]{1,0:T(8,128)(2,1)}, bf16[2048,5504]{1,0:T(8,128)(2,1)}) custom-call(s32[32]{0:T(128)S(1)} %xor_multiply_fusion.target, bf16[256,11008]{1,0:T(8,128)(2,1)S(1)} %bitcast.340, bf16[256,11008]{1,0:T(8,128)(2,1)} %collective-permute-done.9.refs_1_, bf16[256,11008]{1,0:T(8,128)(2,1)} %collective-permute-done.13.refs_2_, ...), custom_call_target="tpu_custom_call" | custom-call | flops 1024 | bytes 1024 | tf_op jit(solution)/shard_map/place/pallas_call | solution.py:149
  848.8 18.8 convolution_convert_fusion.3
  879.6 10.3 multiply_reduce_fusion.10
  893.5 19.0 fusion.120
  912.5 25.3 %multiply_convert_fusion.5 = (bf16[512,5504]{1,0:T(8,128)(2,1)}, f32[512,5504]{1,0:T(8,128)}) fusion(f32[512,5504]{1,0:T(8,128)} %fusion.120, bf16[512,2048]{1,0:T(8,128)(2,1)} %copy-done.40, bf16[2048,5504]{1,0:T(8,128)(2,1)} %get-tuple-element.92), kind=kOutput, calls=%fused_computation.24 | convolution fusion | flops 11559632896 | bytes 52822016 | tf_op jit(solution)/shard_map/dot_general | solution.py:558
  937.8 31.1 %reshape.453 = bf16[5504,2048]{1,0:T(8,128)(2,1)} reshape(bf16[2048,5504]{1,0:T(8,128)(2,1)} %get-tuple-element.97) | data formatting | bytes 45088768 | tf_op jit(solution)/shard_map/reshape | solution.py:564
  969.0 25.2 %multiply_convert_fusion.3 = (bf16[512,5504]{1,0:T(8,128)(2,1)}, bf16[512,5504]{1,0:T(8,128)(2,1)}) fusion(f32[512,5504]{1,0:T(8,128)} %fusion.120, f32[512,5504]{1,0:T(8,128)} %get-tuple-element.276, bf16[512,2048]{1,0:T(8,128)(2,1)} %get-tuple-element.96, bf16[5504,2048]{1,0:T(8,128)(2,1)} %reshape.453), kind=kOutput, calls=%fused_computation.22 | convolution fusion | flops 11579359232 | bytes 58458112 | tf_op jit(solution)/shard_map/re,de->rd/dot_general | solution.py:463
  994.1 22.8 all-to-all-done.2.q_ref.k_ref.v_ref
  1017.0 46.9 %attend.3 = (bf16[8,2,512,128]{3,2,1,0:T(8,128)(2,1)}, f32[2,1,4096]{2,1,0:T(1,128)S(1)}) custom-call(s32[2,4,8]{2,1,0:T(4,128)S(1)} %pad_add_fusion.3.bounds, bf16[8,2,512,384]{3,2,1,0:T(8,128)(2,1)} %all-to-all-done.2.q_ref.k_ref.v_ref, bf16[8,2,512,384]{3,2,1,0:T(8,128)(2,1)} %all-to-all-done.2.q_ref.k_ref.v_ref, ...), custom_call_target="tpu_custom_call" | custom-call | flops 1024 | bytes 1024 | tf_op jit(solution)/shard_map/attend/pallas_call | solution.py:314
  1067.5 19.5 fusion.121
  1087.0 19.4 multiply_reduce_fusion.2
  1108.4 8.9 convolution_convert_fusion.9
  1131.2 10.3 multiply_reduce_fusion.8
  1145.2 19.0 fusion.122
  1164.2 25.3 %multiply_convert_fusion.2 = (bf16[512,5504]{1,0:T(8,128)(2,1)}, f32[512,5504]{1,0:T(8,128)}) fusion(f32[512,5504]{1,0:T(8,128)} %fusion.122, bf16[512,2048]{1,0:T(8,128)(2,1)} %copy-done.42, bf16[2048,5504]{1,0:T(8,128)(2,1)} %get-tuple-element.92), kind=kOutput, calls=%fused_computation.19 | convolution fusion | flops 11559632896 | bytes 52822016 | tf_op jit(solution)/shard_map/dot_general | solution.py:558
  1189.5 11.5 pad_maximum_fusion
  1201.0 31.4 %convolution_convert_fusion = bf16[5504,2048]{1,0:T(8,128)(2,1)} fusion(bf16[1024,5504]{1,0:T(8,128)(2,1)} %pad_maximum_fusion, bf16[1024,2048]{1,0:T(8,128)(2,1)} %bitcast.348), kind=kOutput, calls=%fused_computation | convolution fusion | flops 23096721408 | bytes 38010880 | tf_op jit(solution)/shard_map/dot_general | solution.py:169
  1232.4 10.0 constant_dynamic-slice_fusion.10
  1242.4 32.4 %attend_back.4 = bf16[8,1,512,384]{3,2,1,0:T(8,128)(2,1)S(1)} custom-call(s32[2,4,8]{2,1,0:T(4,128)S(1)} %copy-done.19, bf16[8,2,512,384]{3,2,1,0:T(8,128)(2,1)} %all-to-all-done.q_ref.k_ref.v_ref, bf16[8,2,512,384]{3,2,1,0:T(8,128)(2,1)} %all-to-all-done.q_ref.k_ref.v_ref, bf16[8,2,512,384]{3,2,1,0:T(8,128)(2,1)} %all-to-all-done.q_ref.k_ref.v_ref, ...), custom_call_target="tpu_custom_call" | custom-call | flops 1024 | bytes 1024 | tf_op jit(solution)/shard_map/attend_back/pallas_call | solution.py:391
  1283.0 33.4 %attend_back.5 = bf16[8,1,512,384]{3,2,1,0:T(8,128)(2,1)} custom-call(s32[2,4,8]{2,1,0:T(4,128)S(1)} %copy-done.19, bf16[8,2,512,384]{3,2,1,0:T(8,128)(2,1)} %all-to-all-done.q_ref.k_ref.v_ref, bf16[8,2,512,384]{3,2,1,0:T(8,128)(2,1)} %all-to-all-done.q_ref.k_ref.v_ref, bf16[8,2,512,384]{3,2,1,0:T(8,128)(2,1)} %all-to-all-done.q_ref.k_ref.v_ref, ...), custom_call_target="tpu_custom_call" | custom-call | flops 1024 | bytes 1024 | tf_op jit(solution)/shard_map/attend_back/pallas_call | solution.py:391
  1330.3 10.1 fusion.2
  1340.4 13.7 all-to-all-done.5
  1354.0 24.7 %multiply_convert_fusion = (bf16[512,5504]{1,0:T(8,128)(2,1)}, bf16[512,5504]{1,0:T(8,128)(2,1)}) fusion(f32[512,5504]{1,0:T(8,128)} %fusion.122, f32[512,5504]{1,0:T(8,128)} %get-tuple-element.281, bf16[512,2048]{1,0:T(8,128)(2,1)S(1)} %copy-done.52, bf16[5504,2048]{1,0:T(8,128)(2,1)} %reshape.453), kind=kOutput, calls=%fused_computation.17 | convolution fusion | flops 11579359232 | bytes 58458112 | tf_op jit(solution)/shard_map/re,de->rd/dot_general | solution.py:463
  1378.7 19.4 convolution_convert_fusion.2
  1410.4 11.2 copy.152
  1421.6 19.3 convolution_convert_fusion.1
  1443.4 30.8 %all-to-all-done.6 = bf16[8,1,512,384]{3,2,1,0:T(8,128)(2,1)} async-done(((bf16[8,1,512,384]{3,2,1,0:T(8,128)(2,1)}), bf16[8,1,512,384]{3,2,1,0:T(8,128)(2,1)}, u32[]{:S(2)}, u32[]{:S(2)}) %all-to-all-start.6) | async-done | bytes 3145760 | tf_op jit(solution)/shard_map/all_to_all | solution.py:442
  1474.3 11.7 add_convert_fusion.3
  1487.4 19.5 fusion.123
  1507.0 18.8 multiply_reduce_fusion.1
  1527.8 8.9 convolution_convert_fusion.8
  1546.5 13.3 add_convert_fusion.2
  1567.9 13.1 fusion.1
  1581.0 50.8 %all-to-all-done.7.do_ref = bf16[8,2,512,128]{3,2,1,0:T(8,128)(2,1)S(1)} async-done(((bf16[8,2,512,128]{3,2,1,0:T(8,128)(2,1)}), bf16[8,2,512,128]{3,2,1,0:T(8,128)(2,1)S(1)}, u32[]{:S(2)}, u32[]{:S(2)}) %all-to-all-start.7) | async-done | bytes 2097184 | tf_op jit(solution)/shard_map/all_to_all | solution.py:438
  1631.9 32.0 %attend_back.6 = bf16[8,1,512,384]{3,2,1,0:T(8,128)(2,1)S(1)} custom-call(s32[2,4,8]{2,1,0:T(4,128)S(1)} %copy-done.17, bf16[8,2,512,384]{3,2,1,0:T(8,128)(2,1)} %all-to-all-done.2.q_ref.k_ref.v_ref, bf16[8,2,512,384]{3,2,1,0:T(8,128)(2,1)} %all-to-all-done.2.q_ref.k_ref.v_ref, bf16[8,2,512,384]{3,2,1,0:T(8,128)(2,1)} %all-to-all-done.2.q_ref.k_ref.v_ref, ...), custom_call_target="tpu_custom_call" | custom-call | flops 1024 | bytes 1024 | tf_op jit(solution)/shard_map/attend_back/pallas_call | solution.py:391
  1670.2 32.9 %attend_back.7 = bf16[8,1,512,384]{3,2,1,0:T(8,128)(2,1)} custom-call(s32[2,4,8]{2,1,0:T(4,128)S(1)} %copy-done.17, bf16[8,2,512,384]{3,2,1,0:T(8,128)(2,1)} %all-to-all-done.2.q_ref.k_ref.v_ref, bf16[8,2,512,384]{3,2,1,0:T(8,128)(2,1)} %all-to-all-done.2.q_ref.k_ref.v_ref, bf16[8,2,512,384]{3,2,1,0:T(8,128)(2,1)} %all-to-all-done.2.q_ref.k_ref.v_ref, ...), custom_call_target="tpu_custom_call" | custom-call | flops 1024 | bytes 1024 | tf_op jit(solution)/shard_map/attend_back/pallas_call | solution.py:391
  1751.8 9.0 copy.157
  1768.6 15.8 collective-permute-done.31
  1789.6 10.4 collective-permute-done.32
  1809.5 9.4 fusion.14
  1829.0 14.1 collective-permute-done.30
  1851.3 19.0 add_convert_fusion.9
  1870.4 18.4 add_convert_fusion.8
  1893.9 41.8 %collective-permute-done.33 = bf16[4,64,5504]{2,1,0:T(8,128)(2,1)} collective-permute-done((bf16[4,64,5504]{2,1,0:T(8,128)(2,1)}, bf16[4,64,5504]{2,1,0:T(8,128)(2,1)}, u32[]{:S(2)}, u32[]{:S(2)}) %collective-permute-start.33) | collective-permute-done | bytes 2818080 | tf_op jit(solution)/shard_map/ppermute | solution.py:42
  1954.8 11.4 convolution_convert_fusion.6
  1966.2 10.8 convolution_convert_fusion.5
  1977.6 20.5 multiply_reduce_fusion.4
  2047.1 20.6 multiply_reduce_fusion.3
  2067.8 65.0 %collective-permute-done.37 = bf16[2,64,18560]{2,1,0:T(8,128)(2,1)} collective-permute-done((bf16[2,64,18560]{2,1,0:T(8,128)(2,1)}, bf16[2,64,18560]{2,1,0:T(8,128)(2,1)}, u32[]{:S(2)}, u32[]{:S(2)}) %collective-permute-start.37) | collective-permute-done | bytes 4751392 | tf_op jit(solution)/shard_map/ppermute | solution.py:42
  2183.8 80.5 %collective-permute-done.44 = bf16[1,64,18560]{2,1,0:T(8,128)(2,1)S(1)} collective-permute-done((bf16[1,64,18560]{2,1,0:T(8,128)(2,1)}, bf16[1,64,18560]{2,1,0:T(8,128)(2,1)S(1)}, u32[]{:S(2)}, u32[]{:S(2)}) %collective-permute-start.44) | collective-permute-done | bytes 2375712 | tf_op jit(solution)/shard_map/ppermute | solution.py:42
  2270.6 31.6 %collective-permute-done.48 = f32[2,2,64]{2,0,1:T(2,128)S(1)} collective-permute-done((f32[2,2,64]{2,0,1:T(2,128)S(1)}, f32[2,2,64]{2,0,1:T(2,128)S(1)}, u32[]{:S(2)}, u32[]{:S(2)}) %collective-permute-start.48) | collective-permute-done | bytes 1056 | tf_op jit(solution)/shard_map/ppermute | solution.py:42
  2309.3 31.8 %collective-permute-done.43 = bf16[1,64,6144]{2,1,0:T(8,128)(2,1)} collective-permute-done((bf16[1,64,6144]{2,1,0:T(8,128)(2,1)}, bf16[1,64,6144]{2,1,0:T(8,128)(2,1)}, u32[]{:S(2)}, u32[]{:S(2)}) %collective-permute-start.43) | collective-permute-done | bytes 786464 | tf_op jit(solution)/shard_map/ppermute | solution.py:42
  (464 shorter events, 434.9 us)
Async XLA Ops:
  7.2 448.4 %all-gather.2.cloned.1.call-start = ((), (), s32[]{:S(2)}) async-start(), calls=%async_computation.10 | async-start | bytes 25952256 | tf_op jit(solution)/shard_map/all_gather | solution.py:469
  10.6 4.5 collective-permute-start
  15.2 3.6 collective-permute-start.1
  18.9 4.6 collective-permute-start.2
  23.6 3.4 collective-permute-start.3
  27.0 19.4 collective-permute-start.4
  46.5 1095.1 %copy-start.55 = (f32[1,2048]{1,0:T(1,128)}, f32[1,2048]{1,0:T(1,128)S(1)}, u32[]{:S(2)}) copy-start(f32[1,2048]{1,0:T(1,128)S(1)} %get-tuple-element.251) | copy-start | bytes 24580
  52.8 74.3 %collective-permute-start.5 = (bf16[64,7552]{1,0:T(8,128)(2,1)S(1)}, bf16[64,7552]{1,0:T(8,128)(2,1)S(1)}, u32[]{:S(2)}, u32[]{:S(2)}) collective-permute-start(bf16[64,7552]{1,0:T(8,128)(2,1)S(1)} %pad_maximum_fusion.29), channel_id=1, source_target_pairs={{0,4},{1,5},{2,6},{3,7},{4,0},{5,1},{6,2},{7,3},{8,12},{9,13},{10,... | collective-permute-start | bytes 2899976 | tf_op jit(solution)/shard_map/ppermute | solution.py:42
  127.4 123.7 %collective-permute-start.6 = (bf16[64,11008]{1,0:T(8,128)(2,1)S(1)}, bf16[64,11008]{1,0:T(8,128)(2,1)S(1)}, u32[]{:S(2)}, u32[]{:S(2)}) collective-permute-start(bf16[64,11008]{1,0:T(8,128)(2,1)S(1)} %pad_maximum_fusion.23), channel_id=1, source_target_pairs={{0,4},{1,5},{2,6},{3,7},{4,0},{5,1},{6,2},{7,3},{8,12},{9,13},{10,... | collective-permute-start | bytes 4227080 | tf_op jit(solution)/shard_map/ppermute | solution.py:42
  127.5 140.1 %collective-permute-start.7 = (bf16[128,7552]{1,0:T(8,128)(2,1)S(1)}, bf16[128,7552]{1,0:T(8,128)(2,1)S(1)}, u32[]{:S(2)}, u32[]{:S(2)}) collective-permute-start(bf16[128,7552]{1,0:T(8,128)(2,1)S(1)} %get-tuple-element.246), channel_id=1, source_target_pairs={{0,2},{1,3},{2,0},{3,1},{4,6},{5,7},{6,4},{7,5},{8,10},{9,11},{10,... | collective-permute-start | bytes 5799944 | tf_op jit(solution)/shard_map/ppermute | solution.py:42
  267.8 62.8 %collective-permute-start.8 = (bf16[128,11008]{1,0:T(8,128)(2,1)S(1)}, bf16[128,11008]{1,0:T(8,128)(2,1)S(1)}, u32[]{:S(2)}, u32[]{:S(2)}) collective-permute-start(bf16[128,11008]{1,0:T(8,128)(2,1)S(1)} %constant_dynamic-update-slice_fusion.2), channel_id=1, source_target_pairs={{0,2},{1,3},{2,0},{3,1},{4,6},{5,7},{6,4},{7,5},{8,10},{9,11},{10,... | collective-permute-start | bytes 8454152 | tf_op jit(solution)/shard_map/ppermute | solution.py:42
  333.2 122.4 %collective-permute-start.9 = (bf16[256,11008]{1,0:T(8,128)(2,1)S(1)}, bf16[256,11008]{1,0:T(8,128)(2,1)}, u32[]{:S(2)}, u32[]{:S(2)}) collective-permute-start(bf16[256,11008]{1,0:T(8,128)(2,1)S(1)} %constant_dynamic-update-slice_fusion.7.refs_0_), channel_id=1, source_target_pairs={{0,1},{1,0},{2,3},{3,2},{4,5},{5,4},{6,7},{7,6},{8,9},{9,8},{10,11... | collective-permute-start | bytes 16908296 | tf_op jit(solution)/shard_map/ppermute | solution.py:42
  334.7 84.1 %collective-permute-start.10 = (bf16[256,7552]{1,0:T(8,128)(2,1)S(1)}, bf16[256,7552]{1,0:T(8,128)(2,1)S(1)}, u32[]{:S(2)}, u32[]{:S(2)}) collective-permute-start(bf16[256,7552]{1,0:T(8,128)(2,1)S(1)} %constant_dynamic-update-slice_fusion.4.refs_0_), channel_id=1, source_target_pairs={{0,16},{8,24},{16,0},{24,8},{1,17},{9,25},{17,1},{25,9},{2,18},{10... | collective-permute-start | bytes 11599880 | tf_op jit(solution)/shard_map/ppermute | solution.py:42
  480.3 238.8 %copy-start.61 = (s32[2,1,4096]{2,1,0:T(1,128)S(1)}, s32[2,1,4096]{2,1,0:T(1,128)}, u32[]{:S(2)}) copy-start(s32[2,1,4096]{2,1,0:T(1,128)} %param.12) | copy-start | bytes 98308
  480.3 250.3 %all-to-all-start = ((bf16[8,2,512,384]{3,2,1,0:T(8,128)(2,1)}), bf16[8,2,512,384]{3,2,1,0:T(8,128)(2,1)}, u32[]{:S(2)}, u32[]{:S(2)}) async-start(bf16[8,2,512,384]{3,2,1,0:T(8,128)(2,1)} %bitcast.351), calls=%async_computation | async-start | bytes 12582912 | tf_op jit(solution)/shard_map/all_to_all | solution.py:438
  485.2 153.1 %collective-permute-start.12 = (bf16[256,7552]{1,0:T(8,128)(2,1)}, bf16[256,7552]{1,0:T(8,128)(2,1)}, u32[]{:S(2)}, u32[]{:S(2)}) collective-permute-start(bf16[256,7552]{1,0:T(8,128)(2,1)} %copy-done.6), channel_id=1, source_target_pairs={{0,1},{1,0},{2,3},{3,2},{4,5},{5,4},{6,7},{7,6},{8,9},{9,8},{10,11... | collective-permute-start | bytes 11599880 | tf_op jit(solution)/shard_map/ppermute | solution.py:42
  487.1 232.0 %collective-permute-start.11 = (bf16[256,7552]{1,0:T(8,128)(2,1)}, bf16[256,7552]{1,0:T(8,128)(2,1)}, u32[]{:S(2)}, u32[]{:S(2)}) collective-permute-start(bf16[256,7552]{1,0:T(8,128)(2,1)} %copy-done.4), channel_id=1, source_target_pairs={{0,1},{1,0},{2,3},{3,2},{4,5},{5,4},{6,7},{7,6},{8,9},{9,8},{10,11... | collective-permute-start | bytes 11599880 | tf_op jit(solution)/shard_map/ppermute | solution.py:42
  487.3 240.9 %collective-permute-start.14 = (bf16[256,11008]{1,0:T(8,128)(2,1)}, bf16[256,11008]{1,0:T(8,128)(2,1)}, u32[]{:S(2)}, u32[]{:S(2)}) collective-permute-start(bf16[256,11008]{1,0:T(8,128)(2,1)} %collective-permute-done.9.refs_1_), channel_id=1, source_target_pairs={{0,16},{8,24},{16,0},{24,8},{1,17},{9,25},{17,1},{25,9},{2,18},{10... | collective-permute-start | bytes 16908296 | tf_op jit(solution)/shard_map/ppermute | solution.py:42
  488.7 240.5 %collective-permute-start.13 = (bf16[256,11008]{1,0:T(8,128)(2,1)}, bf16[256,11008]{1,0:T(8,128)(2,1)}, u32[]{:S(2)}, u32[]{:S(2)}) collective-permute-start(bf16[256,11008]{1,0:T(8,128)(2,1)} %copy-done.1), channel_id=1, source_target_pairs={{0,16},{8,24},{16,0},{24,8},{1,17},{9,25},{17,1},{25,9},{2,18},{10... | collective-permute-start | bytes 16908296 | tf_op jit(solution)/shard_map/ppermute | solution.py:42
  489.3 234.6 %collective-permute-start.16 = (bf16[256,7552]{1,0:T(8,128)(2,1)}, bf16[256,7552]{1,0:T(8,128)(2,1)S(1)}, u32[]{:S(2)}, u32[]{:S(2)}) collective-permute-start(bf16[256,7552]{1,0:T(8,128)(2,1)} %copy-done.6), channel_id=1, source_target_pairs={{0,8},{8,0},{16,24},{24,16},{1,9},{9,1},{17,25},{25,17},{2,10},{10... | collective-permute-start | bytes 11599880 | tf_op jit(solution)/shard_map/ppermute | solution.py:42
  638.3 88.1 %collective-permute-start.15 = (bf16[256,7552]{1,0:T(8,128)(2,1)}, bf16[256,7552]{1,0:T(8,128)(2,1)S(1)}, u32[]{:S(2)}, u32[]{:S(2)}) collective-permute-start(bf16[256,7552]{1,0:T(8,128)(2,1)} %copy-done.4), channel_id=1, source_target_pairs={{0,8},{8,0},{16,24},{24,16},{1,9},{9,1},{17,25},{25,17},{2,10},{10... | collective-permute-start | bytes 11599880 | tf_op jit(solution)/shard_map/ppermute | solution.py:42
  719.1 10.8 collective-permute-start.18
  725.9 89.5 %collective-permute-start.20 = (bf16[256,11008]{1,0:T(8,128)(2,1)}, bf16[256,11008]{1,0:T(8,128)(2,1)}, u32[]{:S(2)}, u32[]{:S(2)}) collective-permute-start(bf16[256,11008]{1,0:T(8,128)(2,1)} %collective-permute-done.9.refs_1_), channel_id=1, source_target_pairs={{0,8},{8,0},{16,24},{24,16},{1,9},{9,1},{17,25},{25,17},{2,10},{10... | collective-permute-start | bytes 16908296 | tf_op jit(solution)/shard_map/ppermute | solution.py:42
  728.2 87.1 %collective-permute-start.19 = (bf16[256,11008]{1,0:T(8,128)(2,1)}, bf16[256,11008]{1,0:T(8,128)(2,1)}, u32[]{:S(2)}, u32[]{:S(2)}) collective-permute-start(bf16[256,11008]{1,0:T(8,128)(2,1)} %copy-done.1), channel_id=1, source_target_pairs={{0,8},{8,0},{16,24},{24,16},{1,9},{9,1},{17,25},{25,17},{2,10},{10... | collective-permute-start | bytes 16908296 | tf_op jit(solution)/shard_map/ppermute | solution.py:42
  728.3 87.1 %collective-permute-start.22 = (bf16[256,11008]{1,0:T(8,128)(2,1)}, bf16[256,11008]{1,0:T(8,128)(2,1)}, u32[]{:S(2)}, u32[]{:S(2)}) collective-permute-start(bf16[256,11008]{1,0:T(8,128)(2,1)} %collective-permute-done.14.refs_3_), channel_id=1, source_target_pairs={{0,8},{8,0},{16,24},{24,16},{1,9},{9,1},{17,25},{25,17},{2,10},{10... | collective-permute-start | bytes 16908296 | tf_op jit(solution)/shard_map/ppermute | solution.py:42
  729.2 86.2 %collective-permute-start.21 = (bf16[256,11008]{1,0:T(8,128)(2,1)}, bf16[256,11008]{1,0:T(8,128)(2,1)}, u32[]{:S(2)}, u32[]{:S(2)}) collective-permute-start(bf16[256,11008]{1,0:T(8,128)(2,1)} %collective-permute-done.13.refs_2_), channel_id=1, source_target_pairs={{0,8},{8,0},{16,24},{24,16},{1,9},{9,1},{17,25},{25,17},{2,10},{10... | collective-permute-start | bytes 16908296 | tf_op jit(solution)/shard_map/ppermute | solution.py:42
  729.9 287.0 %copy-start.12 = (s32[2,1,4096]{2,1,0:T(1,128)}, s32[2,1,4096]{2,1,0:T(1,128)S(1)}, u32[]{:S(2)}) copy-start(s32[2,1,4096]{2,1,0:T(1,128)S(1)} %get-tuple-element.290.lo_ref) | copy-start | bytes 98308
  730.0 58.7 %collective-permute-start.17 = (bf16[256,7552]{1,0:T(8,128)(2,1)}, bf16[256,7552]{1,0:T(8,128)(2,1)}, u32[]{:S(2)}, u32[]{:S(2)}) collective-permute-start(bf16[256,7552]{1,0:T(8,128)(2,1)} %collective-permute-done.11.refs_2_), channel_id=1, source_target_pairs={{0,8},{8,0},{16,24},{24,16},{1,9},{9,1},{17,25},{25,17},{2,10},{10... | collective-permute-start | bytes 11599880 | tf_op jit(solution)/shard_map/ppermute | solution.py:42
  777.5 67.4 %all-to-all-start.1 = ((bf16[8,2,512,128]{3,2,1,0:T(8,128)(2,1)}), bf16[8,2,512,128]{3,2,1,0:T(8,128)(2,1)}, u32[]{:S(2)}, u32[]{:S(2)}) async-start(bf16[8,2,512,128]{3,2,1,0:T(8,128)(2,1)} %get-tuple-element.89.o_ref), calls=%async_computation.1 | async-start | bytes 4194304 | tf_op jit(solution)/shard_map/all_to_all | solution.py:442
  873.4 143.6 %all-to-all-start.2 = ((bf16[8,2,512,384]{3,2,1,0:T(8,128)(2,1)}), bf16[8,2,512,384]{3,2,1,0:T(8,128)(2,1)}, u32[]{:S(2)}, u32[]{:S(2)}) async-start(bf16[8,2,512,384]{3,2,1,0:T(8,128)(2,1)} %bitcast.352), calls=%async_computation.2 | async-start | bytes 12582912 | tf_op jit(solution)/shard_map/all_to_all | solution.py:438
  1063.9 55.9 %all-to-all-start.3 = ((bf16[8,2,512,128]{3,2,1,0:T(8,128)(2,1)}), bf16[8,2,512,128]{3,2,1,0:T(8,128)(2,1)S(1)}, u32[]{:S(2)}, u32[]{:S(2)}) async-start(bf16[8,2,512,128]{3,2,1,0:T(8,128)(2,1)} %get-tuple-element.99.o_ref), calls=%async_computation.3 | async-start | bytes 4194304 | tf_op jit(solution)/shard_map/all_to_all | solution.py:442
  1121.1 80.0 %all-to-all-start.4 = ((bf16[8,2,512,128]{3,2,1,0:T(8,128)(2,1)}), bf16[8,2,512,128]{3,2,1,0:T(8,128)(2,1)S(1)}, u32[]{:S(2)}, u32[]{:S(2)}) async-start(bf16[8,2,512,128]{3,2,1,0:T(8,128)(2,1)} %bitcast.381), calls=%async_computation.4 | async-start | bytes 4194304 | tf_op jit(solution)/shard_map/all_to_all | solution.py:438
  1242.3 87.9 %collective-permute-start.23 = (bf16[2752,2048]{1,0:T(8,128)(2,1)}, bf16[2752,2048]{1,0:T(8,128)(2,1)}, u32[]{:S(2)}, u32[]{:S(2)}) collective-permute-start(bf16[2752,2048]{1,0:T(8,128)(2,1)} %bitcast.47), channel_id=1, source_target_pairs={{0,8},{8,0},{16,24},{24,16},{1,9},{9,1},{17,25},{25,17},{2,10},{10... | collective-permute-start | bytes 33816584 | tf_op jit(solution)/shard_map/ppermute | solution.py:42
  1276.4 77.6 %all-to-all-start.5 = ((bf16[8,1,512,384]{3,2,1,0:T(8,128)(2,1)}), bf16[8,1,512,384]{3,2,1,0:T(8,128)(2,1)}, u32[]{:S(2)}, u32[]{:S(2)}) async-start(bf16[8,1,512,384]{3,2,1,0:T(8,128)(2,1)} %copy-done.3), calls=%async_computation.5 | async-start | bytes 6291456 | tf_op jit(solution)/shard_map/all_to_all | solution.py:442
  1398.1 76.1 %collective-permute-start.24 = (bf16[1024,5504]{1,0:T(8,128)(2,1)}, bf16[1024,5504]{1,0:T(8,128)(2,1)}, u32[]{:S(2)}, u32[]{:S(2)}) collective-permute-start(bf16[1024,5504]{1,0:T(8,128)(2,1)} %convolution_convert_fusion.2), channel_id=1, source_target_pairs={{0,8},{8,0},{16,24},{24,16},{1,9},{9,1},{17,25},{25,17},{2,10},{10... | collective-permute-start | bytes 33816584 | tf_op jit(solution)/shard_map/ppermute | solution.py:42
  1398.1 76.1 %all-to-all-start.6 = ((bf16[8,1,512,384]{3,2,1,0:T(8,128)(2,1)}), bf16[8,1,512,384]{3,2,1,0:T(8,128)(2,1)}, u32[]{:S(2)}, u32[]{:S(2)}) async-start(bf16[8,1,512,384]{3,2,1,0:T(8,128)(2,1)} %attend_back.5), calls=%async_computation.6 | async-start | bytes 6291456 | tf_op jit(solution)/shard_map/all_to_all | solution.py:442
  1440.9 105.6 %collective-permute-start.25 = (bf16[1024,5504]{1,0:T(8,128)(2,1)}, bf16[1024,5504]{1,0:T(8,128)(2,1)}, u32[]{:S(2)}, u32[]{:S(2)}) collective-permute-start(bf16[1024,5504]{1,0:T(8,128)(2,1)} %convolution_convert_fusion.1), channel_id=1, source_target_pairs={{0,8},{8,0},{16,24},{24,16},{1,9},{9,1},{17,25},{25,17},{2,10},{10... | collective-permute-start | bytes 33816584 | tf_op jit(solution)/shard_map/ppermute | solution.py:42
  1441.4 126.5 %collective-permute-start.26 = (bf16[1376,2048]{1,0:T(8,128)(2,1)}, bf16[1376,2048]{1,0:T(8,128)(2,1)}, u32[]{:S(2)}, u32[]{:S(2)}) collective-permute-start(bf16[1376,2048]{1,0:T(8,128)(2,1)} %fusion.2), channel_id=1, source_target_pairs={{0,16},{8,24},{16,0},{24,8},{1,17},{9,25},{17,1},{25,9},{2,18},{10... | collective-permute-start | bytes 16908296 | tf_op jit(solution)/shard_map/ppermute | solution.py:42
  1486.0 239.8 %collective-permute-start.27 = (bf16[512,5504]{1,0:T(8,128)(2,1)}, bf16[512,5504]{1,0:T(8,128)(2,1)}, u32[]{:S(2)}, u32[]{:S(2)}) collective-permute-start(bf16[512,5504]{1,0:T(8,128)(2,1)} %add_convert_fusion.3), channel_id=1, source_target_pairs={{0,1},{1,0},{2,3},{3,2},{4,5},{5,4},{6,7},{7,6},{8,9},{9,8},{10,11... | collective-permute-start | bytes 16908296 | tf_op jit(solution)/shard_map/ppermute | solution.py:42
  1539.2 92.7 %all-to-all-start.7 = ((bf16[8,2,512,128]{3,2,1,0:T(8,128)(2,1)}), bf16[8,2,512,128]{3,2,1,0:T(8,128)(2,1)S(1)}, u32[]{:S(2)}, u32[]{:S(2)}) async-start(bf16[8,2,512,128]{3,2,1,0:T(8,128)(2,1)} %bitcast.379), calls=%async_computation.7 | async-start | bytes 4194304 | tf_op jit(solution)/shard_map/all_to_all | solution.py:438
  1565.9 195.6 %collective-permute-start.28 = (bf16[1024,2048]{1,0:T(8,128)(2,1)}, bf16[1024,2048]{1,0:T(8,128)(2,1)}, u32[]{:S(2)}, u32[]{:S(2)}) collective-permute-start(bf16[1024,2048]{1,0:T(8,128)(2,1)} %convolution_convert_fusion.7), channel_id=1, source_target_pairs={{0,8},{8,0},{16,24},{24,16},{1,9},{9,1},{17,25},{25,17},{2,10},{10... | collective-permute-start | bytes 12582920 | tf_op jit(solution)/shard_map/ppermute | solution.py:42
  1565.9 253.0 %collective-permute-start.29 = (bf16[512,5504]{1,0:T(8,128)(2,1)}, bf16[512,5504]{1,0:T(8,128)(2,1)}, u32[]{:S(2)}, u32[]{:S(2)}) collective-permute-start(bf16[512,5504]{1,0:T(8,128)(2,1)} %add_convert_fusion.2), channel_id=1, source_target_pairs={{0,16},{8,24},{16,0},{24,8},{1,17},{9,25},{17,1},{25,9},{2,18},{10... | collective-permute-start | bytes 16908296 | tf_op jit(solution)/shard_map/ppermute | solution.py:42
  1665.6 139.3 %all-to-all-start.8 = ((bf16[8,1,512,384]{3,2,1,0:T(8,128)(2,1)}), bf16[8,1,512,384]{3,2,1,0:T(8,128)(2,1)}, u32[]{:S(2)}, u32[]{:S(2)}) async-start(bf16[8,1,512,384]{3,2,1,0:T(8,128)(2,1)} %copy-done.2), calls=%async_computation.8 | async-start | bytes 6291456 | tf_op jit(solution)/shard_map/all_to_all | solution.py:442
  1715.1 69.2 %collective-permute-start.31 = (bf16[4,172,2048]{2,0,1:T(4,128)(2,1)}, bf16[4,172,2048]{2,0,1:T(4,128)(2,1)}, u32[]{:S(2)}, u32[]{:S(2)}) collective-permute-start(bf16[4,172,2048]{2,0,1:T(4,128)(2,1)} %copy.160), channel_id=1, source_target_pairs={{0,1},{1,0},{2,3},{3,2},{4,5},{5,4},{6,7},{7,6},{8,9},{9,8},{10,11... | collective-permute-start | bytes 8454152 | tf_op jit(solution)/shard_map/ppermute | solution.py:42
  1735.7 64.3 %collective-permute-start.32 = (bf16[256,5504]{1,0:T(8,128)(2,1)}, bf16[256,5504]{1,0:T(8,128)(2,1)}, u32[]{:S(2)}, u32[]{:S(2)}) collective-permute-start(bf16[256,5504]{1,0:T(8,128)(2,1)} %dynamic-slice_bitcast_fusion.3), channel_id=1, source_target_pairs={{0,16},{8,24},{16,0},{24,8},{1,17},{9,25},{17,1},{25,9},{2,18},{10... | collective-permute-start | bytes 8454152 | tf_op jit(solution)/shard_map/ppermute | solution.py:42
  1768.5 74.5 %collective-permute-start.30 = (bf16[512,2048]{1,0:T(8,128)(2,1)}, bf16[512,2048]{1,0:T(8,128)(2,1)}, u32[]{:S(2)}, u32[]{:S(2)}) collective-permute-start(bf16[512,2048]{1,0:T(8,128)(2,1)} %add_convert_fusion.11), channel_id=1, source_target_pairs={{0,16},{8,24},{16,0},{24,8},{1,17},{9,25},{17,1},{25,9},{2,18},{10... | collective-permute-start | bytes 6291464 | tf_op jit(solution)/shard_map/ppermute | solution.py:42
  1804.9 134.9 %all-to-all-start.9 = ((bf16[8,1,512,384]{3,2,1,0:T(8,128)(2,1)}), bf16[8,1,512,384]{3,2,1,0:T(8,128)(2,1)}, u32[]{:S(2)}, u32[]{:S(2)}) async-start(bf16[8,1,512,384]{3,2,1,0:T(8,128)(2,1)} %attend_back.7), calls=%async_computation.9 | async-start | bytes 6291456 | tf_op jit(solution)/shard_map/all_to_all | solution.py:442
  1847.5 43.8 %collective-permute-start.34 = (bf16[4,64,2048]{2,1,0:T(8,128)(2,1)}, bf16[4,64,2048]{2,1,0:T(8,128)(2,1)}, u32[]{:S(2)}, u32[]{:S(2)}) collective-permute-start(bf16[4,64,2048]{2,1,0:T(8,128)(2,1)} %dynamic-slice_bitcast_fusion.7), channel_id=1, source_target_pairs={{0,1},{1,0},{2,3},{3,2},{4,5},{5,4},{6,7},{7,6},{8,9},{9,8},{10,11... | collective-permute-start | bytes 3145736 | tf_op jit(solution)/shard_map/ppermute | solution.py:42
  1849.7 86.0 %collective-permute-start.33 = (bf16[4,64,5504]{2,1,0:T(8,128)(2,1)}, bf16[4,64,5504]{2,1,0:T(8,128)(2,1)}, u32[]{:S(2)}, u32[]{:S(2)}) collective-permute-start(bf16[4,64,5504]{2,1,0:T(8,128)(2,1)} %dynamic-slice_bitcast_fusion.2), channel_id=1, source_target_pairs={{0,1},{1,0},{2,3},{3,2},{4,5},{5,4},{6,7},{7,6},{8,9},{9,8},{10,11... | collective-permute-start | bytes 8454152 | tf_op jit(solution)/shard_map/ppermute | solution.py:42
  1966.1 63.7 %collective-permute-start.35 = (bf16[1024,3072]{1,0:T(8,128)(2,1)}, bf16[1024,3072]{1,0:T(8,128)(2,1)}, u32[]{:S(2)}, u32[]{:S(2)}) collective-permute-start(bf16[1024,3072]{1,0:T(8,128)(2,1)} %convolution_convert_fusion.6), channel_id=1, source_target_pairs={{0,8},{8,0},{16,24},{24,16},{1,9},{9,1},{17,25},{25,17},{2,10},{10... | collective-permute-start | bytes 18874376 | tf_op jit(solution)/shard_map/ppermute | solution.py:42
  1977.0 61.6 %collective-permute-start.36 = (bf16[1024,3072]{1,0:T(8,128)(2,1)}, bf16[1024,3072]{1,0:T(8,128)(2,1)}, u32[]{:S(2)}, u32[]{:S(2)}) collective-permute-start(bf16[1024,3072]{1,0:T(8,128)(2,1)} %convolution_convert_fusion.5), channel_id=1, source_target_pairs={{0,8},{8,0},{16,24},{24,16},{1,9},{9,1},{17,25},{25,17},{2,10},{10... | collective-permute-start | bytes 18874376 | tf_op jit(solution)/shard_map/ppermute | solution.py:42
  2021.6 111.2 %collective-permute-start.37 = (bf16[2,64,18560]{2,1,0:T(8,128)(2,1)}, bf16[2,64,18560]{2,1,0:T(8,128)(2,1)}, u32[]{:S(2)}, u32[]{:S(2)}) collective-permute-start(bf16[2,64,18560]{2,1,0:T(8,128)(2,1)} %dynamic-slice_bitcast_fusion), channel_id=1, source_target_pairs={{0,2},{1,3},{2,0},{3,1},{4,6},{5,7},{6,4},{7,5},{8,10},{9,11},{10,... | collective-permute-start | bytes 14254088 | tf_op jit(solution)/shard_map/ppermute | solution.py:42
  2037.4 122.0 %collective-permute-start.38 = (bf16[512,3072]{1,0:T(8,128)(2,1)}, bf16[512,3072]{1,0:T(8,128)(2,1)}, u32[]{:S(2)}, u32[]{:S(2)}) collective-permute-start(bf16[512,3072]{1,0:T(8,128)(2,1)} %add_convert_fusion.7), channel_id=1, source_target_pairs={{0,16},{8,24},{16,0},{24,8},{1,17},{9,25},{17,1},{25,9},{2,18},{10... | collective-permute-start | bytes 9437192 | tf_op jit(solution)/shard_map/ppermute | solution.py:42
  2047.0 127.2 %collective-permute-start.39 = (bf16[512,3072]{1,0:T(8,128)(2,1)}, bf16[512,3072]{1,0:T(8,128)(2,1)}, u32[]{:S(2)}, u32[]{:S(2)}) collective-permute-start(bf16[512,3072]{1,0:T(8,128)(2,1)} %add_convert_fusion.6), channel_id=1, source_target_pairs={{0,1},{1,0},{2,3},{3,2},{4,5},{5,4},{6,7},{7,6},{8,9},{9,8},{10,11... | collective-permute-start | bytes 9437192 | tf_op jit(solution)/shard_map/ppermute | solution.py:42
  2067.8 78.8 %collective-permute-start.45 = (f32[2,2,2,2,2,64]{5,4,3,2,1,0:T(2,128)S(1)}, f32[2,2,2,2,2,64]{5,4,3,2,1,0:T(2,128)S(1)}, u32[]{:S(2)}, u32[]{:S(2)}) collective-permute-start(f32[2,2,2,2,2,64]{5,4,3,2,1,0:T(2,128)S(1)} %dynamic-slice_bitcast_fusion.8), channel_id=1, source_target_pairs={{0,8},{8,0},{16,24},{24,16},{1,9},{9,1},{17,25},{25,17},{2,10},{10... | collective-permute-start | bytes 24584 | tf_op jit(solution)/shard_map/ppermute | solution.py:42
  2146.7 8.6 collective-permute-start.46
  2155.3 4.1 collective-permute-start.47
  2159.4 104.9 %collective-permute-start.44 = (bf16[1,64,18560]{2,1,0:T(8,128)(2,1)}, bf16[1,64,18560]{2,1,0:T(8,128)(2,1)S(1)}, u32[]{:S(2)}, u32[]{:S(2)}) collective-permute-start(bf16[1,64,18560]{2,1,0:T(8,128)(2,1)} %constant_dynamic-slice_fusion.8), channel_id=1, source_target_pairs={{0,4},{1,5},{2,6},{3,7},{4,0},{5,1},{6,2},{7,3},{8,12},{9,13},{10,... | collective-permute-start | bytes 7127048 | tf_op jit(solution)/shard_map/ppermute | solution.py:42
  2180.4 84.7 %collective-permute-start.40 = (bf16[4,64,3072]{2,1,0:T(8,128)(2,1)S(1)}, bf16[4,64,3072]{2,1,0:T(8,128)(2,1)S(1)}, u32[]{:S(2)}, u32[]{:S(2)}) collective-permute-start(bf16[4,64,3072]{2,1,0:T(8,128)(2,1)S(1)} %dynamic-slice_bitcast_fusion.6), channel_id=1, source_target_pairs={{0,1},{1,0},{2,3},{3,2},{4,5},{5,4},{6,7},{7,6},{8,9},{9,8},{10,11... | collective-permute-start | bytes 4718600 | tf_op jit(solution)/shard_map/ppermute | solution.py:42
  2182.6 83.1 %collective-permute-start.41 = (bf16[256,3072]{1,0:T(8,128)(2,1)S(1)}, bf16[256,3072]{1,0:T(8,128)(2,1)S(1)}, u32[]{:S(2)}, u32[]{:S(2)}) collective-permute-start(bf16[256,3072]{1,0:T(8,128)(2,1)S(1)} %dynamic-slice_bitcast_fusion.5), channel_id=1, source_target_pairs={{0,16},{8,24},{16,0},{24,8},{1,17},{9,25},{17,1},{25,9},{2,18},{10... | collective-permute-start | bytes 4718600 | tf_op jit(solution)/shard_map/ppermute | solution.py:42
  2266.6 35.5 %collective-permute-start.42 = (bf16[2,64,6144]{2,1,0:T(8,128)(2,1)S(1)}, bf16[2,64,6144]{2,1,0:T(8,128)(2,1)S(1)}, u32[]{:S(2)}, u32[]{:S(2)}) collective-permute-start(bf16[2,64,6144]{2,1,0:T(8,128)(2,1)S(1)} %dynamic-slice_bitcast_fusion.4), channel_id=1, source_target_pairs={{0,2},{1,3},{2,0},{3,1},{4,6},{5,7},{6,4},{7,5},{8,10},{9,11},{10,... | collective-permute-start | bytes 4718600 | tf_op jit(solution)/shard_map/ppermute | solution.py:42
  2266.8 35.4 %collective-permute-start.48 = (f32[2,2,64]{2,0,1:T(2,128)S(1)}, f32[2,2,64]{2,0,1:T(2,128)S(1)}, u32[]{:S(2)}, u32[]{:S(2)}) collective-permute-start(f32[2,2,64]{2,0,1:T(2,128)S(1)} %bitcast.456), channel_id=1, source_target_pairs={{0,2},{1,3},{2,0},{3,1},{4,6},{5,7},{6,4},{7,5},{8,10},{9,11},{10,... | collective-permute-start | bytes 3080 | tf_op jit(solution)/shard_map/ppermute | solution.py:42
  2302.6 6.2 collective-permute-start.49
  2304.4 36.7 %collective-permute-start.43 = (bf16[1,64,6144]{2,1,0:T(8,128)(2,1)}, bf16[1,64,6144]{2,1,0:T(8,128)(2,1)}, u32[]{:S(2)}, u32[]{:S(2)}) collective-permute-start(bf16[1,64,6144]{2,1,0:T(8,128)(2,1)} %constant_dynamic-slice_fusion.9), channel_id=1, source_target_pairs={{0,4},{1,5},{2,6},{3,7},{4,0},{5,1},{6,2},{7,3},{8,12},{9,13},{10,... | collective-permute-start | bytes 2359304 | tf_op jit(solution)/shard_map/ppermute | solution.py:42
  (95 other events, 1842.6 us)
Sparse Core Ops, SparseCore 0:
  11.6 250.1 all-gather.1

commit v8 on v7

--- a/solution.py
+++ b/solution.py
@@ -632,6 +632,7 @@
         mark = (layer_outs[-1],)
     mark = mark + tuple(rows_grad[-1]) + tuple(r.total for r in early)
     first = Finish(early, *mark)
+    mark = mark + (first.total,)
     h_sides = [pieces_of(h_kept, False), pieces_of(h_kept, True)]
     for g in range(groups - 1):
         grad_qkv.append(rows_of(jnp.concatenate(rows_grad[g], axis=1), micros))
@@ -642,11 +643,12 @@
     late = [Reduce(h_sides[0], all_qkv[:, :half], False), Reduce(h_sides[1], all_qkv[:, half:], True)]
     for r in late:
         mark = (r.cross(*mark),)
-    for g in range(groups - 1):
-        mark = (finish_tokens(g, *mark),)
     for r in late:
         mark = (r.send(*mark),)
     first.step(0, hold=mark)
+    mark = mark + (first.total,)
+    for g in range(groups - 1):
+        mark = (finish_tokens(g, *mark),)
     g = groups - 1
     grad_h_attn = nt(after(last_rows, *mark), full_qkv)
     grad_norm, gain_part = norm_backward(grad_h_attn, of(x, g), of(scale_a, g), gain_a)

time: 2360 us -> 2380 us (level)
  transfers between devices with their start and end apart: 61 -> 61, of which waited for: 24 -> 24; matrix products, arithmetic and copies ran while one was open for 30% -> 30% of each run, Pallas kernels for 10% -> 9%
where the time goes in v8:
time: 2380 us; the launch traced here: 2370 us
  waiting for transfers between devices  1050 us (44%)
  matrix products  554 us (23%)
  Pallas kernels  271 us (11%)
  local copies, waits for them, and re-layouts  214 us (9%)
  other arithmetic  163 us (7%)
  starting transfers between devices  109 us (5%)
    ppermute x50, waiting for transfers between devices, swap(): lax.ppermute(block, axis, [(i, i ^ stride) for i in range(lax.axis_size(a...  929 us
    dot_general x10, matrix products, nt(): return jnp.einsum('re,de->rd', a, b, preferred_element_type=f32)  186 us
    dot_general x16, matrix products, tn(): lax.dot_general(a, b, (((0,), (0,)), ((), ())), preferred_element_type=f32)  183 us
    pallas_call x4, Pallas kernels, attend_back(): pl.pallas_call(functools.partial(backward_kernel, pair), grid_spec=pltpu....  131 us
    pallas_call x2, Pallas kernels, attend(): pl.pallas_call(forward_kernel, grid_spec=pltpu.PrefetchScalarGridSpec(num...  93.8 us
    all_to_all x4, waiting for transfers between devices, to_heads(): return lax.all_to_all(split, 'seq', 0, 0, tiled=True)  72.7 us
    ppermute x50, starting transfers between devices, swap(): lax.ppermute(block, axis, [(i, i ^ stride) for i in range(lax.axis_size(a...  57.9 us
    dot_general x2, matrix products, shards(): up = jnp.dot(after(h_mlp, *mark), full_up, preferred_element_type=f32)  50.7 us
  transfers between devices with their start and end apart: 61, of which 24 were waited for; matrix products, arithmetic and copies ran while one was open for 30% of the time, Pallas kernels for 9%

profile of v8, /device:TPU:0, one launch (start us, length us, event | category | flops | bytes accessed | tf_op | source)
XLA Modules:
  0.0 2372.2 jit_solution(361645783601059193)
XLA Ops:
  36.2 9.3 copy.145
  55.1 72.0 %collective-permute-done.5 = bf16[64,7552]{1,0:T(8,128)(2,1)S(1)} collective-permute-done((bf16[64,7552]{1,0:T(8,128)(2,1)S(1)}, bf16[64,7552]{1,0:T(8,128)(2,1)S(1)}, u32[]{:S(2)}, u32[]{:S(2)}) %collective-permute-start.5) | collective-permute-done | bytes 966688 | tf_op jit(solution)/shard_map/ppermute | solution.py:42
  129.4 121.8 %collective-permute-done.6 = bf16[64,11008]{1,0:T(8,128)(2,1)S(1)} collective-permute-done((bf16[64,11008]{1,0:T(8,128)(2,1)S(1)}, bf16[64,11008]{1,0:T(8,128)(2,1)S(1)}, u32[]{:S(2)}, u32[]{:S(2)}) %collective-permute-start.6) | collective-permute-done | bytes 1409056 | tf_op jit(solution)/shard_map/ppermute | solution.py:42
  251.2 16.3 collective-permute-done.7
  268.4 62.2 %collective-permute-done.8 = bf16[128,11008]{1,0:T(8,128)(2,1)S(1)} collective-permute-done((bf16[128,11008]{1,0:T(8,128)(2,1)S(1)}, bf16[128,11008]{1,0:T(8,128)(2,1)S(1)}, u32[]{:S(2)}, u32[]{:S(2)}) %collective-permute-start.8) | collective-permute-done | bytes 2818080 | tf_op jit(solution)/shard_map/ppermute | solution.py:42
  336.1 82.7 %collective-permute-done.10.refs_1_ = bf16[256,7552]{1,0:T(8,128)(2,1)S(1)} collective-permute-done((bf16[256,7552]{1,0:T(8,128)(2,1)S(1)}, bf16[256,7552]{1,0:T(8,128)(2,1)S(1)}, u32[]{:S(2)}, u32[]{:S(2)}) %collective-permute-start.10) | collective-permute-done | bytes 3866656 | tf_op jit(solution)/shard_map/ppermute | solution.py:42
  420.7 34.9 %collective-permute-done.9.refs_1_ = bf16[256,11008]{1,0:T(8,128)(2,1)} collective-permute-done((bf16[256,11008]{1,0:T(8,128)(2,1)S(1)}, bf16[256,11008]{1,0:T(8,128)(2,1)}, u32[]{:S(2)}, u32[]{:S(2)}) %collective-permute-start.9) | collective-permute-done | bytes 5636128 | tf_op jit(solution)/shard_map/ppermute | solution.py:42
  455.6 19.0 convolution_convert_fusion.4
  489.3 149.0 %collective-permute-done.12.refs_3_ = bf16[256,7552]{1,0:T(8,128)(2,1)} collective-permute-done((bf16[256,7552]{1,0:T(8,128)(2,1)}, bf16[256,7552]{1,0:T(8,128)(2,1)}, u32[]{:S(2)}, u32[]{:S(2)}) %collective-permute-start.12) | collective-permute-done | bytes 3866656 | tf_op jit(solution)/shard_map/ppermute | solution.py:42
  638.3 80.8 %collective-permute-done.11.refs_2_ = bf16[256,7552]{1,0:T(8,128)(2,1)} collective-permute-done((bf16[256,7552]{1,0:T(8,128)(2,1)}, bf16[256,7552]{1,0:T(8,128)(2,1)}, u32[]{:S(2)}, u32[]{:S(2)}) %collective-permute-start.11) | collective-permute-done | bytes 3866656 | tf_op jit(solution)/shard_map/ppermute | solution.py:42
  730.6 46.9 %attend.2 = (bf16[8,2,512,128]{3,2,1,0:T(8,128)(2,1)}, f32[2,1,4096]{2,1,0:T(1,128)S(1)}) custom-call(s32[2,4,8]{2,1,0:T(4,128)S(1)} %pad_add_fusion.2.bounds, bf16[8,2,512,384]{3,2,1,0:T(8,128)(2,1)} %all-to-all-done.q_ref.k_ref.v_ref, bf16[8,2,512,384]{3,2,1,0:T(8,128)(2,1)} %all-to-all-done.q_ref.k_ref.v_ref, ...), custom_call_target="tpu_custom_call" | custom-call | flops 1024 | bytes 1024 | tf_op jit(solution)/shard_map/attend/pallas_call | solution.py:314
  795.0 17.0 place.2
  815.4 29.4 %place.3 = (bf16[2048,5504]{1,0:T(8,128)(2,1)}, bf16[2048,5504]{1,0:T(8,128)(2,1)}) custom-call(s32[32]{0:T(128)S(1)} %xor_multiply_fusion.target, bf16[256,11008]{1,0:T(8,128)(2,1)S(1)} %bitcast.340, bf16[256,11008]{1,0:T(8,128)(2,1)} %collective-permute-done.9.refs_1_, bf16[256,11008]{1,0:T(8,128)(2,1)} %collective-permute-done.13.refs_2_, ...), custom_call_target="tpu_custom_call" | custom-call | flops 1024 | bytes 1024 | tf_op jit(solution)/shard_map/place/pallas_call | solution.py:149
  848.8 18.8 convolution_convert_fusion.3
  879.5 10.3 multiply_reduce_fusion.10
  893.5 19.0 fusion.120
  912.5 25.3 %multiply_convert_fusion.5 = (bf16[512,5504]{1,0:T(8,128)(2,1)}, f32[512,5504]{1,0:T(8,128)}) fusion(f32[512,5504]{1,0:T(8,128)} %fusion.120, bf16[512,2048]{1,0:T(8,128)(2,1)} %copy-done.37, bf16[2048,5504]{1,0:T(8,128)(2,1)} %get-tuple-element.92), kind=kOutput, calls=%fused_computation.24 | convolution fusion | flops 11559632896 | bytes 52822016 | tf_op jit(solution)/shard_map/dot_general | solution.py:558
  937.8 31.1 %reshape.453 = bf16[5504,2048]{1,0:T(8,128)(2,1)} reshape(bf16[2048,5504]{1,0:T(8,128)(2,1)} %get-tuple-element.97) | data formatting | bytes 45088768 | tf_op jit(solution)/shard_map/reshape | solution.py:564
  968.9 25.1 %multiply_convert_fusion.3 = (bf16[512,5504]{1,0:T(8,128)(2,1)}, bf16[512,5504]{1,0:T(8,128)(2,1)}) fusion(f32[512,5504]{1,0:T(8,128)} %fusion.120, f32[512,5504]{1,0:T(8,128)} %get-tuple-element.276, bf16[512,2048]{1,0:T(8,128)(2,1)} %get-tuple-element.96, bf16[5504,2048]{1,0:T(8,128)(2,1)} %reshape.453), kind=kOutput, calls=%fused_computation.22 | convolution fusion | flops 11579359232 | bytes 58458112 | tf_op jit(solution)/shard_map/re,de->rd/dot_general | solution.py:463
  994.0 22.8 all-to-all-done.2.q_ref.k_ref.v_ref
  1016.9 46.9 %attend.3 = (bf16[8,2,512,128]{3,2,1,0:T(8,128)(2,1)}, f32[2,1,4096]{2,1,0:T(1,128)S(1)}) custom-call(s32[2,4,8]{2,1,0:T(4,128)S(1)} %pad_add_fusion.3.bounds, bf16[8,2,512,384]{3,2,1,0:T(8,128)(2,1)} %all-to-all-done.2.q_ref.k_ref.v_ref, bf16[8,2,512,384]{3,2,1,0:T(8,128)(2,1)} %all-to-all-done.2.q_ref.k_ref.v_ref, ...), custom_call_target="tpu_custom_call" | custom-call | flops 1024 | bytes 1024 | tf_op jit(solution)/shard_map/attend/pallas_call | solution.py:314
  1067.5 19.4 fusion.121
  1086.8 19.4 multiply_reduce_fusion.2
  1131.0 10.3 multiply_reduce_fusion.8
  1145.0 19.0 fusion.122
  1163.9 25.4 %multiply_convert_fusion.2 = (bf16[512,5504]{1,0:T(8,128)(2,1)}, f32[512,5504]{1,0:T(8,128)}) fusion(f32[512,5504]{1,0:T(8,128)} %fusion.122, bf16[512,2048]{1,0:T(8,128)(2,1)} %copy-done.39, bf16[2048,5504]{1,0:T(8,128)(2,1)} %get-tuple-element.92), kind=kOutput, calls=%fused_computation.19 | convolution fusion | flops 11559632896 | bytes 52822016 | tf_op jit(solution)/shard_map/dot_general | solution.py:558
  1189.3 11.6 pad_maximum_fusion
  1200.9 31.4 %convolution_convert_fusion = bf16[5504,2048]{1,0:T(8,128)(2,1)} fusion(bf16[1024,5504]{1,0:T(8,128)(2,1)} %pad_maximum_fusion, bf16[1024,2048]{1,0:T(8,128)(2,1)} %bitcast.348), kind=kOutput, calls=%fused_computation | convolution fusion | flops 23096721408 | bytes 38010880 | tf_op jit(solution)/shard_map/dot_general | solution.py:169
  1232.2 10.0 constant_dynamic-slice_fusion.10
  1242.2 32.4 %attend_back.4 = bf16[8,1,512,384]{3,2,1,0:T(8,128)(2,1)S(1)} custom-call(s32[2,4,8]{2,1,0:T(4,128)S(1)} %copy-done.19, bf16[8,2,512,384]{3,2,1,0:T(8,128)(2,1)} %all-to-all-done.q_ref.k_ref.v_ref, bf16[8,2,512,384]{3,2,1,0:T(8,128)(2,1)} %all-to-all-done.q_ref.k_ref.v_ref, bf16[8,2,512,384]{3,2,1,0:T(8,128)(2,1)} %all-to-all-done.q_ref.k_ref.v_ref, ...), custom_call_target="tpu_custom_call" | custom-call | flops 1024 | bytes 1024 | tf_op jit(solution)/shard_map/attend_back/pallas_call | solution.py:391
  1282.8 33.4 %attend_back.5 = bf16[8,1,512,384]{3,2,1,0:T(8,128)(2,1)} custom-call(s32[2,4,8]{2,1,0:T(4,128)S(1)} %copy-done.19, bf16[8,2,512,384]{3,2,1,0:T(8,128)(2,1)} %all-to-all-done.q_ref.k_ref.v_ref, bf16[8,2,512,384]{3,2,1,0:T(8,128)(2,1)} %all-to-all-done.q_ref.k_ref.v_ref, bf16[8,2,512,384]{3,2,1,0:T(8,128)(2,1)} %all-to-all-done.q_ref.k_ref.v_ref, ...), custom_call_target="tpu_custom_call" | custom-call | flops 1024 | bytes 1024 | tf_op jit(solution)/shard_map/attend_back/pallas_call | solution.py:391
  1330.1 10.1 fusion.2
  1340.2 13.7 all-to-all-done.5
  1353.9 24.5 %multiply_convert_fusion = (bf16[512,5504]{1,0:T(8,128)(2,1)}, bf16[512,5504]{1,0:T(8,128)(2,1)}) fusion(f32[512,5504]{1,0:T(8,128)} %fusion.122, f32[512,5504]{1,0:T(8,128)} %get-tuple-element.281, bf16[512,2048]{1,0:T(8,128)(2,1)S(1)} %copy-done.51, bf16[5504,2048]{1,0:T(8,128)(2,1)} %reshape.453), kind=kOutput, calls=%fused_computation.17 | convolution fusion | flops 11579359232 | bytes 58458112 | tf_op jit(solution)/shard_map/re,de->rd/dot_general | solution.py:463
  1378.3 19.4 convolution_convert_fusion.2
  1410.0 11.2 copy.152
  1421.2 19.3 convolution_convert_fusion.1
  1443.4 30.5 %all-to-all-done.6 = bf16[8,1,512,384]{3,2,1,0:T(8,128)(2,1)} async-done(((bf16[8,1,512,384]{3,2,1,0:T(8,128)(2,1)}), bf16[8,1,512,384]{3,2,1,0:T(8,128)(2,1)}, u32[]{:S(2)}, u32[]{:S(2)}) %all-to-all-start.6) | async-done | bytes 3145760 | tf_op jit(solution)/shard_map/all_to_all | solution.py:442
  1473.9 11.8 add_convert_fusion.3
  1487.1 19.4 fusion.123
  1506.5 19.4 multiply_reduce_fusion.1
  1527.9 8.9 convolution_convert_fusion.8
  1546.7 13.3 add_convert_fusion.2
  1568.4 13.1 fusion.1
  1581.5 49.9 %all-to-all-done.7.do_ref = bf16[8,2,512,128]{3,2,1,0:T(8,128)(2,1)S(1)} async-done(((bf16[8,2,512,128]{3,2,1,0:T(8,128)(2,1)}), bf16[8,2,512,128]{3,2,1,0:T(8,128)(2,1)S(1)}, u32[]{:S(2)}, u32[]{:S(2)}) %all-to-all-start.7) | async-done | bytes 2097184 | tf_op jit(solution)/shard_map/all_to_all | solution.py:438
  1631.4 32.1 %attend_back.6 = bf16[8,1,512,384]{3,2,1,0:T(8,128)(2,1)S(1)} custom-call(s32[2,4,8]{2,1,0:T(4,128)S(1)} %copy-done.17, bf16[8,2,512,384]{3,2,1,0:T(8,128)(2,1)} %all-to-all-done.2.q_ref.k_ref.v_ref, bf16[8,2,512,384]{3,2,1,0:T(8,128)(2,1)} %all-to-all-done.2.q_ref.k_ref.v_ref, bf16[8,2,512,384]{3,2,1,0:T(8,128)(2,1)} %all-to-all-done.2.q_ref.k_ref.v_ref, ...), custom_call_target="tpu_custom_call" | custom-call | flops 1024 | bytes 1024 | tf_op jit(solution)/shard_map/attend_back/pallas_call | solution.py:391
  1669.8 32.9 %attend_back.7 = bf16[8,1,512,384]{3,2,1,0:T(8,128)(2,1)} custom-call(s32[2,4,8]{2,1,0:T(4,128)S(1)} %copy-done.17, bf16[8,2,512,384]{3,2,1,0:T(8,128)(2,1)} %all-to-all-done.2.q_ref.k_ref.v_ref, bf16[8,2,512,384]{3,2,1,0:T(8,128)(2,1)} %all-to-all-done.2.q_ref.k_ref.v_ref, bf16[8,2,512,384]{3,2,1,0:T(8,128)(2,1)} %all-to-all-done.2.q_ref.k_ref.v_ref, ...), custom_call_target="tpu_custom_call" | custom-call | flops 1024 | bytes 1024 | tf_op jit(solution)/shard_map/attend_back/pallas_call | solution.py:391
  1751.5 9.1 copy.157
  1767.7 15.9 collective-permute-done.31
  1788.9 11.6 collective-permute-done.32
  1810.0 9.5 fusion.14
  1829.5 13.0 collective-permute-done.30
  1850.7 19.1 add_convert_fusion.9
  1869.9 19.3 add_convert_fusion.8
  1891.8 42.3 %collective-permute-done.33 = bf16[4,64,5504]{2,1,0:T(8,128)(2,1)} collective-permute-done((bf16[4,64,5504]{2,1,0:T(8,128)(2,1)}, bf16[4,64,5504]{2,1,0:T(8,128)(2,1)}, u32[]{:S(2)}, u32[]{:S(2)}) %collective-permute-start.33) | collective-permute-done | bytes 2818080 | tf_op jit(solution)/shard_map/ppermute | solution.py:42
  1966.1 11.4 convolution_convert_fusion.6
  1977.5 9.0 convolution_convert_fusion.5
  2014.0 9.5 add_convert_fusion.6
  2023.5 80.2 %collective-permute-done.37 = bf16[2,64,18560]{2,1,0:T(8,128)(2,1)} collective-permute-done((bf16[2,64,18560]{2,1,0:T(8,128)(2,1)}, bf16[2,64,18560]{2,1,0:T(8,128)(2,1)}, u32[]{:S(2)}, u32[]{:S(2)}) %collective-permute-start.37) | collective-permute-done | bytes 4751392 | tf_op jit(solution)/shard_map/ppermute | solution.py:42
  2109.4 20.4 multiply_reduce_fusion.4
  2136.2 20.2 multiply_reduce_fusion.3
  2204.3 79.6 %collective-permute-done.44 = bf16[1,64,18560]{2,1,0:T(8,128)(2,1)S(1)} collective-permute-done((bf16[1,64,18560]{2,1,0:T(8,128)(2,1)S(1)}, bf16[1,64,18560]{2,1,0:T(8,128)(2,1)S(1)}, u32[]{:S(2)}, u32[]{:S(2)}) %collective-permute-start.44) | collective-permute-done | bytes 2375712 | tf_op jit(solution)/shard_map/ppermute | solution.py:42
  2290.2 31.3 %collective-permute-done.48 = f32[2,2,64]{2,0,1:T(2,128)S(1)} collective-permute-done((f32[2,2,64]{2,0,1:T(2,128)S(1)}, f32[2,2,64]{2,0,1:T(2,128)S(1)}, u32[]{:S(2)}, u32[]{:S(2)}) %collective-permute-start.48) | collective-permute-done | bytes 1056 | tf_op jit(solution)/shard_map/ppermute | solution.py:42
  2328.6 31.6 %collective-permute-done.43 = bf16[1,64,6144]{2,1,0:T(8,128)(2,1)} collective-permute-done((bf16[1,64,6144]{2,1,0:T(8,128)(2,1)}, bf16[1,64,6144]{2,1,0:T(8,128)(2,1)}, u32[]{:S(2)}, u32[]{:S(2)}) %collective-permute-start.43) | collective-permute-done | bytes 786464 | tf_op jit(solution)/shard_map/ppermute | solution.py:42
  (465 shorter events, 441.2 us)
Async XLA Ops:
  7.2 448.4 %all-gather.2.cloned.1.call-start = ((), (), s32[]{:S(2)}) async-start(), calls=%async_computation.10 | async-start | bytes 25952256 | tf_op jit(solution)/shard_map/all_gather | solution.py:469
  10.6 4.5 collective-permute-start
  15.2 3.6 collective-permute-start.1
  18.9 4.6 collective-permute-start.2
  23.6 3.4 collective-permute-start.3
  27.0 19.4 collective-permute-start.4
  46.4 1094.9 %copy-start.54 = (f32[1,2048]{1,0:T(1,128)}, f32[1,2048]{1,0:T(1,128)S(1)}, u32[]{:S(2)}) copy-start(f32[1,2048]{1,0:T(1,128)S(1)} %get-tuple-element.251) | copy-start | bytes 24580
  52.8 74.4 %collective-permute-start.5 = (bf16[64,7552]{1,0:T(8,128)(2,1)S(1)}, bf16[64,7552]{1,0:T(8,128)(2,1)S(1)}, u32[]{:S(2)}, u32[]{:S(2)}) collective-permute-start(bf16[64,7552]{1,0:T(8,128)(2,1)S(1)} %pad_maximum_fusion.29), channel_id=1, source_target_pairs={{0,4},{1,5},{2,6},{3,7},{4,0},{5,1},{6,2},{7,3},{8,12},{9,13},{10,... | collective-permute-start | bytes 2899976 | tf_op jit(solution)/shard_map/ppermute | solution.py:42
  127.4 123.7 %collective-permute-start.6 = (bf16[64,11008]{1,0:T(8,128)(2,1)S(1)}, bf16[64,11008]{1,0:T(8,128)(2,1)S(1)}, u32[]{:S(2)}, u32[]{:S(2)}) collective-permute-start(bf16[64,11008]{1,0:T(8,128)(2,1)S(1)} %pad_maximum_fusion.23), channel_id=1, source_target_pairs={{0,4},{1,5},{2,6},{3,7},{4,0},{5,1},{6,2},{7,3},{8,12},{9,13},{10,... | collective-permute-start | bytes 4227080 | tf_op jit(solution)/shard_map/ppermute | solution.py:42
  127.5 140.1 %collective-permute-start.7 = (bf16[128,7552]{1,0:T(8,128)(2,1)S(1)}, bf16[128,7552]{1,0:T(8,128)(2,1)S(1)}, u32[]{:S(2)}, u32[]{:S(2)}) collective-permute-start(bf16[128,7552]{1,0:T(8,128)(2,1)S(1)} %get-tuple-element.246), channel_id=1, source_target_pairs={{0,2},{1,3},{2,0},{3,1},{4,6},{5,7},{6,4},{7,5},{8,10},{9,11},{10,... | collective-permute-start | bytes 5799944 | tf_op jit(solution)/shard_map/ppermute | solution.py:42
  267.8 62.8 %collective-permute-start.8 = (bf16[128,11008]{1,0:T(8,128)(2,1)S(1)}, bf16[128,11008]{1,0:T(8,128)(2,1)S(1)}, u32[]{:S(2)}, u32[]{:S(2)}) collective-permute-start(bf16[128,11008]{1,0:T(8,128)(2,1)S(1)} %constant_dynamic-update-slice_fusion.2), channel_id=1, source_target_pairs={{0,2},{1,3},{2,0},{3,1},{4,6},{5,7},{6,4},{7,5},{8,10},{9,11},{10,... | collective-permute-start | bytes 8454152 | tf_op jit(solution)/shard_map/ppermute | solution.py:42
  333.2 122.4 %collective-permute-start.9 = (bf16[256,11008]{1,0:T(8,128)(2,1)S(1)}, bf16[256,11008]{1,0:T(8,128)(2,1)}, u32[]{:S(2)}, u32[]{:S(2)}) collective-permute-start(bf16[256,11008]{1,0:T(8,128)(2,1)S(1)} %constant_dynamic-update-slice_fusion.7.refs_0_), channel_id=1, source_target_pairs={{0,1},{1,0},{2,3},{3,2},{4,5},{5,4},{6,7},{7,6},{8,9},{9,8},{10,11... | collective-permute-start | bytes 16908296 | tf_op jit(solution)/shard_map/ppermute | solution.py:42
  334.7 84.1 %collective-permute-start.10 = (bf16[256,7552]{1,0:T(8,128)(2,1)S(1)}, bf16[256,7552]{1,0:T(8,128)(2,1)S(1)}, u32[]{:S(2)}, u32[]{:S(2)}) collective-permute-start(bf16[256,7552]{1,0:T(8,128)(2,1)S(1)} %constant_dynamic-update-slice_fusion.4.refs_0_), channel_id=1, source_target_pairs={{0,16},{8,24},{16,0},{24,8},{1,17},{9,25},{17,1},{25,9},{2,18},{10... | collective-permute-start | bytes 11599880 | tf_op jit(solution)/shard_map/ppermute | solution.py:42
  480.3 238.8 %copy-start.60 = (s32[2,1,4096]{2,1,0:T(1,128)S(1)}, s32[2,1,4096]{2,1,0:T(1,128)}, u32[]{:S(2)}) copy-start(s32[2,1,4096]{2,1,0:T(1,128)} %param.12) | copy-start | bytes 98308
  480.3 250.2 %all-to-all-start = ((bf16[8,2,512,384]{3,2,1,0:T(8,128)(2,1)}), bf16[8,2,512,384]{3,2,1,0:T(8,128)(2,1)}, u32[]{:S(2)}, u32[]{:S(2)}) async-start(bf16[8,2,512,384]{3,2,1,0:T(8,128)(2,1)} %bitcast.351), calls=%async_computation | async-start | bytes 12582912 | tf_op jit(solution)/shard_map/all_to_all | solution.py:438
  485.2 153.1 %collective-permute-start.12 = (bf16[256,7552]{1,0:T(8,128)(2,1)}, bf16[256,7552]{1,0:T(8,128)(2,1)}, u32[]{:S(2)}, u32[]{:S(2)}) collective-permute-start(bf16[256,7552]{1,0:T(8,128)(2,1)} %copy-done.6), channel_id=1, source_target_pairs={{0,1},{1,0},{2,3},{3,2},{4,5},{5,4},{6,7},{7,6},{8,9},{9,8},{10,11... | collective-permute-start | bytes 11599880 | tf_op jit(solution)/shard_map/ppermute | solution.py:42
  487.1 232.0 %collective-permute-start.11 = (bf16[256,7552]{1,0:T(8,128)(2,1)}, bf16[256,7552]{1,0:T(8,128)(2,1)}, u32[]{:S(2)}, u32[]{:S(2)}) collective-permute-start(bf16[256,7552]{1,0:T(8,128)(2,1)} %copy-done.4), channel_id=1, source_target_pairs={{0,1},{1,0},{2,3},{3,2},{4,5},{5,4},{6,7},{7,6},{8,9},{9,8},{10,11... | collective-permute-start | bytes 11599880 | tf_op jit(solution)/shard_map/ppermute | solution.py:42
  487.3 240.8 %collective-permute-start.14 = (bf16[256,11008]{1,0:T(8,128)(2,1)}, bf16[256,11008]{1,0:T(8,128)(2,1)}, u32[]{:S(2)}, u32[]{:S(2)}) collective-permute-start(bf16[256,11008]{1,0:T(8,128)(2,1)} %collective-permute-done.9.refs_1_), channel_id=1, source_target_pairs={{0,16},{8,24},{16,0},{24,8},{1,17},{9,25},{17,1},{25,9},{2,18},{10... | collective-permute-start | bytes 16908296 | tf_op jit(solution)/shard_map/ppermute | solution.py:42
  488.7 240.5 %collective-permute-start.13 = (bf16[256,11008]{1,0:T(8,128)(2,1)}, bf16[256,11008]{1,0:T(8,128)(2,1)}, u32[]{:S(2)}, u32[]{:S(2)}) collective-permute-start(bf16[256,11008]{1,0:T(8,128)(2,1)} %copy-done.1), channel_id=1, source_target_pairs={{0,16},{8,24},{16,0},{24,8},{1,17},{9,25},{17,1},{25,9},{2,18},{10... | collective-permute-start | bytes 16908296 | tf_op jit(solution)/shard_map/ppermute | solution.py:42
  489.3 234.5 %collective-permute-start.16 = (bf16[256,7552]{1,0:T(8,128)(2,1)}, bf16[256,7552]{1,0:T(8,128)(2,1)S(1)}, u32[]{:S(2)}, u32[]{:S(2)}) collective-permute-start(bf16[256,7552]{1,0:T(8,128)(2,1)} %copy-done.6), channel_id=1, source_target_pairs={{0,8},{8,0},{16,24},{24,16},{1,9},{9,1},{17,25},{25,17},{2,10},{10... | collective-permute-start | bytes 11599880 | tf_op jit(solution)/shard_map/ppermute | solution.py:42
  638.3 88.0 %collective-permute-start.15 = (bf16[256,7552]{1,0:T(8,128)(2,1)}, bf16[256,7552]{1,0:T(8,128)(2,1)S(1)}, u32[]{:S(2)}, u32[]{:S(2)}) collective-permute-start(bf16[256,7552]{1,0:T(8,128)(2,1)} %copy-done.4), channel_id=1, source_target_pairs={{0,8},{8,0},{16,24},{24,16},{1,9},{9,1},{17,25},{25,17},{2,10},{10... | collective-permute-start | bytes 11599880 | tf_op jit(solution)/shard_map/ppermute | solution.py:42
  719.1 10.8 collective-permute-start.18
  725.7 89.6 %collective-permute-start.20 = (bf16[256,11008]{1,0:T(8,128)(2,1)}, bf16[256,11008]{1,0:T(8,128)(2,1)}, u32[]{:S(2)}, u32[]{:S(2)}) collective-permute-start(bf16[256,11008]{1,0:T(8,128)(2,1)} %collective-permute-done.9.refs_1_), channel_id=1, source_target_pairs={{0,8},{8,0},{16,24},{24,16},{1,9},{9,1},{17,25},{25,17},{2,10},{10... | collective-permute-start | bytes 16908296 | tf_op jit(solution)/shard_map/ppermute | solution.py:42
  728.1 87.2 %collective-permute-start.19 = (bf16[256,11008]{1,0:T(8,128)(2,1)}, bf16[256,11008]{1,0:T(8,128)(2,1)}, u32[]{:S(2)}, u32[]{:S(2)}) collective-permute-start(bf16[256,11008]{1,0:T(8,128)(2,1)} %copy-done.1), channel_id=1, source_target_pairs={{0,8},{8,0},{16,24},{24,16},{1,9},{9,1},{17,25},{25,17},{2,10},{10... | collective-permute-start | bytes 16908296 | tf_op jit(solution)/shard_map/ppermute | solution.py:42
  728.1 87.2 %collective-permute-start.22 = (bf16[256,11008]{1,0:T(8,128)(2,1)}, bf16[256,11008]{1,0:T(8,128)(2,1)}, u32[]{:S(2)}, u32[]{:S(2)}) collective-permute-start(bf16[256,11008]{1,0:T(8,128)(2,1)} %collective-permute-done.14.refs_3_), channel_id=1, source_target_pairs={{0,8},{8,0},{16,24},{24,16},{1,9},{9,1},{17,25},{25,17},{2,10},{10... | collective-permute-start | bytes 16908296 | tf_op jit(solution)/shard_map/ppermute | solution.py:42
  729.2 86.2 %collective-permute-start.21 = (bf16[256,11008]{1,0:T(8,128)(2,1)}, bf16[256,11008]{1,0:T(8,128)(2,1)}, u32[]{:S(2)}, u32[]{:S(2)}) collective-permute-start(bf16[256,11008]{1,0:T(8,128)(2,1)} %collective-permute-done.13.refs_2_), channel_id=1, source_target_pairs={{0,8},{8,0},{16,24},{24,16},{1,9},{9,1},{17,25},{25,17},{2,10},{10... | collective-permute-start | bytes 16908296 | tf_op jit(solution)/shard_map/ppermute | solution.py:42
  729.9 286.9 %copy-start.12 = (s32[2,1,4096]{2,1,0:T(1,128)}, s32[2,1,4096]{2,1,0:T(1,128)S(1)}, u32[]{:S(2)}) copy-start(s32[2,1,4096]{2,1,0:T(1,128)S(1)} %get-tuple-element.290.lo_ref) | copy-start | bytes 98308
  730.0 58.7 %collective-permute-start.17 = (bf16[256,7552]{1,0:T(8,128)(2,1)}, bf16[256,7552]{1,0:T(8,128)(2,1)}, u32[]{:S(2)}, u32[]{:S(2)}) collective-permute-start(bf16[256,7552]{1,0:T(8,128)(2,1)} %collective-permute-done.11.refs_2_), channel_id=1, source_target_pairs={{0,8},{8,0},{16,24},{24,16},{1,9},{9,1},{17,25},{25,17},{2,10},{10... | collective-permute-start | bytes 11599880 | tf_op jit(solution)/shard_map/ppermute | solution.py:42
  777.5 67.4 %all-to-all-start.1 = ((bf16[8,2,512,128]{3,2,1,0:T(8,128)(2,1)}), bf16[8,2,512,128]{3,2,1,0:T(8,128)(2,1)}, u32[]{:S(2)}, u32[]{:S(2)}) async-start(bf16[8,2,512,128]{3,2,1,0:T(8,128)(2,1)} %get-tuple-element.89.o_ref), calls=%async_computation.1 | async-start | bytes 4194304 | tf_op jit(solution)/shard_map/all_to_all | solution.py:442
  873.3 143.6 %all-to-all-start.2 = ((bf16[8,2,512,384]{3,2,1,0:T(8,128)(2,1)}), bf16[8,2,512,384]{3,2,1,0:T(8,128)(2,1)}, u32[]{:S(2)}, u32[]{:S(2)}) async-start(bf16[8,2,512,384]{3,2,1,0:T(8,128)(2,1)} %bitcast.352), calls=%async_computation.2 | async-start | bytes 12582912 | tf_op jit(solution)/shard_map/all_to_all | solution.py:438
  1063.8 55.8 %all-to-all-start.3 = ((bf16[8,2,512,128]{3,2,1,0:T(8,128)(2,1)}), bf16[8,2,512,128]{3,2,1,0:T(8,128)(2,1)S(1)}, u32[]{:S(2)}, u32[]{:S(2)}) async-start(bf16[8,2,512,128]{3,2,1,0:T(8,128)(2,1)} %get-tuple-element.99.o_ref), calls=%async_computation.3 | async-start | bytes 4194304 | tf_op jit(solution)/shard_map/all_to_all | solution.py:442
  1120.9 80.0 %all-to-all-start.4 = ((bf16[8,2,512,128]{3,2,1,0:T(8,128)(2,1)}), bf16[8,2,512,128]{3,2,1,0:T(8,128)(2,1)S(1)}, u32[]{:S(2)}, u32[]{:S(2)}) async-start(bf16[8,2,512,128]{3,2,1,0:T(8,128)(2,1)} %bitcast.383), calls=%async_computation.4 | async-start | bytes 4194304 | tf_op jit(solution)/shard_map/all_to_all | solution.py:438
  1242.2 87.9 %collective-permute-start.23 = (bf16[2752,2048]{1,0:T(8,128)(2,1)}, bf16[2752,2048]{1,0:T(8,128)(2,1)}, u32[]{:S(2)}, u32[]{:S(2)}) collective-permute-start(bf16[2752,2048]{1,0:T(8,128)(2,1)} %bitcast.47), channel_id=1, source_target_pairs={{0,8},{8,0},{16,24},{24,16},{1,9},{9,1},{17,25},{25,17},{2,10},{10... | collective-permute-start | bytes 33816584 | tf_op jit(solution)/shard_map/ppermute | solution.py:42
  1276.2 77.6 %all-to-all-start.5 = ((bf16[8,1,512,384]{3,2,1,0:T(8,128)(2,1)}), bf16[8,1,512,384]{3,2,1,0:T(8,128)(2,1)}, u32[]{:S(2)}, u32[]{:S(2)}) async-start(bf16[8,1,512,384]{3,2,1,0:T(8,128)(2,1)} %copy-done.3), calls=%async_computation.5 | async-start | bytes 6291456 | tf_op jit(solution)/shard_map/all_to_all | solution.py:442
  1397.8 76.1 %collective-permute-start.24 = (bf16[1024,5504]{1,0:T(8,128)(2,1)}, bf16[1024,5504]{1,0:T(8,128)(2,1)}, u32[]{:S(2)}, u32[]{:S(2)}) collective-permute-start(bf16[1024,5504]{1,0:T(8,128)(2,1)} %convolution_convert_fusion.2), channel_id=1, source_target_pairs={{0,8},{8,0},{16,24},{24,16},{1,9},{9,1},{17,25},{25,17},{2,10},{10... | collective-permute-start | bytes 33816584 | tf_op jit(solution)/shard_map/ppermute | solution.py:42
  1397.8 76.1 %all-to-all-start.6 = ((bf16[8,1,512,384]{3,2,1,0:T(8,128)(2,1)}), bf16[8,1,512,384]{3,2,1,0:T(8,128)(2,1)}, u32[]{:S(2)}, u32[]{:S(2)}) async-start(bf16[8,1,512,384]{3,2,1,0:T(8,128)(2,1)} %attend_back.5), calls=%async_computation.6 | async-start | bytes 6291456 | tf_op jit(solution)/shard_map/all_to_all | solution.py:442
  1440.5 106.1 %collective-permute-start.25 = (bf16[1024,5504]{1,0:T(8,128)(2,1)}, bf16[1024,5504]{1,0:T(8,128)(2,1)}, u32[]{:S(2)}, u32[]{:S(2)}) collective-permute-start(bf16[1024,5504]{1,0:T(8,128)(2,1)} %convolution_convert_fusion.1), channel_id=1, source_target_pairs={{0,8},{8,0},{16,24},{24,16},{1,9},{9,1},{17,25},{25,17},{2,10},{10... | collective-permute-start | bytes 33816584 | tf_op jit(solution)/shard_map/ppermute | solution.py:42
  1441.0 127.4 %collective-permute-start.26 = (bf16[1376,2048]{1,0:T(8,128)(2,1)}, bf16[1376,2048]{1,0:T(8,128)(2,1)}, u32[]{:S(2)}, u32[]{:S(2)}) collective-permute-start(bf16[1376,2048]{1,0:T(8,128)(2,1)} %fusion.2), channel_id=1, source_target_pairs={{0,16},{8,24},{16,0},{24,8},{1,17},{9,25},{17,1},{25,9},{2,18},{10... | collective-permute-start | bytes 16908296 | tf_op jit(solution)/shard_map/ppermute | solution.py:42
  1485.7 239.7 %collective-permute-start.27 = (bf16[512,5504]{1,0:T(8,128)(2,1)}, bf16[512,5504]{1,0:T(8,128)(2,1)}, u32[]{:S(2)}, u32[]{:S(2)}) collective-permute-start(bf16[512,5504]{1,0:T(8,128)(2,1)} %add_convert_fusion.3), channel_id=1, source_target_pairs={{0,1},{1,0},{2,3},{3,2},{4,5},{5,4},{6,7},{7,6},{8,9},{9,8},{10,11... | collective-permute-start | bytes 16908296 | tf_op jit(solution)/shard_map/ppermute | solution.py:42
  1539.3 92.1 %all-to-all-start.7 = ((bf16[8,2,512,128]{3,2,1,0:T(8,128)(2,1)}), bf16[8,2,512,128]{3,2,1,0:T(8,128)(2,1)S(1)}, u32[]{:S(2)}, u32[]{:S(2)}) async-start(bf16[8,2,512,128]{3,2,1,0:T(8,128)(2,1)} %bitcast.381), calls=%async_computation.7 | async-start | bytes 4194304 | tf_op jit(solution)/shard_map/all_to_all | solution.py:438
  1566.0 194.6 %collective-permute-start.28 = (bf16[1024,2048]{1,0:T(8,128)(2,1)}, bf16[1024,2048]{1,0:T(8,128)(2,1)}, u32[]{:S(2)}, u32[]{:S(2)}) collective-permute-start(bf16[1024,2048]{1,0:T(8,128)(2,1)} %convolution_convert_fusion.7), channel_id=1, source_target_pairs={{0,8},{8,0},{16,24},{24,16},{1,9},{9,1},{17,25},{25,17},{2,10},{10... | collective-permute-start | bytes 12582920 | tf_op jit(solution)/shard_map/ppermute | solution.py:42
  1566.0 253.4 %collective-permute-start.29 = (bf16[512,5504]{1,0:T(8,128)(2,1)}, bf16[512,5504]{1,0:T(8,128)(2,1)}, u32[]{:S(2)}, u32[]{:S(2)}) collective-permute-start(bf16[512,5504]{1,0:T(8,128)(2,1)} %add_convert_fusion.2), channel_id=1, source_target_pairs={{0,16},{8,24},{16,0},{24,8},{1,17},{9,25},{17,1},{25,9},{2,18},{10... | collective-permute-start | bytes 16908296 | tf_op jit(solution)/shard_map/ppermute | solution.py:42
  1665.1 140.3 %all-to-all-start.8 = ((bf16[8,1,512,384]{3,2,1,0:T(8,128)(2,1)}), bf16[8,1,512,384]{3,2,1,0:T(8,128)(2,1)}, u32[]{:S(2)}, u32[]{:S(2)}) async-start(bf16[8,1,512,384]{3,2,1,0:T(8,128)(2,1)} %copy-done.2), calls=%async_computation.8 | async-start | bytes 6291456 | tf_op jit(solution)/shard_map/all_to_all | solution.py:442
  1714.6 69.0 %collective-permute-start.31 = (bf16[4,172,2048]{2,0,1:T(4,128)(2,1)}, bf16[4,172,2048]{2,0,1:T(4,128)(2,1)}, u32[]{:S(2)}, u32[]{:S(2)}) collective-permute-start(bf16[4,172,2048]{2,0,1:T(4,128)(2,1)} %copy.160), channel_id=1, source_target_pairs={{0,1},{1,0},{2,3},{3,2},{4,5},{5,4},{6,7},{7,6},{8,9},{9,8},{10,11... | collective-permute-start | bytes 8454152 | tf_op jit(solution)/shard_map/ppermute | solution.py:42
  1735.2 65.3 %collective-permute-start.32 = (bf16[256,5504]{1,0:T(8,128)(2,1)}, bf16[256,5504]{1,0:T(8,128)(2,1)}, u32[]{:S(2)}, u32[]{:S(2)}) collective-permute-start(bf16[256,5504]{1,0:T(8,128)(2,1)} %dynamic-slice_bitcast_fusion.3), channel_id=1, source_target_pairs={{0,16},{8,24},{16,0},{24,8},{1,17},{9,25},{17,1},{25,9},{2,18},{10... | collective-permute-start | bytes 8454152 | tf_op jit(solution)/shard_map/ppermute | solution.py:42
  1767.7 74.8 %collective-permute-start.30 = (bf16[512,2048]{1,0:T(8,128)(2,1)}, bf16[512,2048]{1,0:T(8,128)(2,1)}, u32[]{:S(2)}, u32[]{:S(2)}) collective-permute-start(bf16[512,2048]{1,0:T(8,128)(2,1)} %add_convert_fusion.11), channel_id=1, source_target_pairs={{0,16},{8,24},{16,0},{24,8},{1,17},{9,25},{17,1},{25,9},{2,18},{10... | collective-permute-start | bytes 6291464 | tf_op jit(solution)/shard_map/ppermute | solution.py:42
  1805.4 132.8 %all-to-all-start.9 = ((bf16[8,1,512,384]{3,2,1,0:T(8,128)(2,1)}), bf16[8,1,512,384]{3,2,1,0:T(8,128)(2,1)}, u32[]{:S(2)}, u32[]{:S(2)}) async-start(bf16[8,1,512,384]{3,2,1,0:T(8,128)(2,1)} %attend_back.7), calls=%async_computation.9 | async-start | bytes 6291456 | tf_op jit(solution)/shard_map/all_to_all | solution.py:442
  1846.9 42.2 %collective-permute-start.34 = (bf16[4,64,2048]{2,1,0:T(8,128)(2,1)}, bf16[4,64,2048]{2,1,0:T(8,128)(2,1)}, u32[]{:S(2)}, u32[]{:S(2)}) collective-permute-start(bf16[4,64,2048]{2,1,0:T(8,128)(2,1)} %dynamic-slice_bitcast_fusion.7), channel_id=1, source_target_pairs={{0,1},{1,0},{2,3},{3,2},{4,5},{5,4},{6,7},{7,6},{8,9},{9,8},{10,11... | collective-permute-start | bytes 3145736 | tf_op jit(solution)/shard_map/ppermute | solution.py:42
  1849.1 85.0 %collective-permute-start.33 = (bf16[4,64,5504]{2,1,0:T(8,128)(2,1)}, bf16[4,64,5504]{2,1,0:T(8,128)(2,1)}, u32[]{:S(2)}, u32[]{:S(2)}) collective-permute-start(bf16[4,64,5504]{2,1,0:T(8,128)(2,1)} %dynamic-slice_bitcast_fusion.2), channel_id=1, source_target_pairs={{0,1},{1,0},{2,3},{3,2},{4,5},{5,4},{6,7},{7,6},{8,9},{9,8},{10,11... | collective-permute-start | bytes 8454152 | tf_op jit(solution)/shard_map/ppermute | solution.py:42
  1977.5 27.4 %collective-permute-start.35 = (bf16[1024,3072]{1,0:T(8,128)(2,1)}, bf16[1024,3072]{1,0:T(8,128)(2,1)}, u32[]{:S(2)}, u32[]{:S(2)}) collective-permute-start(bf16[1024,3072]{1,0:T(8,128)(2,1)} %convolution_convert_fusion.6), channel_id=1, source_target_pairs={{0,8},{8,0},{16,24},{24,16},{1,9},{9,1},{17,25},{25,17},{2,10},{10... | collective-permute-start | bytes 18874376 | tf_op jit(solution)/shard_map/ppermute | solution.py:42
  1986.5 27.5 %collective-permute-start.36 = (bf16[1024,3072]{1,0:T(8,128)(2,1)}, bf16[1024,3072]{1,0:T(8,128)(2,1)}, u32[]{:S(2)}, u32[]{:S(2)}) collective-permute-start(bf16[1024,3072]{1,0:T(8,128)(2,1)} %convolution_convert_fusion.5), channel_id=1, source_target_pairs={{0,8},{8,0},{16,24},{24,16},{1,9},{9,1},{17,25},{25,17},{2,10},{10... | collective-permute-start | bytes 18874376 | tf_op jit(solution)/shard_map/ppermute | solution.py:42
  1992.0 111.6 %collective-permute-start.37 = (bf16[2,64,18560]{2,1,0:T(8,128)(2,1)}, bf16[2,64,18560]{2,1,0:T(8,128)(2,1)}, u32[]{:S(2)}, u32[]{:S(2)}) collective-permute-start(bf16[2,64,18560]{2,1,0:T(8,128)(2,1)} %dynamic-slice_bitcast_fusion), channel_id=1, source_target_pairs={{0,2},{1,3},{2,0},{3,1},{4,6},{5,7},{6,4},{7,5},{8,10},{9,11},{10,... | collective-permute-start | bytes 14254088 | tf_op jit(solution)/shard_map/ppermute | solution.py:42
  2012.6 167.4 %collective-permute-start.38 = (bf16[512,3072]{1,0:T(8,128)(2,1)}, bf16[512,3072]{1,0:T(8,128)(2,1)}, u32[]{:S(2)}, u32[]{:S(2)}) collective-permute-start(bf16[512,3072]{1,0:T(8,128)(2,1)} %add_convert_fusion.7), channel_id=1, source_target_pairs={{0,16},{8,24},{16,0},{24,8},{1,17},{9,25},{17,1},{25,9},{2,18},{10... | collective-permute-start | bytes 9437192 | tf_op jit(solution)/shard_map/ppermute | solution.py:42
  2023.5 171.5 %collective-permute-start.39 = (bf16[512,3072]{1,0:T(8,128)(2,1)}, bf16[512,3072]{1,0:T(8,128)(2,1)}, u32[]{:S(2)}, u32[]{:S(2)}) collective-permute-start(bf16[512,3072]{1,0:T(8,128)(2,1)} %add_convert_fusion.6), channel_id=1, source_target_pairs={{0,1},{1,0},{2,3},{3,2},{4,5},{5,4},{6,7},{7,6},{8,9},{9,8},{10,11... | collective-permute-start | bytes 9437192 | tf_op jit(solution)/shard_map/ppermute | solution.py:42
  2156.6 10.2 collective-permute-start.45
  2166.9 8.1 collective-permute-start.46
  2175.0 5.0 collective-permute-start.47
  2179.1 104.8 %collective-permute-start.44 = (bf16[1,64,18560]{2,1,0:T(8,128)(2,1)S(1)}, bf16[1,64,18560]{2,1,0:T(8,128)(2,1)S(1)}, u32[]{:S(2)}, u32[]{:S(2)}) collective-permute-start(bf16[1,64,18560]{2,1,0:T(8,128)(2,1)S(1)} %constant_dynamic-slice_fusion.8), channel_id=1, source_target_pairs={{0,4},{1,5},{2,6},{3,7},{4,0},{5,1},{6,2},{7,3},{8,12},{9,13},{10,... | collective-permute-start | bytes 7127048 | tf_op jit(solution)/shard_map/ppermute | solution.py:42
  2201.2 83.4 %collective-permute-start.40 = (bf16[4,64,3072]{2,1,0:T(8,128)(2,1)S(1)}, bf16[4,64,3072]{2,1,0:T(8,128)(2,1)S(1)}, u32[]{:S(2)}, u32[]{:S(2)}) collective-permute-start(bf16[4,64,3072]{2,1,0:T(8,128)(2,1)S(1)} %dynamic-slice_bitcast_fusion.6), channel_id=1, source_target_pairs={{0,1},{1,0},{2,3},{3,2},{4,5},{5,4},{6,7},{7,6},{8,9},{9,8},{10,11... | collective-permute-start | bytes 4718600 | tf_op jit(solution)/shard_map/ppermute | solution.py:42
  2203.4 81.9 %collective-permute-start.41 = (bf16[256,3072]{1,0:T(8,128)(2,1)S(1)}, bf16[256,3072]{1,0:T(8,128)(2,1)S(1)}, u32[]{:S(2)}, u32[]{:S(2)}) collective-permute-start(bf16[256,3072]{1,0:T(8,128)(2,1)S(1)} %dynamic-slice_bitcast_fusion.5), channel_id=1, source_target_pairs={{0,16},{8,24},{16,0},{24,8},{1,17},{9,25},{17,1},{25,9},{2,18},{10... | collective-permute-start | bytes 4718600 | tf_op jit(solution)/shard_map/ppermute | solution.py:42
  2286.3 35.2 %collective-permute-start.42 = (bf16[2,64,6144]{2,1,0:T(8,128)(2,1)S(1)}, bf16[2,64,6144]{2,1,0:T(8,128)(2,1)S(1)}, u32[]{:S(2)}, u32[]{:S(2)}) collective-permute-start(bf16[2,64,6144]{2,1,0:T(8,128)(2,1)S(1)} %dynamic-slice_bitcast_fusion.4), channel_id=1, source_target_pairs={{0,2},{1,3},{2,0},{3,1},{4,6},{5,7},{6,4},{7,5},{8,10},{9,11},{10,... | collective-permute-start | bytes 4718600 | tf_op jit(solution)/shard_map/ppermute | solution.py:42
  2286.4 35.1 %collective-permute-start.48 = (f32[2,2,64]{2,0,1:T(2,128)S(1)}, f32[2,2,64]{2,0,1:T(2,128)S(1)}, u32[]{:S(2)}, u32[]{:S(2)}) collective-permute-start(f32[2,2,64]{2,0,1:T(2,128)S(1)} %bitcast.458), channel_id=1, source_target_pairs={{0,2},{1,3},{2,0},{3,1},{4,6},{5,7},{6,4},{7,5},{8,10},{9,11},{10,... | collective-permute-start | bytes 3080 | tf_op jit(solution)/shard_map/ppermute | solution.py:42
  2321.9 6.2 collective-permute-start.49
  2324.0 36.3 %collective-permute-start.43 = (bf16[1,64,6144]{2,1,0:T(8,128)(2,1)}, bf16[1,64,6144]{2,1,0:T(8,128)(2,1)}, u32[]{:S(2)}, u32[]{:S(2)}) collective-permute-start(bf16[1,64,6144]{2,1,0:T(8,128)(2,1)} %constant_dynamic-slice_fusion.9), channel_id=1, source_target_pairs={{0,4},{1,5},{2,6},{3,7},{4,0},{5,1},{6,2},{7,3},{8,12},{9,13},{10,... | collective-permute-start | bytes 2359304 | tf_op jit(solution)/shard_map/ppermute | solution.py:42
  (95 other events, 2477.0 us)
Sparse Core Ops, SparseCore 0:
  11.6 250.1 all-gather.1

commit v9 on v8

--- a/solution.py
+++ b/solution.py
@@ -646,9 +646,9 @@
     for r in late:
         mark = (r.send(*mark),)
     first.step(0, hold=mark)
-    mark = mark + (first.total,)
     for g in range(groups - 1):
         mark = (finish_tokens(g, *mark),)
+    mark = mark + (first.total,)
     g = groups - 1
     grad_h_attn = nt(after(last_rows, *mark), full_qkv)
     grad_norm, gain_part = norm_backward(grad_h_attn, of(x, g), of(scale_a, g), gain_a)

time: 2380 us -> 2380 us (level)
  no operation moved by 1% of the time
where the time goes in v9:
time: 2380 us; the launch traced here: 2370 us
  waiting for transfers between devices  1050 us (44%)
  matrix products  551 us (23%)
  Pallas kernels  271 us (11%)
  local copies, waits for them, and re-layouts  214 us (9%)
  other arithmetic  165 us (7%)
  starting transfers between devices  106 us (4%)
    ppermute x50, waiting for transfers between devices, swap(): lax.ppermute(block, axis, [(i, i ^ stride) for i in range(lax.axis_size(a...  932 us
    dot_general x10, matrix products, nt(): return jnp.einsum('re,de->rd', a, b, preferred_element_type=f32)  184 us
    dot_general x16, matrix products, tn(): lax.dot_general(a, b, (((0,), (0,)), ((), ())), preferred_element_type=f32)  182 us
    pallas_call x4, Pallas kernels, attend_back(): pl.pallas_call(functools.partial(backward_kernel, pair), grid_spec=pltpu....  131 us
    pallas_call x2, Pallas kernels, attend(): pl.pallas_call(forward_kernel, grid_spec=pltpu.PrefetchScalarGridSpec(num...  93.8 us
    all_to_all x4, waiting for transfers between devices, to_heads(): return lax.all_to_all(split, 'seq', 0, 0, tiled=True)  73.8 us
    ppermute x50, starting transfers between devices, swap(): lax.ppermute(block, axis, [(i, i ^ stride) for i in range(lax.axis_size(a...  54.4 us
    dot_general x2, matrix products, shards(): up = jnp.dot(after(h_mlp, *mark), full_up, preferred_element_type=f32)  50.6 us
  transfers between devices with their start and end apart: 61, of which 24 were waited for; matrix products, arithmetic and copies ran while one was open for 30% of the time, Pallas kernels for 9%

profile of v9, /device:TPU:0, one launch (start us, length us, event | category | flops | bytes accessed | tf_op | source)
XLA Modules:
  0.0 2373.1 jit_solution(9749737176092633705)
XLA Ops:
  36.2 9.3 copy.145
  55.2 72.0 %collective-permute-done.5 = bf16[64,7552]{1,0:T(8,128)(2,1)S(1)} collective-permute-done((bf16[64,7552]{1,0:T(8,128)(2,1)S(1)}, bf16[64,7552]{1,0:T(8,128)(2,1)S(1)}, u32[]{:S(2)}, u32[]{:S(2)}) %collective-permute-start.5) | collective-permute-done | bytes 966688 | tf_op jit(solution)/shard_map/ppermute | solution.py:42
  129.4 121.8 %collective-permute-done.6 = bf16[64,11008]{1,0:T(8,128)(2,1)S(1)} collective-permute-done((bf16[64,11008]{1,0:T(8,128)(2,1)S(1)}, bf16[64,11008]{1,0:T(8,128)(2,1)S(1)}, u32[]{:S(2)}, u32[]{:S(2)}) %collective-permute-start.6) | collective-permute-done | bytes 1409056 | tf_op jit(solution)/shard_map/ppermute | solution.py:42
  251.2 16.3 collective-permute-done.7
  268.4 62.2 %collective-permute-done.8 = bf16[128,11008]{1,0:T(8,128)(2,1)S(1)} collective-permute-done((bf16[128,11008]{1,0:T(8,128)(2,1)S(1)}, bf16[128,11008]{1,0:T(8,128)(2,1)S(1)}, u32[]{:S(2)}, u32[]{:S(2)}) %collective-permute-start.8) | collective-permute-done | bytes 2818080 | tf_op jit(solution)/shard_map/ppermute | solution.py:42
  336.1 82.7 %collective-permute-done.10.refs_1_ = bf16[256,7552]{1,0:T(8,128)(2,1)S(1)} collective-permute-done((bf16[256,7552]{1,0:T(8,128)(2,1)S(1)}, bf16[256,7552]{1,0:T(8,128)(2,1)S(1)}, u32[]{:S(2)}, u32[]{:S(2)}) %collective-permute-start.10) | collective-permute-done | bytes 3866656 | tf_op jit(solution)/shard_map/ppermute | solution.py:42
  420.7 35.0 %collective-permute-done.9.refs_1_ = bf16[256,11008]{1,0:T(8,128)(2,1)} collective-permute-done((bf16[256,11008]{1,0:T(8,128)(2,1)S(1)}, bf16[256,11008]{1,0:T(8,128)(2,1)}, u32[]{:S(2)}, u32[]{:S(2)}) %collective-permute-start.9) | collective-permute-done | bytes 5636128 | tf_op jit(solution)/shard_map/ppermute | solution.py:42
  455.6 19.0 convolution_convert_fusion.4
  489.3 149.0 %collective-permute-done.12.refs_3_ = bf16[256,7552]{1,0:T(8,128)(2,1)} collective-permute-done((bf16[256,7552]{1,0:T(8,128)(2,1)}, bf16[256,7552]{1,0:T(8,128)(2,1)}, u32[]{:S(2)}, u32[]{:S(2)}) %collective-permute-start.12) | collective-permute-done | bytes 3866656 | tf_op jit(solution)/shard_map/ppermute | solution.py:42
  638.3 80.8 %collective-permute-done.11.refs_2_ = bf16[256,7552]{1,0:T(8,128)(2,1)} collective-permute-done((bf16[256,7552]{1,0:T(8,128)(2,1)}, bf16[256,7552]{1,0:T(8,128)(2,1)}, u32[]{:S(2)}, u32[]{:S(2)}) %collective-permute-start.11) | collective-permute-done | bytes 3866656 | tf_op jit(solution)/shard_map/ppermute | solution.py:42
  730.6 46.9 %attend.2 = (bf16[8,2,512,128]{3,2,1,0:T(8,128)(2,1)}, f32[2,1,4096]{2,1,0:T(1,128)S(1)}) custom-call(s32[2,4,8]{2,1,0:T(4,128)S(1)} %pad_add_fusion.2.bounds, bf16[8,2,512,384]{3,2,1,0:T(8,128)(2,1)} %all-to-all-done.q_ref.k_ref.v_ref, bf16[8,2,512,384]{3,2,1,0:T(8,128)(2,1)} %all-to-all-done.q_ref.k_ref.v_ref, ...), custom_call_target="tpu_custom_call" | custom-call | flops 1024 | bytes 1024 | tf_op jit(solution)/shard_map/attend/pallas_call | solution.py:314
  795.0 17.0 place.2
  815.4 29.4 %place.3 = (bf16[2048,5504]{1,0:T(8,128)(2,1)}, bf16[2048,5504]{1,0:T(8,128)(2,1)}) custom-call(s32[32]{0:T(128)S(1)} %xor_multiply_fusion.target, bf16[256,11008]{1,0:T(8,128)(2,1)S(1)} %bitcast.340, bf16[256,11008]{1,0:T(8,128)(2,1)} %collective-permute-done.9.refs_1_, bf16[256,11008]{1,0:T(8,128)(2,1)} %collective-permute-done.13.refs_2_, ...), custom_call_target="tpu_custom_call" | custom-call | flops 1024 | bytes 1024 | tf_op jit(solution)/shard_map/place/pallas_call | solution.py:149
  848.8 18.8 convolution_convert_fusion.3
  879.5 10.3 multiply_reduce_fusion.10
  893.5 19.1 fusion.120
  912.6 25.3 %multiply_convert_fusion.5 = (bf16[512,5504]{1,0:T(8,128)(2,1)}, f32[512,5504]{1,0:T(8,128)}) fusion(f32[512,5504]{1,0:T(8,128)} %fusion.120, bf16[512,2048]{1,0:T(8,128)(2,1)} %copy-done.37, bf16[2048,5504]{1,0:T(8,128)(2,1)} %get-tuple-element.92), kind=kOutput, calls=%fused_computation.24 | convolution fusion | flops 11559632896 | bytes 52822016 | tf_op jit(solution)/shard_map/dot_general | solution.py:558
  937.9 31.1 %reshape.453 = bf16[5504,2048]{1,0:T(8,128)(2,1)} reshape(bf16[2048,5504]{1,0:T(8,128)(2,1)} %get-tuple-element.97) | data formatting | bytes 45088768 | tf_op jit(solution)/shard_map/reshape | solution.py:564
  969.1 25.2 %multiply_convert_fusion.3 = (bf16[512,5504]{1,0:T(8,128)(2,1)}, bf16[512,5504]{1,0:T(8,128)(2,1)}) fusion(f32[512,5504]{1,0:T(8,128)} %fusion.120, f32[512,5504]{1,0:T(8,128)} %get-tuple-element.276, bf16[512,2048]{1,0:T(8,128)(2,1)} %get-tuple-element.96, bf16[5504,2048]{1,0:T(8,128)(2,1)} %reshape.453), kind=kOutput, calls=%fused_computation.22 | convolution fusion | flops 11579359232 | bytes 58458112 | tf_op jit(solution)/shard_map/re,de->rd/dot_general | solution.py:463
  994.2 23.0 all-to-all-done.2.q_ref.k_ref.v_ref
  1017.3 46.9 %attend.3 = (bf16[8,2,512,128]{3,2,1,0:T(8,128)(2,1)}, f32[2,1,4096]{2,1,0:T(1,128)S(1)}) custom-call(s32[2,4,8]{2,1,0:T(4,128)S(1)} %pad_add_fusion.3.bounds, bf16[8,2,512,384]{3,2,1,0:T(8,128)(2,1)} %all-to-all-done.2.q_ref.k_ref.v_ref, bf16[8,2,512,384]{3,2,1,0:T(8,128)(2,1)} %all-to-all-done.2.q_ref.k_ref.v_ref, ...), custom_call_target="tpu_custom_call" | custom-call | flops 1024 | bytes 1024 | tf_op jit(solution)/shard_map/attend/pallas_call | solution.py:314
  1067.8 19.4 fusion.121
  1087.3 19.4 multiply_reduce_fusion.2
  1108.6 8.9 convolution_convert_fusion.9
  1131.4 10.3 multiply_reduce_fusion.8
  1145.4 19.1 fusion.122
  1164.5 25.3 %multiply_convert_fusion.2 = (bf16[512,5504]{1,0:T(8,128)(2,1)}, f32[512,5504]{1,0:T(8,128)}) fusion(f32[512,5504]{1,0:T(8,128)} %fusion.122, bf16[512,2048]{1,0:T(8,128)(2,1)} %copy-done.39, bf16[2048,5504]{1,0:T(8,128)(2,1)} %get-tuple-element.92), kind=kOutput, calls=%fused_computation.19 | convolution fusion | flops 11559632896 | bytes 52822016 | tf_op jit(solution)/shard_map/dot_general | solution.py:558
  1189.8 11.5 pad_maximum_fusion
  1201.3 31.4 %convolution_convert_fusion = bf16[5504,2048]{1,0:T(8,128)(2,1)} fusion(bf16[1024,5504]{1,0:T(8,128)(2,1)} %pad_maximum_fusion, bf16[1024,2048]{1,0:T(8,128)(2,1)} %bitcast.346), kind=kOutput, calls=%fused_computation | convolution fusion | flops 23096721408 | bytes 38010880 | tf_op jit(solution)/shard_map/dot_general | solution.py:169
  1232.7 10.0 constant_dynamic-slice_fusion.10
  1242.7 32.3 %attend_back.4 = bf16[8,1,512,384]{3,2,1,0:T(8,128)(2,1)S(1)} custom-call(s32[2,4,8]{2,1,0:T(4,128)S(1)} %copy-done.19, bf16[8,2,512,384]{3,2,1,0:T(8,128)(2,1)} %all-to-all-done.q_ref.k_ref.v_ref, bf16[8,2,512,384]{3,2,1,0:T(8,128)(2,1)} %all-to-all-done.q_ref.k_ref.v_ref, bf16[8,2,512,384]{3,2,1,0:T(8,128)(2,1)} %all-to-all-done.q_ref.k_ref.v_ref, ...), custom_call_target="tpu_custom_call" | custom-call | flops 1024 | bytes 1024 | tf_op jit(solution)/shard_map/attend_back/pallas_call | solution.py:391
  1283.3 33.4 %attend_back.5 = bf16[8,1,512,384]{3,2,1,0:T(8,128)(2,1)} custom-call(s32[2,4,8]{2,1,0:T(4,128)S(1)} %copy-done.19, bf16[8,2,512,384]{3,2,1,0:T(8,128)(2,1)} %all-to-all-done.q_ref.k_ref.v_ref, bf16[8,2,512,384]{3,2,1,0:T(8,128)(2,1)} %all-to-all-done.q_ref.k_ref.v_ref, bf16[8,2,512,384]{3,2,1,0:T(8,128)(2,1)} %all-to-all-done.q_ref.k_ref.v_ref, ...), custom_call_target="tpu_custom_call" | custom-call | flops 1024 | bytes 1024 | tf_op jit(solution)/shard_map/attend_back/pallas_call | solution.py:391
  1330.6 10.1 fusion.2
  1340.7 14.0 all-to-all-done.5
  1354.7 24.7 %multiply_convert_fusion = (bf16[512,5504]{1,0:T(8,128)(2,1)}, bf16[512,5504]{1,0:T(8,128)(2,1)}) fusion(f32[512,5504]{1,0:T(8,128)} %fusion.122, f32[512,5504]{1,0:T(8,128)} %get-tuple-element.281, bf16[512,2048]{1,0:T(8,128)(2,1)S(1)} %copy-done.51, bf16[5504,2048]{1,0:T(8,128)(2,1)} %reshape.453), kind=kOutput, calls=%fused_computation.17 | convolution fusion | flops 11579359232 | bytes 58458112 | tf_op jit(solution)/shard_map/re,de->rd/dot_general | solution.py:463
  1379.4 19.4 convolution_convert_fusion.2
  1411.1 11.2 copy.152
  1422.3 19.3 convolution_convert_fusion.1
  1443.5 31.5 %all-to-all-done.6 = bf16[8,1,512,384]{3,2,1,0:T(8,128)(2,1)} async-done(((bf16[8,1,512,384]{3,2,1,0:T(8,128)(2,1)}), bf16[8,1,512,384]{3,2,1,0:T(8,128)(2,1)}, u32[]{:S(2)}, u32[]{:S(2)}) %all-to-all-start.6) | async-done | bytes 3145760 | tf_op jit(solution)/shard_map/all_to_all | solution.py:442
  1474.9 11.7 add_convert_fusion.3
  1488.1 19.4 fusion.123
  1507.6 19.4 multiply_reduce_fusion.1
  1529.0 8.9 convolution_convert_fusion.8
  1547.7 13.3 add_convert_fusion.2
  1568.5 13.1 fusion.1
  1581.6 50.8 %all-to-all-done.7.do_ref = bf16[8,2,512,128]{3,2,1,0:T(8,128)(2,1)S(1)} async-done(((bf16[8,2,512,128]{3,2,1,0:T(8,128)(2,1)}), bf16[8,2,512,128]{3,2,1,0:T(8,128)(2,1)S(1)}, u32[]{:S(2)}, u32[]{:S(2)}) %all-to-all-start.7) | async-done | bytes 2097184 | tf_op jit(solution)/shard_map/all_to_all | solution.py:438
  1632.5 32.1 %attend_back.6 = bf16[8,1,512,384]{3,2,1,0:T(8,128)(2,1)S(1)} custom-call(s32[2,4,8]{2,1,0:T(4,128)S(1)} %copy-done.17, bf16[8,2,512,384]{3,2,1,0:T(8,128)(2,1)} %all-to-all-done.2.q_ref.k_ref.v_ref, bf16[8,2,512,384]{3,2,1,0:T(8,128)(2,1)} %all-to-all-done.2.q_ref.k_ref.v_ref, bf16[8,2,512,384]{3,2,1,0:T(8,128)(2,1)} %all-to-all-done.2.q_ref.k_ref.v_ref, ...), custom_call_target="tpu_custom_call" | custom-call | flops 1024 | bytes 1024 | tf_op jit(solution)/shard_map/attend_back/pallas_call | solution.py:391
  1670.8 32.9 %attend_back.7 = bf16[8,1,512,384]{3,2,1,0:T(8,128)(2,1)} custom-call(s32[2,4,8]{2,1,0:T(4,128)S(1)} %copy-done.17, bf16[8,2,512,384]{3,2,1,0:T(8,128)(2,1)} %all-to-all-done.2.q_ref.k_ref.v_ref, bf16[8,2,512,384]{3,2,1,0:T(8,128)(2,1)} %all-to-all-done.2.q_ref.k_ref.v_ref, bf16[8,2,512,384]{3,2,1,0:T(8,128)(2,1)} %all-to-all-done.2.q_ref.k_ref.v_ref, ...), custom_call_target="tpu_custom_call" | custom-call | flops 1024 | bytes 1024 | tf_op jit(solution)/shard_map/attend_back/pallas_call | solution.py:391
  1751.0 9.1 copy.157
  1767.8 16.1 collective-permute-done.31
  1789.2 11.4 collective-permute-done.32
  1810.1 9.4 fusion.14
  1829.6 13.3 collective-permute-done.30
  1851.2 19.1 add_convert_fusion.9
  1870.3 19.3 add_convert_fusion.8
  1892.2 42.6 %collective-permute-done.33 = bf16[4,64,5504]{2,1,0:T(8,128)(2,1)} collective-permute-done((bf16[4,64,5504]{2,1,0:T(8,128)(2,1)}, bf16[4,64,5504]{2,1,0:T(8,128)(2,1)}, u32[]{:S(2)}, u32[]{:S(2)}) %collective-permute-start.33) | collective-permute-done | bytes 2818080 | tf_op jit(solution)/shard_map/ppermute | solution.py:42
  1966.8 11.3 convolution_convert_fusion.6
  1978.2 9.1 convolution_convert_fusion.5
  2023.6 81.0 %collective-permute-done.37 = bf16[2,64,18560]{2,1,0:T(8,128)(2,1)} collective-permute-done((bf16[2,64,18560]{2,1,0:T(8,128)(2,1)}, bf16[2,64,18560]{2,1,0:T(8,128)(2,1)}, u32[]{:S(2)}, u32[]{:S(2)}) %collective-permute-start.37) | collective-permute-done | bytes 4751392 | tf_op jit(solution)/shard_map/ppermute | solution.py:42
  2104.7 18.4 multiply_reduce_fusion.4
  2136.7 20.1 multiply_reduce_fusion.3
  2203.9 80.3 %collective-permute-done.44 = bf16[1,64,18560]{2,1,0:T(8,128)(2,1)S(1)} collective-permute-done((bf16[1,64,18560]{2,1,0:T(8,128)(2,1)S(1)}, bf16[1,64,18560]{2,1,0:T(8,128)(2,1)S(1)}, u32[]{:S(2)}, u32[]{:S(2)}) %collective-permute-start.44) | collective-permute-done | bytes 2375712 | tf_op jit(solution)/shard_map/ppermute | solution.py:42
  2290.5 31.3 %collective-permute-done.48 = f32[2,2,64]{2,0,1:T(2,128)S(1)} collective-permute-done((f32[2,2,64]{2,0,1:T(2,128)S(1)}, f32[2,2,64]{2,0,1:T(2,128)S(1)}, u32[]{:S(2)}, u32[]{:S(2)}) %collective-permute-start.48) | collective-permute-done | bytes 1056 | tf_op jit(solution)/shard_map/ppermute | solution.py:42
  2329.0 32.2 %collective-permute-done.43 = bf16[1,64,6144]{2,1,0:T(8,128)(2,1)} collective-permute-done((bf16[1,64,6144]{2,1,0:T(8,128)(2,1)}, bf16[1,64,6144]{2,1,0:T(8,128)(2,1)}, u32[]{:S(2)}, u32[]{:S(2)}) %collective-permute-start.43) | collective-permute-done | bytes 786464 | tf_op jit(solution)/shard_map/ppermute | solution.py:42
  (463 shorter events, 439.0 us)
Async XLA Ops:
  7.2 448.4 %all-gather.2.cloned.1.call-start = ((), (), s32[]{:S(2)}) async-start(), calls=%async_computation.10 | async-start | bytes 25952256 | tf_op jit(solution)/shard_map/all_gather | solution.py:469
  10.6 4.5 collective-permute-start
  15.2 3.6 collective-permute-start.1
  18.9 4.6 collective-permute-start.2
  23.6 3.4 collective-permute-start.3
  27.0 19.4 collective-permute-start.4
  46.5 1095.2 %copy-start.54 = (f32[1,2048]{1,0:T(1,128)}, f32[1,2048]{1,0:T(1,128)S(1)}, u32[]{:S(2)}) copy-start(f32[1,2048]{1,0:T(1,128)S(1)} %get-tuple-element.251) | copy-start | bytes 24580
  52.8 74.3 %collective-permute-start.5 = (bf16[64,7552]{1,0:T(8,128)(2,1)S(1)}, bf16[64,7552]{1,0:T(8,128)(2,1)S(1)}, u32[]{:S(2)}, u32[]{:S(2)}) collective-permute-start(bf16[64,7552]{1,0:T(8,128)(2,1)S(1)} %pad_maximum_fusion.29), channel_id=1, source_target_pairs={{0,4},{1,5},{2,6},{3,7},{4,0},{5,1},{6,2},{7,3},{8,12},{9,13},{10,... | collective-permute-start | bytes 2899976 | tf_op jit(solution)/shard_map/ppermute | solution.py:42
  127.4 123.7 %collective-permute-start.6 = (bf16[64,11008]{1,0:T(8,128)(2,1)S(1)}, bf16[64,11008]{1,0:T(8,128)(2,1)S(1)}, u32[]{:S(2)}, u32[]{:S(2)}) collective-permute-start(bf16[64,11008]{1,0:T(8,128)(2,1)S(1)} %pad_maximum_fusion.23), channel_id=1, source_target_pairs={{0,4},{1,5},{2,6},{3,7},{4,0},{5,1},{6,2},{7,3},{8,12},{9,13},{10,... | collective-permute-start | bytes 4227080 | tf_op jit(solution)/shard_map/ppermute | solution.py:42
  127.5 140.1 %collective-permute-start.7 = (bf16[128,7552]{1,0:T(8,128)(2,1)S(1)}, bf16[128,7552]{1,0:T(8,128)(2,1)S(1)}, u32[]{:S(2)}, u32[]{:S(2)}) collective-permute-start(bf16[128,7552]{1,0:T(8,128)(2,1)S(1)} %get-tuple-element.246), channel_id=1, source_target_pairs={{0,2},{1,3},{2,0},{3,1},{4,6},{5,7},{6,4},{7,5},{8,10},{9,11},{10,... | collective-permute-start | bytes 5799944 | tf_op jit(solution)/shard_map/ppermute | solution.py:42
  267.8 62.8 %collective-permute-start.8 = (bf16[128,11008]{1,0:T(8,128)(2,1)S(1)}, bf16[128,11008]{1,0:T(8,128)(2,1)S(1)}, u32[]{:S(2)}, u32[]{:S(2)}) collective-permute-start(bf16[128,11008]{1,0:T(8,128)(2,1)S(1)} %constant_dynamic-update-slice_fusion.2), channel_id=1, source_target_pairs={{0,2},{1,3},{2,0},{3,1},{4,6},{5,7},{6,4},{7,5},{8,10},{9,11},{10,... | collective-permute-start | bytes 8454152 | tf_op jit(solution)/shard_map/ppermute | solution.py:42
  333.2 122.4 %collective-permute-start.9 = (bf16[256,11008]{1,0:T(8,128)(2,1)S(1)}, bf16[256,11008]{1,0:T(8,128)(2,1)}, u32[]{:S(2)}, u32[]{:S(2)}) collective-permute-start(bf16[256,11008]{1,0:T(8,128)(2,1)S(1)} %constant_dynamic-update-slice_fusion.7.refs_0_), channel_id=1, source_target_pairs={{0,1},{1,0},{2,3},{3,2},{4,5},{5,4},{6,7},{7,6},{8,9},{9,8},{10,11... | collective-permute-start | bytes 16908296 | tf_op jit(solution)/shard_map/ppermute | solution.py:42
  334.7 84.1 %collective-permute-start.10 = (bf16[256,7552]{1,0:T(8,128)(2,1)S(1)}, bf16[256,7552]{1,0:T(8,128)(2,1)S(1)}, u32[]{:S(2)}, u32[]{:S(2)}) collective-permute-start(bf16[256,7552]{1,0:T(8,128)(2,1)S(1)} %constant_dynamic-update-slice_fusion.4.refs_0_), channel_id=1, source_target_pairs={{0,16},{8,24},{16,0},{24,8},{1,17},{9,25},{17,1},{25,9},{2,18},{10... | collective-permute-start | bytes 11599880 | tf_op jit(solution)/shard_map/ppermute | solution.py:42
  480.3 238.8 %copy-start.60 = (s32[2,1,4096]{2,1,0:T(1,128)S(1)}, s32[2,1,4096]{2,1,0:T(1,128)}, u32[]{:S(2)}) copy-start(s32[2,1,4096]{2,1,0:T(1,128)} %param.12) | copy-start | bytes 98308
  480.3 250.2 %all-to-all-start = ((bf16[8,2,512,384]{3,2,1,0:T(8,128)(2,1)}), bf16[8,2,512,384]{3,2,1,0:T(8,128)(2,1)}, u32[]{:S(2)}, u32[]{:S(2)}) async-start(bf16[8,2,512,384]{3,2,1,0:T(8,128)(2,1)} %bitcast.349), calls=%async_computation | async-start | bytes 12582912 | tf_op jit(solution)/shard_map/all_to_all | solution.py:438
  485.2 153.1 %collective-permute-start.12 = (bf16[256,7552]{1,0:T(8,128)(2,1)}, bf16[256,7552]{1,0:T(8,128)(2,1)}, u32[]{:S(2)}, u32[]{:S(2)}) collective-permute-start(bf16[256,7552]{1,0:T(8,128)(2,1)} %copy-done.6), channel_id=1, source_target_pairs={{0,1},{1,0},{2,3},{3,2},{4,5},{5,4},{6,7},{7,6},{8,9},{9,8},{10,11... | collective-permute-start | bytes 11599880 | tf_op jit(solution)/shard_map/ppermute | solution.py:42
  487.1 232.0 %collective-permute-start.11 = (bf16[256,7552]{1,0:T(8,128)(2,1)}, bf16[256,7552]{1,0:T(8,128)(2,1)}, u32[]{:S(2)}, u32[]{:S(2)}) collective-permute-start(bf16[256,7552]{1,0:T(8,128)(2,1)} %copy-done.4), channel_id=1, source_target_pairs={{0,1},{1,0},{2,3},{3,2},{4,5},{5,4},{6,7},{7,6},{8,9},{9,8},{10,11... | collective-permute-start | bytes 11599880 | tf_op jit(solution)/shard_map/ppermute | solution.py:42
  487.3 240.8 %collective-permute-start.14 = (bf16[256,11008]{1,0:T(8,128)(2,1)}, bf16[256,11008]{1,0:T(8,128)(2,1)}, u32[]{:S(2)}, u32[]{:S(2)}) collective-permute-start(bf16[256,11008]{1,0:T(8,128)(2,1)} %collective-permute-done.9.refs_1_), channel_id=1, source_target_pairs={{0,16},{8,24},{16,0},{24,8},{1,17},{9,25},{17,1},{25,9},{2,18},{10... | collective-permute-start | bytes 16908296 | tf_op jit(solution)/shard_map/ppermute | solution.py:42
  488.7 240.5 %collective-permute-start.13 = (bf16[256,11008]{1,0:T(8,128)(2,1)}, bf16[256,11008]{1,0:T(8,128)(2,1)}, u32[]{:S(2)}, u32[]{:S(2)}) collective-permute-start(bf16[256,11008]{1,0:T(8,128)(2,1)} %copy-done.1), channel_id=1, source_target_pairs={{0,16},{8,24},{16,0},{24,8},{1,17},{9,25},{17,1},{25,9},{2,18},{10... | collective-permute-start | bytes 16908296 | tf_op jit(solution)/shard_map/ppermute | solution.py:42
  489.3 234.4 %collective-permute-start.16 = (bf16[256,7552]{1,0:T(8,128)(2,1)}, bf16[256,7552]{1,0:T(8,128)(2,1)S(1)}, u32[]{:S(2)}, u32[]{:S(2)}) collective-permute-start(bf16[256,7552]{1,0:T(8,128)(2,1)} %copy-done.6), channel_id=1, source_target_pairs={{0,8},{8,0},{16,24},{24,16},{1,9},{9,1},{17,25},{25,17},{2,10},{10... | collective-permute-start | bytes 11599880 | tf_op jit(solution)/shard_map/ppermute | solution.py:42
  638.3 87.9 %collective-permute-start.15 = (bf16[256,7552]{1,0:T(8,128)(2,1)}, bf16[256,7552]{1,0:T(8,128)(2,1)S(1)}, u32[]{:S(2)}, u32[]{:S(2)}) collective-permute-start(bf16[256,7552]{1,0:T(8,128)(2,1)} %copy-done.4), channel_id=1, source_target_pairs={{0,8},{8,0},{16,24},{24,16},{1,9},{9,1},{17,25},{25,17},{2,10},{10... | collective-permute-start | bytes 11599880 | tf_op jit(solution)/shard_map/ppermute | solution.py:42
  719.1 10.8 collective-permute-start.18
  725.6 89.7 %collective-permute-start.20 = (bf16[256,11008]{1,0:T(8,128)(2,1)}, bf16[256,11008]{1,0:T(8,128)(2,1)}, u32[]{:S(2)}, u32[]{:S(2)}) collective-permute-start(bf16[256,11008]{1,0:T(8,128)(2,1)} %collective-permute-done.9.refs_1_), channel_id=1, source_target_pairs={{0,8},{8,0},{16,24},{24,16},{1,9},{9,1},{17,25},{25,17},{2,10},{10... | collective-permute-start | bytes 16908296 | tf_op jit(solution)/shard_map/ppermute | solution.py:42
  728.0 87.3 %collective-permute-start.19 = (bf16[256,11008]{1,0:T(8,128)(2,1)}, bf16[256,11008]{1,0:T(8,128)(2,1)}, u32[]{:S(2)}, u32[]{:S(2)}) collective-permute-start(bf16[256,11008]{1,0:T(8,128)(2,1)} %copy-done.1), channel_id=1, source_target_pairs={{0,8},{8,0},{16,24},{24,16},{1,9},{9,1},{17,25},{25,17},{2,10},{10... | collective-permute-start | bytes 16908296 | tf_op jit(solution)/shard_map/ppermute | solution.py:42
  728.0 87.3 %collective-permute-start.22 = (bf16[256,11008]{1,0:T(8,128)(2,1)}, bf16[256,11008]{1,0:T(8,128)(2,1)}, u32[]{:S(2)}, u32[]{:S(2)}) collective-permute-start(bf16[256,11008]{1,0:T(8,128)(2,1)} %collective-permute-done.14.refs_3_), channel_id=1, source_target_pairs={{0,8},{8,0},{16,24},{24,16},{1,9},{9,1},{17,25},{25,17},{2,10},{10... | collective-permute-start | bytes 16908296 | tf_op jit(solution)/shard_map/ppermute | solution.py:42
  729.2 86.2 %collective-permute-start.21 = (bf16[256,11008]{1,0:T(8,128)(2,1)}, bf16[256,11008]{1,0:T(8,128)(2,1)}, u32[]{:S(2)}, u32[]{:S(2)}) collective-permute-start(bf16[256,11008]{1,0:T(8,128)(2,1)} %collective-permute-done.13.refs_2_), channel_id=1, source_target_pairs={{0,8},{8,0},{16,24},{24,16},{1,9},{9,1},{17,25},{25,17},{2,10},{10... | collective-permute-start | bytes 16908296 | tf_op jit(solution)/shard_map/ppermute | solution.py:42
  729.9 287.3 %copy-start.12 = (s32[2,1,4096]{2,1,0:T(1,128)}, s32[2,1,4096]{2,1,0:T(1,128)S(1)}, u32[]{:S(2)}) copy-start(s32[2,1,4096]{2,1,0:T(1,128)S(1)} %get-tuple-element.290.lo_ref) | copy-start | bytes 98308
  729.9 58.7 %collective-permute-start.17 = (bf16[256,7552]{1,0:T(8,128)(2,1)}, bf16[256,7552]{1,0:T(8,128)(2,1)}, u32[]{:S(2)}, u32[]{:S(2)}) collective-permute-start(bf16[256,7552]{1,0:T(8,128)(2,1)} %collective-permute-done.11.refs_2_), channel_id=1, source_target_pairs={{0,8},{8,0},{16,24},{24,16},{1,9},{9,1},{17,25},{25,17},{2,10},{10... | collective-permute-start | bytes 11599880 | tf_op jit(solution)/shard_map/ppermute | solution.py:42
  777.5 67.4 %all-to-all-start.1 = ((bf16[8,2,512,128]{3,2,1,0:T(8,128)(2,1)}), bf16[8,2,512,128]{3,2,1,0:T(8,128)(2,1)}, u32[]{:S(2)}, u32[]{:S(2)}) async-start(bf16[8,2,512,128]{3,2,1,0:T(8,128)(2,1)} %get-tuple-element.89.o_ref), calls=%async_computation.1 | async-start | bytes 4194304 | tf_op jit(solution)/shard_map/all_to_all | solution.py:442
  873.3 144.0 %all-to-all-start.2 = ((bf16[8,2,512,384]{3,2,1,0:T(8,128)(2,1)}), bf16[8,2,512,384]{3,2,1,0:T(8,128)(2,1)}, u32[]{:S(2)}, u32[]{:S(2)}) async-start(bf16[8,2,512,384]{3,2,1,0:T(8,128)(2,1)} %bitcast.350), calls=%async_computation.2 | async-start | bytes 12582912 | tf_op jit(solution)/shard_map/all_to_all | solution.py:438
  1064.2 55.8 %all-to-all-start.3 = ((bf16[8,2,512,128]{3,2,1,0:T(8,128)(2,1)}), bf16[8,2,512,128]{3,2,1,0:T(8,128)(2,1)S(1)}, u32[]{:S(2)}, u32[]{:S(2)}) async-start(bf16[8,2,512,128]{3,2,1,0:T(8,128)(2,1)} %get-tuple-element.99.o_ref), calls=%async_computation.3 | async-start | bytes 4194304 | tf_op jit(solution)/shard_map/all_to_all | solution.py:442
  1121.3 80.1 %all-to-all-start.4 = ((bf16[8,2,512,128]{3,2,1,0:T(8,128)(2,1)}), bf16[8,2,512,128]{3,2,1,0:T(8,128)(2,1)S(1)}, u32[]{:S(2)}, u32[]{:S(2)}) async-start(bf16[8,2,512,128]{3,2,1,0:T(8,128)(2,1)} %bitcast.381), calls=%async_computation.4 | async-start | bytes 4194304 | tf_op jit(solution)/shard_map/all_to_all | solution.py:438
  1242.7 87.9 %collective-permute-start.23 = (bf16[2752,2048]{1,0:T(8,128)(2,1)}, bf16[2752,2048]{1,0:T(8,128)(2,1)}, u32[]{:S(2)}, u32[]{:S(2)}) collective-permute-start(bf16[2752,2048]{1,0:T(8,128)(2,1)} %bitcast.47), channel_id=1, source_target_pairs={{0,8},{8,0},{16,24},{24,16},{1,9},{9,1},{17,25},{25,17},{2,10},{10... | collective-permute-start | bytes 33816584 | tf_op jit(solution)/shard_map/ppermute | solution.py:42
  1276.7 77.9 %all-to-all-start.5 = ((bf16[8,1,512,384]{3,2,1,0:T(8,128)(2,1)}), bf16[8,1,512,384]{3,2,1,0:T(8,128)(2,1)}, u32[]{:S(2)}, u32[]{:S(2)}) async-start(bf16[8,1,512,384]{3,2,1,0:T(8,128)(2,1)} %copy-done.3), calls=%async_computation.5 | async-start | bytes 6291456 | tf_op jit(solution)/shard_map/all_to_all | solution.py:442
  1398.8 76.1 %collective-permute-start.24 = (bf16[1024,5504]{1,0:T(8,128)(2,1)}, bf16[1024,5504]{1,0:T(8,128)(2,1)}, u32[]{:S(2)}, u32[]{:S(2)}) collective-permute-start(bf16[1024,5504]{1,0:T(8,128)(2,1)} %convolution_convert_fusion.2), channel_id=1, source_target_pairs={{0,8},{8,0},{16,24},{24,16},{1,9},{9,1},{17,25},{25,17},{2,10},{10... | collective-permute-start | bytes 33816584 | tf_op jit(solution)/shard_map/ppermute | solution.py:42
  1398.8 76.1 %all-to-all-start.6 = ((bf16[8,1,512,384]{3,2,1,0:T(8,128)(2,1)}), bf16[8,1,512,384]{3,2,1,0:T(8,128)(2,1)}, u32[]{:S(2)}, u32[]{:S(2)}) async-start(bf16[8,1,512,384]{3,2,1,0:T(8,128)(2,1)} %attend_back.5), calls=%async_computation.6 | async-start | bytes 6291456 | tf_op jit(solution)/shard_map/all_to_all | solution.py:442
  1441.6 106.1 %collective-permute-start.25 = (bf16[1024,5504]{1,0:T(8,128)(2,1)}, bf16[1024,5504]{1,0:T(8,128)(2,1)}, u32[]{:S(2)}, u32[]{:S(2)}) collective-permute-start(bf16[1024,5504]{1,0:T(8,128)(2,1)} %convolution_convert_fusion.1), channel_id=1, source_target_pairs={{0,8},{8,0},{16,24},{24,16},{1,9},{9,1},{17,25},{25,17},{2,10},{10... | collective-permute-start | bytes 33816584 | tf_op jit(solution)/shard_map/ppermute | solution.py:42
  1442.1 126.4 %collective-permute-start.26 = (bf16[1376,2048]{1,0:T(8,128)(2,1)}, bf16[1376,2048]{1,0:T(8,128)(2,1)}, u32[]{:S(2)}, u32[]{:S(2)}) collective-permute-start(bf16[1376,2048]{1,0:T(8,128)(2,1)} %fusion.2), channel_id=1, source_target_pairs={{0,16},{8,24},{16,0},{24,8},{1,17},{9,25},{17,1},{25,9},{2,18},{10... | collective-permute-start | bytes 16908296 | tf_op jit(solution)/shard_map/ppermute | solution.py:42
  1486.7 239.7 %collective-permute-start.27 = (bf16[512,5504]{1,0:T(8,128)(2,1)}, bf16[512,5504]{1,0:T(8,128)(2,1)}, u32[]{:S(2)}, u32[]{:S(2)}) collective-permute-start(bf16[512,5504]{1,0:T(8,128)(2,1)} %add_convert_fusion.3), channel_id=1, source_target_pairs={{0,1},{1,0},{2,3},{3,2},{4,5},{5,4},{6,7},{7,6},{8,9},{9,8},{10,11... | collective-permute-start | bytes 16908296 | tf_op jit(solution)/shard_map/ppermute | solution.py:42
  1540.4 92.0 %all-to-all-start.7 = ((bf16[8,2,512,128]{3,2,1,0:T(8,128)(2,1)}), bf16[8,2,512,128]{3,2,1,0:T(8,128)(2,1)S(1)}, u32[]{:S(2)}, u32[]{:S(2)}) async-start(bf16[8,2,512,128]{3,2,1,0:T(8,128)(2,1)} %bitcast.379), calls=%async_computation.7 | async-start | bytes 4194304 | tf_op jit(solution)/shard_map/all_to_all | solution.py:438
  1567.1 193.0 %collective-permute-start.28 = (bf16[1024,2048]{1,0:T(8,128)(2,1)}, bf16[1024,2048]{1,0:T(8,128)(2,1)}, u32[]{:S(2)}, u32[]{:S(2)}) collective-permute-start(bf16[1024,2048]{1,0:T(8,128)(2,1)} %convolution_convert_fusion.7), channel_id=1, source_target_pairs={{0,8},{8,0},{16,24},{24,16},{1,9},{9,1},{17,25},{25,17},{2,10},{10... | collective-permute-start | bytes 12582920 | tf_op jit(solution)/shard_map/ppermute | solution.py:42
  1567.2 252.4 %collective-permute-start.29 = (bf16[512,5504]{1,0:T(8,128)(2,1)}, bf16[512,5504]{1,0:T(8,128)(2,1)}, u32[]{:S(2)}, u32[]{:S(2)}) collective-permute-start(bf16[512,5504]{1,0:T(8,128)(2,1)} %add_convert_fusion.2), channel_id=1, source_target_pairs={{0,16},{8,24},{16,0},{24,8},{1,17},{9,25},{17,1},{25,9},{2,18},{10... | collective-permute-start | bytes 16908296 | tf_op jit(solution)/shard_map/ppermute | solution.py:42
  1666.2 139.3 %all-to-all-start.8 = ((bf16[8,1,512,384]{3,2,1,0:T(8,128)(2,1)}), bf16[8,1,512,384]{3,2,1,0:T(8,128)(2,1)}, u32[]{:S(2)}, u32[]{:S(2)}) async-start(bf16[8,1,512,384]{3,2,1,0:T(8,128)(2,1)} %copy-done.2), calls=%async_computation.8 | async-start | bytes 6291456 | tf_op jit(solution)/shard_map/all_to_all | solution.py:442
  1715.7 68.3 %collective-permute-start.31 = (bf16[4,172,2048]{2,0,1:T(4,128)(2,1)}, bf16[4,172,2048]{2,0,1:T(4,128)(2,1)}, u32[]{:S(2)}, u32[]{:S(2)}) collective-permute-start(bf16[4,172,2048]{2,0,1:T(4,128)(2,1)} %copy.160), channel_id=1, source_target_pairs={{0,1},{1,0},{2,3},{3,2},{4,5},{5,4},{6,7},{7,6},{8,9},{9,8},{10,11... | collective-permute-start | bytes 8454152 | tf_op jit(solution)/shard_map/ppermute | solution.py:42
  1736.3 64.3 %collective-permute-start.32 = (bf16[256,5504]{1,0:T(8,128)(2,1)}, bf16[256,5504]{1,0:T(8,128)(2,1)}, u32[]{:S(2)}, u32[]{:S(2)}) collective-permute-start(bf16[256,5504]{1,0:T(8,128)(2,1)} %dynamic-slice_bitcast_fusion.3), channel_id=1, source_target_pairs={{0,16},{8,24},{16,0},{24,8},{1,17},{9,25},{17,1},{25,9},{2,18},{10... | collective-permute-start | bytes 8454152 | tf_op jit(solution)/shard_map/ppermute | solution.py:42
  1767.1 75.7 %collective-permute-start.30 = (bf16[512,2048]{1,0:T(8,128)(2,1)}, bf16[512,2048]{1,0:T(8,128)(2,1)}, u32[]{:S(2)}, u32[]{:S(2)}) collective-permute-start(bf16[512,2048]{1,0:T(8,128)(2,1)} %add_convert_fusion.11), channel_id=1, source_target_pairs={{0,16},{8,24},{16,0},{24,8},{1,17},{9,25},{17,1},{25,9},{2,18},{10... | collective-permute-start | bytes 6291464 | tf_op jit(solution)/shard_map/ppermute | solution.py:42
  1805.5 133.4 %all-to-all-start.9 = ((bf16[8,1,512,384]{3,2,1,0:T(8,128)(2,1)}), bf16[8,1,512,384]{3,2,1,0:T(8,128)(2,1)}, u32[]{:S(2)}, u32[]{:S(2)}) async-start(bf16[8,1,512,384]{3,2,1,0:T(8,128)(2,1)} %attend_back.7), calls=%async_computation.9 | async-start | bytes 6291456 | tf_op jit(solution)/shard_map/all_to_all | solution.py:442
  1847.4 42.3 %collective-permute-start.34 = (bf16[4,64,2048]{2,1,0:T(8,128)(2,1)}, bf16[4,64,2048]{2,1,0:T(8,128)(2,1)}, u32[]{:S(2)}, u32[]{:S(2)}) collective-permute-start(bf16[4,64,2048]{2,1,0:T(8,128)(2,1)} %dynamic-slice_bitcast_fusion.7), channel_id=1, source_target_pairs={{0,1},{1,0},{2,3},{3,2},{4,5},{5,4},{6,7},{7,6},{8,9},{9,8},{10,11... | collective-permute-start | bytes 3145736 | tf_op jit(solution)/shard_map/ppermute | solution.py:42
  1849.5 85.3 %collective-permute-start.33 = (bf16[4,64,5504]{2,1,0:T(8,128)(2,1)}, bf16[4,64,5504]{2,1,0:T(8,128)(2,1)}, u32[]{:S(2)}, u32[]{:S(2)}) collective-permute-start(bf16[4,64,5504]{2,1,0:T(8,128)(2,1)} %dynamic-slice_bitcast_fusion.2), channel_id=1, source_target_pairs={{0,1},{1,0},{2,3},{3,2},{4,5},{5,4},{6,7},{7,6},{8,9},{9,8},{10,11... | collective-permute-start | bytes 8454152 | tf_op jit(solution)/shard_map/ppermute | solution.py:42
  1978.1 28.0 %collective-permute-start.35 = (bf16[1024,3072]{1,0:T(8,128)(2,1)}, bf16[1024,3072]{1,0:T(8,128)(2,1)}, u32[]{:S(2)}, u32[]{:S(2)}) collective-permute-start(bf16[1024,3072]{1,0:T(8,128)(2,1)} %convolution_convert_fusion.6), channel_id=1, source_target_pairs={{0,8},{8,0},{16,24},{24,16},{1,9},{9,1},{17,25},{25,17},{2,10},{10... | collective-permute-start | bytes 18874376 | tf_op jit(solution)/shard_map/ppermute | solution.py:42
  1987.3 28.0 %collective-permute-start.36 = (bf16[1024,3072]{1,0:T(8,128)(2,1)}, bf16[1024,3072]{1,0:T(8,128)(2,1)}, u32[]{:S(2)}, u32[]{:S(2)}) collective-permute-start(bf16[1024,3072]{1,0:T(8,128)(2,1)} %convolution_convert_fusion.5), channel_id=1, source_target_pairs={{0,8},{8,0},{16,24},{24,16},{1,9},{9,1},{17,25},{25,17},{2,10},{10... | collective-permute-start | bytes 18874376 | tf_op jit(solution)/shard_map/ppermute | solution.py:42
  1992.8 111.8 %collective-permute-start.37 = (bf16[2,64,18560]{2,1,0:T(8,128)(2,1)}, bf16[2,64,18560]{2,1,0:T(8,128)(2,1)}, u32[]{:S(2)}, u32[]{:S(2)}) collective-permute-start(bf16[2,64,18560]{2,1,0:T(8,128)(2,1)} %dynamic-slice_bitcast_fusion), channel_id=1, source_target_pairs={{0,2},{1,3},{2,0},{3,1},{4,6},{5,7},{6,4},{7,5},{8,10},{9,11},{10,... | collective-permute-start | bytes 14254088 | tf_op jit(solution)/shard_map/ppermute | solution.py:42
  2013.9 165.6 %collective-permute-start.38 = (bf16[512,3072]{1,0:T(8,128)(2,1)}, bf16[512,3072]{1,0:T(8,128)(2,1)}, u32[]{:S(2)}, u32[]{:S(2)}) collective-permute-start(bf16[512,3072]{1,0:T(8,128)(2,1)} %add_convert_fusion.7), channel_id=1, source_target_pairs={{0,16},{8,24},{16,0},{24,8},{1,17},{9,25},{17,1},{25,9},{2,18},{10... | collective-permute-start | bytes 9437192 | tf_op jit(solution)/shard_map/ppermute | solution.py:42
  2023.6 170.9 %collective-permute-start.39 = (bf16[512,3072]{1,0:T(8,128)(2,1)}, bf16[512,3072]{1,0:T(8,128)(2,1)}, u32[]{:S(2)}, u32[]{:S(2)}) collective-permute-start(bf16[512,3072]{1,0:T(8,128)(2,1)} %add_convert_fusion.6), channel_id=1, source_target_pairs={{0,1},{1,0},{2,3},{3,2},{4,5},{5,4},{6,7},{7,6},{8,9},{9,8},{10,11... | collective-permute-start | bytes 9437192 | tf_op jit(solution)/shard_map/ppermute | solution.py:42
  2157.0 10.2 collective-permute-start.45
  2167.2 8.1 collective-permute-start.46
  2175.4 4.1 collective-permute-start.47
  2179.4 104.8 %collective-permute-start.44 = (bf16[1,64,18560]{2,1,0:T(8,128)(2,1)S(1)}, bf16[1,64,18560]{2,1,0:T(8,128)(2,1)S(1)}, u32[]{:S(2)}, u32[]{:S(2)}) collective-permute-start(bf16[1,64,18560]{2,1,0:T(8,128)(2,1)S(1)} %constant_dynamic-slice_fusion.8), channel_id=1, source_target_pairs={{0,4},{1,5},{2,6},{3,7},{4,0},{5,1},{6,2},{7,3},{8,12},{9,13},{10,... | collective-permute-start | bytes 7127048 | tf_op jit(solution)/shard_map/ppermute | solution.py:42
  2200.7 84.3 %collective-permute-start.40 = (bf16[4,64,3072]{2,1,0:T(8,128)(2,1)S(1)}, bf16[4,64,3072]{2,1,0:T(8,128)(2,1)S(1)}, u32[]{:S(2)}, u32[]{:S(2)}) collective-permute-start(bf16[4,64,3072]{2,1,0:T(8,128)(2,1)S(1)} %dynamic-slice_bitcast_fusion.6), channel_id=1, source_target_pairs={{0,1},{1,0},{2,3},{3,2},{4,5},{5,4},{6,7},{7,6},{8,9},{9,8},{10,11... | collective-permute-start | bytes 4718600 | tf_op jit(solution)/shard_map/ppermute | solution.py:42
  2202.8 82.8 %collective-permute-start.41 = (bf16[256,3072]{1,0:T(8,128)(2,1)S(1)}, bf16[256,3072]{1,0:T(8,128)(2,1)S(1)}, u32[]{:S(2)}, u32[]{:S(2)}) collective-permute-start(bf16[256,3072]{1,0:T(8,128)(2,1)S(1)} %dynamic-slice_bitcast_fusion.5), channel_id=1, source_target_pairs={{0,16},{8,24},{16,0},{24,8},{1,17},{9,25},{17,1},{25,9},{2,18},{10... | collective-permute-start | bytes 4718600 | tf_op jit(solution)/shard_map/ppermute | solution.py:42
  2286.6 35.2 %collective-permute-start.42 = (bf16[2,64,6144]{2,1,0:T(8,128)(2,1)S(1)}, bf16[2,64,6144]{2,1,0:T(8,128)(2,1)S(1)}, u32[]{:S(2)}, u32[]{:S(2)}) collective-permute-start(bf16[2,64,6144]{2,1,0:T(8,128)(2,1)S(1)} %dynamic-slice_bitcast_fusion.4), channel_id=1, source_target_pairs={{0,2},{1,3},{2,0},{3,1},{4,6},{5,7},{6,4},{7,5},{8,10},{9,11},{10,... | collective-permute-start | bytes 4718600 | tf_op jit(solution)/shard_map/ppermute | solution.py:42
  2286.7 35.1 %collective-permute-start.48 = (f32[2,2,64]{2,0,1:T(2,128)S(1)}, f32[2,2,64]{2,0,1:T(2,128)S(1)}, u32[]{:S(2)}, u32[]{:S(2)}) collective-permute-start(f32[2,2,64]{2,0,1:T(2,128)S(1)} %bitcast.458), channel_id=1, source_target_pairs={{0,2},{1,3},{2,0},{3,1},{4,6},{5,7},{6,4},{7,5},{8,10},{9,11},{10,... | collective-permute-start | bytes 3080 | tf_op jit(solution)/shard_map/ppermute | solution.py:42
  2322.2 6.2 collective-permute-start.49
  2324.5 36.7 %collective-permute-start.43 = (bf16[1,64,6144]{2,1,0:T(8,128)(2,1)}, bf16[1,64,6144]{2,1,0:T(8,128)(2,1)}, u32[]{:S(2)}, u32[]{:S(2)}) collective-permute-start(bf16[1,64,6144]{2,1,0:T(8,128)(2,1)} %constant_dynamic-slice_fusion.9), channel_id=1, source_target_pairs={{0,4},{1,5},{2,6},{3,7},{4,0},{5,1},{6,2},{7,3},{8,12},{9,13},{10,... | collective-permute-start | bytes 2359304 | tf_op jit(solution)/shard_map/ppermute | solution.py:42
  (94 other events, 2157.4 us)
Sparse Core Ops, SparseCore 0:
  11.6 250.1 all-gather.1
